TPU v7x, 32 devices: a whole 2x2x4 slice. The times are simulated.
32 devices in a mesh: gx: 4 (over y, core), gy: 8 (over z, x).
Axes of the slice: x: 2, y: 2, z: 4, core: 2. Of those that a mesh axis runs over, the one named last changes fastest.
Arguments:
- adjoint_in: float32 [19, 64, 4, 1024], P(None, 'gx', None, 'gy'), may hold values from -6 to 6
- velocity: bfloat16 [2, 3, 64, 4, 1024], P(None, None, 'gx', None, 'gy')
- solid_tiles: int32 [16, 4, 256], P('gx', None, 'gy'), may hold values from 0 to 1, as said below
- link_blocked: int32 [18, 64, 4, 1024], P(None, 'gx', None, 'gy'), may hold values from 0 to 1, as said below
Outputs:
- adjoint_out: float32 [19, 64, 4, 1024], P(None, 'gx', None, 'gy')
- drag_sens: float32 [1], replicated
Inputs may be any that keep to these rules, and one draw needn't show every extreme that they name: `solid_tiles`: 1 on the levels below a tile's building height, heights 0 to 3 per tile. `link_blocked`: entry i - 1 is 1 exactly where the cell x + c_i (periodic in the plane) is solid or lies outside the 4 levels.
All inputs are finite; a program needn't handle non-finite values.
Results may differ from a plain program's by a relative error of at most 0.0003.
Values sent between devices are 32-bit elements; how exact they have to be, the bound alone decides.
No kernel may reach another device: no remote copies, remote signals or barrier semaphores. Data moves between devices by JAX's collectives and lax.ppermute only.
A program may use at most 64 MiB of HBM per device.

v0:
```python
import math

import jax
import jax.numpy as jnp
from jax import lax
from jax.sharding import PartitionSpec as P

TILE = 4
STEPS = 2


lattice_speeds = (
    (0, 0, 0),
    (1, 0, 0),
    (-1, 0, 0),
    (0, 1, 0),
    (0, -1, 0),
    (0, 0, 1),
    (0, 0, -1),
    (1, 1, 0),
    (-1, -1, 0),
    (1, -1, 0),
    (-1, 1, 0),
    (1, 0, 1),
    (-1, 0, -1),
    (1, 0, -1),
    (-1, 0, 1),
    (0, 1, 1),
    (0, -1, -1),
    (0, 1, -1),
    (0, -1, 1),
)
lattice_weights = (1.0 / 3.0,) + (1.0 / 18.0,) * 6 + (1.0 / 36.0,) * 12
relax_rate = 1.6
drag_factor = 20.0


def with_halo(block, sides, width):
    for axis, dim in sides:
        count = lax.axis_size(axis)
        forward = [(i, i + 1) for i in range(count - 1)]
        forward.append((count - 1, 0))
        backward = [(target, source) for source, target in forward]
        low = lax.ppermute(
            lax.slice_in_dim(block, block.shape[dim] - width, None, axis=dim), axis, forward
        )
        high = lax.ppermute(lax.slice_in_dim(block, 0, width, axis=dim), axis, backward)
        block = jnp.concatenate([low, block, high], axis=dim)
    return block


def opposite_of(number):
    return number + 1 if number % 2 == 1 else number - 1


def shift_level(field, lift):
    if lift == 1:
        return jnp.concatenate([field[:, 1:], jnp.zeros_like(field[:, :1])], axis=1)
    if lift == -1:
        return jnp.concatenate([jnp.zeros_like(field[:, :1]), field[:, :-1]], axis=1)
    return field


def adjoint_collide(moved, flow, fluid):
    speed_sq = flow[0] * flow[0] + flow[1] * flow[1] + flow[2] * flow[2]
    scalar_part = jnp.zeros_like(speed_sq)
    vector_part = [jnp.zeros_like(speed_sq) for axis_number in range(3)]
    drag_local = jnp.zeros_like(speed_sq)
    for number in range(19):
        speed = lattice_speeds[number]
        along = speed[0] * flow[0] + speed[1] * flow[1] + speed[2] * flow[2]
        weighted = lattice_weights[number] * moved[number]
        scalar_part = scalar_part + weighted * (
            1.0 + 3.0 * along + 4.5 * along * along - 1.5 * speed_sq
        )
        for axis_number in range(3):
            vector_part[axis_number] = vector_part[axis_number] + weighted * (
                3.0 * speed[axis_number]
                + 9.0 * along * speed[axis_number]
                - 3.0 * flow[axis_number]
            )
        drag_local = drag_local + 3.0 * weighted * along
    results = []
    for number in range(19):
        speed = lattice_speeds[number]
        projected = scalar_part
        for axis_number in range(3):
            projected = projected + vector_part[axis_number] * (
                speed[axis_number] - flow[axis_number]
            )
        results.append(fluid * ((1.0 - relax_rate) * moved[number] + relax_rate * projected))
    return (jnp.stack(results), fluid * drag_local)


def stream_back(padded, centre, blocked, span_x, span_y):
    moved = [centre[0]]
    for number in range(1, 19):
        speed = lattice_speeds[number]
        source = padded[
            number, 1 + speed[0] : 1 + speed[0] + span_x, :, 1 + speed[1] : 1 + speed[1] + span_y
        ]
        source = shift_level(source, speed[2])
        bounced = centre[opposite_of(number)] + 2.0 * speed[0]
        moved.append(jnp.where(blocked[number - 1] == 1, bounced, source))
    return moved


def per_device(adjoint_in, velocity, solid_tiles, link_blocked):
    rows_x = adjoint_in.shape[1]
    rows_y = adjoint_in.shape[3]
    levels = adjoint_in.shape[2]
    solid = jnp.repeat(jnp.repeat(solid_tiles, TILE, axis=0), TILE, axis=2)
    fluid = 1.0 - solid.astype(jnp.float32)
    state = adjoint_in
    step_terms = []
    for adjoint_step in range(STEPS):
        flow = velocity[adjoint_step].astype(jnp.float32)
        padded = with_halo(state, (("gx", 1), ("gy", 3)), 1)
        moved = stream_back(padded, state, link_blocked, rows_x, rows_y)
        state, drag_field = adjoint_collide(moved, flow, fluid)
        step_terms.append(jnp.sum(drag_field))
    total = jnp.zeros((), jnp.float32)
    for adjoint_step in range(STEPS):
        total = total + lax.psum(step_terms[adjoint_step], ("gx", "gy"))
    cell_count = rows_x * lax.axis_size("gx") * rows_y * lax.axis_size("gy") * levels
    scale = drag_factor / math.sqrt(cell_count)
    return (state, (-scale * total).reshape(1))


def solution(mesh):
    placed = (
        P(None, "gx", None, "gy"),
        P(None, None, "gx", None, "gy"),
        P("gx", None, "gy"),
        P(None, "gx", None, "gy"),
    )
    return jax.shard_map(
        per_device,
        mesh=mesh,
        in_specs=placed,
        out_specs=(P(None, "gx", None, "gy"), P()),
        check_vma=False,
    )
```

profile of v0, /device:TPU:0, one launch (start us, length us, event | category | flops | bytes accessed | tf_op | source)
XLA Modules:
  0.0 97.5 jit_solution(1880866343997107080)
XLA Ops:
  0.6 0.8 fusion.265
  1.9 2.0 %collective-permute-start = (f32[19,1,4,128]{3,2,1,0:T(4,128)S(1)}, f32[19,1,4,128]{3,2,1,0:T(4,128)S(1)}, u32[]{:S(2)}, u32[]{:S(2)}) collective-permute-start(f32[19,1,4,128]{3,2,1,0:T(4,128)S(1)} %get-tuple-element.194), channel_id=1, source_target_pairs={{8,0},{16,8},{24,16},{0,24},{9,1},{17,9},{25,17},{1,25},{10,2},{18... | collective-permute-start | bytes 116744 | tf_op jit(solution)/shard_map/ppermute | solution.py:47
  3.9 1.7 %fusion.264 = (f32[1,16,4,128]{3,2,1,0:T(4,128)S(1)}, f32[1,16,4,128]{3,2,1,0:T(4,128)S(1)}, f32[1,16,4,128]{3,2,1,0:T(4,128)S(1)}, f32[1,16,4,128]{3,2,1,0:T(4,...) fusion(f32[19,16,4,128]{3,2,1,0:T(4,128)} %param.4), kind=kLoop, calls=%fused_computation.493 | loop fusion | bytes 1245184 | tf_op jit(solution)/shard_map/slice | solution.py:103
  5.7 0.8 fusion.266
  6.6 0.6 copy-done.67
  9.3 0.6 fusion.262
  9.9 0.6 fusion.261
  12.0 5.3 %collective-permute-start.2 = (f32[19,18,4,1]{0,2,3,1:T(4,128)S(1)}, f32[19,18,4,1]{0,2,3,1:T(4,128)}, u32[]{:S(2)}, u32[]{:S(2)}) collective-permute-start(f32[19,18,4,1]{0,2,3,1:T(4,128)S(1)} %copy.538), channel_id=1, source_target_pairs={{1,0},{2,1},{3,2},{4,3},{5,4},{6,5},{7,6},{0,7},{9,8},{10,9},{11,1... | collective-permute-start | bytes 16424 | tf_op jit(solution)/shard_map/ppermute | solution.py:47
  19.8 4.1 %collective-permute-done.3 = f32[19,18,4,1]{0,2,3,1:T(4,128)S(1)} collective-permute-done((f32[19,18,4,1]{0,2,3,1:T(4,128)S(1)}, f32[19,18,4,1]{0,2,3,1:T(4,128)S(1)}, u32[]{:S(2)}, u32[]{:S(2)}) %collective-permute-start.3) | collective-permute-done | bytes 5504 | tf_op jit(solution)/shard_map/ppermute | solution.py:44
  23.9 1.0 %copy.442 = f32[19,18,4,1]{3,1,2,0:T(8,128)S(1)} copy(f32[19,18,4,1]{0,2,3,1:T(4,128)S(1)} %collective-permute-done.3) | data formatting | bytes 10944 | tf_op jit(solution)/shard_map/ppermute | solution.py:44
  25.0 1.8 %copy.438 = f32[19,18,4,1]{3,1,2,0:T(8,128)S(1)} copy(f32[19,18,4,1]{0,2,3,1:T(4,128)} %collective-permute-done.2) | data formatting | bytes 10944 | tf_op jit(solution)/shard_map/ppermute | solution.py:47
  28.1 1.7 %multiply_reduce_fusion.1 = (f32[]{:T(128)}, f32[16,4,128]{2,0,1:T(8,128)S(1)}, f32[16,4,128]{2,0,1:T(8,128)S(1)}, pred[16,4,128]{2,0,1:T(8,128)(4,1)}, f32[16,4...) fusion(f32[16,4,128]{2,0,1:T(8,128)S(1)} %copy.506, ...), kind=kLoop, calls=%fused_computation.356 | loop fusion | flops 1171455 | bytes 3136196 | tf_op jit(solution)/shard_map/reduce_sum | solution.py:121
  30.6 0.6 constant_dynamic-update-slice_fusion.17
  31.2 0.6 constant_dynamic-update-slice_fusion.16
  31.8 0.6 constant_dynamic-update-slice_fusion.15
  32.5 0.6 constant_dynamic-update-slice_fusion.14
  33.1 0.6 constant_dynamic-update-slice_fusion.13
  33.7 0.6 constant_dynamic-update-slice_fusion.12
  34.4 0.6 constant_dynamic-update-slice_fusion.11
  35.0 0.6 constant_dynamic-update-slice_fusion.10
  35.6 0.6 constant_dynamic-update-slice_fusion.9
  36.2 0.6 constant_dynamic-update-slice_fusion.8
  36.9 0.6 constant_dynamic-update-slice_fusion.7
  39.3 2.1 %collective-permute-done.5 = f32[19,1,4,128]{3,2,1,0:T(4,128)S(1)} collective-permute-done((f32[19,1,4,128]{3,2,1,0:T(4,128)S(1)}, f32[19,1,4,128]{3,2,1,0:T(4,128)S(1)}, u32[]{:S(2)}, u32[]{:S(2)}) %collective-permute-start.5) | collective-permute-done | bytes 38944 | tf_op jit(solution)/shard_map/ppermute | solution.py:44
  43.1 0.6 collective-permute-start.6
  43.8 1.4 %collective-permute-start.7 = (f32[19,18,4,1]{0,2,3,1:T(4,128)S(1)}, f32[19,18,4,1]{0,2,3,1:T(4,128)S(1)}, u32[]{:S(2)}, u32[]{:S(2)}) collective-permute-start(f32[19,18,4,1]{0,2,3,1:T(4,128)S(1)} %copy.504), channel_id=1, source_target_pairs={{0,1},{1,2},{2,3},{3,4},{4,5},{5,6},{6,7},{7,0},{8,9},{9,10},{10,1... | collective-permute-start | bytes 16424 | tf_op jit(solution)/shard_map/ppermute | solution.py:44
  47.0 3.4 %collective-permute-done.7 = f32[19,18,4,1]{0,2,3,1:T(4,128)S(1)} collective-permute-done((f32[19,18,4,1]{0,2,3,1:T(4,128)S(1)}, f32[19,18,4,1]{0,2,3,1:T(4,128)S(1)}, u32[]{:S(2)}, u32[]{:S(2)}) %collective-permute-start.7) | collective-permute-done | bytes 5504 | tf_op jit(solution)/shard_map/ppermute | solution.py:44
  50.5 1.0 %copy.505 = f32[19,18,4,1]{3,1,2,0:T(8,128)S(1)} copy(f32[19,18,4,1]{0,2,3,1:T(4,128)S(1)} %collective-permute-done.7) | data formatting | bytes 10944 | tf_op jit(solution)/shard_map/ppermute | solution.py:44
  51.5 1.1 %copy.503 = f32[19,18,4,1]{3,1,2,0:T(8,128)S(1)} copy(f32[19,18,4,1]{0,2,3,1:T(4,128)S(1)} %collective-permute-done.6) | data formatting | bytes 10944 | tf_op jit(solution)/shard_map/ppermute | solution.py:47
  53.9 1.6 %multiply_reduce_fusion = (f32[]{:T(128)}, f32[16,4,128]{2,0,1:T(8,128)}, f32[16,4,128]{2,0,1:T(8,128)S(1)}, f32[16,4,128]{2,0,1:T(8,128)S(1)}, f32[16,4,128]{2,...) fusion(f32[16,4,128]{2,0,1:T(8,128)S(1)} %copy.506, ...), kind=kLoop, calls=%fused_computation.355 | loop fusion | flops 1138687 | bytes 2480836 | tf_op jit(solution)/shard_map/reduce_sum | solution.py:121
  56.8 36.9 %psum.16 = f32[]{:T(128)} all-reduce(f32[]{:T(128)S(6)} %add.2107), channel_id=1, replica_groups=mesh['gx'=4,'gy'=8] {'gx','gy'}, use_global_device_ids=true, to_apply=%region_1.2 | all-reduce | flops 1 | bytes 8 | tf_op jit(solution)/shard_map/psum | solution.py:124
  94.7 1.1 %copy.527 = f32[19,16,4,128]{3,2,1,0:T(4,128)} copy(f32[19,16,4,128]{3,1,2,0:T(8,128)S(1)} %constant_dynamic-update-slice_fusion.26) | data formatting | bytes 1245184
  (217 shorter events, 15.5 us)
Async XLA Ops:
  1.4 7.3 %collective-permute-start.1 = (f32[19,1,4,128]{3,2,1,0:T(4,128)S(1)}, f32[19,1,4,128]{3,2,1,0:T(4,128)S(1)}, u32[]{:S(2)}, u32[]{:S(2)}) collective-permute-start(f32[19,1,4,128]{3,2,1,0:T(4,128)S(1)} %get-tuple-element.193), channel_id=1, source_target_pairs={{0,8},{8,16},{16,24},{24,0},{1,9},{9,17},{17,25},{25,1},{2,10},{10... | collective-permute-start | bytes 116744 | tf_op jit(solution)/shard_map/ppermute | solution.py:44
  1.9 3.8 %copy-start.48 = (bf16[2,3,16,4,128]{4,3,2,1,0:T(4,128)(2,1)S(1)}, bf16[2,3,16,4,128]{4,3,2,1,0:T(4,128)(2,1)}, u32[]{:S(2)}) copy-start(bf16[2,3,16,4,128]{4,3,2,1,0:T(4,128)(2,1)} %param.5) | copy-start | bytes 294916
  1.9 3.8 %copy-start.1 = (s32[18,16,4,128]{3,2,1,0:T(4,128)S(1)}, s32[18,16,4,128]{3,2,1,0:T(4,128)}, u32[]{:S(2)}) copy-start(s32[18,16,4,128]{3,2,1,0:T(4,128)} %param.7) | copy-start | bytes 1769476
  1.9 7.3 %collective-permute-start = (f32[19,1,4,128]{3,2,1,0:T(4,128)S(1)}, f32[19,1,4,128]{3,2,1,0:T(4,128)S(1)}, u32[]{:S(2)}, u32[]{:S(2)}) collective-permute-start(f32[19,1,4,128]{3,2,1,0:T(4,128)S(1)} %get-tuple-element.194), channel_id=1, source_target_pairs={{8,0},{16,8},{24,16},{0,24},{9,1},{17,9},{25,17},{1,25},{10,2},{18... | collective-permute-start | bytes 116744 | tf_op jit(solution)/shard_map/ppermute | solution.py:47
  6.6 2.2 %copy-start = (f32[19,16,4,128]{3,2,1,0:T(4,128)S(1)}, f32[19,16,4,128]{3,2,1,0:T(4,128)}, u32[]{:S(2)}) copy-start(f32[19,16,4,128]{3,2,1,0:T(4,128)} %param.4) | copy-start | bytes 1867780
  12.0 13.0 %collective-permute-start.2 = (f32[19,18,4,1]{0,2,3,1:T(4,128)S(1)}, f32[19,18,4,1]{0,2,3,1:T(4,128)}, u32[]{:S(2)}, u32[]{:S(2)}) collective-permute-start(f32[19,18,4,1]{0,2,3,1:T(4,128)S(1)} %copy.538), channel_id=1, source_target_pairs={{1,0},{2,1},{3,2},{4,3},{5,4},{6,5},{7,6},{0,7},{9,8},{10,9},{11,1... | collective-permute-start | bytes 16424 | tf_op jit(solution)/shard_map/ppermute | solution.py:47
  17.3 6.7 %collective-permute-start.3 = (f32[19,18,4,1]{0,2,3,1:T(4,128)S(1)}, f32[19,18,4,1]{0,2,3,1:T(4,128)S(1)}, u32[]{:S(2)}, u32[]{:S(2)}) collective-permute-start(f32[19,18,4,1]{0,2,3,1:T(4,128)S(1)} %copy.541), channel_id=1, source_target_pairs={{0,1},{1,2},{2,3},{3,4},{4,5},{5,6},{6,7},{7,0},{8,9},{9,10},{10,1... | collective-permute-start | bytes 16424 | tf_op jit(solution)/shard_map/ppermute | solution.py:44
  26.9 0.8 copy-start.18
  26.9 0.8 copy-start.19
  26.9 0.8 copy-start.20
  26.9 0.9 copy-start.21
  26.9 0.9 copy-start.22
  26.9 0.9 copy-start.23
  26.9 0.9 copy-start.35
  26.9 0.9 copy-start.36
  27.0 0.9 copy-start.37
  27.0 0.9 copy-start.38
  27.0 0.9 copy-start.41
  27.0 0.9 copy-start.42
  27.0 0.9 copy-start.43
  27.0 0.9 copy-start.45
  27.2 0.8 copy-start.10
  27.2 0.8 copy-start.7
  27.2 0.8 copy-start.4
  27.3 0.8 copy-start.2
  27.3 0.8 copy-start.3
  37.5 1.8 %collective-permute-start.4 = (f32[19,1,4,128]{3,2,1,0:T(4,128)S(1)}, f32[19,1,4,128]{3,2,1,0:T(4,128)S(1)}, u32[]{:S(2)}, u32[]{:S(2)}) collective-permute-start(f32[19,1,4,128]{3,2,1,0:T(4,128)S(1)} %bitcast.557), channel_id=1, source_target_pairs={{8,0},{16,8},{24,16},{0,24},{9,1},{17,9},{25,17},{1,25},{10,2},{18... | collective-permute-start | bytes 116744 | tf_op jit(solution)/shard_map/ppermute | solution.py:47
  37.6 3.9 %collective-permute-start.5 = (f32[19,1,4,128]{3,2,1,0:T(4,128)S(1)}, f32[19,1,4,128]{3,2,1,0:T(4,128)S(1)}, u32[]{:S(2)}, u32[]{:S(2)}) collective-permute-start(f32[19,1,4,128]{3,2,1,0:T(4,128)S(1)} %bitcast.556), channel_id=1, source_target_pairs={{0,8},{8,16},{16,24},{24,0},{1,9},{9,17},{17,25},{25,1},{2,10},{10... | collective-permute-start | bytes 116744 | tf_op jit(solution)/shard_map/ppermute | solution.py:44
  43.1 8.3 %collective-permute-start.6 = (f32[19,18,4,1]{0,2,3,1:T(4,128)S(1)}, f32[19,18,4,1]{0,2,3,1:T(4,128)S(1)}, u32[]{:S(2)}, u32[]{:S(2)}) collective-permute-start(f32[19,18,4,1]{0,2,3,1:T(4,128)S(1)} %copy.502), channel_id=1, source_target_pairs={{1,0},{2,1},{3,2},{4,3},{5,4},{6,5},{7,6},{0,7},{9,8},{10,9},{11,1... | collective-permute-start | bytes 16424 | tf_op jit(solution)/shard_map/ppermute | solution.py:47
  43.8 6.7 %collective-permute-start.7 = (f32[19,18,4,1]{0,2,3,1:T(4,128)S(1)}, f32[19,18,4,1]{0,2,3,1:T(4,128)S(1)}, u32[]{:S(2)}, u32[]{:S(2)}) collective-permute-start(f32[19,18,4,1]{0,2,3,1:T(4,128)S(1)} %copy.504), channel_id=1, source_target_pairs={{0,1},{1,2},{2,3},{3,4},{4,5},{5,6},{6,7},{7,0},{8,9},{9,10},{10,1... | collective-permute-start | bytes 16424 | tf_op jit(solution)/shard_map/ppermute | solution.py:44
  52.7 0.8 copy-start.59
  55.5 38.2 %copy-start.34 = (f32[16,4,128]{2,0,1:T(8,128)S(1)}, f32[16,4,128]{2,0,1:T(8,128)}, u32[]{:S(2)}) copy-start(f32[16,4,128]{2,0,1:T(8,128)} %get-tuple-element.15) | copy-start | bytes 98308
  (44 other events, 35.0 us)
where the time goes:
time: 99 us; the launch traced here: 97.5 us
  blocking collectives  36.9 us (37%)
  local copies, waits for them, and re-layouts  23.7 us (24%)
  other arithmetic  12.3 us (12%)
  starting transfers between devices  10.4 us (11%)
  waiting for transfers between devices  9.67 us (10%)
  between operations  4.59 us (5%)
    psum x1, blocking collectives, per_device(): total = total + lax.psum(step_terms[adjoint_step], ('gx', 'gy'))  36.9 us
    ppermute x4, waiting for transfers between devices, with_halo(): lax.ppermute(lax.slice_in_dim(block, block.shape[dim] - width, None, axis...  9.66 us
    ppermute x4, starting transfers between devices, with_halo(): lax.ppermute(lax.slice_in_dim(block, 0, width, axis=dim), axis, backward)  8.01 us
    unnamed x36, other arithmetic  7.93 us
    unnamed x141, local copies, waits for them, and re-layouts  4.99 us
    slice x10, local copies, waits for them, and re-layouts, shift_level(): return jnp.concatenate([field[:, 1:], jnp.zeros_like(field[:, :1])], axis=1)  3.66 us
    reduce_sum x2, other arithmetic, per_device(): step_terms.append(jnp.sum(drag_field))  3.32 us
    slice x10, local copies, waits for them, and re-layouts, shift_level(): field[:, :-1]  3.05 us
  transfers between devices with their start and end apart: 8, of which 3 were waited for; matrix products, arithmetic and copies ran while one was open for 13% of the time, Pallas kernels for 0%

commit v1 on v0

--- a/solution.py
+++ b/solution.py
@@ -119,9 +119,16 @@
         moved = stream_back(padded, state, link_blocked, rows_x, rows_y)
         state, drag_field = adjoint_collide(moved, flow, fluid)
         step_terms.append(jnp.sum(drag_field))
-    total = jnp.zeros((), jnp.float32)
-    for adjoint_step in range(STEPS):
-        total = total + lax.psum(step_terms[adjoint_step], ("gx", "gy"))
+    count = lax.axis_size("gx") * lax.axis_size("gy")
+    own = step_terms[0] + step_terms[1]
+    shared = lax.all_to_all(
+        jnp.broadcast_to(own.reshape(1, 1, 1), (count, 1, 128)),
+        ("gx", "gy"),
+        split_axis=0,
+        concat_axis=0,
+        tiled=True,
+    )
+    total = jnp.sum(shared[:, 0, 0])
     cell_count = rows_x * lax.axis_size("gx") * rows_y * lax.axis_size("gy") * levels
     scale = drag_factor / math.sqrt(cell_count)
     return (state, (-scale * total).reshape(1))

time: 99 us -> 70.1 us (0.71)
  blocking collectives: 36.9 us -> 0 us
  waiting for transfers between devices: 9.67 us -> 14.7 us
  starting transfers between devices: 10.4 us -> 13 us
    psum x1 -> x0, blocking collectives: 36.9 us -> none  [per_device(): total = total + lax.psum(step_terms[adjoint_step], ('gx', 'gy'))]
    all_to_all x0 -> x1, waiting for transfers between devices: none -> 4.99 us  [per_device(): lax.all_to_all(jnp.broadcast_to(own.reshape(1, 1, 1), (count, 1, 128)), (...]
    all_to_all x0 -> x1, starting transfers between devices: none -> 2.59 us  [per_device(): lax.all_to_all(jnp.broadcast_to(own.reshape(1, 1, 1), (count, 1, 128)), (...]
  transfers between devices with their start and end apart: 8 -> 9, of which waited for: 3 -> 4; matrix products, arithmetic and copies ran while one was open for 13% -> 21% of each run, Pallas kernels for 0% -> 0%
where the time goes in v1:
time: 70.1 us; the launch traced here: 69.4 us
  local copies, waits for them, and re-layouts  24.3 us (35%)
  waiting for transfers between devices  14.7 us (21%)
  starting transfers between devices  13 us (19%)
  other arithmetic  12.9 us (18%)
  between operations  4.51 us (6%)
    ppermute x4, waiting for transfers between devices, with_halo(): lax.ppermute(lax.slice_in_dim(block, block.shape[dim] - width, None, axis...  9.65 us
    ppermute x4, starting transfers between devices, with_halo(): lax.ppermute(lax.slice_in_dim(block, 0, width, axis=dim), axis, backward)  8.02 us
    unnamed x36, other arithmetic  7.96 us
    unnamed x141, local copies, waits for them, and re-layouts  5 us
    all_to_all x1, waiting for transfers between devices, per_device(): lax.all_to_all(jnp.broadcast_to(own.reshape(1, 1, 1), (count, 1, 128)), (...  4.99 us
    slice x10, local copies, waits for them, and re-layouts, shift_level(): return jnp.concatenate([field[:, 1:], jnp.zeros_like(field[:, :1])], axis=1)  3.66 us
    reduce_sum x2, other arithmetic, per_device(): step_terms.append(jnp.sum(drag_field))  3.24 us
    slice x10, local copies, waits for them, and re-layouts, shift_level(): field[:, :-1]  3.07 us
  transfers between devices with their start and end apart: 9, of which 4 were waited for; matrix products, arithmetic and copies ran while one was open for 21% of the time, Pallas kernels for 0%

profile of v1, /device:TPU:0, one launch (start us, length us, event | category | flops | bytes accessed | tf_op | source)
XLA Modules:
  0.0 69.4 jit_solution(4892424599318530182)
XLA Ops:
  0.6 0.8 %fusion.265 = (f32[19,1,4,128]{3,2,1,0:T(4,128)S(1)}, f32[19,1,4,128]{3,2,1,0:T(4,128)S(1)}) fusion(f32[19,16,4,128]{3,2,1,0:T(4,128)} %param.4), kind=kLoop, calls=%fused_computation.495 | loop fusion | bytes 155648 | tf_op jit(solution)/shard_map/slice | solution.py:45
  1.9 2.0 %collective-permute-start = (f32[19,1,4,128]{3,2,1,0:T(4,128)S(1)}, f32[19,1,4,128]{3,2,1,0:T(4,128)S(1)}, u32[]{:S(2)}, u32[]{:S(2)}) collective-permute-start(f32[19,1,4,128]{3,2,1,0:T(4,128)S(1)} %get-tuple-element.196), channel_id=1, source_target_pairs={{8,0},{16,8},{24,16},{0,24},{9,1},{17,9},{25,17},{1,25},{10,2},{18... | collective-permute-start | bytes 116744 | tf_op jit(solution)/shard_map/ppermute | solution.py:47
  3.9 1.7 %fusion.264 = (f32[1,16,4,128]{3,2,1,0:T(4,128)S(1)}, f32[1,16,4,128]{3,2,1,0:T(4,128)S(1)}, f32[1,16,4,128]{3,2,1,0:T(4,128)S(1)}, f32[1,16,4,128]{3,2,1,0:T(4,...) fusion(f32[19,16,4,128]{3,2,1,0:T(4,128)} %param.4), kind=kLoop, calls=%fused_computation.494 | loop fusion | bytes 1245184 | tf_op jit(solution)/shard_map/slice | solution.py:103
  5.7 0.9 %fusion.266 = (s32[1,16,4,128]{3,2,1,0:T(4,128)}, s32[1,16,4,128]{3,2,1,0:T(4,128)}, s32[1,16,4,128]{3,2,1,0:T(4,128)}, s32[1,16,4,128]{3,2,1,0:T(4,128)}, s32[1...) fusion(s32[18,16,4,128]{3,2,1,0:T(4,128)S(1)} %copy-done.1), kind=kLoop, calls=%fused_computation.496 | loop fusion | bytes 1179648 | tf_op jit(solution)/shard_map/slice | solution.py:104
  6.6 0.7 copy-done.67
  9.3 0.6 fusion.262
  12.0 5.3 %collective-permute-start.2 = (f32[19,18,4,1]{0,2,3,1:T(4,128)S(1)}, f32[19,18,4,1]{0,2,3,1:T(4,128)}, u32[]{:S(2)}, u32[]{:S(2)}) collective-permute-start(f32[19,18,4,1]{0,2,3,1:T(4,128)S(1)} %copy.624), channel_id=1, source_target_pairs={{1,0},{2,1},{3,2},{4,3},{5,4},{6,5},{7,6},{0,7},{9,8},{10,9},{11,1... | collective-permute-start | bytes 16424 | tf_op jit(solution)/shard_map/ppermute | solution.py:47
  19.8 4.1 %collective-permute-done.3 = f32[19,18,4,1]{0,2,3,1:T(4,128)S(1)} collective-permute-done((f32[19,18,4,1]{0,2,3,1:T(4,128)S(1)}, f32[19,18,4,1]{0,2,3,1:T(4,128)S(1)}, u32[]{:S(2)}, u32[]{:S(2)}) %collective-permute-start.3) | collective-permute-done | bytes 5504 | tf_op jit(solution)/shard_map/ppermute | solution.py:44
  23.9 1.0 %copy.526 = f32[19,18,4,1]{3,1,2,0:T(8,128)S(1)} copy(f32[19,18,4,1]{0,2,3,1:T(4,128)S(1)} %collective-permute-done.3) | data formatting | bytes 10944 | tf_op jit(solution)/shard_map/ppermute | solution.py:44
  25.0 1.8 %copy.522 = f32[19,18,4,1]{3,1,2,0:T(8,128)S(1)} copy(f32[19,18,4,1]{0,2,3,1:T(4,128)} %collective-permute-done.2) | data formatting | bytes 10944 | tf_op jit(solution)/shard_map/ppermute | solution.py:47
  28.1 1.7 %multiply_reduce_fusion.1 = (f32[]{:T(128)}, f32[16,4,128]{2,0,1:T(8,128)S(1)}, f32[16,4,128]{2,0,1:T(8,128)S(1)}, pred[16,4,128]{2,0,1:T(8,128)(4,1)}, f32[16,4...) fusion(f32[16,4,128]{2,0,1:T(8,128)S(1)} %copy.590, ...), kind=kLoop, calls=%fused_computation.356 | loop fusion | flops 1171455 | bytes 3136196 | tf_op jit(solution)/shard_map/reduce_sum | solution.py:121
  30.6 0.6 constant_dynamic-update-slice_fusion.17
  31.2 0.6 constant_dynamic-update-slice_fusion.16
  31.9 0.6 constant_dynamic-update-slice_fusion.15
  32.5 0.6 constant_dynamic-update-slice_fusion.14
  33.1 0.6 constant_dynamic-update-slice_fusion.13
  33.7 0.6 constant_dynamic-update-slice_fusion.12
  35.0 0.6 constant_dynamic-update-slice_fusion.10
  35.6 0.6 constant_dynamic-update-slice_fusion.9
  36.2 0.6 constant_dynamic-update-slice_fusion.8
  36.9 0.6 constant_dynamic-update-slice_fusion.7
  39.3 2.1 %collective-permute-done.5 = f32[19,1,4,128]{3,2,1,0:T(4,128)S(1)} collective-permute-done((f32[19,1,4,128]{3,2,1,0:T(4,128)S(1)}, f32[19,1,4,128]{3,2,1,0:T(4,128)S(1)}, u32[]{:S(2)}, u32[]{:S(2)}) %collective-permute-start.5) | collective-permute-done | bytes 38944 | tf_op jit(solution)/shard_map/ppermute | solution.py:44
  43.2 0.7 collective-permute-start.6
  43.8 1.4 %collective-permute-start.7 = (f32[19,18,4,1]{0,2,3,1:T(4,128)S(1)}, f32[19,18,4,1]{0,2,3,1:T(4,128)S(1)}, u32[]{:S(2)}, u32[]{:S(2)}) collective-permute-start(f32[19,18,4,1]{0,2,3,1:T(4,128)S(1)} %copy.588), channel_id=1, source_target_pairs={{0,1},{1,2},{2,3},{3,4},{4,5},{5,6},{6,7},{7,0},{8,9},{9,10},{10,1... | collective-permute-start | bytes 16424 | tf_op jit(solution)/shard_map/ppermute | solution.py:44
  47.0 3.4 %collective-permute-done.7 = f32[19,18,4,1]{0,2,3,1:T(4,128)S(1)} collective-permute-done((f32[19,18,4,1]{0,2,3,1:T(4,128)S(1)}, f32[19,18,4,1]{0,2,3,1:T(4,128)S(1)}, u32[]{:S(2)}, u32[]{:S(2)}) %collective-permute-start.7) | collective-permute-done | bytes 5504 | tf_op jit(solution)/shard_map/ppermute | solution.py:44
  50.5 1.0 %copy.589 = f32[19,18,4,1]{3,1,2,0:T(8,128)S(1)} copy(f32[19,18,4,1]{0,2,3,1:T(4,128)S(1)} %collective-permute-done.7) | data formatting | bytes 10944 | tf_op jit(solution)/shard_map/ppermute | solution.py:44
  51.5 1.1 %copy.587 = f32[19,18,4,1]{3,1,2,0:T(8,128)S(1)} copy(f32[19,18,4,1]{0,2,3,1:T(4,128)S(1)} %collective-permute-done.6) | data formatting | bytes 10944 | tf_op jit(solution)/shard_map/ppermute | solution.py:47
  53.9 1.5 %multiply_reduce_fusion = (f32[]{:T(128)}, f32[16,4,128]{2,0,1:T(8,128)}, f32[16,4,128]{2,0,1:T(8,128)S(1)}, f32[16,4,128]{2,0,1:T(8,128)S(1)}, f32[16,4,128]{2,...) fusion(f32[16,4,128]{2,0,1:T(8,128)S(1)} %copy.590, ...), kind=kLoop, calls=%fused_computation.355 | loop fusion | flops 1138687 | bytes 2480836 | tf_op jit(solution)/shard_map/reduce_sum | solution.py:121
  57.2 2.6 %all-to-all-start = ((f32[32,1,128]{2,1,0:T(1,128)}), f32[32,1,128]{2,1,0:T(1,128)S(1)}, u32[]{:S(2)}, u32[]{:S(2)}) async-start(f32[32,1,128]{2,1,0:T(1,128)} %broadcast_in_dim.13), calls=%async_computation | async-start | bytes 32768 | tf_op jit(solution)/shard_map/all_to_all | solution.py:124
  60.9 1.1 %copy.612 = f32[19,16,4,128]{3,2,1,0:T(4,128)} copy(f32[19,16,4,128]{3,1,2,0:T(8,128)S(1)} %constant_dynamic-update-slice_fusion.26) | data formatting | bytes 1245184
  62.0 5.0 %all-to-all-done = f32[32,1,128]{2,1,0:T(1,128)S(1)} async-done(((f32[32,1,128]{2,1,0:T(1,128)}), f32[32,1,128]{2,1,0:T(1,128)S(1)}, u32[]{:S(2)}, u32[]{:S(2)}) %all-to-all-start) | async-done | bytes 16416 | tf_op jit(solution)/shard_map/all_to_all | solution.py:124
  66.9 0.6 slice_reduce_fusion
  (220 shorter events, 17.4 us)
Async XLA Ops:
  1.4 7.3 %collective-permute-start.1 = (f32[19,1,4,128]{3,2,1,0:T(4,128)S(1)}, f32[19,1,4,128]{3,2,1,0:T(4,128)S(1)}, u32[]{:S(2)}, u32[]{:S(2)}) collective-permute-start(f32[19,1,4,128]{3,2,1,0:T(4,128)S(1)} %get-tuple-element.195), channel_id=1, source_target_pairs={{0,8},{8,16},{16,24},{24,0},{1,9},{9,17},{17,25},{25,1},{2,10},{10... | collective-permute-start | bytes 116744 | tf_op jit(solution)/shard_map/ppermute | solution.py:44
  1.9 3.8 %copy-start.48 = (bf16[2,3,16,4,128]{4,3,2,1,0:T(4,128)(2,1)S(1)}, bf16[2,3,16,4,128]{4,3,2,1,0:T(4,128)(2,1)}, u32[]{:S(2)}) copy-start(bf16[2,3,16,4,128]{4,3,2,1,0:T(4,128)(2,1)} %param.5) | copy-start | bytes 294916
  1.9 3.8 %copy-start.1 = (s32[18,16,4,128]{3,2,1,0:T(4,128)S(1)}, s32[18,16,4,128]{3,2,1,0:T(4,128)}, u32[]{:S(2)}) copy-start(s32[18,16,4,128]{3,2,1,0:T(4,128)} %param.7) | copy-start | bytes 1769476
  1.9 7.3 %collective-permute-start = (f32[19,1,4,128]{3,2,1,0:T(4,128)S(1)}, f32[19,1,4,128]{3,2,1,0:T(4,128)S(1)}, u32[]{:S(2)}, u32[]{:S(2)}) collective-permute-start(f32[19,1,4,128]{3,2,1,0:T(4,128)S(1)} %get-tuple-element.196), channel_id=1, source_target_pairs={{8,0},{16,8},{24,16},{0,24},{9,1},{17,9},{25,17},{1,25},{10,2},{18... | collective-permute-start | bytes 116744 | tf_op jit(solution)/shard_map/ppermute | solution.py:47
  6.6 2.2 %copy-start = (f32[19,16,4,128]{3,2,1,0:T(4,128)S(1)}, f32[19,16,4,128]{3,2,1,0:T(4,128)}, u32[]{:S(2)}) copy-start(f32[19,16,4,128]{3,2,1,0:T(4,128)} %param.4) | copy-start | bytes 1867780
  12.0 13.0 %collective-permute-start.2 = (f32[19,18,4,1]{0,2,3,1:T(4,128)S(1)}, f32[19,18,4,1]{0,2,3,1:T(4,128)}, u32[]{:S(2)}, u32[]{:S(2)}) collective-permute-start(f32[19,18,4,1]{0,2,3,1:T(4,128)S(1)} %copy.624), channel_id=1, source_target_pairs={{1,0},{2,1},{3,2},{4,3},{5,4},{6,5},{7,6},{0,7},{9,8},{10,9},{11,1... | collective-permute-start | bytes 16424 | tf_op jit(solution)/shard_map/ppermute | solution.py:47
  17.3 6.7 %collective-permute-start.3 = (f32[19,18,4,1]{0,2,3,1:T(4,128)S(1)}, f32[19,18,4,1]{0,2,3,1:T(4,128)S(1)}, u32[]{:S(2)}, u32[]{:S(2)}) collective-permute-start(f32[19,18,4,1]{0,2,3,1:T(4,128)S(1)} %copy.627), channel_id=1, source_target_pairs={{0,1},{1,2},{2,3},{3,4},{4,5},{5,6},{6,7},{7,0},{8,9},{9,10},{10,1... | collective-permute-start | bytes 16424 | tf_op jit(solution)/shard_map/ppermute | solution.py:44
  26.9 0.8 %copy-start.18 = (s32[1,16,4,128]{3,2,1,0:T(4,128)S(1)}, s32[1,16,4,128]{3,2,1,0:T(4,128)}, u32[]{:S(2)}) copy-start(s32[1,16,4,128]{3,2,1,0:T(4,128)} %get-tuple-element.209) | copy-start | bytes 98308
  26.9 0.8 %copy-start.19 = (s32[1,16,4,128]{3,2,1,0:T(4,128)S(1)}, s32[1,16,4,128]{3,2,1,0:T(4,128)}, u32[]{:S(2)}) copy-start(s32[1,16,4,128]{3,2,1,0:T(4,128)} %get-tuple-element.210) | copy-start | bytes 98308
  26.9 0.8 %copy-start.20 = (s32[1,16,4,128]{3,2,1,0:T(4,128)S(1)}, s32[1,16,4,128]{3,2,1,0:T(4,128)}, u32[]{:S(2)}) copy-start(s32[1,16,4,128]{3,2,1,0:T(4,128)} %get-tuple-element.211) | copy-start | bytes 98308
  26.9 0.9 %copy-start.21 = (s32[1,16,4,128]{3,2,1,0:T(4,128)S(1)}, s32[1,16,4,128]{3,2,1,0:T(4,128)}, u32[]{:S(2)}) copy-start(s32[1,16,4,128]{3,2,1,0:T(4,128)} %get-tuple-element.212) | copy-start | bytes 98308
  26.9 0.9 %copy-start.22 = (s32[1,16,4,128]{3,2,1,0:T(4,128)S(1)}, s32[1,16,4,128]{3,2,1,0:T(4,128)}, u32[]{:S(2)}) copy-start(s32[1,16,4,128]{3,2,1,0:T(4,128)} %get-tuple-element.213) | copy-start | bytes 98308
  26.9 0.9 %copy-start.23 = (s32[1,16,4,128]{3,2,1,0:T(4,128)S(1)}, s32[1,16,4,128]{3,2,1,0:T(4,128)}, u32[]{:S(2)}) copy-start(s32[1,16,4,128]{3,2,1,0:T(4,128)} %get-tuple-element.214) | copy-start | bytes 98308
  26.9 0.9 %copy-start.35 = (f32[1,16,4,128]{3,2,1,0:T(4,128)S(1)}, f32[1,16,4,128]{3,2,1,0:T(4,128)}, u32[]{:S(2)}) copy-start(f32[1,16,4,128]{3,2,1,0:T(4,128)} %get-tuple-element.169) | copy-start | bytes 98308
  26.9 0.9 %copy-start.36 = (f32[1,16,4,128]{3,2,1,0:T(4,128)S(1)}, f32[1,16,4,128]{3,2,1,0:T(4,128)}, u32[]{:S(2)}) copy-start(f32[1,16,4,128]{3,2,1,0:T(4,128)} %get-tuple-element.166) | copy-start | bytes 98308
  27.0 0.9 %copy-start.37 = (f32[16,3,128]{2,0,1:T(8,128)S(1)}, f32[16,3,128]{2,0,1:T(8,128)}, u32[]{:S(2)}) copy-start(f32[16,3,128]{2,0,1:T(8,128)} %slice.363) | copy-start | bytes 73732
  27.0 0.9 %copy-start.38 = (f32[16,3,128]{2,0,1:T(8,128)S(1)}, f32[16,3,128]{2,0,1:T(8,128)}, u32[]{:S(2)}) copy-start(f32[16,3,128]{2,0,1:T(8,128)} %slice.364) | copy-start | bytes 73732
  27.0 0.9 %copy-start.41 = (f32[16,3,128]{2,0,1:T(8,128)S(1)}, f32[16,3,128]{2,0,1:T(8,128)}, u32[]{:S(2)}) copy-start(f32[16,3,128]{2,0,1:T(8,128)} %slice.370) | copy-start | bytes 73732
  27.0 0.9 %copy-start.42 = (f32[16,3,128]{2,0,1:T(8,128)S(1)}, f32[16,3,128]{2,0,1:T(8,128)}, u32[]{:S(2)}) copy-start(f32[16,3,128]{2,0,1:T(8,128)} %slice.366) | copy-start | bytes 73732
  27.0 0.9 %copy-start.43 = (f32[16,3,128]{2,0,1:T(8,128)S(1)}, f32[16,3,128]{2,0,1:T(8,128)}, u32[]{:S(2)}) copy-start(f32[16,3,128]{2,0,1:T(8,128)} %slice.372) | copy-start | bytes 73732
  27.0 0.9 %copy-start.45 = (f32[16,3,128]{2,0,1:T(8,128)S(1)}, f32[16,3,128]{2,0,1:T(8,128)}, u32[]{:S(2)}) copy-start(f32[16,3,128]{2,0,1:T(8,128)} %slice.368) | copy-start | bytes 73732
  27.2 0.8 %copy-start.10 = (s32[1,16,4,128]{3,2,1,0:T(4,128)S(1)}, s32[1,16,4,128]{3,2,1,0:T(4,128)}, u32[]{:S(2)}) copy-start(s32[1,16,4,128]{3,2,1,0:T(4,128)} %get-tuple-element.201) | copy-start | bytes 98308
  27.2 0.8 %copy-start.7 = (s32[1,16,4,128]{3,2,1,0:T(4,128)S(1)}, s32[1,16,4,128]{3,2,1,0:T(4,128)}, u32[]{:S(2)}) copy-start(s32[1,16,4,128]{3,2,1,0:T(4,128)} %get-tuple-element.198) | copy-start | bytes 98308
  27.2 0.8 %copy-start.4 = (f32[1,16,4,128]{3,2,1,0:T(4,128)S(1)}, f32[1,16,4,128]{3,2,1,0:T(4,128)}, u32[]{:S(2)}) copy-start(f32[1,16,4,128]{3,2,1,0:T(4,128)} %get-tuple-element.190) | copy-start | bytes 98308
  27.2 0.8 %copy-start.2 = (f32[1,16,4,128]{3,2,1,0:T(4,128)S(1)}, f32[1,16,4,128]{3,2,1,0:T(4,128)}, u32[]{:S(2)}) copy-start(f32[1,16,4,128]{3,2,1,0:T(4,128)} %get-tuple-element.188) | copy-start | bytes 98308
  27.3 0.8 %copy-start.3 = (f32[1,16,4,128]{3,2,1,0:T(4,128)S(1)}, f32[1,16,4,128]{3,2,1,0:T(4,128)}, u32[]{:S(2)}) copy-start(f32[1,16,4,128]{3,2,1,0:T(4,128)} %get-tuple-element.189) | copy-start | bytes 98308
  37.6 1.8 %collective-permute-start.4 = (f32[19,1,4,128]{3,2,1,0:T(4,128)S(1)}, f32[19,1,4,128]{3,2,1,0:T(4,128)S(1)}, u32[]{:S(2)}, u32[]{:S(2)}) collective-permute-start(f32[19,1,4,128]{3,2,1,0:T(4,128)S(1)} %bitcast.557), channel_id=1, source_target_pairs={{8,0},{16,8},{24,16},{0,24},{9,1},{17,9},{25,17},{1,25},{10,2},{18... | collective-permute-start | bytes 116744 | tf_op jit(solution)/shard_map/ppermute | solution.py:47
  37.6 3.9 %collective-permute-start.5 = (f32[19,1,4,128]{3,2,1,0:T(4,128)S(1)}, f32[19,1,4,128]{3,2,1,0:T(4,128)S(1)}, u32[]{:S(2)}, u32[]{:S(2)}) collective-permute-start(f32[19,1,4,128]{3,2,1,0:T(4,128)S(1)} %bitcast.556), channel_id=1, source_target_pairs={{0,8},{8,16},{16,24},{24,0},{1,9},{9,17},{17,25},{25,1},{2,10},{10... | collective-permute-start | bytes 116744 | tf_op jit(solution)/shard_map/ppermute | solution.py:44
  43.2 8.4 %collective-permute-start.6 = (f32[19,18,4,1]{0,2,3,1:T(4,128)S(1)}, f32[19,18,4,1]{0,2,3,1:T(4,128)S(1)}, u32[]{:S(2)}, u32[]{:S(2)}) collective-permute-start(f32[19,18,4,1]{0,2,3,1:T(4,128)S(1)} %copy.586), channel_id=1, source_target_pairs={{1,0},{2,1},{3,2},{4,3},{5,4},{6,5},{7,6},{0,7},{9,8},{10,9},{11,1... | collective-permute-start | bytes 16424 | tf_op jit(solution)/shard_map/ppermute | solution.py:47
  43.8 6.7 %collective-permute-start.7 = (f32[19,18,4,1]{0,2,3,1:T(4,128)S(1)}, f32[19,18,4,1]{0,2,3,1:T(4,128)S(1)}, u32[]{:S(2)}, u32[]{:S(2)}) collective-permute-start(f32[19,18,4,1]{0,2,3,1:T(4,128)S(1)} %copy.588), channel_id=1, source_target_pairs={{0,1},{1,2},{2,3},{3,4},{4,5},{5,6},{6,7},{7,0},{8,9},{9,10},{10,1... | collective-permute-start | bytes 16424 | tf_op jit(solution)/shard_map/ppermute | solution.py:44
  57.2 2.6 %copy-start.34 = (f32[16,4,128]{2,0,1:T(8,128)S(1)}, f32[16,4,128]{2,0,1:T(8,128)}, u32[]{:S(2)}) copy-start(f32[16,4,128]{2,0,1:T(8,128)} %get-tuple-element.17) | copy-start | bytes 98308
  57.2 9.7 %all-to-all-start = ((f32[32,1,128]{2,1,0:T(1,128)}), f32[32,1,128]{2,1,0:T(1,128)S(1)}, u32[]{:S(2)}, u32[]{:S(2)}) async-start(f32[32,1,128]{2,1,0:T(1,128)} %broadcast_in_dim.13), calls=%async_computation | async-start | bytes 32768 | tf_op jit(solution)/shard_map/all_to_all | solution.py:124
  (45 other events, 35.8 us)

commit v2 on v0

v2 whole, which is shorter than its diff:
```python
import math

import jax
import jax.numpy as jnp
from jax import lax
from jax.experimental import pallas as pl
from jax.experimental.pallas import tpu as pltpu
from jax.sharding import PartitionSpec as P

TILE = 4
STEPS = 2

lattice_speeds = (
    (0, 0, 0),
    (1, 0, 0),
    (-1, 0, 0),
    (0, 1, 0),
    (0, -1, 0),
    (0, 0, 1),
    (0, 0, -1),
    (1, 1, 0),
    (-1, -1, 0),
    (1, -1, 0),
    (-1, 1, 0),
    (1, 0, 1),
    (-1, 0, -1),
    (1, 0, -1),
    (-1, 0, 1),
    (0, 1, 1),
    (0, -1, -1),
    (0, 1, -1),
    (0, -1, 1),
)
relax_rate = 1.6
drag_factor = 20.0
LEVELS = 4
LANES = 128
GUARD = 8

x_up = [n for n in range(19) if lattice_speeds[n][0] == 1]
x_down = [n for n in range(19) if lattice_speeds[n][0] == -1]
y_up = [n for n in range(19) if lattice_speeds[n][1] == 1]
y_down = [n for n in range(19) if lattice_speeds[n][1] == -1]
vmem = pl.BlockSpec(memory_space=pltpu.VMEM)


def opposite_of(number):
    return number + 1 if number % 2 == 1 else number - 1


def lane_index():
    return lax.broadcasted_iota(jnp.int32, (8, LANES), 1)


def pack_edges(read, rows, x_low, x_high, y_low, y_high):
    lane = lane_index()
    groups = rows // 8
    for slot, number in enumerate(x_up):
        x_low[slot] = read(number, 0, LEVELS)
    for slot, number in enumerate(x_down):
        x_high[slot] = read(number, rows - LEVELS, LEVELS)
    for numbers, out, edge in ((y_up, y_low, 0), (y_down, y_high, LANES - 1)):
        packed = jnp.zeros((8, LANES), jnp.float32)
        for slot, number in enumerate(numbers):
            for group in range(groups):
                place = slot * groups + group
                value = pltpu.roll(read(number, 8 * group, 8), (place - edge) % LANES, 1)
                packed = jnp.where(lane == place, value, packed)
        out[...] = packed


def fill_gathered(read, rows, gathered, halos):
    x_after, x_before, y_after, y_before, corners = halos
    lane = lane_index()
    groups = rows // 8
    y_after_all = y_after[...]
    y_before_all = y_before[...]
    for number in range(1, 19):
        cx, cy, cz = lattice_speeds[number]
        for group in range(groups):
            value = read(number, 8 * group, 8)
            if cy == 1:
                place = y_up.index(number) * groups + group
                halo = pltpu.roll(y_after_all, (LANES - 1 - place) % LANES, 1)
                value = jnp.where(lane == LANES - 1, halo, pltpu.roll(value, LANES - 1, 1))
            elif cy == -1:
                place = y_down.index(number) * groups + group
                halo = pltpu.roll(y_before_all, (-place) % LANES, 1)
                value = jnp.where(lane == 0, halo, pltpu.roll(value, 1, 1))
            gathered[number, pl.ds(GUARD + 8 * group, 8), :] = value
        if cx == 0:
            continue
        if cx == 1:
            row = x_after[x_up.index(number)]
            first = GUARD + rows
        else:
            row = x_before[x_down.index(number)]
            first = GUARD - LEVELS
        if cy != 0:
            corner = corners[(cx, cy)][...]
            edge = 0 if cy == 1 else LANES - 1
            row = jnp.where(lane[:LEVELS] == edge, corner, row)
            row = pltpu.roll(row, (-cy) % LANES, 1)
        gathered[number, pl.ds(first, LEVELS), :] = row


def collide(moved, flow, fluid):
    ux, uy, uz = flow
    total = {n: moved[n] + moved[n + 1] for n in range(1, 19, 2)}
    gap = {n: moved[n] - moved[n + 1] for n in range(1, 19, 2)}
    xy, xz, yz = total[7] + total[9], total[11] + total[13], total[15] + total[17]
    axis_x, axis_y, axis_z = 2.0 * total[1], 2.0 * total[3], 2.0 * total[5]
    density = 12.0 * moved[0] + (axis_x + axis_y + axis_z) + (xy + xz + yz)
    pxx = axis_x + xy + xz
    pyy = axis_y + xy + yz
    pzz = axis_z + xz + yz
    pxy = total[7] - total[9]
    pxz = total[11] - total[13]
    pyz = total[15] - total[17]
    dx = 2.0 * gap[1] + (gap[7] + gap[9]) + (gap[11] + gap[13])
    dy = 2.0 * gap[3] + (gap[7] - gap[9]) + (gap[15] + gap[17])
    dz = 2.0 * gap[5] + (gap[11] - gap[13]) + (gap[15] - gap[17])
    vx = pxx * ux + pxy * uy + pxz * uz
    vy = pxy * ux + pyy * uy + pyz * uz
    vz = pxz * ux + pyz * uy + pzz * uz
    speed_sq = ux * ux + uy * uy + uz * uz
    drag = fluid * (ux * dx + uy * dy + uz * dz)
    scaled = (relax_rate / 36.0) * fluid
    base = scaled * (density + 1.5 * (speed_sq * density) - 4.5 * (ux * vx + uy * vy + uz * vz))
    scaled3 = 3.0 * scaled
    bx = scaled3 * (dx + 3.0 * vx - ux * density)
    by = scaled3 * (dy + 3.0 * vy - uy * density)
    bz = scaled3 * (dz + 3.0 * vz - uz * density)
    keep = (1.0 - relax_rate) * fluid
    results = [keep * moved[0] + base]
    for number in range(1, 19, 2):
        along = None
        for speed, part in zip(lattice_speeds[number], (bx, by, bz)):
            if speed == 0:
                continue
            if along is None:
                along = part if speed == 1 else -part
            else:
                along = along + part if speed == 1 else along - part
        results.append(keep * moved[number] + (base + along))
        results.append(keep * moved[number + 1] + (base - along))
    return results, drag


def spread_fluid(solid):
    tiles = solid.shape[1]
    row = lax.broadcasted_iota(jnp.int32, (tiles, LANES), 0)
    column = lax.broadcasted_iota(jnp.int32, (tiles, LANES), 1)
    spread = (column // TILE == row).astype(jnp.float32)
    fluid = 1.0 - jnp.dot(solid[...].astype(jnp.float32), spread, preferred_element_type=jnp.float32)
    blocks = []
    for tile_row in range(solid.shape[0] // LEVELS):
        part = fluid[tile_row * LEVELS : (tile_row + 1) * LEVELS]
        blocks.append(jnp.concatenate([part, part], axis=0))
    return blocks


def run_step(step, read, write, gathered, velocity, blocked, solid, rows):
    fluid_blocks = spread_fluid(solid)
    drag_sum = jnp.zeros((8, LANES), jnp.float32)
    for pair in range(rows // 16):
        flow_pair = [velocity[step, axis, pl.ds(16 * pair, 16), :].astype(jnp.float32) for axis in range(3)]
        for half in range(2):
            first = 16 * pair + 8 * half
            flow = [part[8 * half : 8 * half + 8] for part in flow_pair]
            here = [read(n, first, 8) for n in range(19)]
            moved = [here[0]]
            for number in range(1, 19):
                cx, cy, cz = lattice_speeds[number]
                source = gathered[number, pl.ds(GUARD + first + LEVELS * cx + cz, 8), :]
                bounced = here[opposite_of(number)]
                if cx != 0:
                    bounced = bounced + 2.0 * cx
                moved.append(jnp.where(blocked[number - 1, pl.ds(first, 8), :] == 1, bounced, source))
            results, drag = collide(moved, flow, fluid_blocks[first // (LEVELS * TILE)])
            for number in range(19):
                write(number, first, results[number])
            drag_sum = drag_sum + drag
    return drag_sum


def pack_kernel(state, x_low, x_high, y_low, y_high):
    def read(number, first, count):
        return state[number, pl.ds(first, count), :]

    pack_edges(read, state.shape[1], x_low, x_high, y_low, y_high)


def step_kernel(step, last, *refs):
    if last:
        (state, xa, xb, ya, yb, c0, c1, c2, c3, velocity, blocked, solid, before, out, shared, gathered) = refs
    else:
        (state, xa, xb, ya, yb, c0, c1, c2, c3, velocity, blocked, solid, out, drag_out) = refs[:14]
        x_low, x_high, y_low, y_high, gathered = refs[14:]
    rows = state.shape[1]

    def read(number, first, count):
        return state[number, pl.ds(first, count), :]

    def write(number, first, value):
        out[number, pl.ds(first, 8), :] = value

    corners = {(1, 1): c0, (-1, -1): c1, (1, -1): c2, (-1, 1): c3}
    fill_gathered(read, rows, gathered, (xa, xb, ya, yb, corners))
    drag_sum = run_step(step, read, write, gathered, velocity, blocked, solid, rows)
    if last:
        drag_sum = drag_sum + before[...]
        shared[...] = jnp.broadcast_to(jnp.sum(drag_sum), shared.shape)
    else:
        drag_out[...] = drag_sum

        def read_out(number, first, count):
            return out[number, pl.ds(first, count), :]

        pack_edges(read_out, rows, x_low, x_high, y_low, y_high)


def exchange(x_low, x_high, y_low, y_high):
    nx, ny = lax.axis_size("gx"), lax.axis_size("gy")
    from_after_x = [((i + 1) % nx, i) for i in range(nx)]
    from_before_x = [(i, (i + 1) % nx) for i in range(nx)]
    from_after_y = [((i + 1) % ny, i) for i in range(ny)]
    from_before_y = [(i, (i + 1) % ny) for i in range(ny)]

    def diagonal(cx, cy):
        return [
            (((i + cx) % nx) * ny + (j + cy) % ny, i * ny + j) for i in range(nx) for j in range(ny)
        ]

    both = ("gx", "gy")
    x_after = lax.ppermute(x_low, "gx", from_after_x)
    x_before = lax.ppermute(x_high, "gx", from_before_x)
    y_after = lax.ppermute(y_low, "gy", from_after_y)
    y_before = lax.ppermute(y_high, "gy", from_before_y)
    c0 = lax.ppermute(x_low[x_up.index(7)], both, diagonal(1, 1))
    c1 = lax.ppermute(x_high[x_down.index(8)], both, diagonal(-1, -1))
    c2 = lax.ppermute(x_low[x_up.index(9)], both, diagonal(1, -1))
    c3 = lax.ppermute(x_high[x_down.index(10)], both, diagonal(-1, 1))
    return x_after, x_before, y_after, y_before, c0, c1, c2, c3


def per_device(adjoint_in, velocity, solid_tiles, link_blocked):
    rows_x, levels, rows_y = adjoint_in.shape[1:]
    rows = rows_x * levels
    state = adjoint_in.reshape(19, rows, rows_y)
    flow = velocity.reshape(STEPS, 3, rows, rows_y)
    solid = solid_tiles.reshape(-1, solid_tiles.shape[2])
    blocked = link_blocked.reshape(18, rows, rows_y)
    edges = (
        jax.ShapeDtypeStruct((5, levels, rows_y), jnp.float32),
        jax.ShapeDtypeStruct((5, levels, rows_y), jnp.float32),
        jax.ShapeDtypeStruct((8, rows_y), jnp.float32),
        jax.ShapeDtypeStruct((8, rows_y), jnp.float32),
    )
    field = jax.ShapeDtypeStruct(state.shape, jnp.float32)
    scratch = [pltpu.VMEM((19, rows + 2 * GUARD, rows_y), jnp.float32)]
    params = pltpu.CompilerParams(vmem_limit_bytes=16 * 1024 * 1024)
    packed = pl.pallas_call(
        pack_kernel, out_shape=edges, in_specs=[vmem], out_specs=(vmem,) * 4, compiler_params=params
    )(state)
    halos = exchange(*packed)
    results = pl.pallas_call(
        lambda *refs: step_kernel(0, False, *refs),
        out_shape=(field, jax.ShapeDtypeStruct((8, rows_y), jnp.float32)) + edges,
        in_specs=[vmem] * 12,
        out_specs=(vmem,) * 6,
        scratch_shapes=scratch,
        compiler_params=params,
    )(state, *halos, flow, blocked, solid)
    state, drag = results[:2]
    halos = exchange(*results[2:])
    count = lax.axis_size("gx") * lax.axis_size("gy")
    state, own = pl.pallas_call(
        lambda *refs: step_kernel(1, True, *refs),
        out_shape=(field, jax.ShapeDtypeStruct((count, 1, rows_y), jnp.float32)),
        in_specs=[vmem] * 13,
        out_specs=(vmem,) * 2,
        scratch_shapes=scratch,
        compiler_params=params,
    )(state, *halos, flow, blocked, solid, drag)
    shared = lax.all_to_all(own, ("gx", "gy"), split_axis=0, concat_axis=0, tiled=True)
    cell_count = rows * rows_y * count
    scale = drag_factor / math.sqrt(cell_count) * 3.0 / 36.0
    total = jnp.sum(shared[:, 0, 0])
    return (state.reshape(adjoint_in.shape), (-scale * total).reshape(1))


def solution(mesh):
    placed = (
        P(None, "gx", None, "gy"),
        P(None, None, "gx", None, "gy"),
        P("gx", None, "gy"),
        P(None, "gx", None, "gy"),
    )
    return jax.shard_map(
        per_device,
        mesh=mesh,
        in_specs=placed,
        out_specs=(P(None, "gx", None, "gy"), P()),
        check_vma=False,
    )
```

time: 99 us -> 57.2 us (0.58); the launches traced: 97.5 us -> 57 us
  blocking collectives: 36.9 us -> 12.4 us
  local copies, waits for them, and re-layouts: 23.7 us -> 1.98 us
  starting transfers between devices: 10.4 us -> 30.7 us
  other arithmetic: 12.3 us -> 0.63 us
  waiting for transfers between devices: 9.67 us -> 6.78 us
  between operations: 4.59 us -> 2.48 us
  Pallas kernels: 0 us -> 1.99 us
    psum x1 -> x0, blocking collectives: 36.9 us -> none  [per_device(): total = total + lax.psum(step_terms[adjoint_step], ('gx', 'gy'))]
    ppermute x8 -> x16, starting transfers between devices: 10.4 us -> 30.7 us  [the longest x2 11.1 us: exchange(): c3 = lax.ppermute(x_high[x_down.index(10)], both, diagonal(-1, 1))]
    slice x31 -> x0, local copies, waits for them, and re-layouts: 13.3 us -> none  [the longest x10 3.66 us: shift_level(): return jnp.concatenate([field[:, 1:], jnp.zeros_like(field[:, :1])], axis=1)]
    all_to_all x0 -> x1, blocking collectives: none -> 12.4 us  [per_device(): lax.all_to_all(own, ('gx', 'gy'), split_axis=0, concat_axis=0, tiled=True)]
    unnamed x36 -> x0, other arithmetic: 7.93 us -> none
    ppermute x4 -> x0, local copies, waits for them, and re-layouts: 4.97 us -> none  [the longest x2 2.89 us: with_halo(): lax.ppermute(lax.slice_in_dim(block, 0, width, axis=dim), axis, backward)]
    unnamed x141 -> x10, local copies, waits for them, and re-layouts: 4.99 us -> 1.97 us
    ppermute x8 -> x16, waiting for transfers between devices: 9.67 us -> 6.78 us  [the longest x2 2.62 us: exchange(): c0 = lax.ppermute(x_low[x_up.index(7)], both, diagonal(1, 1))]
  transfers between devices with their start and end apart: 8 -> 16, of which waited for: 3 -> 9; matrix products, arithmetic and copies ran while one was open for 13% -> 0% of each run, Pallas kernels for 0% -> 0%
where the time goes in v2:
time: 57.2 us; the launch traced here: 57 us
  starting transfers between devices  30.7 us (54%)
  blocking collectives  12.4 us (22%)
  waiting for transfers between devices  6.78 us (12%)
  between operations  2.48 us (4%)
  Pallas kernels  1.99 us (3%)
  local copies, waits for them, and re-layouts  1.98 us (3%)
  other arithmetic  0.63 us (1%)
    all_to_all x1, blocking collectives, per_device(): lax.all_to_all(own, ('gx', 'gy'), split_axis=0, concat_axis=0, tiled=True)  12.4 us
    ppermute x2, starting transfers between devices, exchange(): c3 = lax.ppermute(x_high[x_down.index(10)], both, diagonal(-1, 1))  11.1 us
    ppermute x2, starting transfers between devices, exchange(): y_after = lax.ppermute(y_low, 'gy', from_after_y)  9.8 us
    ppermute x2, starting transfers between devices, exchange(): c0 = lax.ppermute(x_low[x_up.index(7)], both, diagonal(1, 1))  7.69 us
    ppermute x2, waiting for transfers between devices, exchange(): c0 = lax.ppermute(x_low[x_up.index(7)], both, diagonal(1, 1))  2.62 us
    ppermute x2, waiting for transfers between devices, exchange(): y_before = lax.ppermute(y_high, 'gy', from_before_y)  2.16 us
    unnamed x10, local copies, waits for them, and re-layouts  1.97 us
    pallas_call x1, Pallas kernels, per_device(): pl.pallas_call(lambda *refs: step_kernel(1, True, *refs), out_shape=(fiel...  1.28 us
  transfers between devices with their start and end apart: 16, of which 9 were waited for; matrix products, arithmetic and copies ran while one was open for 0% of the time, Pallas kernels for 0%

profile of v2, /device:TPU:0, one launch (start us, length us, event | category | flops | bytes accessed | tf_op | source)
XLA Modules:
  0.0 57.0 jit_solution(7392764195069317909)
XLA Ops:
  0.6 1.1 %copy-done = f32[19,16,4,128]{3,2,1,0:T(4,128)S(1)} copy-done((f32[19,16,4,128]{3,2,1,0:T(4,128)S(1)}, f32[19,16,4,128]{3,2,1,0:T(4,128)}, u32[]{:S(2)}) %copy-start) | copy-done | bytes 622616
  1.7 0.1 shard_map.59
  1.9 0.5 collective-permute-start.1
  2.4 6.8 %collective-permute-start.7 = (f32[4,128]{1,0:T(4,128)S(1)}, f32[4,128]{1,0:T(4,128)S(1)}, u32[]{:S(2)}, u32[]{:S(2)}) collective-permute-start(f32[4,128]{1,0:T(4,128)S(1)} %get-tuple-element.30), channel_id=1, source_target_pairs={{25,0},{26,1},{27,2},{28,3},{29,4},{30,5},{31,6},{24,7},{1,8},{2,9... | collective-permute-start | bytes 6152 | tf_op jit(solution)/shard_map/ppermute | solution.py:243
  9.1 0.0 collective-permute-start
  9.2 0.5 collective-permute-start.6
  9.6 0.8 %collective-permute-done.7.refs_8_ = f32[4,128]{1,0:T(4,128)S(1)} collective-permute-done((f32[4,128]{1,0:T(4,128)S(1)}, f32[4,128]{1,0:T(4,128)S(1)}, u32[]{:S(2)}, u32[]{:S(2)}) %collective-permute-start.7) | collective-permute-done | bytes 2080 | tf_op jit(solution)/shard_map/ppermute | solution.py:243
  10.4 4.7 %collective-permute-start.2 = (f32[8,128]{1,0:T(8,128)S(1)}, f32[8,128]{1,0:T(8,128)S(1)}, u32[]{:S(2)}, u32[]{:S(2)}) collective-permute-start(f32[8,128]{1,0:T(8,128)S(1)} %get-tuple-element.16), channel_id=1, source_target_pairs={{1,0},{2,1},{3,2},{4,3},{5,4},{6,5},{7,6},{0,7},{9,8},{10,9},{11,1... | collective-permute-start | bytes 12296 | tf_op jit(solution)/shard_map/ppermute | solution.py:238
  15.1 0.6 %collective-permute-done.5.refs_6_ = f32[4,128]{1,0:T(4,128)S(1)} collective-permute-done((f32[4,128]{1,0:T(4,128)S(1)}, f32[4,128]{1,0:T(4,128)S(1)}, u32[]{:S(2)}, u32[]{:S(2)}) %collective-permute-start.5) | collective-permute-done | bytes 2080 | tf_op jit(solution)/shard_map/ppermute | solution.py:241
  15.7 3.5 %collective-permute-start.4 = (f32[4,128]{1,0:T(4,128)S(1)}, f32[4,128]{1,0:T(4,128)S(1)}, u32[]{:S(2)}, u32[]{:S(2)}) collective-permute-start(f32[4,128]{1,0:T(4,128)S(1)} %get-tuple-element.33), channel_id=1, source_target_pairs={{9,0},{10,1},{11,2},{12,3},{13,4},{14,5},{15,6},{8,7},{17,8},{18,9... | collective-permute-start | bytes 6152 | tf_op jit(solution)/shard_map/ppermute | solution.py:240
  19.2 1.3 %collective-permute-done.4.refs_5_ = f32[4,128]{1,0:T(4,128)S(1)} collective-permute-done((f32[4,128]{1,0:T(4,128)S(1)}, f32[4,128]{1,0:T(4,128)S(1)}, u32[]{:S(2)}, u32[]{:S(2)}) %collective-permute-start.4) | collective-permute-done | bytes 2080 | tf_op jit(solution)/shard_map/ppermute | solution.py:240
  20.6 0.0 collective-permute-done.2.refs_3_
  20.6 1.5 %collective-permute-done.3.refs_4_ = f32[8,128]{1,0:T(8,128)S(1)} collective-permute-done((f32[8,128]{1,0:T(8,128)S(1)}, f32[8,128]{1,0:T(8,128)S(1)}, u32[]{:S(2)}, u32[]{:S(2)}) %collective-permute-start.3) | collective-permute-done | bytes 4128 | tf_op jit(solution)/shard_map/ppermute | solution.py:239
  22.0 0.0 collective-permute-done.1.refs_2_
  22.1 0.0 copy-start.2
  22.1 0.9 %copy-done.2 = bf16[2,3,16,4,128]{4,3,2,1,0:T(4,128)(2,1)S(1)} copy-done((bf16[2,3,16,4,128]{4,3,2,1,0:T(4,128)(2,1)S(1)}, bf16[2,3,16,4,128]{4,3,2,1,0:T(4,128)(2,1)}, u32[]{:S(2)}) %copy-start.2) | copy-done | bytes 98328
  23.0 0.6 shard_map.60
  23.5 0.1 collective-permute-start.9
  23.6 4.4 %collective-permute-start.15 = (f32[4,128]{1,0:T(4,128)S(1)}, f32[4,128]{1,0:T(4,128)S(1)}, u32[]{:S(2)}, u32[]{:S(2)}) collective-permute-start(f32[4,128]{1,0:T(4,128)S(1)} %get-tuple-element.26), channel_id=1, source_target_pairs={{25,0},{26,1},{27,2},{28,3},{29,4},{30,5},{31,6},{24,7},{1,8},{2,9... | collective-permute-start | bytes 6152 | tf_op jit(solution)/shard_map/ppermute | solution.py:243
  28.0 0.0 collective-permute-start.13
  28.0 1.0 %collective-permute-start.8 = (f32[5,4,128]{2,1,0:T(4,128)S(1)}, f32[5,4,128]{2,1,0:T(4,128)S(1)}, u32[]{:S(2)}, u32[]{:S(2)}) collective-permute-start(f32[5,4,128]{2,1,0:T(4,128)S(1)} %get-tuple-element.19), channel_id=1, source_target_pairs={{8,0},{16,8},{24,16},{0,24},{9,1},{17,9},{25,17},{1,25},{10,2},{18... | collective-permute-start | bytes 30728 | tf_op jit(solution)/shard_map/ppermute | solution.py:236
  29.0 0.0 collective-permute-start.14
  29.0 0.3 collective-permute-done.15.refs_8_
  29.3 5.1 %collective-permute-start.10 = (f32[8,128]{1,0:T(8,128)S(1)}, f32[8,128]{1,0:T(8,128)S(1)}, u32[]{:S(2)}, u32[]{:S(2)}) collective-permute-start(f32[8,128]{1,0:T(8,128)S(1)} %get-tuple-element.21), channel_id=1, source_target_pairs={{1,0},{2,1},{3,2},{4,3},{5,4},{6,5},{7,6},{0,7},{9,8},{10,9},{11,1... | collective-permute-start | bytes 12296 | tf_op jit(solution)/shard_map/ppermute | solution.py:238
  34.4 0.2 collective-permute-done.13.refs_6_
  34.6 0.1 collective-permute-done.14.refs_7_
  34.7 4.2 %collective-permute-start.12 = (f32[4,128]{1,0:T(4,128)S(1)}, f32[4,128]{1,0:T(4,128)S(1)}, u32[]{:S(2)}, u32[]{:S(2)}) collective-permute-start(f32[4,128]{1,0:T(4,128)S(1)} %get-tuple-element.29), channel_id=1, source_target_pairs={{9,0},{10,1},{11,2},{12,3},{13,4},{14,5},{15,6},{8,7},{17,8},{18,9... | collective-permute-start | bytes 6152 | tf_op jit(solution)/shard_map/ppermute | solution.py:240
  38.9 1.3 %collective-permute-done.12.refs_5_ = f32[4,128]{1,0:T(4,128)S(1)} collective-permute-done((f32[4,128]{1,0:T(4,128)S(1)}, f32[4,128]{1,0:T(4,128)S(1)}, u32[]{:S(2)}, u32[]{:S(2)}) %collective-permute-start.12) | collective-permute-done | bytes 2080 | tf_op jit(solution)/shard_map/ppermute | solution.py:240
  40.2 0.7 %collective-permute-done.11.refs_4_ = f32[8,128]{1,0:T(8,128)S(1)} collective-permute-done((f32[8,128]{1,0:T(8,128)S(1)}, f32[8,128]{1,0:T(8,128)S(1)}, u32[]{:S(2)}, u32[]{:S(2)}) %collective-permute-start.11) | collective-permute-done | bytes 4128 | tf_op jit(solution)/shard_map/ppermute | solution.py:239
  40.9 1.3 %shard_map.61 = (f32[19,64,128]{2,1,0:T(8,128)}, f32[32,1,128]{2,1,0:T(1,128)S(1)}) custom-call(f32[19,64,128]{2,1,0:T(8,128)S(1)} %get-tuple-element.18.refs_0_, f32[5,4,128]{2,1,0:T(4,128)S(1)} %collective-permute-done.8.refs_1_, f32[5,4,128]{2,1,0:T(4,128)S(1)} %collective-permute-done.9.refs_2_, f32[8,128]{1,0:T(8,128)S(1)} %collective-permute-done.10.refs_3_, ...), custom_call_target="tpu_custom_call" | custom-call | tf_op jit(solution)/shard_map/pallas_call | solution.py:278
  42.2 12.4 %all_to_all.5 = f32[32,1,128]{2,1,0:T(1,128)S(1)} all-to-all(f32[32,1,128]{2,1,0:T(1,128)S(1)} %get-tuple-element.25), channel_id=1, replica_groups=mesh['gx'=4,'gy'=8] {'gx','gy'}, dimensions={0} | all-to-all | bytes 32768 | tf_op jit(solution)/shard_map/all_to_all | solution.py:286
  54.6 0.6 %slice_reduce_fusion = f32[]{:T(128)} fusion(f32[32,1,128]{2,1,0:T(1,128)S(1)} %all_to_all.5), kind=kLoop, calls=%fused_computation | loop fusion | flops 31 | bytes 132 | tf_op jit(solution)/shard_map/reduce_sum | solution.py:289
  (19 shorter events, 0.0 us)
Async XLA Ops:
  0.6 1.1 %copy-start = (f32[19,16,4,128]{3,2,1,0:T(4,128)S(1)}, f32[19,16,4,128]{3,2,1,0:T(4,128)}, u32[]{:S(2)}) copy-start(f32[19,16,4,128]{3,2,1,0:T(4,128)} %param.4) | copy-start | bytes 1867780
  1.7 20.3 %copy-start.1 = (s32[18,16,4,128]{3,2,1,0:T(4,128)S(1)}, s32[18,16,4,128]{3,2,1,0:T(4,128)}, u32[]{:S(2)}) copy-start(s32[18,16,4,128]{3,2,1,0:T(4,128)} %param.7) | copy-start | bytes 1769476
  1.9 20.2 %collective-permute-start.1 = (f32[5,4,128]{2,1,0:T(4,128)S(1)}, f32[5,4,128]{2,1,0:T(4,128)S(1)}, u32[]{:S(2)}, u32[]{:S(2)}) collective-permute-start(f32[5,4,128]{2,1,0:T(4,128)S(1)} %get-tuple-element.15), channel_id=1, source_target_pairs={{0,8},{8,16},{16,24},{24,0},{1,9},{9,17},{17,25},{25,1},{2,10},{10... | collective-permute-start | bytes 30728 | tf_op jit(solution)/shard_map/ppermute | solution.py:237
  2.4 8.1 %collective-permute-start.7 = (f32[4,128]{1,0:T(4,128)S(1)}, f32[4,128]{1,0:T(4,128)S(1)}, u32[]{:S(2)}, u32[]{:S(2)}) collective-permute-start(f32[4,128]{1,0:T(4,128)S(1)} %get-tuple-element.30), channel_id=1, source_target_pairs={{25,0},{26,1},{27,2},{28,3},{29,4},{30,5},{31,6},{24,7},{1,8},{2,9... | collective-permute-start | bytes 6152 | tf_op jit(solution)/shard_map/ppermute | solution.py:243
  9.1 6.6 %collective-permute-start.5 = (f32[4,128]{1,0:T(4,128)S(1)}, f32[4,128]{1,0:T(4,128)S(1)}, u32[]{:S(2)}, u32[]{:S(2)}) collective-permute-start(f32[4,128]{1,0:T(4,128)S(1)} %get-tuple-element.31), channel_id=1, source_target_pairs={{31,0},{24,1},{25,2},{26,3},{27,4},{28,5},{29,6},{30,7},{7,8},{0,9... | collective-permute-start | bytes 6152 | tf_op jit(solution)/shard_map/ppermute | solution.py:241
  9.1 12.9 %collective-permute-start = (f32[5,4,128]{2,1,0:T(4,128)S(1)}, f32[5,4,128]{2,1,0:T(4,128)S(1)}, u32[]{:S(2)}, u32[]{:S(2)}) collective-permute-start(f32[5,4,128]{2,1,0:T(4,128)S(1)} %get-tuple-element.14), channel_id=1, source_target_pairs={{8,0},{16,8},{24,16},{0,24},{9,1},{17,9},{25,17},{1,25},{10,2},{18... | collective-permute-start | bytes 30728 | tf_op jit(solution)/shard_map/ppermute | solution.py:236
  9.2 12.9 %copy-start.4 = (s32[4,4,32]{2,1,0:T(4,128)S(1)}, s32[4,4,32]{2,1,0:T(4,128)}, u32[]{:S(2)}) copy-start(s32[4,4,32]{2,1,0:T(4,128)} %param.6) | copy-start | bytes 6148
  9.2 6.6 %collective-permute-start.6 = (f32[4,128]{1,0:T(4,128)S(1)}, f32[4,128]{1,0:T(4,128)S(1)}, u32[]{:S(2)}, u32[]{:S(2)}) collective-permute-start(f32[4,128]{1,0:T(4,128)S(1)} %get-tuple-element.32), channel_id=1, source_target_pairs={{15,0},{8,1},{9,2},{10,3},{11,4},{12,5},{13,6},{14,7},{23,8},{16,9... | collective-permute-start | bytes 6152 | tf_op jit(solution)/shard_map/ppermute | solution.py:242
  10.4 10.1 %collective-permute-start.2 = (f32[8,128]{1,0:T(8,128)S(1)}, f32[8,128]{1,0:T(8,128)S(1)}, u32[]{:S(2)}, u32[]{:S(2)}) collective-permute-start(f32[8,128]{1,0:T(8,128)S(1)} %get-tuple-element.16), channel_id=1, source_target_pairs={{1,0},{2,1},{3,2},{4,3},{5,4},{6,5},{7,6},{0,7},{9,8},{10,9},{11,1... | collective-permute-start | bytes 12296 | tf_op jit(solution)/shard_map/ppermute | solution.py:238
  15.7 6.3 %collective-permute-start.3 = (f32[8,128]{1,0:T(8,128)S(1)}, f32[8,128]{1,0:T(8,128)S(1)}, u32[]{:S(2)}, u32[]{:S(2)}) collective-permute-start(f32[8,128]{1,0:T(8,128)S(1)} %get-tuple-element.17), channel_id=1, source_target_pairs={{0,1},{1,2},{2,3},{3,4},{4,5},{5,6},{6,7},{7,0},{8,9},{9,10},{10,1... | collective-permute-start | bytes 12296 | tf_op jit(solution)/shard_map/ppermute | solution.py:239
  15.7 4.8 %collective-permute-start.4 = (f32[4,128]{1,0:T(4,128)S(1)}, f32[4,128]{1,0:T(4,128)S(1)}, u32[]{:S(2)}, u32[]{:S(2)}) collective-permute-start(f32[4,128]{1,0:T(4,128)S(1)} %get-tuple-element.33), channel_id=1, source_target_pairs={{9,0},{10,1},{11,2},{12,3},{13,4},{14,5},{15,6},{8,7},{17,8},{18,9... | collective-permute-start | bytes 6152 | tf_op jit(solution)/shard_map/ppermute | solution.py:240
  22.1 0.9 %copy-start.2 = (bf16[2,3,16,4,128]{4,3,2,1,0:T(4,128)(2,1)S(1)}, bf16[2,3,16,4,128]{4,3,2,1,0:T(4,128)(2,1)}, u32[]{:S(2)}) copy-start(bf16[2,3,16,4,128]{4,3,2,1,0:T(4,128)(2,1)} %param.5) | copy-start | bytes 294916
  23.0 17.9 %copy-start.3 = (bf16[2,3,16,4,128]{4,3,2,1,0:T(4,128)(2,1)S(1)}, bf16[2,3,16,4,128]{4,3,2,1,0:T(4,128)(2,1)}, u32[]{:S(2)}) copy-start(bf16[2,3,16,4,128]{4,3,2,1,0:T(4,128)(2,1)} %param.5) | copy-start | bytes 294916
  23.5 17.3 %collective-permute-start.9 = (f32[5,4,128]{2,1,0:T(4,128)S(1)}, f32[5,4,128]{2,1,0:T(4,128)S(1)}, u32[]{:S(2)}, u32[]{:S(2)}) collective-permute-start(f32[5,4,128]{2,1,0:T(4,128)S(1)} %get-tuple-element.20), channel_id=1, source_target_pairs={{0,8},{8,16},{16,24},{24,0},{1,9},{9,17},{17,25},{25,1},{2,10},{10... | collective-permute-start | bytes 30728 | tf_op jit(solution)/shard_map/ppermute | solution.py:237
  23.6 5.7 %collective-permute-start.15 = (f32[4,128]{1,0:T(4,128)S(1)}, f32[4,128]{1,0:T(4,128)S(1)}, u32[]{:S(2)}, u32[]{:S(2)}) collective-permute-start(f32[4,128]{1,0:T(4,128)S(1)} %get-tuple-element.26), channel_id=1, source_target_pairs={{25,0},{26,1},{27,2},{28,3},{29,4},{30,5},{31,6},{24,7},{1,8},{2,9... | collective-permute-start | bytes 6152 | tf_op jit(solution)/shard_map/ppermute | solution.py:243
  28.0 6.6 %collective-permute-start.13 = (f32[4,128]{1,0:T(4,128)S(1)}, f32[4,128]{1,0:T(4,128)S(1)}, u32[]{:S(2)}, u32[]{:S(2)}) collective-permute-start(f32[4,128]{1,0:T(4,128)S(1)} %get-tuple-element.27), channel_id=1, source_target_pairs={{31,0},{24,1},{25,2},{26,3},{27,4},{28,5},{29,6},{30,7},{7,8},{0,9... | collective-permute-start | bytes 6152 | tf_op jit(solution)/shard_map/ppermute | solution.py:241
  28.0 12.9 %collective-permute-start.8 = (f32[5,4,128]{2,1,0:T(4,128)S(1)}, f32[5,4,128]{2,1,0:T(4,128)S(1)}, u32[]{:S(2)}, u32[]{:S(2)}) collective-permute-start(f32[5,4,128]{2,1,0:T(4,128)S(1)} %get-tuple-element.19), channel_id=1, source_target_pairs={{8,0},{16,8},{24,16},{0,24},{9,1},{17,9},{25,17},{1,25},{10,2},{18... | collective-permute-start | bytes 30728 | tf_op jit(solution)/shard_map/ppermute | solution.py:236
  29.0 5.7 %collective-permute-start.14 = (f32[4,128]{1,0:T(4,128)S(1)}, f32[4,128]{1,0:T(4,128)S(1)}, u32[]{:S(2)}, u32[]{:S(2)}) collective-permute-start(f32[4,128]{1,0:T(4,128)S(1)} %get-tuple-element.28), channel_id=1, source_target_pairs={{15,0},{8,1},{9,2},{10,3},{11,4},{12,5},{13,6},{14,7},{23,8},{16,9... | collective-permute-start | bytes 6152 | tf_op jit(solution)/shard_map/ppermute | solution.py:242
  29.3 10.9 %collective-permute-start.10 = (f32[8,128]{1,0:T(8,128)S(1)}, f32[8,128]{1,0:T(8,128)S(1)}, u32[]{:S(2)}, u32[]{:S(2)}) collective-permute-start(f32[8,128]{1,0:T(8,128)S(1)} %get-tuple-element.21), channel_id=1, source_target_pairs={{1,0},{2,1},{3,2},{4,3},{5,4},{6,5},{7,6},{0,7},{9,8},{10,9},{11,1... | collective-permute-start | bytes 12296 | tf_op jit(solution)/shard_map/ppermute | solution.py:238
  34.6 6.3 %collective-permute-start.11 = (f32[8,128]{1,0:T(8,128)S(1)}, f32[8,128]{1,0:T(8,128)S(1)}, u32[]{:S(2)}, u32[]{:S(2)}) collective-permute-start(f32[8,128]{1,0:T(8,128)S(1)} %get-tuple-element.22), channel_id=1, source_target_pairs={{0,1},{1,2},{2,3},{3,4},{4,5},{5,6},{6,7},{7,0},{8,9},{9,10},{10,1... | collective-permute-start | bytes 12296 | tf_op jit(solution)/shard_map/ppermute | solution.py:239
  34.7 5.5 %collective-permute-start.12 = (f32[4,128]{1,0:T(4,128)S(1)}, f32[4,128]{1,0:T(4,128)S(1)}, u32[]{:S(2)}, u32[]{:S(2)}) collective-permute-start(f32[4,128]{1,0:T(4,128)S(1)} %get-tuple-element.29), channel_id=1, source_target_pairs={{9,0},{10,1},{11,2},{12,3},{13,4},{14,5},{15,6},{8,7},{17,8},{18,9... | collective-permute-start | bytes 6152 | tf_op jit(solution)/shard_map/ppermute | solution.py:240

commit v3 on v0

v3 whole, which is shorter than its diff:
```python
import math

import jax
import jax.numpy as jnp
from jax import lax
from jax.experimental import pallas as pl
from jax.experimental.pallas import tpu as pltpu
from jax.sharding import PartitionSpec as P

TILE = 4
STEPS = 2

lattice_speeds = (
    (0, 0, 0),
    (1, 0, 0),
    (-1, 0, 0),
    (0, 1, 0),
    (0, -1, 0),
    (0, 0, 1),
    (0, 0, -1),
    (1, 1, 0),
    (-1, -1, 0),
    (1, -1, 0),
    (-1, 1, 0),
    (1, 0, 1),
    (-1, 0, -1),
    (1, 0, -1),
    (-1, 0, 1),
    (0, 1, 1),
    (0, -1, -1),
    (0, 1, -1),
    (0, -1, 1),
)
relax_rate = 1.6
drag_factor = 20.0
LEVELS = 4
LANES = 128
GUARD = 8

x_up = [n for n in range(19) if lattice_speeds[n][0] == 1]
x_down = [n for n in range(19) if lattice_speeds[n][0] == -1]
y_up = [n for n in range(19) if lattice_speeds[n][1] == 1]
y_down = [n for n in range(19) if lattice_speeds[n][1] == -1]
vmem = pl.BlockSpec(memory_space=pltpu.VMEM)

FLOW = 19
SOLID = 22
SECOND = 23
QUANTITIES = 28
BEFORE_LANE = 16
AFTER_LANE = 32


def opposite_of(number):
    return number + 1 if number % 2 == 1 else number - 1


def lane_index(rows=8):
    return lax.broadcasted_iota(jnp.int32, (rows, LANES), 1)


def spread_solid(solid):
    tiles = solid.shape[1]
    row = lax.broadcasted_iota(jnp.int32, (tiles, LANES), 0)
    column = lax.broadcasted_iota(jnp.int32, (tiles, LANES), 1)
    spread = (column // TILE == row).astype(jnp.float32)
    cells = jnp.dot(solid[...].astype(jnp.float32), spread, preferred_element_type=jnp.float32)
    blocks = []
    for tile_row in range(solid.shape[0] // LEVELS):
        part = cells[tile_row * LEVELS : (tile_row + 1) * LEVELS]
        blocks.append(jnp.concatenate([part, part], axis=0))
    return blocks


def flow_blocks(velocity, step, rows):
    blocks = []
    for pair in range(rows // 16):
        both = [velocity[step, axis, pl.ds(16 * pair, 16), :].astype(jnp.float32) for axis in range(3)]
        blocks.append([part[:8] for part in both])
        blocks.append([part[8:] for part in both])
    return blocks


def row_message_kernel(state, velocity, solid, low, high):
    rows = state.shape[1]
    solid_parts = spread_solid(solid)
    flow = flow_blocks(velocity, 0, rows)
    for out, first, second, group, moving in (
        (low, 0, LEVELS, 0, x_up),
        (high, rows - LEVELS, rows - 2 * LEVELS, -1, x_down),
    ):
        for number in range(19):
            out[number] = state[number, pl.ds(first, LEVELS), :]
        start = first % 8
        for axis in range(3):
            out[FLOW + axis] = flow[group][axis][start : start + LEVELS]
        out[SOLID] = solid_parts[group][:LEVELS]
        for slot, number in enumerate(moving):
            out[SECOND + slot] = state[number, pl.ds(second, LEVELS), :]


def slot_place(slot, group, groups):
    per_block = LANES // groups
    return slot // per_block, (slot % per_block) * groups + group


def column_message_kernel(state, velocity, solid, after, before, low, high, ends):
    rows = state.shape[1]
    groups = rows // 8 + 2
    solid_parts = spread_solid(solid)
    flow = flow_blocks(velocity, 0, rows)
    lane = lane_index()
    for slot in range(SECOND):
        ends[0, slot, pl.ds(LEVELS, LEVELS), :] = before[slot]
        ends[1, slot, pl.ds(0, LEVELS), :] = after[slot]
        in_second = SOLID if slot == SOLID else None
        low_second = SECOND + x_down.index(slot) if slot in x_down else in_second
        high_second = SECOND + x_up.index(slot) if slot in x_up else in_second
        if low_second is not None:
            ends[0, slot, pl.ds(0, LEVELS), :] = before[low_second]
        else:
            ends[0, slot, pl.ds(0, LEVELS), :] = jnp.zeros((LEVELS, LANES), jnp.float32)
        if high_second is not None:
            ends[1, slot, pl.ds(LEVELS, LEVELS), :] = after[high_second]
        else:
            ends[1, slot, pl.ds(LEVELS, LEVELS), :] = jnp.zeros((LEVELS, LANES), jnp.float32)

    def block(slot, group):
        if group == 0:
            return ends[0, slot]
        if group == groups - 1:
            return ends[1, slot]
        if slot < FLOW:
            return state[slot, pl.ds(8 * (group - 1), 8), :]
        if slot < SOLID:
            return flow[group - 1][slot - FLOW]
        return solid_parts[(group - 1) * 8 // (LEVELS * TILE)]

    count = low.shape[0]
    low_parts = [jnp.zeros((8, LANES), jnp.float32) for _ in range(count)]
    high_parts = [jnp.zeros((8, LANES), jnp.float32) for _ in range(count)]
    for slot in range(SECOND):
        for group in range(groups):
            value = block(slot, group)
            part, place = slot_place(slot, group, groups)
            turned = pltpu.roll(value, (place + 1) % LANES, 1)
            low_parts[part] = jnp.where(lane == place + 1, turned, low_parts[part])
            high_parts[part] = jnp.where(lane == place, turned, high_parts[part])
            for moving, parts, edge, ahead in ((y_up, low_parts, 1, 1), (y_down, high_parts, LANES - 2, 0)):
                if slot in moving:
                    part, place = slot_place(SECOND + moving.index(slot), group, groups)
                    turned = pltpu.roll(value, (place + ahead - edge) % LANES, 1)
                    parts[part] = jnp.where(lane == place + ahead, turned, parts[part])
    for part in range(count):
        low[part] = low_parts[part]
        high[part] = high_parts[part]


def collide(moved, flow, fluid):
    ux, uy, uz = flow
    total = {n: moved[n] + moved[n + 1] for n in range(1, 19, 2)}
    gap = {n: moved[n] - moved[n + 1] for n in range(1, 19, 2)}
    xy, xz, yz = total[7] + total[9], total[11] + total[13], total[15] + total[17]
    axis_x, axis_y, axis_z = 2.0 * total[1], 2.0 * total[3], 2.0 * total[5]
    density = 12.0 * moved[0] + (axis_x + axis_y + axis_z) + (xy + xz + yz)
    pxx = axis_x + xy + xz
    pyy = axis_y + xy + yz
    pzz = axis_z + xz + yz
    pxy = total[7] - total[9]
    pxz = total[11] - total[13]
    pyz = total[15] - total[17]
    dx = 2.0 * gap[1] + (gap[7] + gap[9]) + (gap[11] + gap[13])
    dy = 2.0 * gap[3] + (gap[7] - gap[9]) + (gap[15] + gap[17])
    dz = 2.0 * gap[5] + (gap[11] - gap[13]) + (gap[15] - gap[17])
    vx = pxx * ux + pxy * uy + pxz * uz
    vy = pxy * ux + pyy * uy + pyz * uz
    vz = pxz * ux + pyz * uy + pzz * uz
    speed_sq = ux * ux + uy * uy + uz * uz
    drag = fluid * (ux * dx + uy * dy + uz * dz)
    scaled = (relax_rate / 36.0) * fluid
    base = scaled * (density + 1.5 * (speed_sq * density) - 4.5 * (ux * vx + uy * vy + uz * vz))
    scaled3 = 3.0 * scaled
    bx = scaled3 * (dx + 3.0 * vx - ux * density)
    by = scaled3 * (dy + 3.0 * vy - uy * density)
    bz = scaled3 * (dz + 3.0 * vz - uz * density)
    keep = (1.0 - relax_rate) * fluid
    results = [keep * moved[0] + base]
    for number in range(1, 19, 2):
        along = None
        for speed, part in zip(lattice_speeds[number], (bx, by, bz)):
            if speed == 0:
                continue
            if along is None:
                along = part if speed == 1 else -part
            else:
                along = along + part if speed == 1 else along - part
        results.append(keep * moved[number] + (base + along))
        results.append(keep * moved[number + 1] + (base - along))
    return results, drag


def outside(cz):
    level = lax.broadcasted_iota(jnp.int32, (8, LANES), 0) % LEVELS
    return level == (LEVELS - 1 if cz == 1 else 0)


def link_closed(solid_there, cz):
    closed = solid_there > 0.5
    return closed | outside(cz) if cz != 0 else closed


def shift_lanes(value, cy, edge_value):
    lane = lane_index(value.shape[0])
    if cy == 1:
        return jnp.where(lane == LANES - 1, edge_value, pltpu.roll(value, LANES - 1, 1))
    return jnp.where(lane == 0, edge_value, pltpu.roll(value, 1, 1))


def step_cells(held, shifted, first, flow, fluid, closed):
    here = [held[n, pl.ds(first, 8), :] for n in range(19)]
    moved = [here[0]]
    for number in range(1, 19):
        cx, cy, cz = lattice_speeds[number]
        field = held if cy == 0 else shifted
        if cx == cy == cz == 0:
            source = here[number]
        else:
            source = field[number, pl.ds(first + LEVELS * cx + cz, 8), :]
        bounced = here[opposite_of(number)]
        if cx != 0:
            bounced = bounced + 2.0 * cx
        moved.append(jnp.where(closed(number), bounced, source))
    return collide(moved, flow, fluid)


def main_kernel(
    state, velocity, blocked, solid, after, before, y_after, y_before, low, high, out, shared,
    held, shifted, later, row_flow, solid_rows,
):
    rows = state.shape[1]
    groups = rows // 8 + 2
    own = GUARD + 8
    near, far = own - LEVELS, own + rows
    lane = lane_index()
    solid_parts = spread_solid(solid)

    def column(message, slot, lane_first, group=0):
        part, place = slot_place(slot, group, groups)
        ahead = 1 if message is y_after or message is low else 0
        return pltpu.roll(message[part], (lane_first - place - ahead) % LANES, 1)

    for number in range(19):
        for group in range(rows // 8):
            held[number, pl.ds(own + 8 * group, 8), :] = state[number, pl.ds(8 * group, 8), :]
        held[number, pl.ds(near, LEVELS), :] = before[number]
        held[number, pl.ds(far, LEVELS), :] = after[number]
        if number in x_down:
            held[number, pl.ds(near - LEVELS, LEVELS), :] = before[SECOND + x_down.index(number)]
        if number in x_up:
            held[number, pl.ds(far + LEVELS, LEVELS), :] = after[SECOND + x_up.index(number)]
    for number in y_up + y_down:
        cy = lattice_speeds[number][1]
        for group in range(groups):
            value = held[number, pl.ds(GUARD + 8 * group, 8), :]
            if cy == 1:
                edge = column(y_after, number, LANES - 1, group)
            else:
                edge = column(y_before, number, 0, group)
            shifted[number, pl.ds(GUARD + 8 * group, 8), :] = shift_lanes(value, cy, edge)

    for group in (0, 1, groups - 2, groups - 1):
        first = GUARD + 8 * group
        if group == 0:
            solid_rows[0, pl.ds(first, LEVELS), :] = before[SOLID]
            solid_rows[0, pl.ds(first + LEVELS, LEVELS), :] = before[SOLID]
        elif group == groups - 1:
            solid_rows[0, pl.ds(first, LEVELS), :] = after[SOLID]
            solid_rows[0, pl.ds(first + LEVELS, LEVELS), :] = after[SOLID]
        else:
            solid_rows[0, pl.ds(first, 8), :] = solid_parts[(group - 1) * 8 // (LEVELS * TILE)]
        value = solid_rows[0, pl.ds(first, 8), :]
        solid_rows[1, pl.ds(first, 8), :] = shift_lanes(value, 1, column(y_after, SOLID, LANES - 1, group))
        solid_rows[2, pl.ds(first, 8), :] = shift_lanes(value, -1, column(y_before, SOLID, 0, group))
    for axis in range(3):
        row_flow[axis, pl.ds(0, LEVELS), :] = before[FLOW + axis]
        row_flow[axis, pl.ds(LEVELS, LEVELS), :] = after[FLOW + axis]
    row_flow[3, pl.ds(0, LEVELS), :] = before[SOLID]
    row_flow[3, pl.ds(LEVELS, LEVELS), :] = after[SOLID]

    def both_rows(field, index, shift):
        ends = [field[index, pl.ds(place + shift, LEVELS), :] for place in (near, far)]
        return jnp.concatenate(ends, axis=0)

    here = [both_rows(held, n, 0) for n in range(19)]
    moved = [here[0]]
    for number in range(1, 19):
        cx, cy, cz = lattice_speeds[number]
        shift = LEVELS * cx + cz
        source = both_rows(held if cy == 0 else shifted, number, shift)
        closed = link_closed(both_rows(solid_rows, cy % 3, shift), cz)
        moved.append(jnp.where(closed, here[opposite_of(number)] + 2.0 * cx, source))
    row_results, _ = collide(moved, [row_flow[axis] for axis in range(3)], 1.0 - row_flow[3])

    def columns(number_before, number_after, message_before, message_after):
        return jnp.where(
            lane < AFTER_LANE,
            column(message_before, number_before, BEFORE_LANE),
            column(message_after, number_after, AFTER_LANE),
        )

    def neighbours(slot, cy):
        if cy == 0:
            return columns(slot, slot, y_before, y_after)
        if cy == 1:
            beyond = SOLID if slot == SOLID else SECOND + y_up.index(slot)
            return columns(slot, beyond, low, y_after)
        beyond = SOLID if slot == SOLID else SECOND + y_down.index(slot)
        return columns(beyond, slot, y_before, high)

    upper = lax.broadcasted_iota(jnp.int32, (8, LANES), 0) < LEVELS

    def shift_rows(value, cx, cz):
        if cx != 0:
            swapped = pltpu.roll(value, LEVELS, 0)
            if cx == 1:
                value = jnp.where(upper, swapped, pltpu.roll(swapped, LANES - 1, 1))
            else:
                value = jnp.where(upper, pltpu.roll(swapped, 1, 1), swapped)
        if cz != 0:
            value = pltpu.roll(value, (-cz) % 8, 0)
        return value

    here = [neighbours(n, 0) for n in range(19)]
    solid_columns = [neighbours(SOLID, cy) for cy in (0, 1, -1)]
    moved = [here[0]]
    for number in range(1, 19):
        cx, cy, cz = lattice_speeds[number]
        source = shift_rows(here[number] if cy == 0 else neighbours(number, cy), cx, cz)
        closed = link_closed(shift_rows(solid_columns[cy % 3], cx, cz), cz)
        moved.append(jnp.where(closed, here[opposite_of(number)] + 2.0 * cx, source))
    column_flow = [neighbours(FLOW + axis, 0) for axis in range(3)]
    column_results, _ = collide(moved, column_flow, 1.0 - solid_columns[0])

    def closed_at(first):
        return lambda number: blocked[number - 1, pl.ds(first, 8), :] == 1

    def fluid_at(first):
        return 1.0 - solid_parts[first // (LEVELS * TILE)]

    drag_sum = jnp.zeros((8, LANES), jnp.float32)
    flow = flow_blocks(velocity, 0, rows)
    for group in range(rows // 8):
        first = 8 * group
        results, drag = step_cells(
            held, shifted, own + first, flow[group], fluid_at(first), closed_at(first)
        )
        for number in range(19):
            later[number, pl.ds(own + first, 8), :] = results[number]
        drag_sum = drag_sum + drag
    for number in x_down:
        later[number, pl.ds(near, LEVELS), :] = row_results[number][:LEVELS]
    for number in x_up:
        later[number, pl.ds(far, LEVELS), :] = row_results[number][LEVELS:]
    for number in y_up + y_down:
        cy = lattice_speeds[number][1]
        for group in range(groups):
            value = later[number, pl.ds(GUARD + 8 * group, 8), :]
            if cy == 1:
                edge = pltpu.roll(column_results[number], (LANES - 1 - AFTER_LANE - group) % LANES, 1)
            else:
                edge = pltpu.roll(column_results[number], (-BEFORE_LANE - group) % LANES, 1)
            shifted[number, pl.ds(GUARD + 8 * group, 8), :] = shift_lanes(value, cy, edge)

    flow = flow_blocks(velocity, 1, rows)
    for group in range(rows // 8):
        first = 8 * group
        results, drag = step_cells(
            later, shifted, own + first, flow[group], fluid_at(first), closed_at(first)
        )
        for number in range(19):
            out[number, pl.ds(first, 8), :] = results[number]
        drag_sum = drag_sum + drag
    shared[...] = jnp.broadcast_to(jnp.sum(drag_sum), shared.shape)


def swap_edges(low, high, axis):
    count = lax.axis_size(axis)
    from_after = [((i + 1) % count, i) for i in range(count)]
    from_before = [(i, (i + 1) % count) for i in range(count)]
    return lax.ppermute(low, axis, from_after), lax.ppermute(high, axis, from_before)


def per_device(adjoint_in, velocity, solid_tiles, link_blocked):
    rows_x, levels, rows_y = adjoint_in.shape[1:]
    rows = rows_x * levels
    padded = rows + 16 + 2 * GUARD
    groups = rows // 8 + 2
    parts = -(-QUANTITIES // (LANES // groups))
    state = adjoint_in.reshape(19, rows, rows_y)
    flow = velocity.reshape(STEPS, 3, rows, rows_y)
    solid = solid_tiles.reshape(-1, solid_tiles.shape[2])
    blocked = link_blocked.reshape(18, rows, rows_y)

    def shape_of(*sizes):
        return jax.ShapeDtypeStruct(sizes, jnp.float32)

    params = pltpu.CompilerParams(vmem_limit_bytes=16 * 1024 * 1024)
    row_low, row_high = pl.pallas_call(
        row_message_kernel,
        out_shape=(shape_of(QUANTITIES, levels, rows_y),) * 2,
        in_specs=[vmem] * 3,
        out_specs=(vmem,) * 2,
        compiler_params=params,
    )(state, flow, solid)
    after, before = swap_edges(row_low, row_high, "gx")
    low, high = pl.pallas_call(
        column_message_kernel,
        out_shape=(shape_of(parts, 8, rows_y),) * 2,
        in_specs=[vmem] * 5,
        out_specs=(vmem,) * 2,
        scratch_shapes=[pltpu.VMEM((2, SECOND, 8, rows_y), jnp.float32)],
        compiler_params=params,
    )(state, flow, solid, after, before)
    y_after, y_before = swap_edges(low, high, "gy")
    count = lax.axis_size("gx") * lax.axis_size("gy")
    field = pltpu.VMEM((19, padded, rows_y), jnp.float32)
    result, own = pl.pallas_call(
        main_kernel,
        out_shape=(shape_of(19, rows, rows_y), shape_of(count, 1, rows_y)),
        in_specs=[vmem] * 10,
        out_specs=(vmem,) * 2,
        scratch_shapes=[
            field,
            field,
            field,
            pltpu.VMEM((4, 8, rows_y), jnp.float32),
            pltpu.VMEM((3, padded, rows_y), jnp.float32),
        ],
        compiler_params=params,
    )(state, flow, blocked, solid, after, before, y_after, y_before, low, high)
    shared = lax.all_to_all(own, ("gx", "gy"), split_axis=0, concat_axis=0, tiled=True)
    cell_count = rows * rows_y * count
    scale = drag_factor / math.sqrt(cell_count) * 3.0 / 36.0
    total = jnp.sum(shared[:, 0, 0])
    return (result.reshape(adjoint_in.shape), (-scale * total).reshape(1))


def solution(mesh):
    placed = (
        P(None, "gx", None, "gy"),
        P(None, None, "gx", None, "gy"),
        P("gx", None, "gy"),
        P(None, "gx", None, "gy"),
    )
    return jax.shard_map(
        per_device,
        mesh=mesh,
        in_specs=placed,
        out_specs=(P(None, "gx", None, "gy"), P()),
        check_vma=False,
    )
```

time: 99 us -> 34.4 us (0.35); the launches traced: 97.5 us -> 34.1 us
  blocking collectives: 36.9 us -> 8.79 us
  local copies, waits for them, and re-layouts: 23.7 us -> 2.66 us
  other arithmetic: 12.3 us -> 0.63 us
  starting transfers between devices: 10.4 us -> 6.99 us
  Pallas kernels: 0 us -> 2.64 us
  between operations: 4.59 us -> 2.43 us
    psum x1 -> x0, blocking collectives: 36.9 us -> none  [per_device(): total = total + lax.psum(step_terms[adjoint_step], ('gx', 'gy'))]
    slice x31 -> x0, local copies, waits for them, and re-layouts: 13.3 us -> none  [the longest x10 3.66 us: shift_level(): return jnp.concatenate([field[:, 1:], jnp.zeros_like(field[:, :1])], axis=1)]
    all_to_all x0 -> x1, blocking collectives: none -> 8.79 us  [per_device(): lax.all_to_all(own, ('gx', 'gy'), split_axis=0, concat_axis=0, tiled=True)]
    unnamed x36 -> x0, other arithmetic: 7.93 us -> none
    ppermute x4 -> x0, local copies, waits for them, and re-layouts: 4.97 us -> none  [the longest x2 2.89 us: with_halo(): lax.ppermute(lax.slice_in_dim(block, 0, width, axis=dim), axis, backward)]
    ppermute x8 -> x4, starting transfers between devices: 10.4 us -> 6.99 us  [the longest x2 6.99 us: swap_edges(): lax.ppermute(low, axis, from_after)]
    reduce_sum x2 -> x1, other arithmetic: 3.32 us -> 0.63 us  [per_device(): total = jnp.sum(shared[:, 0, 0])]
    pallas_call x0 -> x3, Pallas kernels: none -> 2.64 us  [the longest x1 2.09 us: per_device(): pl.pallas_call(main_kernel, out_shape=(shape_of(19, rows, rows_y), shape_...]
  transfers between devices with their start and end apart: 8 -> 4, of which waited for: 3 -> 4; matrix products, arithmetic and copies ran while one was open for 13% -> 0% of each run, Pallas kernels for 0% -> 0%
where the time goes in v3:
time: 34.4 us; the launch traced here: 34.1 us
  waiting for transfers between devices  9.99 us (29%)
  blocking collectives  8.79 us (26%)
  starting transfers between devices  6.99 us (20%)
  local copies, waits for them, and re-layouts  2.66 us (8%)
  Pallas kernels  2.64 us (8%)
  between operations  2.43 us (7%)
  other arithmetic  0.63 us (2%)
    all_to_all x1, blocking collectives, per_device(): lax.all_to_all(own, ('gx', 'gy'), split_axis=0, concat_axis=0, tiled=True)  8.79 us
    ppermute x2, starting transfers between devices, swap_edges(): lax.ppermute(low, axis, from_after)  6.99 us
    ppermute x2, waiting for transfers between devices, swap_edges(): lax.ppermute(high, axis, from_before)  6.31 us
    ppermute x2, waiting for transfers between devices, swap_edges(): lax.ppermute(low, axis, from_after)  3.68 us
    unnamed x8, local copies, waits for them, and re-layouts  2.66 us
    pallas_call x1, Pallas kernels, per_device(): pl.pallas_call(main_kernel, out_shape=(shape_of(19, rows, rows_y), shape_...  2.09 us
  transfers between devices with their start and end apart: 4, of which 4 were waited for; matrix products, arithmetic and copies ran while one was open for 0% of the time, Pallas kernels for 0%

profile of v3, /device:TPU:0, one launch (start us, length us, event | category | flops | bytes accessed | tf_op | source)
XLA Modules:
  0.0 34.1 jit_solution(16961952182871918892)
XLA Ops:
  0.6 0.0 copy-start
  0.6 1.1 %copy-done = f32[19,16,4,128]{3,2,1,0:T(4,128)S(1)} copy-done((f32[19,16,4,128]{3,2,1,0:T(4,128)S(1)}, f32[19,16,4,128]{3,2,1,0:T(4,128)}, u32[]{:S(2)}) %copy-start) | copy-done | bytes 622616
  1.7 0.0 copy-start.1
  1.7 0.9 %copy-done.1 = bf16[2,3,16,4,128]{4,3,2,1,0:T(4,128)(2,1)S(1)} copy-done((bf16[2,3,16,4,128]{4,3,2,1,0:T(4,128)(2,1)S(1)}, bf16[2,3,16,4,128]{4,3,2,1,0:T(4,128)(2,1)}, u32[]{:S(2)}) %copy-start.1) | copy-done | bytes 98328
  2.6 0.0 copy-start.3
  2.6 0.7 %copy-done.3 = s32[4,4,32]{2,1,0:T(4,128)S(1)} copy-done((s32[4,4,32]{2,1,0:T(4,128)S(1)}, s32[4,4,32]{2,1,0:T(4,128)}, u32[]{:S(2)}) %copy-start.3) | copy-done | bytes 2072
  3.3 0.1 shard_map.59
  3.4 0.0 copy-start.2
  3.4 2.4 %collective-permute-start = (f32[28,4,128]{2,1,0:T(4,128)S(1)}, f32[28,4,128]{2,1,0:T(4,128)S(1)}, u32[]{:S(2)}, u32[]{:S(2)}) collective-permute-start(f32[28,4,128]{2,1,0:T(4,128)S(1)} %get-tuple-element.8), channel_id=1, source_target_pairs={{8,0},{16,8},{24,16},{0,24},{9,1},{17,9},{25,17},{1,25},{10,2},{18... | collective-permute-start | bytes 172040 | tf_op jit(solution)/shard_map/ppermute | solution.py:390
  5.8 0.0 collective-permute-start.1
  5.8 2.3 %collective-permute-done.after = f32[28,4,128]{2,1,0:T(4,128)S(1)} collective-permute-done((f32[28,4,128]{2,1,0:T(4,128)S(1)}, f32[28,4,128]{2,1,0:T(4,128)S(1)}, u32[]{:S(2)}, u32[]{:S(2)}) %collective-permute-start) | collective-permute-done | bytes 57376 | tf_op jit(solution)/shard_map/ppermute | solution.py:390
  8.1 1.3 %collective-permute-done.1.before = f32[28,4,128]{2,1,0:T(4,128)S(1)} collective-permute-done((f32[28,4,128]{2,1,0:T(4,128)S(1)}, f32[28,4,128]{2,1,0:T(4,128)S(1)}, u32[]{:S(2)}, u32[]{:S(2)}) %collective-permute-start.1) | collective-permute-done | bytes 57376 | tf_op jit(solution)/shard_map/ppermute | solution.py:390
  9.4 0.4 %shard_map.60 = (f32[3,8,128]{2,1,0:T(8,128)S(1)}, f32[3,8,128]{2,1,0:T(8,128)S(1)}) custom-call(f32[19,64,128]{2,1,0:T(8,128)S(1)} %bitcast.7, bf16[2,3,64,128]{3,2,1,0:T(8,128)(2,1)S(1)} %bitcast.10, s32[16,32]{1,0:T(8,128)S(1)} %bitcast.14, f32[28,4,128]{2,1,0:T(4,128)S(1)} %collective-permute-done.after, f32[28,4,128]{2,1,0:T(4,128)S(1)} %collective-permute-done.1.before), custom_call_target="tpu_custom_call" | custom-call | tf_op jit(solution)/shard_map/pallas_call | solution.py:416
  9.9 4.6 %collective-permute-start.2 = (f32[3,8,128]{2,1,0:T(8,128)S(1)}, f32[3,8,128]{2,1,0:T(8,128)S(1)}, u32[]{:S(2)}, u32[]{:S(2)}) collective-permute-start(f32[3,8,128]{2,1,0:T(8,128)S(1)} %get-tuple-element.10.low), channel_id=1, source_target_pairs={{1,0},{2,1},{3,2},{4,3},{5,4},{6,5},{7,6},{0,7},{9,8},{10,9},{11,1... | collective-permute-start | bytes 36872 | tf_op jit(solution)/shard_map/ppermute | solution.py:390
  14.4 0.0 collective-permute-start.3
  14.5 1.4 %collective-permute-done.2.y_after = f32[3,8,128]{2,1,0:T(8,128)S(1)} collective-permute-done((f32[3,8,128]{2,1,0:T(8,128)S(1)}, f32[3,8,128]{2,1,0:T(8,128)S(1)}, u32[]{:S(2)}, u32[]{:S(2)}) %collective-permute-start.2) | collective-permute-done | bytes 12320 | tf_op jit(solution)/shard_map/ppermute | solution.py:390
  15.9 5.0 %collective-permute-done.3.y_before = f32[3,8,128]{2,1,0:T(8,128)S(1)} collective-permute-done((f32[3,8,128]{2,1,0:T(8,128)S(1)}, f32[3,8,128]{2,1,0:T(8,128)S(1)}, u32[]{:S(2)}, u32[]{:S(2)}) %collective-permute-start.3) | collective-permute-done | bytes 12320 | tf_op jit(solution)/shard_map/ppermute | solution.py:390
  20.8 0.0 copy-done.2
  20.8 2.1 %shard_map.61 = (f32[19,64,128]{2,1,0:T(8,128)}, f32[32,1,128]{2,1,0:T(1,128)S(1)}) custom-call(f32[19,64,128]{2,1,0:T(8,128)S(1)} %bitcast.8, bf16[2,3,64,128]{3,2,1,0:T(8,128)(2,1)S(1)} %bitcast.11, s32[18,64,128]{2,1,0:T(8,128)S(1)} %bitcast.12, s32[16,32]{1,0:T(8,128)S(1)} %bitcast.15, f32[28,4,128]{2,1,0:T(4,128)S(1)} %collective-permute-done.after, ...), custom_call_target="tpu_custom_call" | custom-call | tf_op jit(solution)/shard_map/pallas_call | solution.py:427
  22.9 8.8 %all_to_all.5 = f32[32,1,128]{2,1,0:T(1,128)S(1)} all-to-all(f32[32,1,128]{2,1,0:T(1,128)S(1)} %get-tuple-element.13), channel_id=1, replica_groups=mesh['gx'=4,'gy'=8] {'gx','gy'}, dimensions={0} | all-to-all | bytes 32768 | tf_op jit(solution)/shard_map/all_to_all | solution.py:441
  31.7 0.6 %slice_reduce_fusion = f32[]{:T(128)} fusion(f32[32,1,128]{2,1,0:T(1,128)S(1)} %all_to_all.5), kind=kLoop, calls=%fused_computation | loop fusion | flops 31 | bytes 132 | tf_op jit(solution)/shard_map/reduce_sum | solution.py:444
Async XLA Ops:
  0.6 1.1 %copy-start = (f32[19,16,4,128]{3,2,1,0:T(4,128)S(1)}, f32[19,16,4,128]{3,2,1,0:T(4,128)}, u32[]{:S(2)}) copy-start(f32[19,16,4,128]{3,2,1,0:T(4,128)} %param.4) | copy-start | bytes 1867780
  1.7 0.9 %copy-start.1 = (bf16[2,3,16,4,128]{4,3,2,1,0:T(4,128)(2,1)S(1)}, bf16[2,3,16,4,128]{4,3,2,1,0:T(4,128)(2,1)}, u32[]{:S(2)}) copy-start(bf16[2,3,16,4,128]{4,3,2,1,0:T(4,128)(2,1)} %param.5) | copy-start | bytes 294916
  2.6 0.7 %copy-start.3 = (s32[4,4,32]{2,1,0:T(4,128)S(1)}, s32[4,4,32]{2,1,0:T(4,128)}, u32[]{:S(2)}) copy-start(s32[4,4,32]{2,1,0:T(4,128)} %param.6) | copy-start | bytes 6148
  3.4 17.4 %copy-start.2 = (s32[18,16,4,128]{3,2,1,0:T(4,128)S(1)}, s32[18,16,4,128]{3,2,1,0:T(4,128)}, u32[]{:S(2)}) copy-start(s32[18,16,4,128]{3,2,1,0:T(4,128)} %param.7) | copy-start | bytes 1769476
  3.4 4.7 %collective-permute-start = (f32[28,4,128]{2,1,0:T(4,128)S(1)}, f32[28,4,128]{2,1,0:T(4,128)S(1)}, u32[]{:S(2)}, u32[]{:S(2)}) collective-permute-start(f32[28,4,128]{2,1,0:T(4,128)S(1)} %get-tuple-element.8), channel_id=1, source_target_pairs={{8,0},{16,8},{24,16},{0,24},{9,1},{17,9},{25,17},{1,25},{10,2},{18... | collective-permute-start | bytes 172040 | tf_op jit(solution)/shard_map/ppermute | solution.py:390
  5.8 3.6 %collective-permute-start.1 = (f32[28,4,128]{2,1,0:T(4,128)S(1)}, f32[28,4,128]{2,1,0:T(4,128)S(1)}, u32[]{:S(2)}, u32[]{:S(2)}) collective-permute-start(f32[28,4,128]{2,1,0:T(4,128)S(1)} %get-tuple-element.9), channel_id=1, source_target_pairs={{0,8},{8,16},{16,24},{24,0},{1,9},{9,17},{17,25},{25,1},{2,10},{10... | collective-permute-start | bytes 172040 | tf_op jit(solution)/shard_map/ppermute | solution.py:390
  9.9 6.0 %collective-permute-start.2 = (f32[3,8,128]{2,1,0:T(8,128)S(1)}, f32[3,8,128]{2,1,0:T(8,128)S(1)}, u32[]{:S(2)}, u32[]{:S(2)}) collective-permute-start(f32[3,8,128]{2,1,0:T(8,128)S(1)} %get-tuple-element.10.low), channel_id=1, source_target_pairs={{1,0},{2,1},{3,2},{4,3},{5,4},{6,5},{7,6},{0,7},{9,8},{10,9},{11,1... | collective-permute-start | bytes 36872 | tf_op jit(solution)/shard_map/ppermute | solution.py:390
  14.4 6.4 %collective-permute-start.3 = (f32[3,8,128]{2,1,0:T(8,128)S(1)}, f32[3,8,128]{2,1,0:T(8,128)S(1)}, u32[]{:S(2)}, u32[]{:S(2)}) collective-permute-start(f32[3,8,128]{2,1,0:T(8,128)S(1)} %get-tuple-element.11.high), channel_id=1, source_target_pairs={{0,1},{1,2},{2,3},{3,4},{4,5},{5,6},{6,7},{7,0},{8,9},{9,10},{10,1... | collective-permute-start | bytes 36872 | tf_op jit(solution)/shard_map/ppermute | solution.py:390

commit v4 on v3

--- a/solution.py
+++ b/solution.py
@@ -81,8 +81,15 @@
     return blocks
 
 
-def row_message_kernel(state, velocity, solid, low, high):
+def ring(slots, axis):
+    count = slots.shape[0]
+    place = lax.axis_index(axis)
+    return slots.at[lax.rem(place + count - 1, count)], slots.at[lax.rem(place + 1, count)]
+
+
+def row_message_kernel(state, velocity, solid, sent):
     rows = state.shape[1]
+    low, high = ring(sent, "gx")
     solid_parts = spread_solid(solid)
     flow = flow_blocks(velocity, 0, rows)
     for out, first, second, group, moving in (
@@ -104,8 +111,10 @@
     return slot // per_block, (slot % per_block) * groups + group
 
 
-def column_message_kernel(state, velocity, solid, after, before, low, high, ends):
+def column_message_kernel(state, velocity, solid, row_slots, sent, ends):
     rows = state.shape[1]
+    before, after = ring(row_slots, "gx")
+    low, high = ring(sent, "gy")
     groups = rows // 8 + 2
     solid_parts = spread_solid(solid)
     flow = flow_blocks(velocity, 0, rows)
@@ -234,10 +243,13 @@
 
 
 def main_kernel(
-    state, velocity, blocked, solid, after, before, y_after, y_before, low, high, out, shared,
+    state, velocity, blocked, solid, row_slots, column_slots, sent, out, shared,
     held, shifted, later, row_flow, solid_rows,
 ):
     rows = state.shape[1]
+    before, after = ring(row_slots, "gx")
+    y_before, y_after = ring(column_slots, "gy")
+    low, high = ring(sent, "gy")
     groups = rows // 8 + 2
     own = GUARD + 8
     near, far = own - LEVELS, own + rows
@@ -383,11 +395,8 @@
     shared[...] = jnp.broadcast_to(jnp.sum(drag_sum), shared.shape)
 
 
-def swap_edges(low, high, axis):
-    count = lax.axis_size(axis)
-    from_after = [((i + 1) % count, i) for i in range(count)]
-    from_before = [(i, (i + 1) % count) for i in range(count)]
-    return lax.ppermute(low, axis, from_after), lax.ppermute(high, axis, from_before)
+def swap_slots(slots, axis):
+    return lax.all_to_all(slots, axis, split_axis=0, concat_axis=0, tiled=True)
 
 
 def per_device(adjoint_in, velocity, solid_tiles, link_blocked):
@@ -405,29 +414,29 @@
         return jax.ShapeDtypeStruct(sizes, jnp.float32)
 
     params = pltpu.CompilerParams(vmem_limit_bytes=16 * 1024 * 1024)
-    row_low, row_high = pl.pallas_call(
+    row_slots = pl.pallas_call(
         row_message_kernel,
-        out_shape=(shape_of(QUANTITIES, levels, rows_y),) * 2,
+        out_shape=shape_of(lax.axis_size("gx"), QUANTITIES, levels, rows_y),
         in_specs=[vmem] * 3,
-        out_specs=(vmem,) * 2,
+        out_specs=vmem,
         compiler_params=params,
     )(state, flow, solid)
-    after, before = swap_edges(row_low, row_high, "gx")
-    low, high = pl.pallas_call(
+    row_slots = swap_slots(row_slots, "gx")
+    sent = pl.pallas_call(
         column_message_kernel,
-        out_shape=(shape_of(parts, 8, rows_y),) * 2,
-        in_specs=[vmem] * 5,
-        out_specs=(vmem,) * 2,
+        out_shape=shape_of(lax.axis_size("gy"), parts, 8, rows_y),
+        in_specs=[vmem] * 4,
+        out_specs=vmem,
         scratch_shapes=[pltpu.VMEM((2, SECOND, 8, rows_y), jnp.float32)],
         compiler_params=params,
-    )(state, flow, solid, after, before)
-    y_after, y_before = swap_edges(low, high, "gy")
+    )(state, flow, solid, row_slots)
+    column_slots = swap_slots(sent, "gy")
     count = lax.axis_size("gx") * lax.axis_size("gy")
     field = pltpu.VMEM((19, padded, rows_y), jnp.float32)
     result, own = pl.pallas_call(
         main_kernel,
-        out_shape=(shape_of(19, rows, rows_y), shape_of(count, 1, rows_y)),
-        in_specs=[vmem] * 10,
+        out_shape=(shape_of(19, rows, rows_y), shape_of(1, rows_y)),
+        in_specs=[vmem] * 7,
         out_specs=(vmem,) * 2,
         scratch_shapes=[
             field,
@@ -437,8 +446,8 @@
             pltpu.VMEM((3, padded, rows_y), jnp.float32),
         ],
         compiler_params=params,
-    )(state, flow, blocked, solid, after, before, y_after, y_before, low, high)
-    shared = lax.all_to_all(own, ("gx", "gy"), split_axis=0, concat_axis=0, tiled=True)
+    )(state, flow, blocked, solid, row_slots, column_slots, sent)
+    shared = lax.all_gather(own, ("gx", "gy"), axis=0)
     cell_count = rows * rows_y * count
     scale = drag_factor / math.sqrt(cell_count) * 3.0 / 36.0
     total = jnp.sum(shared[:, 0, 0])

time: 34.4 us -> 94.4 us (2.74)
  blocking collectives: 8.79 us -> 85.6 us
  waiting for transfers between devices: 9.99 us -> 0 us
  starting transfers between devices: 6.99 us -> 0 us
    all_gather x0 -> x1, blocking collectives: none -> 63.2 us  [per_device(): shared = lax.all_gather(own, ('gx', 'gy'), axis=0)]
    all_to_all x1 -> x2, blocking collectives: 8.79 us -> 22.4 us  [swap_slots(): return lax.all_to_all(slots, axis, split_axis=0, concat_axis=0, tiled=True)]
    ppermute x4 -> x0, waiting for transfers between devices: 9.99 us -> none  [the longest x2 6.31 us: swap_edges(): lax.ppermute(high, axis, from_before)]
    ppermute x4 -> x0, starting transfers between devices: 6.99 us -> none  [the longest x2 6.99 us: swap_edges(): lax.ppermute(low, axis, from_after)]
  transfers between devices with their start and end apart: 4 -> 0, of which waited for: 4 -> 0; matrix products, arithmetic and copies ran while one was open for 0% -> 0% of each run, Pallas kernels for 0% -> 0%
where the time goes in v4:
time: 94.4 us; the launch traced here: 94.1 us
  blocking collectives  85.6 us (91%)
  Pallas kernels  2.73 us (3%)
  local copies, waits for them, and re-layouts  2.66 us (3%)
  between operations  2.43 us (3%)
    all_gather x1, blocking collectives, per_device(): shared = lax.all_gather(own, ('gx', 'gy'), axis=0)  63.2 us
    all_to_all x2, blocking collectives, swap_slots(): return lax.all_to_all(slots, axis, split_axis=0, concat_axis=0, tiled=True)  22.4 us
    unnamed x8, local copies, waits for them, and re-layouts  2.66 us
    pallas_call x1, Pallas kernels, per_device(): pl.pallas_call(main_kernel, out_shape=(shape_of(19, rows, rows_y), shape_...  2.19 us

profile of v4, /device:TPU:0, one launch (start us, length us, event | category | flops | bytes accessed | tf_op | source)
XLA Modules:
  0.0 94.1 jit_solution(1869147383641377902)
XLA Ops:
  0.6 0.0 copy-start
  0.6 1.1 %copy-done = f32[19,16,4,128]{3,2,1,0:T(4,128)S(1)} copy-done((f32[19,16,4,128]{3,2,1,0:T(4,128)S(1)}, f32[19,16,4,128]{3,2,1,0:T(4,128)}, u32[]{:S(2)}) %copy-start) | copy-done | bytes 622616
  1.7 0.0 copy-start.1
  1.7 0.9 copy-done.1
  2.6 0.0 copy-start.3
  2.6 0.7 copy-done.3
  3.3 0.1 shard_map.59
  3.4 9.7 %all_to_all.10.row_slots = f32[4,28,4,128]{3,2,1,0:T(4,128)S(1)} all-to-all(f32[4,28,4,128]{3,2,1,0:T(4,128)S(1)} %shard_map.59), channel_id=1, replica_groups=mesh['gx'=4,'gy'=8] {'gx'}, dimensions={0} | all-to-all | bytes 458752 | tf_op jit(solution)/shard_map/all_to_all | solution.py:399
  13.1 0.0 copy-start.2
  13.1 0.4 shard_map.60.sent
  13.6 12.7 %all_to_all.11.column_slots = f32[8,3,8,128]{3,2,1,0:T(8,128)S(1)} all-to-all(f32[8,3,8,128]{3,2,1,0:T(8,128)S(1)} %shard_map.60.sent), channel_id=1, replica_groups=mesh['gx'=4,'gy'=8] {'gy'}, dimensions={0} | all-to-all | bytes 196608 | tf_op jit(solution)/shard_map/all_to_all | solution.py:399
  26.3 0.0 copy-done.2
  26.3 2.2 %shard_map.61 = (f32[19,64,128]{2,1,0:T(8,128)}, f32[1,128]{1,0:T(1,128)S(1)}) custom-call(f32[19,64,128]{2,1,0:T(8,128)S(1)} %bitcast.9, bf16[2,3,64,128]{3,2,1,0:T(8,128)(2,1)S(1)} %bitcast.12, s32[18,64,128]{2,1,0:T(8,128)S(1)} %bitcast.13, s32[16,32]{1,0:T(8,128)S(1)} %bitcast.16, f32[4,28,4,128]{3,2,1,0:T(4,128)S(1)} %all_to_all.10.row_slots, ...), custom_call_target="tpu_custom_call" | custom-call | tf_op jit(solution)/shard_map/pallas_call | solution.py:436
  28.5 63.2 %all-gather.1 = f32[32,1,128]{2,1,0:T(1,128)S(1)} all-gather(f32[1,1,128]{2,1,0:T(1,128)S(1)} %bitcast.17), channel_id=2, replica_groups=mesh['gx'=4,'gy'=8] {'gx','gy'}, dimensions={0}, use_global_device_ids=true | all-gather | bytes 16896 | tf_op jit(solution)/shard_map/all_gather | solution.py:450
  91.7 0.6 slice_reduce_fusion
Async XLA Ops:
  0.6 1.1 %copy-start = (f32[19,16,4,128]{3,2,1,0:T(4,128)S(1)}, f32[19,16,4,128]{3,2,1,0:T(4,128)}, u32[]{:S(2)}) copy-start(f32[19,16,4,128]{3,2,1,0:T(4,128)} %param.4) | copy-start | bytes 1867780
  1.7 0.9 copy-start.1
  2.6 0.7 copy-start.3
  13.1 13.2 %copy-start.2 = (s32[18,16,4,128]{3,2,1,0:T(4,128)S(1)}, s32[18,16,4,128]{3,2,1,0:T(4,128)}, u32[]{:S(2)}) copy-start(s32[18,16,4,128]{3,2,1,0:T(4,128)} %param.7) | copy-start | bytes 1769476

commit v5 on v3

--- a/solution.py
+++ b/solution.py
@@ -81,22 +81,59 @@
     return blocks
 
 
-def row_message_kernel(state, velocity, solid, low, high):
+def on_even(axis):
+    return lax.rem(lax.axis_index(axis), 2) == 0
+
+
+def row_message_kernel(
+    state, velocity, solid, first_out, second_out, low_rows, high_rows, low_flow, high_flow, tiles, arrived
+):
     rows = state.shape[1]
-    solid_parts = spread_solid(solid)
-    flow = flow_blocks(velocity, 0, rows)
-    for out, first, second, group, moving in (
-        (low, 0, LEVELS, 0, x_up),
-        (high, rows - LEVELS, rows - 2 * LEVELS, -1, x_down),
-    ):
-        for number in range(19):
-            out[number] = state[number, pl.ds(first, LEVELS), :]
-        start = first % 8
-        for axis in range(3):
-            out[FLOW + axis] = flow[group][axis][start : start + LEVELS]
-        out[SOLID] = solid_parts[group][:LEVELS]
-        for slot, number in enumerate(moving):
-            out[SECOND + slot] = state[number, pl.ds(second, LEVELS), :]
+    copies = [
+        pltpu.make_async_copy(source, target, arrived.at[number])
+        for number, (source, target) in enumerate(
+            (
+                (state.at[:, pl.ds(0, 8), :], low_rows),
+                (state.at[:, pl.ds(rows - 8, 8), :], high_rows),
+                (velocity.at[0, :, pl.ds(0, 16), :], low_flow),
+                (velocity.at[0, :, pl.ds(rows - 16, 16), :], high_flow),
+                (solid, tiles),
+            )
+        )
+    ]
+    for copy in copies:
+        copy.start()
+    for copy in copies:
+        copy.wait()
+    even = on_even("gx")
+    solid_parts = spread_solid(tiles)
+
+    def put(slot, low, high):
+        first_out[slot] = jnp.where(even, high, low)
+        second_out[slot] = jnp.where(even, low, high)
+
+    for number in range(19):
+        put(number, low_rows[number, pl.ds(0, LEVELS), :], high_rows[number, pl.ds(LEVELS, LEVELS), :])
+    for axis in range(3):
+        low = low_flow[axis].astype(jnp.float32)
+        high = high_flow[axis].astype(jnp.float32)
+        put(FLOW + axis, low[:LEVELS], high[16 - LEVELS :])
+    put(SOLID, solid_parts[0][:LEVELS], solid_parts[-1][:LEVELS])
+    for slot in range(5):
+        put(
+            SECOND + slot,
+            low_rows[x_up[slot], pl.ds(LEVELS, LEVELS), :],
+            high_rows[x_down[slot], pl.ds(0, LEVELS), :],
+        )
+
+
+class Chosen:
+    def __init__(self, choice, yes, no):
+        self.choice, self.yes, self.no = choice, yes, no
+        self.shape = yes.shape
+
+    def __getitem__(self, index):
+        return jnp.where(self.choice, self.yes[index], self.no[index])
 
 
 def slot_place(slot, group, groups):
@@ -104,8 +141,12 @@
     return slot // per_block, (slot % per_block) * groups + group
 
 
-def column_message_kernel(state, velocity, solid, after, before, low, high, ends):
+def column_message_kernel(
+    state, velocity, solid, row_first, row_second, first_out, second_out, ends
+):
     rows = state.shape[1]
+    even = on_even("gx")
+    after, before = Chosen(even, row_first, row_second), Chosen(even, row_second, row_first)
     groups = rows // 8 + 2
     solid_parts = spread_solid(solid)
     flow = flow_blocks(velocity, 0, rows)
@@ -136,7 +177,7 @@
             return flow[group - 1][slot - FLOW]
         return solid_parts[(group - 1) * 8 // (LEVELS * TILE)]
 
-    count = low.shape[0]
+    count = first_out.shape[0]
     low_parts = [jnp.zeros((8, LANES), jnp.float32) for _ in range(count)]
     high_parts = [jnp.zeros((8, LANES), jnp.float32) for _ in range(count)]
     for slot in range(SECOND):
@@ -151,15 +192,15 @@
                     part, place = slot_place(SECOND + moving.index(slot), group, groups)
                     turned = pltpu.roll(value, (place + ahead - edge) % LANES, 1)
                     parts[part] = jnp.where(lane == place + ahead, turned, parts[part])
+    even = on_even("gy")
     for part in range(count):
-        low[part] = low_parts[part]
-        high[part] = high_parts[part]
+        first_out[part] = jnp.where(even, high_parts[part], low_parts[part])
+        second_out[part] = jnp.where(even, low_parts[part], high_parts[part])
 
 
 def collide(moved, flow, fluid):
     ux, uy, uz = flow
     total = {n: moved[n] + moved[n + 1] for n in range(1, 19, 2)}
-    gap = {n: moved[n] - moved[n + 1] for n in range(1, 19, 2)}
     xy, xz, yz = total[7] + total[9], total[11] + total[13], total[15] + total[17]
     axis_x, axis_y, axis_z = 2.0 * total[1], 2.0 * total[3], 2.0 * total[5]
     density = 12.0 * moved[0] + (axis_x + axis_y + axis_z) + (xy + xz + yz)
@@ -169,14 +210,11 @@
     pxy = total[7] - total[9]
     pxz = total[11] - total[13]
     pyz = total[15] - total[17]
-    dx = 2.0 * gap[1] + (gap[7] + gap[9]) + (gap[11] + gap[13])
-    dy = 2.0 * gap[3] + (gap[7] - gap[9]) + (gap[15] + gap[17])
-    dz = 2.0 * gap[5] + (gap[11] - gap[13]) + (gap[15] - gap[17])
+    dx, dy, dz = momentum(moved)
     vx = pxx * ux + pxy * uy + pxz * uz
     vy = pxy * ux + pyy * uy + pyz * uz
     vz = pxz * ux + pyz * uy + pzz * uz
     speed_sq = ux * ux + uy * uy + uz * uz
-    drag = fluid * (ux * dx + uy * dy + uz * dz)
     scaled = (relax_rate / 36.0) * fluid
     base = scaled * (density + 1.5 * (speed_sq * density) - 4.5 * (ux * vx + uy * vy + uz * vz))
     scaled3 = 3.0 * scaled
@@ -196,7 +234,7 @@
                 along = along + part if speed == 1 else along - part
         results.append(keep * moved[number] + (base + along))
         results.append(keep * moved[number + 1] + (base - along))
-    return results, drag
+    return results
 
 
 def outside(cz):
@@ -216,28 +254,47 @@
     return jnp.where(lane == 0, edge_value, pltpu.roll(value, 1, 1))
 
 
-def step_cells(held, shifted, first, flow, fluid, closed):
+def gather_cells(held, shifted, first, closed):
     here = [held[n, pl.ds(first, 8), :] for n in range(19)]
     moved = [here[0]]
     for number in range(1, 19):
         cx, cy, cz = lattice_speeds[number]
         field = held if cy == 0 else shifted
-        if cx == cy == cz == 0:
-            source = here[number]
-        else:
-            source = field[number, pl.ds(first + LEVELS * cx + cz, 8), :]
+        source = field[number, pl.ds(first + LEVELS * cx + cz, 8), :]
         bounced = here[opposite_of(number)]
         if cx != 0:
             bounced = bounced + 2.0 * cx
         moved.append(jnp.where(closed(number), bounced, source))
-    return collide(moved, flow, fluid)
-
-
-def main_kernel(
-    state, velocity, blocked, solid, after, before, y_after, y_before, low, high, out, shared,
-    held, shifted, later, row_flow, solid_rows,
+    return moved
+
+
+def momentum(moved):
+    gap = {n: moved[n] - moved[n + 1] for n in range(1, 19, 2)}
+    dx = 2.0 * gap[1] + (gap[7] + gap[9]) + (gap[11] + gap[13])
+    dy = 2.0 * gap[3] + (gap[7] - gap[9]) + (gap[15] + gap[17])
+    dz = 2.0 * gap[5] + (gap[11] - gap[13]) + (gap[15] - gap[17])
+    return dx, dy, dz
+
+
+def drag_term(moved, flow, fluid):
+    return fluid * sum(speed * part for speed, part in zip(flow, momentum(moved)))
+
+
+def first_step_kernel(
+    state, velocity, blocked, solid, row_first, row_second, column_first, column_second,
+    sent_first, sent_second, later, later_shifted, shared, held, shifted, row_flow, solid_rows,
 ):
     rows = state.shape[1]
+    even = on_even("gx")
+    after, before = Chosen(even, row_first, row_second), Chosen(even, row_second, row_first)
+    even = on_even("gy")
+    parts = range(column_first.shape[0])
+
+    def chosen(yes, no):
+        return [jnp.where(even, yes[part], no[part]) for part in parts]
+
+    y_after, y_before = chosen(column_first, column_second), chosen(column_second, column_first)
+    low, high = chosen(sent_second, sent_first), chosen(sent_first, sent_second)
     groups = rows // 8 + 2
     own = GUARD + 8
     near, far = own - LEVELS, own + rows
@@ -299,7 +356,7 @@
         source = both_rows(held if cy == 0 else shifted, number, shift)
         closed = link_closed(both_rows(solid_rows, cy % 3, shift), cz)
         moved.append(jnp.where(closed, here[opposite_of(number)] + 2.0 * cx, source))
-    row_results, _ = collide(moved, [row_flow[axis] for axis in range(3)], 1.0 - row_flow[3])
+    row_results = collide(moved, [row_flow[axis] for axis in range(3)], 1.0 - row_flow[3])
 
     def columns(number_before, number_after, message_before, message_after):
         return jnp.where(
@@ -339,7 +396,7 @@
         closed = link_closed(shift_rows(solid_columns[cy % 3], cx, cz), cz)
         moved.append(jnp.where(closed, here[opposite_of(number)] + 2.0 * cx, source))
     column_flow = [neighbours(FLOW + axis, 0) for axis in range(3)]
-    column_results, _ = collide(moved, column_flow, 1.0 - solid_columns[0])
+    column_results = collide(moved, column_flow, 1.0 - solid_columns[0])
 
     def closed_at(first):
         return lambda number: blocked[number - 1, pl.ds(first, 8), :] == 1
@@ -351,12 +408,11 @@
     flow = flow_blocks(velocity, 0, rows)
     for group in range(rows // 8):
         first = 8 * group
-        results, drag = step_cells(
-            held, shifted, own + first, flow[group], fluid_at(first), closed_at(first)
-        )
+        moved = gather_cells(held, shifted, own + first, closed_at(first))
+        results = collide(moved, flow[group], fluid_at(first))
         for number in range(19):
             later[number, pl.ds(own + first, 8), :] = results[number]
-        drag_sum = drag_sum + drag
+        drag_sum = drag_sum + drag_term(moved, flow[group], fluid_at(first))
     for number in x_down:
         later[number, pl.ds(near, LEVELS), :] = row_results[number][:LEVELS]
     for number in x_up:
@@ -369,25 +425,37 @@
                 edge = pltpu.roll(column_results[number], (LANES - 1 - AFTER_LANE - group) % LANES, 1)
             else:
                 edge = pltpu.roll(column_results[number], (-BEFORE_LANE - group) % LANES, 1)
-            shifted[number, pl.ds(GUARD + 8 * group, 8), :] = shift_lanes(value, cy, edge)
+            later_shifted[number, pl.ds(GUARD + 8 * group, 8), :] = shift_lanes(value, cy, edge)
 
     flow = flow_blocks(velocity, 1, rows)
     for group in range(rows // 8):
         first = 8 * group
-        results, drag = step_cells(
-            later, shifted, own + first, flow[group], fluid_at(first), closed_at(first)
-        )
+        moved = gather_cells(later, later_shifted, own + first, closed_at(first))
+        drag_sum = drag_sum + drag_term(moved, flow[group], fluid_at(first))
+    shared[...] = jnp.broadcast_to(jnp.sum(drag_sum), shared.shape)
+
+
+def second_step_kernel(later, later_shifted, velocity, blocked, solid, out):
+    rows = out.shape[1]
+    solid_parts = spread_solid(solid)
+    flow = flow_blocks(velocity, 1, rows)
+    for group in range(rows // 8):
+        first = 8 * group
+
+        def closed(number):
+            return blocked[number - 1, pl.ds(first, 8), :] == 1
+
+        moved = gather_cells(later, later_shifted, GUARD + 8 + first, closed)
+        results = collide(moved, flow[group], 1.0 - solid_parts[first // (LEVELS * TILE)])
         for number in range(19):
             out[number, pl.ds(first, 8), :] = results[number]
-        drag_sum = drag_sum + drag
-    shared[...] = jnp.broadcast_to(jnp.sum(drag_sum), shared.shape)
-
-
-def swap_edges(low, high, axis):
+
+
+def swap_pairs(first, second, axis):
     count = lax.axis_size(axis)
-    from_after = [((i + 1) % count, i) for i in range(count)]
-    from_before = [(i, (i + 1) % count) for i in range(count)]
-    return lax.ppermute(low, axis, from_after), lax.ppermute(high, axis, from_before)
+    inside = [(i, i ^ 1) for i in range(count)]
+    across = [(i, (i + 1) % count if i % 2 == 1 else (i - 1) % count) for i in range(count)]
+    return lax.ppermute(first, axis, inside), lax.ppermute(second, axis, across)
 
 
 def per_device(adjoint_in, velocity, solid_tiles, link_blocked):
@@ -405,40 +473,56 @@
         return jax.ShapeDtypeStruct(sizes, jnp.float32)
 
     params = pltpu.CompilerParams(vmem_limit_bytes=16 * 1024 * 1024)
-    row_low, row_high = pl.pallas_call(
+    anywhere = pl.BlockSpec(memory_space=pl.ANY)
+    row_sent = pl.pallas_call(
         row_message_kernel,
         out_shape=(shape_of(QUANTITIES, levels, rows_y),) * 2,
-        in_specs=[vmem] * 3,
+        in_specs=[anywhere] * 3,
         out_specs=(vmem,) * 2,
-        compiler_params=params,
+        scratch_shapes=[
+            pltpu.VMEM((19, 8, rows_y), jnp.float32),
+            pltpu.VMEM((19, 8, rows_y), jnp.float32),
+            pltpu.VMEM((3, 16, rows_y), velocity.dtype),
+            pltpu.VMEM((3, 16, rows_y), velocity.dtype),
+            pltpu.VMEM(solid.shape, solid.dtype),
+            pltpu.SemaphoreType.DMA((5,)),
+        ],
+        compiler_params=pltpu.CompilerParams(vmem_limit_bytes=60 * 1024 * 1024),
     )(state, flow, solid)
-    after, before = swap_edges(row_low, row_high, "gx")
-    low, high = pl.pallas_call(
+    row_got = swap_pairs(*row_sent, "gx")
+    column_sent = pl.pallas_call(
         column_message_kernel,
         out_shape=(shape_of(parts, 8, rows_y),) * 2,
         in_specs=[vmem] * 5,
         out_specs=(vmem,) * 2,
         scratch_shapes=[pltpu.VMEM((2, SECOND, 8, rows_y), jnp.float32)],
         compiler_params=params,
-    )(state, flow, solid, after, before)
-    y_after, y_before = swap_edges(low, high, "gy")
+    )(state, flow, solid, *row_got)
+    column_got = swap_pairs(*column_sent, "gy")
     count = lax.axis_size("gx") * lax.axis_size("gy")
     field = pltpu.VMEM((19, padded, rows_y), jnp.float32)
-    result, own = pl.pallas_call(
-        main_kernel,
-        out_shape=(shape_of(19, rows, rows_y), shape_of(count, 1, rows_y)),
+    later, later_shifted, own = pl.pallas_call(
+        first_step_kernel,
+        out_shape=(shape_of(19, padded, rows_y),) * 2 + (shape_of(count, 1, rows_y),),
         in_specs=[vmem] * 10,
-        out_specs=(vmem,) * 2,
+        out_specs=(vmem,) * 3,
         scratch_shapes=[
-            field,
             field,
             field,
             pltpu.VMEM((4, 8, rows_y), jnp.float32),
             pltpu.VMEM((3, padded, rows_y), jnp.float32),
         ],
         compiler_params=params,
-    )(state, flow, blocked, solid, after, before, y_after, y_before, low, high)
+    )(state, flow, blocked, solid, *row_got, *column_got, *column_sent)
     shared = lax.all_to_all(own, ("gx", "gy"), split_axis=0, concat_axis=0, tiled=True)
+    result = pl.pallas_call(
+        second_step_kernel,
+        out_shape=shape_of(19, rows, rows_y),
+        in_specs=[vmem] * 5,
+        out_specs=vmem,
+        compiler_params=params,
+        cost_estimate=pl.CostEstimate(flops=4_000_000, bytes_accessed=4_000_000, transcendentals=0),
+    )(later, later_shifted, flow, blocked, solid)
     cell_count = rows * rows_y * count
     scale = drag_factor / math.sqrt(cell_count) * 3.0 / 36.0
     total = jnp.sum(shared[:, 0, 0])

time: 34.4 us -> 32.8 us (0.953)
  blocking collectives: 8.79 us -> 0 us
  starting transfers between devices: 6.99 us -> 13 us
  local copies, waits for them, and re-layouts: 2.66 us -> 0.02 us
  Pallas kernels: 2.64 us -> 5.21 us
  waiting for transfers between devices: 9.99 us -> 11.2 us
    all_to_all x1 -> x0, blocking collectives: 8.79 us -> none  [per_device(): lax.all_to_all(own, ('gx', 'gy'), split_axis=0, concat_axis=0, tiled=True)]
    all_to_all x0 -> x1, waiting for transfers between devices: none -> 5.99 us  [per_device(): lax.all_to_all(own, ('gx', 'gy'), split_axis=0, concat_axis=0, tiled=True)]
    all_to_all x0 -> x1, starting transfers between devices: none -> 4.89 us  [per_device(): lax.all_to_all(own, ('gx', 'gy'), split_axis=0, concat_axis=0, tiled=True)]
    ppermute x4, waiting for transfers between devices: 9.99 us -> 5.22 us  [the longest x2 5.22 us: swap_pairs(): lax.ppermute(second, axis, across)]
    unnamed x8, local copies, waits for them, and re-layouts: 2.66 us -> 0.02 us
    pallas_call x1, Pallas kernels: 0.13 us -> 1.81 us  [per_device(): pl.pallas_call(row_message_kernel, out_shape=(shape_of(QUANTITIES, levels...]
    ppermute x4, starting transfers between devices: 6.99 us -> 8.13 us  [the longest x2 6.22 us: swap_pairs(): lax.ppermute(second, axis, across)]
    pallas_call x1 -> x2, Pallas kernels: 2.09 us -> 2.98 us  [the longest x1 1.85 us: per_device(): pl.pallas_call(first_step_kernel, out_shape=(shape_of(19, padded, rows_y)...]
  transfers between devices with their start and end apart: 4 -> 5, of which waited for: 4 -> 3; matrix products, arithmetic and copies ran while one was open for 0% -> 0% of each run, Pallas kernels for 0% -> 3%
where the time goes in v5:
time: 32.8 us; the launch traced here: 32.6 us
  starting transfers between devices  13 us (40%)
  waiting for transfers between devices  11.2 us (34%)
  Pallas kernels  5.21 us (16%)
  between operations  2.47 us (8%)
  other arithmetic  0.63 us (2%)
    ppermute x2, starting transfers between devices, swap_pairs(): lax.ppermute(second, axis, across)  6.22 us
    all_to_all x1, waiting for transfers between devices, per_device(): lax.all_to_all(own, ('gx', 'gy'), split_axis=0, concat_axis=0, tiled=True)  5.99 us
    ppermute x2, waiting for transfers between devices, swap_pairs(): lax.ppermute(second, axis, across)  5.22 us
    all_to_all x1, starting transfers between devices, per_device(): lax.all_to_all(own, ('gx', 'gy'), split_axis=0, concat_axis=0, tiled=True)  4.89 us
    ppermute x2, starting transfers between devices, swap_pairs(): lax.ppermute(first, axis, inside)  1.91 us
    pallas_call x1, Pallas kernels, per_device(): pl.pallas_call(first_step_kernel, out_shape=(shape_of(19, padded, rows_y)...  1.85 us
    pallas_call x1, Pallas kernels, per_device(): pl.pallas_call(row_message_kernel, out_shape=(shape_of(QUANTITIES, levels...  1.81 us
    pallas_call x1, Pallas kernels, per_device(): pl.pallas_call(second_step_kernel, out_shape=shape_of(19, rows, rows_y),...  1.13 us
  transfers between devices with their start and end apart: 5, of which 3 were waited for; matrix products, arithmetic and copies ran while one was open for 0% of the time, Pallas kernels for 3%

profile of v5, /device:TPU:0, one launch (start us, length us, event | category | flops | bytes accessed | tf_op | source)
XLA Modules:
  0.0 32.6 jit_solution(18404768662964631807)
XLA Ops:
  0.6 0.0 copy-start
  0.6 0.0 copy-start.2
  0.6 0.0 copy-start.3
  0.7 1.8 %shard_map.59 = (f32[28,4,128]{2,1,0:T(4,128)}, f32[28,4,128]{2,1,0:T(4,128)}) custom-call(f32[19,64,128]{2,1,0:T(8,128)} %bitcast.6, bf16[2,3,64,128]{3,2,1,0:T(8,128)(2,1)} %bitcast.11, s32[16,32]{1,0:T(8,128)} %bitcast.15), custom_call_target="tpu_custom_call" | custom-call | tf_op jit(solution)/shard_map/pallas_call | solution.py:477
  2.5 0.0 copy-start.1
  2.5 0.5 %collective-permute-start = (f32[28,4,128]{2,1,0:T(4,128)}, f32[28,4,128]{2,1,0:T(4,128)S(1)}, u32[]{:S(2)}, u32[]{:S(2)}) collective-permute-start(f32[28,4,128]{2,1,0:T(4,128)} %get-tuple-element.9), channel_id=1, source_target_pairs={{0,8},{8,0},{16,24},{24,16},{1,9},{9,1},{17,25},{25,17},{2,10},{10... | collective-permute-start | bytes 172040 | tf_op jit(solution)/shard_map/ppermute | solution.py:458
  3.0 2.6 %collective-permute-start.1 = (f32[28,4,128]{2,1,0:T(4,128)}, f32[28,4,128]{2,1,0:T(4,128)S(1)}, u32[]{:S(2)}, u32[]{:S(2)}) collective-permute-start(f32[28,4,128]{2,1,0:T(4,128)} %get-tuple-element.10), channel_id=1, source_target_pairs={{0,24},{8,16},{16,8},{24,0},{1,25},{9,17},{17,9},{25,1},{2,26},{10... | collective-permute-start | bytes 172040 | tf_op jit(solution)/shard_map/ppermute | solution.py:458
  5.6 0.0 collective-permute-done.row_first
  5.7 2.4 %collective-permute-done.1.row_second = f32[28,4,128]{2,1,0:T(4,128)S(1)} collective-permute-done((f32[28,4,128]{2,1,0:T(4,128)}, f32[28,4,128]{2,1,0:T(4,128)S(1)}, u32[]{:S(2)}, u32[]{:S(2)}) %collective-permute-start.1) | collective-permute-done | bytes 57376 | tf_op jit(solution)/shard_map/ppermute | solution.py:458
  8.1 0.0 copy-done
  8.1 0.0 copy-done.2
  8.1 0.0 copy-done.3
  8.1 0.4 %shard_map.60 = (f32[3,8,128]{2,1,0:T(8,128)S(1)}, f32[3,8,128]{2,1,0:T(8,128)S(1)}) custom-call(f32[19,64,128]{2,1,0:T(8,128)S(1)} %bitcast.7, bf16[2,3,64,128]{3,2,1,0:T(8,128)(2,1)S(1)} %bitcast.12, s32[16,32]{1,0:T(8,128)S(1)} %bitcast.16, f32[28,4,128]{2,1,0:T(4,128)S(1)} %collective-permute-done.row_first, ...), custom_call_target="tpu_custom_call" | custom-call | tf_op jit(solution)/shard_map/pallas_call | solution.py:493
  8.5 1.4 %collective-permute-start.2 = (f32[3,8,128]{2,1,0:T(8,128)S(1)}, f32[3,8,128]{2,1,0:T(8,128)S(1)}, u32[]{:S(2)}, u32[]{:S(2)}) collective-permute-start(f32[3,8,128]{2,1,0:T(8,128)S(1)} %get-tuple-element.11.sent_first), channel_id=1, source_target_pairs={{0,1},{1,0},{2,3},{3,2},{4,5},{5,4},{6,7},{7,6},{8,9},{9,8},{10,11... | collective-permute-start | bytes 36872 | tf_op jit(solution)/shard_map/ppermute | solution.py:458
  9.9 3.6 %collective-permute-start.3 = (f32[3,8,128]{2,1,0:T(8,128)S(1)}, f32[3,8,128]{2,1,0:T(8,128)S(1)}, u32[]{:S(2)}, u32[]{:S(2)}) collective-permute-start(f32[3,8,128]{2,1,0:T(8,128)S(1)} %get-tuple-element.12.sent_second), channel_id=1, source_target_pairs={{0,7},{1,2},{2,1},{3,4},{4,3},{5,6},{6,5},{7,0},{8,15},{9,10},{10,... | collective-permute-start | bytes 36872 | tf_op jit(solution)/shard_map/ppermute | solution.py:458
  13.5 0.0 collective-permute-done.2.column_first
  13.5 2.8 %collective-permute-done.3.column_second = f32[3,8,128]{2,1,0:T(8,128)S(1)} collective-permute-done((f32[3,8,128]{2,1,0:T(8,128)S(1)}, f32[3,8,128]{2,1,0:T(8,128)S(1)}, u32[]{:S(2)}, u32[]{:S(2)}) %collective-permute-start.3) | collective-permute-done | bytes 12320 | tf_op jit(solution)/shard_map/ppermute | solution.py:458
  16.3 0.0 copy-done.1
  16.3 1.8 %shard_map.61 = (f32[19,96,128]{2,1,0:T(8,128)S(1)}, f32[19,96,128]{2,1,0:T(8,128)S(1)}, f32[32,1,128]{2,1,0:T(1,128)}) custom-call(f32[19,64,128]{2,1,0:T(8,128)S(1)} %bitcast.8, bf16[2,3,64,128]{3,2,1,0:T(8,128)(2,1)S(1)} %bitcast.13, s32[18,64,128]{2,1,0:T(8,128)S(1)} %bitcast.9, s32[16,32]{1,0:T(8,128)S(1)} %bitcast.17, ...), custom_call_target="tpu_custom_call" | custom-call | tf_op jit(solution)/shard_map/pallas_call | solution.py:504
  18.1 4.9 %all-to-all-start = ((f32[32,1,128]{2,1,0:T(1,128)}), f32[32,1,128]{2,1,0:T(1,128)S(1)}, u32[]{:S(2)}, u32[]{:S(2)}) async-start(f32[32,1,128]{2,1,0:T(1,128)} %get-tuple-element.15), calls=%async_computation | async-start | bytes 32768 | tf_op jit(solution)/shard_map/all_to_all | solution.py:517
  23.0 1.1 %shard_map.62 = f32[19,64,128]{2,1,0:T(8,128)} custom-call(f32[19,96,128]{2,1,0:T(8,128)S(1)} %get-tuple-element.13.later, f32[19,96,128]{2,1,0:T(8,128)S(1)} %get-tuple-element.14.later_shifted, bf16[2,3,64,128]{3,2,1,0:T(8,128)(2,1)S(1)} %bitcast.14, s32[18,64,128]{2,1,0:T(8,128)S(1)} %bitcast.10, s32[16,32]{1,0:T(8,128)S(1)} %bitcast.18), custom_call_target="tpu_custom_call" | custom-call | flops 4000000 | bytes 4000000 | tf_op jit(solution)/shard_map/pallas_call | solution.py:518
  24.2 6.0 %all-to-all-done = f32[32,1,128]{2,1,0:T(1,128)S(1)} async-done(((f32[32,1,128]{2,1,0:T(1,128)}), f32[32,1,128]{2,1,0:T(1,128)S(1)}, u32[]{:S(2)}, u32[]{:S(2)}) %all-to-all-start) | async-done | bytes 16416 | tf_op jit(solution)/shard_map/all_to_all | solution.py:517
  30.2 0.6 %slice_reduce_fusion = f32[]{:T(128)} fusion(f32[32,1,128]{2,1,0:T(1,128)S(1)} %all-to-all-done), kind=kLoop, calls=%fused_computation | loop fusion | flops 31 | bytes 132 | tf_op jit(solution)/shard_map/reduce_sum | solution.py:528
Async XLA Ops:
  0.6 7.4 %copy-start = (f32[19,16,4,128]{3,2,1,0:T(4,128)S(1)}, f32[19,16,4,128]{3,2,1,0:T(4,128)}, u32[]{:S(2)}) copy-start(f32[19,16,4,128]{3,2,1,0:T(4,128)} %param.4) | copy-start | bytes 1867780
  0.6 7.4 %copy-start.2 = (bf16[2,3,16,4,128]{4,3,2,1,0:T(4,128)(2,1)S(1)}, bf16[2,3,16,4,128]{4,3,2,1,0:T(4,128)(2,1)}, u32[]{:S(2)}) copy-start(bf16[2,3,16,4,128]{4,3,2,1,0:T(4,128)(2,1)} %param.5) | copy-start | bytes 294916
  0.6 7.4 %copy-start.3 = (s32[4,4,32]{2,1,0:T(4,128)S(1)}, s32[4,4,32]{2,1,0:T(4,128)}, u32[]{:S(2)}) copy-start(s32[4,4,32]{2,1,0:T(4,128)} %param.6) | copy-start | bytes 6148
  2.5 13.8 %copy-start.1 = (s32[18,16,4,128]{3,2,1,0:T(4,128)S(1)}, s32[18,16,4,128]{3,2,1,0:T(4,128)}, u32[]{:S(2)}) copy-start(s32[18,16,4,128]{3,2,1,0:T(4,128)} %param.7) | copy-start | bytes 1769476
  2.5 3.2 %collective-permute-start = (f32[28,4,128]{2,1,0:T(4,128)}, f32[28,4,128]{2,1,0:T(4,128)S(1)}, u32[]{:S(2)}, u32[]{:S(2)}) collective-permute-start(f32[28,4,128]{2,1,0:T(4,128)} %get-tuple-element.9), channel_id=1, source_target_pairs={{0,8},{8,0},{16,24},{24,16},{1,9},{9,1},{17,25},{25,17},{2,10},{10... | collective-permute-start | bytes 172040 | tf_op jit(solution)/shard_map/ppermute | solution.py:458
  3.0 5.1 %collective-permute-start.1 = (f32[28,4,128]{2,1,0:T(4,128)}, f32[28,4,128]{2,1,0:T(4,128)S(1)}, u32[]{:S(2)}, u32[]{:S(2)}) collective-permute-start(f32[28,4,128]{2,1,0:T(4,128)} %get-tuple-element.10), channel_id=1, source_target_pairs={{0,24},{8,16},{16,8},{24,0},{1,25},{9,17},{17,9},{25,1},{2,26},{10... | collective-permute-start | bytes 172040 | tf_op jit(solution)/shard_map/ppermute | solution.py:458
  8.5 5.0 %collective-permute-start.2 = (f32[3,8,128]{2,1,0:T(8,128)S(1)}, f32[3,8,128]{2,1,0:T(8,128)S(1)}, u32[]{:S(2)}, u32[]{:S(2)}) collective-permute-start(f32[3,8,128]{2,1,0:T(8,128)S(1)} %get-tuple-element.11.sent_first), channel_id=1, source_target_pairs={{0,1},{1,0},{2,3},{3,2},{4,5},{5,4},{6,7},{7,6},{8,9},{9,8},{10,11... | collective-permute-start | bytes 36872 | tf_op jit(solution)/shard_map/ppermute | solution.py:458
  9.9 6.4 %collective-permute-start.3 = (f32[3,8,128]{2,1,0:T(8,128)S(1)}, f32[3,8,128]{2,1,0:T(8,128)S(1)}, u32[]{:S(2)}, u32[]{:S(2)}) collective-permute-start(f32[3,8,128]{2,1,0:T(8,128)S(1)} %get-tuple-element.12.sent_second), channel_id=1, source_target_pairs={{0,7},{1,2},{2,1},{3,4},{4,3},{5,6},{6,5},{7,0},{8,15},{9,10},{10,... | collective-permute-start | bytes 36872 | tf_op jit(solution)/shard_map/ppermute | solution.py:458
  18.1 12.0 %all-to-all-start = ((f32[32,1,128]{2,1,0:T(1,128)}), f32[32,1,128]{2,1,0:T(1,128)S(1)}, u32[]{:S(2)}, u32[]{:S(2)}) async-start(f32[32,1,128]{2,1,0:T(1,128)} %get-tuple-element.15), calls=%async_computation | async-start | bytes 32768 | tf_op jit(solution)/shard_map/all_to_all | solution.py:517

commit v6 on v5

--- a/solution.py
+++ b/solution.py
@@ -85,48 +85,6 @@
     return lax.rem(lax.axis_index(axis), 2) == 0
 
 
-def row_message_kernel(
-    state, velocity, solid, first_out, second_out, low_rows, high_rows, low_flow, high_flow, tiles, arrived
-):
-    rows = state.shape[1]
-    copies = [
-        pltpu.make_async_copy(source, target, arrived.at[number])
-        for number, (source, target) in enumerate(
-            (
-                (state.at[:, pl.ds(0, 8), :], low_rows),
-                (state.at[:, pl.ds(rows - 8, 8), :], high_rows),
-                (velocity.at[0, :, pl.ds(0, 16), :], low_flow),
-                (velocity.at[0, :, pl.ds(rows - 16, 16), :], high_flow),
-                (solid, tiles),
-            )
-        )
-    ]
-    for copy in copies:
-        copy.start()
-    for copy in copies:
-        copy.wait()
-    even = on_even("gx")
-    solid_parts = spread_solid(tiles)
-
-    def put(slot, low, high):
-        first_out[slot] = jnp.where(even, high, low)
-        second_out[slot] = jnp.where(even, low, high)
-
-    for number in range(19):
-        put(number, low_rows[number, pl.ds(0, LEVELS), :], high_rows[number, pl.ds(LEVELS, LEVELS), :])
-    for axis in range(3):
-        low = low_flow[axis].astype(jnp.float32)
-        high = high_flow[axis].astype(jnp.float32)
-        put(FLOW + axis, low[:LEVELS], high[16 - LEVELS :])
-    put(SOLID, solid_parts[0][:LEVELS], solid_parts[-1][:LEVELS])
-    for slot in range(5):
-        put(
-            SECOND + slot,
-            low_rows[x_up[slot], pl.ds(LEVELS, LEVELS), :],
-            high_rows[x_down[slot], pl.ds(0, LEVELS), :],
-        )
-
-
 class Chosen:
     def __init__(self, choice, yes, no):
         self.choice, self.yes, self.no = choice, yes, no
@@ -141,61 +99,86 @@
     return slot // per_block, (slot % per_block) * groups + group
 
 
-def column_message_kernel(
-    state, velocity, solid, row_first, row_second, first_out, second_out, ends
+def insert_column(parts, slot, group, groups, value, edge, ahead):
+    part, place = slot_place(slot, group, groups)
+    lane = lane_index()
+    turned = pltpu.roll(value, (place + ahead - edge) % LANES, 1)
+    parts[part] = jnp.where(lane == place + ahead, turned, parts[part])
+
+
+def message_kernel(
+    state, velocity, solid, row_first, row_second, column_first, column_second, cells, flow, tiles, arrived
 ):
     rows = state.shape[1]
-    even = on_even("gx")
-    after, before = Chosen(even, row_first, row_second), Chosen(even, row_second, row_first)
     groups = rows // 8 + 2
-    solid_parts = spread_solid(solid)
-    flow = flow_blocks(velocity, 0, rows)
-    lane = lane_index()
-    for slot in range(SECOND):
-        ends[0, slot, pl.ds(LEVELS, LEVELS), :] = before[slot]
-        ends[1, slot, pl.ds(0, LEVELS), :] = after[slot]
-        in_second = SOLID if slot == SOLID else None
-        low_second = SECOND + x_down.index(slot) if slot in x_down else in_second
-        high_second = SECOND + x_up.index(slot) if slot in x_up else in_second
-        if low_second is not None:
-            ends[0, slot, pl.ds(0, LEVELS), :] = before[low_second]
-        else:
-            ends[0, slot, pl.ds(0, LEVELS), :] = jnp.zeros((LEVELS, LANES), jnp.float32)
-        if high_second is not None:
-            ends[1, slot, pl.ds(LEVELS, LEVELS), :] = after[high_second]
-        else:
-            ends[1, slot, pl.ds(LEVELS, LEVELS), :] = jnp.zeros((LEVELS, LANES), jnp.float32)
-
-    def block(slot, group):
-        if group == 0:
-            return ends[0, slot]
-        if group == groups - 1:
-            return ends[1, slot]
-        if slot < FLOW:
-            return state[slot, pl.ds(8 * (group - 1), 8), :]
-        if slot < SOLID:
-            return flow[group - 1][slot - FLOW]
-        return solid_parts[(group - 1) * 8 // (LEVELS * TILE)]
-
-    count = first_out.shape[0]
+    chunks = ((0, 7), (7, 6), (13, 6))
+    copies = [
+        pltpu.make_async_copy(velocity.at[0], flow, arrived.at[0]),
+        pltpu.make_async_copy(solid, tiles, arrived.at[1]),
+    ]
+    for number, (first, count) in enumerate(chunks):
+        part = pl.ds(first, count)
+        copies.append(pltpu.make_async_copy(state.at[part], cells.at[part], arrived.at[2 + number]))
+    for copy in copies:
+        copy.start()
+    x_even, y_even = on_even("gx"), on_even("gy")
+
+    def put(slot, low, high):
+        row_first[slot] = jnp.where(x_even, high, low)
+        row_second[slot] = jnp.where(x_even, low, high)
+
+    count = column_first.shape[0]
     low_parts = [jnp.zeros((8, LANES), jnp.float32) for _ in range(count)]
     high_parts = [jnp.zeros((8, LANES), jnp.float32) for _ in range(count)]
-    for slot in range(SECOND):
-        for group in range(groups):
-            value = block(slot, group)
-            part, place = slot_place(slot, group, groups)
-            turned = pltpu.roll(value, (place + 1) % LANES, 1)
-            low_parts[part] = jnp.where(lane == place + 1, turned, low_parts[part])
-            high_parts[part] = jnp.where(lane == place, turned, high_parts[part])
-            for moving, parts, edge, ahead in ((y_up, low_parts, 1, 1), (y_down, high_parts, LANES - 2, 0)):
-                if slot in moving:
-                    part, place = slot_place(SECOND + moving.index(slot), group, groups)
-                    turned = pltpu.roll(value, (place + ahead - edge) % LANES, 1)
-                    parts[part] = jnp.where(lane == place + ahead, turned, parts[part])
+
+    def pack(slot, group, value):
+        part, place = slot_place(slot, group, groups)
+        lane = lane_index()
+        turned = pltpu.roll(value, (place + 1) % LANES, 1)
+        low_parts[part] = jnp.where(lane == place + 1, turned, low_parts[part])
+        high_parts[part] = jnp.where(lane == place, turned, high_parts[part])
+        if slot in y_up:
+            insert_column(low_parts, SECOND + y_up.index(slot), group, groups, value, 1, 1)
+        if slot in y_down:
+            insert_column(high_parts, SECOND + y_down.index(slot), group, groups, value, LANES - 2, 0)
+
+    copies[0].wait()
+    for axis in range(3):
+        blocks = []
+        for pair in range(rows // 16):
+            both = flow[axis, pl.ds(16 * pair, 16), :].astype(jnp.float32)
+            blocks += [both[:8], both[8:]]
+        for group, value in enumerate(blocks):
+            pack(FLOW + axis, group + 1, value)
+        put(FLOW + axis, blocks[0][:LEVELS], blocks[-1][LEVELS:])
+    copies[1].wait()
+    solid_parts = spread_solid(tiles)
+    for group in range(rows // 8):
+        pack(SOLID, group + 1, solid_parts[8 * group // (LEVELS * TILE)])
+    put(SOLID, solid_parts[0][:LEVELS], solid_parts[-1][:LEVELS])
+    for copy, (first, count) in zip(copies[2:], chunks):
+        copy.wait()
+        for number in range(first, first + count):
+            for group in range(rows // 8):
+                pack(number, group + 1, cells[number, pl.ds(8 * group, 8), :])
+            put(number, cells[number, pl.ds(0, LEVELS), :], cells[number, pl.ds(rows - LEVELS, LEVELS), :])
+    for slot in range(5):
+        put(
+            SECOND + slot,
+            cells[x_up[slot], pl.ds(LEVELS, LEVELS), :],
+            cells[x_down[slot], pl.ds(rows - 2 * LEVELS, LEVELS), :],
+        )
+    for part in range(len(low_parts)):
+        column_first[part] = jnp.where(y_even, high_parts[part], low_parts[part])
+        column_second[part] = jnp.where(y_even, low_parts[part], high_parts[part])
+
+
+def corner_kernel(column_first, column_second, out):
     even = on_even("gy")
+    count = column_first.shape[0]
     for part in range(count):
-        first_out[part] = jnp.where(even, high_parts[part], low_parts[part])
-        second_out[part] = jnp.where(even, low_parts[part], high_parts[part])
+        out[part] = jnp.where(even, column_first[part], column_second[part])
+        out[count + part] = jnp.where(even, column_second[part], column_first[part])
 
 
 def collide(moved, flow, fluid):
@@ -254,17 +237,19 @@
     return jnp.where(lane == 0, edge_value, pltpu.roll(value, 1, 1))
 
 
-def gather_cells(held, shifted, first, closed):
+def gather_cells(held, shifted, first, solid_rows):
     here = [held[n, pl.ds(first, 8), :] for n in range(19)]
     moved = [here[0]]
     for number in range(1, 19):
         cx, cy, cz = lattice_speeds[number]
         field = held if cy == 0 else shifted
-        source = field[number, pl.ds(first + LEVELS * cx + cz, 8), :]
+        there = pl.ds(first + LEVELS * cx + cz, 8)
+        source = field[number, there, :]
+        closed = link_closed(solid_rows[cy % 3, there, :], cz)
         bounced = here[opposite_of(number)]
         if cx != 0:
             bounced = bounced + 2.0 * cx
-        moved.append(jnp.where(closed(number), bounced, source))
+        moved.append(jnp.where(closed, bounced, source))
     return moved
 
 
@@ -281,25 +266,41 @@
 
 
 def first_step_kernel(
-    state, velocity, blocked, solid, row_first, row_second, column_first, column_second,
-    sent_first, sent_second, later, later_shifted, shared, held, shifted, row_flow, solid_rows,
+    state, velocity, solid, row_first, row_second, column_first, column_second,
+    sent_first, sent_second, corner_first, corner_second,
+    later, later_shifted, solid_rows, shared, held, shifted, row_flow,
 ):
     rows = state.shape[1]
     even = on_even("gx")
     after, before = Chosen(even, row_first, row_second), Chosen(even, row_second, row_first)
+    corner_after = Chosen(even, corner_first, corner_second)
+    corner_before = Chosen(even, corner_second, corner_first)
     even = on_even("gy")
     parts = range(column_first.shape[0])
 
     def chosen(yes, no):
         return [jnp.where(even, yes[part], no[part]) for part in parts]
 
-    y_after, y_before = chosen(column_first, column_second), chosen(column_second, column_first)
     low, high = chosen(sent_second, sent_first), chosen(sent_first, sent_second)
     groups = rows // 8 + 2
     own = GUARD + 8
     near, far = own - LEVELS, own + rows
     lane = lane_index()
     solid_parts = spread_solid(solid)
+
+    def with_corners(yes, no, first_part, ahead):
+        whole = []
+        group = lax.rem(lane + groups - ahead, groups)
+        inside = jnp.logical_and(lane >= ahead, lane < LANES // groups * groups + ahead)
+        for part, own_rows in enumerate(chosen(yes, no)):
+            above = pltpu.roll(corner_before[first_part + part], LANES - (groups - 2), 1)
+            below = pltpu.roll(corner_after[first_part + part], groups - 2, 1)
+            own_rows = jnp.where(jnp.logical_and(inside, group == 0), above, own_rows)
+            whole.append(jnp.where(jnp.logical_and(inside, group == groups - 1), below, own_rows))
+        return whole
+
+    y_after = with_corners(column_first, column_second, 0, 1)
+    y_before = with_corners(column_second, column_first, len(parts), 0)
 
     def column(message, slot, lane_first, group=0):
         part, place = slot_place(slot, group, groups)
@@ -325,14 +326,12 @@
                 edge = column(y_before, number, 0, group)
             shifted[number, pl.ds(GUARD + 8 * group, 8), :] = shift_lanes(value, cy, edge)
 
-    for group in (0, 1, groups - 2, groups - 1):
+    for group in range(groups):
         first = GUARD + 8 * group
-        if group == 0:
-            solid_rows[0, pl.ds(first, LEVELS), :] = before[SOLID]
-            solid_rows[0, pl.ds(first + LEVELS, LEVELS), :] = before[SOLID]
-        elif group == groups - 1:
-            solid_rows[0, pl.ds(first, LEVELS), :] = after[SOLID]
-            solid_rows[0, pl.ds(first + LEVELS, LEVELS), :] = after[SOLID]
+        if group in (0, groups - 1):
+            halo = before[SOLID] if group == 0 else after[SOLID]
+            solid_rows[0, pl.ds(first, LEVELS), :] = halo
+            solid_rows[0, pl.ds(first + LEVELS, LEVELS), :] = halo
         else:
             solid_rows[0, pl.ds(first, 8), :] = solid_parts[(group - 1) * 8 // (LEVELS * TILE)]
         value = solid_rows[0, pl.ds(first, 8), :]
@@ -344,6 +343,15 @@
     row_flow[3, pl.ds(0, LEVELS), :] = before[SOLID]
     row_flow[3, pl.ds(LEVELS, LEVELS), :] = after[SOLID]
 
+    for group in (0, groups - 1):
+        first = GUARD + 8 * group
+        for slot in y_up + [SOLID]:
+            value = solid_rows[0, pl.ds(first, 8), :] if slot == SOLID else held[slot, pl.ds(first, 8), :]
+            insert_column(low, slot, group, groups, value, 0, 1)
+        for slot in y_down + [SOLID]:
+            value = solid_rows[0, pl.ds(first, 8), :] if slot == SOLID else held[slot, pl.ds(first, 8), :]
+            insert_column(high, slot, group, groups, value, LANES - 1, 0)
+
     def both_rows(field, index, shift):
         ends = [field[index, pl.ds(place + shift, LEVELS), :] for place in (near, far)]
         return jnp.concatenate(ends, axis=0)
@@ -398,9 +406,6 @@
     column_flow = [neighbours(FLOW + axis, 0) for axis in range(3)]
     column_results = collide(moved, column_flow, 1.0 - solid_columns[0])
 
-    def closed_at(first):
-        return lambda number: blocked[number - 1, pl.ds(first, 8), :] == 1
-
     def fluid_at(first):
         return 1.0 - solid_parts[first // (LEVELS * TILE)]
 
@@ -408,7 +413,7 @@
     flow = flow_blocks(velocity, 0, rows)
     for group in range(rows // 8):
         first = 8 * group
-        moved = gather_cells(held, shifted, own + first, closed_at(first))
+        moved = gather_cells(held, shifted, own + first, solid_rows)
         results = collide(moved, flow[group], fluid_at(first))
         for number in range(19):
             later[number, pl.ds(own + first, 8), :] = results[number]
@@ -430,25 +435,29 @@
     flow = flow_blocks(velocity, 1, rows)
     for group in range(rows // 8):
         first = 8 * group
-        moved = gather_cells(later, later_shifted, own + first, closed_at(first))
+        moved = gather_cells(later, later_shifted, own + first, solid_rows)
         drag_sum = drag_sum + drag_term(moved, flow[group], fluid_at(first))
     shared[...] = jnp.broadcast_to(jnp.sum(drag_sum), shared.shape)
 
 
-def second_step_kernel(later, later_shifted, velocity, blocked, solid, out):
+def second_step_kernel(later, later_shifted, solid_rows, velocity, out):
     rows = out.shape[1]
-    solid_parts = spread_solid(solid)
     flow = flow_blocks(velocity, 1, rows)
     for group in range(rows // 8):
-        first = 8 * group
-
-        def closed(number):
-            return blocked[number - 1, pl.ds(first, 8), :] == 1
-
-        moved = gather_cells(later, later_shifted, GUARD + 8 + first, closed)
-        results = collide(moved, flow[group], 1.0 - solid_parts[first // (LEVELS * TILE)])
+        first = GUARD + 8 + 8 * group
+        moved = gather_cells(later, later_shifted, first, solid_rows)
+        results = collide(moved, flow[group], 1.0 - solid_rows[0, pl.ds(first, 8), :])
         for number in range(19):
-            out[number, pl.ds(first, 8), :] = results[number]
+            out[number, pl.ds(8 * group, 8), :] = results[number]
+
+
+def sum_over(value, axis):
+    count = lax.axis_size(axis)
+    distance = 1
+    while distance < count:
+        value = value + lax.ppermute(value, axis, [(i, i ^ distance) for i in range(count)])
+        distance *= 2
+    return value
 
 
 def swap_pairs(first, second, axis):
@@ -467,66 +476,63 @@
     state = adjoint_in.reshape(19, rows, rows_y)
     flow = velocity.reshape(STEPS, 3, rows, rows_y)
     solid = solid_tiles.reshape(-1, solid_tiles.shape[2])
-    blocked = link_blocked.reshape(18, rows, rows_y)
 
     def shape_of(*sizes):
         return jax.ShapeDtypeStruct(sizes, jnp.float32)
 
     params = pltpu.CompilerParams(vmem_limit_bytes=16 * 1024 * 1024)
     anywhere = pl.BlockSpec(memory_space=pl.ANY)
-    row_sent = pl.pallas_call(
-        row_message_kernel,
-        out_shape=(shape_of(QUANTITIES, levels, rows_y),) * 2,
+    sent = pl.pallas_call(
+        message_kernel,
+        out_shape=(shape_of(QUANTITIES, levels, rows_y),) * 2 + (shape_of(parts, 8, rows_y),) * 2,
         in_specs=[anywhere] * 3,
-        out_specs=(vmem,) * 2,
+        out_specs=(vmem,) * 4,
         scratch_shapes=[
-            pltpu.VMEM((19, 8, rows_y), jnp.float32),
-            pltpu.VMEM((19, 8, rows_y), jnp.float32),
-            pltpu.VMEM((3, 16, rows_y), velocity.dtype),
-            pltpu.VMEM((3, 16, rows_y), velocity.dtype),
+            pltpu.VMEM(state.shape, jnp.float32),
+            pltpu.VMEM(flow.shape[1:], velocity.dtype),
             pltpu.VMEM(solid.shape, solid.dtype),
             pltpu.SemaphoreType.DMA((5,)),
         ],
         compiler_params=pltpu.CompilerParams(vmem_limit_bytes=60 * 1024 * 1024),
     )(state, flow, solid)
-    row_got = swap_pairs(*row_sent, "gx")
-    column_sent = pl.pallas_call(
-        column_message_kernel,
-        out_shape=(shape_of(parts, 8, rows_y),) * 2,
-        in_specs=[vmem] * 5,
-        out_specs=(vmem,) * 2,
-        scratch_shapes=[pltpu.VMEM((2, SECOND, 8, rows_y), jnp.float32)],
+    column_sent = sent[2:]
+    column_got = swap_pairs(*column_sent, "gy")
+    row_got = swap_pairs(*sent[:2], "gx")
+    corners = pl.pallas_call(
+        corner_kernel,
+        out_shape=shape_of(2 * parts, 8, rows_y),
+        in_specs=[vmem] * 2,
+        out_specs=vmem,
         compiler_params=params,
-    )(state, flow, solid, *row_got)
-    column_got = swap_pairs(*column_sent, "gy")
+    )(*column_got)
+    corner_got = swap_pairs(corners, corners, "gx")
     count = lax.axis_size("gx") * lax.axis_size("gy")
     field = pltpu.VMEM((19, padded, rows_y), jnp.float32)
-    later, later_shifted, own = pl.pallas_call(
+    later, later_shifted, solid_rows, own = pl.pallas_call(
         first_step_kernel,
-        out_shape=(shape_of(19, padded, rows_y),) * 2 + (shape_of(count, 1, rows_y),),
-        in_specs=[vmem] * 10,
-        out_specs=(vmem,) * 3,
-        scratch_shapes=[
-            field,
-            field,
-            pltpu.VMEM((4, 8, rows_y), jnp.float32),
-            pltpu.VMEM((3, padded, rows_y), jnp.float32),
-        ],
+        out_shape=(
+            shape_of(19, padded, rows_y),
+            shape_of(19, padded, rows_y),
+            shape_of(3, padded, rows_y),
+            shape_of(1, rows_y),
+        ),
+        in_specs=[vmem] * 11,
+        out_specs=(vmem,) * 4,
+        scratch_shapes=[field, field, pltpu.VMEM((4, 8, rows_y), jnp.float32)],
         compiler_params=params,
-    )(state, flow, blocked, solid, *row_got, *column_got, *column_sent)
-    shared = lax.all_to_all(own, ("gx", "gy"), split_axis=0, concat_axis=0, tiled=True)
+    )(state, flow, solid, *row_got, *column_got, *column_sent, *corner_got)
+    total = sum_over(sum_over(own, "gx"), "gy")
     result = pl.pallas_call(
         second_step_kernel,
         out_shape=shape_of(19, rows, rows_y),
-        in_specs=[vmem] * 5,
+        in_specs=[vmem] * 4,
         out_specs=vmem,
         compiler_params=params,
         cost_estimate=pl.CostEstimate(flops=4_000_000, bytes_accessed=4_000_000, transcendentals=0),
-    )(later, later_shifted, flow, blocked, solid)
+    )(later, later_shifted, solid_rows, flow)
     cell_count = rows * rows_y * count
     scale = drag_factor / math.sqrt(cell_count) * 3.0 / 36.0
-    total = jnp.sum(shared[:, 0, 0])
-    return (result.reshape(adjoint_in.shape), (-scale * total).reshape(1))
+    return (result.reshape(adjoint_in.shape), -scale * total[0, :1])
 
 
 def solution(mesh):

time: 32.8 us -> 36.5 us (1.11)
  waiting for transfers between devices: 11.2 us -> 19.2 us
  starting transfers between devices: 13 us -> 10.4 us
  other arithmetic: 0.63 us -> 0.02 us
  between operations: 2.47 us -> 1.9 us
    ppermute x0 -> x5, waiting for transfers between devices: none -> 13.5 us  [sum_over(): lax.ppermute(value, axis, [(i, i ^ distance) for i in range(count)])]
    all_to_all x1 -> x0, waiting for transfers between devices: 5.99 us -> none  [per_device(): lax.all_to_all(own, ('gx', 'gy'), split_axis=0, concat_axis=0, tiled=True)]
    all_to_all x1 -> x0, starting transfers between devices: 4.89 us -> none  [per_device(): lax.all_to_all(own, ('gx', 'gy'), split_axis=0, concat_axis=0, tiled=True)]
    ppermute x0 -> x5, starting transfers between devices: none -> 1.56 us  [sum_over(): lax.ppermute(value, axis, [(i, i ^ distance) for i in range(count)])]
    ppermute x2 -> x3, starting transfers between devices: 1.91 us -> 2.63 us  [swap_pairs(): lax.ppermute(first, axis, inside)]
    reduce_sum x1 -> x0, other arithmetic: 0.63 us -> none  [per_device(): total = jnp.sum(shared[:, 0, 0])]
    ppermute x2 -> x3, waiting for transfers between devices: 5.22 us -> 5.66 us  [swap_pairs(): lax.ppermute(second, axis, across)]
    pallas_call x1, Pallas kernels: 1.85 us -> 1.44 us  [per_device(): pl.pallas_call(first_step_kernel, out_shape=(shape_of(19, padded, rows_y)...]
  transfers between devices with their start and end apart: 5 -> 11, of which waited for: 3 -> 7; matrix products, arithmetic and copies ran while one was open for 0% -> 0% of each run, Pallas kernels for 3% -> 3%
where the time goes in v6:
time: 36.5 us; the launch traced here: 36.4 us
  waiting for transfers between devices  19.2 us (53%)
  starting transfers between devices  10.4 us (28%)
  Pallas kernels  4.85 us (13%)
  between operations  1.9 us (5%)
    ppermute x5, waiting for transfers between devices, sum_over(): lax.ppermute(value, axis, [(i, i ^ distance) for i in range(count)])  13.5 us
    ppermute x3, starting transfers between devices, swap_pairs(): lax.ppermute(second, axis, across)  6.22 us
    ppermute x3, waiting for transfers between devices, swap_pairs(): lax.ppermute(second, axis, across)  5.66 us
    ppermute x3, starting transfers between devices, swap_pairs(): lax.ppermute(first, axis, inside)  2.63 us
    pallas_call x1, Pallas kernels, per_device(): pl.pallas_call(message_kernel, out_shape=(shape_of(QUANTITIES, levels, ro...  2.26 us
    ppermute x5, starting transfers between devices, sum_over(): lax.ppermute(value, axis, [(i, i ^ distance) for i in range(count)])  1.56 us
    pallas_call x1, Pallas kernels, per_device(): pl.pallas_call(first_step_kernel, out_shape=(shape_of(19, padded, rows_y)...  1.44 us
    pallas_call x1, Pallas kernels, per_device(): pl.pallas_call(second_step_kernel, out_shape=shape_of(19, rows, rows_y),...  1.15 us
  transfers between devices with their start and end apart: 11, of which 7 were waited for; matrix products, arithmetic and copies ran while one was open for 0% of the time, Pallas kernels for 3%

profile of v6, /device:TPU:0, one launch (start us, length us, event | category | flops | bytes accessed | tf_op | source)
XLA Modules:
  0.0 36.4 jit_solution(16548302359441593553)
XLA Ops:
  0.6 0.0 copy-start
  0.6 0.0 copy-start.1
  0.6 2.3 %shard_map.50 = (f32[28,4,128]{2,1,0:T(4,128)}, f32[28,4,128]{2,1,0:T(4,128)}, f32[3,8,128]{2,1,0:T(8,128)}, f32[3,8,128]{2,1,0:T(8,128)}) custom-call(f32[19,64,128]{2,1,0:T(8,128)} %bitcast.6, bf16[2,3,64,128]{3,2,1,0:T(8,128)(2,1)} %bitcast.8, s32[16,32]{1,0:T(8,128)} %bitcast.11), custom_call_target="tpu_custom_call" | custom-call | tf_op jit(solution)/shard_map/pallas_call | solution.py:485
  2.9 0.5 %collective-permute-start = (f32[28,4,128]{2,1,0:T(4,128)}, f32[28,4,128]{2,1,0:T(4,128)S(1)}, u32[]{:S(2)}, u32[]{:S(2)}) collective-permute-start(f32[28,4,128]{2,1,0:T(4,128)} %get-tuple-element.10), channel_id=1, source_target_pairs={{0,8},{8,0},{16,24},{24,16},{1,9},{9,1},{17,25},{25,17},{2,10},{10... | collective-permute-start | bytes 172040 | tf_op jit(solution)/shard_map/ppermute | solution.py:467
  3.4 2.6 %collective-permute-start.1 = (f32[28,4,128]{2,1,0:T(4,128)}, f32[28,4,128]{2,1,0:T(4,128)S(1)}, u32[]{:S(2)}, u32[]{:S(2)}) collective-permute-start(f32[28,4,128]{2,1,0:T(4,128)} %get-tuple-element.11), channel_id=1, source_target_pairs={{0,24},{8,16},{16,8},{24,0},{1,25},{9,17},{17,9},{25,1},{2,26},{10... | collective-permute-start | bytes 172040 | tf_op jit(solution)/shard_map/ppermute | solution.py:467
  6.1 1.5 %collective-permute-start.2 = (f32[3,8,128]{2,1,0:T(8,128)}, f32[3,8,128]{2,1,0:T(8,128)S(1)}, u32[]{:S(2)}, u32[]{:S(2)}) collective-permute-start(f32[3,8,128]{2,1,0:T(8,128)} %get-tuple-element.12.sent_first), channel_id=1, source_target_pairs={{0,1},{1,0},{2,3},{3,2},{4,5},{5,4},{6,7},{7,6},{8,9},{9,8},{10,11... | collective-permute-start | bytes 36872 | tf_op jit(solution)/shard_map/ppermute | solution.py:467
  7.6 3.6 %collective-permute-start.3 = (f32[3,8,128]{2,1,0:T(8,128)}, f32[3,8,128]{2,1,0:T(8,128)S(1)}, u32[]{:S(2)}, u32[]{:S(2)}) collective-permute-start(f32[3,8,128]{2,1,0:T(8,128)} %get-tuple-element.13.sent_second), channel_id=1, source_target_pairs={{0,7},{1,2},{2,1},{3,4},{4,3},{5,6},{6,5},{7,0},{8,15},{9,10},{10,... | collective-permute-start | bytes 36872 | tf_op jit(solution)/shard_map/ppermute | solution.py:467
  11.1 0.0 collective-permute-done.2.column_first
  11.2 3.0 %collective-permute-done.3.column_second = f32[3,8,128]{2,1,0:T(8,128)S(1)} collective-permute-done((f32[3,8,128]{2,1,0:T(8,128)}, f32[3,8,128]{2,1,0:T(8,128)S(1)}, u32[]{:S(2)}, u32[]{:S(2)}) %collective-permute-start.3) | collective-permute-done | bytes 12320 | tf_op jit(solution)/shard_map/ppermute | solution.py:467
  14.2 0.0 collective-permute-start.5
  14.2 0.6 %collective-permute-start.4 = (f32[6,8,128]{2,1,0:T(8,128)S(1)}, f32[6,8,128]{2,1,0:T(8,128)S(1)}, u32[]{:S(2)}, u32[]{:S(2)}) collective-permute-start(f32[6,8,128]{2,1,0:T(8,128)S(1)} %shard_map.51), channel_id=1, source_target_pairs={{0,8},{8,0},{16,24},{24,16},{1,9},{9,1},{17,25},{25,17},{2,10},{10... | collective-permute-start | bytes 73736 | tf_op jit(solution)/shard_map/ppermute | solution.py:467
  14.8 2.6 %collective-permute-done.5.corner_second = f32[6,8,128]{2,1,0:T(8,128)S(1)} collective-permute-done((f32[6,8,128]{2,1,0:T(8,128)S(1)}, f32[6,8,128]{2,1,0:T(8,128)S(1)}, u32[]{:S(2)}, u32[]{:S(2)}) %collective-permute-start.5) | collective-permute-done | bytes 24608 | tf_op jit(solution)/shard_map/ppermute | solution.py:467
  17.4 0.0 collective-permute-done.4.corner_first
  17.4 0.0 collective-permute-done.row_first
  17.4 0.0 collective-permute-done.1.row_second
  17.4 0.0 copy-done
  17.5 0.0 copy-done.1
  17.5 0.0 copy-done.2
  17.5 0.0 copy-done.3
  17.5 0.0 copy-done.4
  17.5 1.4 %shard_map.52 = (f32[19,96,128]{2,1,0:T(8,128)S(1)}, f32[19,96,128]{2,1,0:T(8,128)S(1)}, f32[3,96,128]{2,1,0:T(8,128)S(1)}, f32[1,128]{1,0:T(1,128)S(1)}) custom-call(f32[19,64,128]{2,1,0:T(8,128)S(1)} %bitcast.7, bf16[2,3,64,128]{3,2,1,0:T(8,128)(2,1)S(1)} %bitcast.9, s32[16,32]{1,0:T(8,128)S(1)} %bitcast.12, ...), custom_call_target="tpu_custom_call" | custom-call | tf_op jit(solution)/shard_map/pallas_call | solution.py:511
  18.9 0.1 collective-permute-start.6
  19.0 1.1 %collective-permute-done.6 = f32[1,128]{1,0:T(1,128)S(1)} collective-permute-done((f32[1,128]{1,0:T(1,128)S(1)}, f32[1,128]{1,0:T(1,128)S(1)}, u32[]{:S(2)}, u32[]{:S(2)}) %collective-permute-start.6) | collective-permute-done | bytes 544 | tf_op jit(solution)/shard_map/ppermute | solution.py:458
  20.1 0.7 %collective-permute-start.7 = (f32[1,128]{1,0:T(1,128)S(1)}, f32[1,128]{1,0:T(1,128)S(1)}, u32[]{:S(2)}, u32[]{:S(2)}) collective-permute-start(f32[1,128]{1,0:T(1,128)S(1)} %add.15), channel_id=1, source_target_pairs={{0,16},{8,24},{16,0},{24,8},{1,17},{9,25},{17,1},{25,9},{2,18},{10... | collective-permute-start | bytes 1544 | tf_op jit(solution)/shard_map/ppermute | solution.py:458
  20.8 2.8 %collective-permute-done.7 = f32[1,128]{1,0:T(1,128)S(1)} collective-permute-done((f32[1,128]{1,0:T(1,128)S(1)}, f32[1,128]{1,0:T(1,128)S(1)}, u32[]{:S(2)}, u32[]{:S(2)}) %collective-permute-start.7) | collective-permute-done | bytes 544 | tf_op jit(solution)/shard_map/ppermute | solution.py:458
  23.7 0.0 collective-permute-start.8
  23.7 3.5 %collective-permute-done.8 = f32[1,128]{1,0:T(1,128)S(1)} collective-permute-done((f32[1,128]{1,0:T(1,128)S(1)}, f32[1,128]{1,0:T(1,128)S(1)}, u32[]{:S(2)}, u32[]{:S(2)}) %collective-permute-start.8) | collective-permute-done | bytes 544 | tf_op jit(solution)/shard_map/ppermute | solution.py:458
  27.2 0.0 collective-permute-start.9
  27.2 3.5 %collective-permute-done.9 = f32[1,128]{1,0:T(1,128)S(1)} collective-permute-done((f32[1,128]{1,0:T(1,128)S(1)}, f32[1,128]{1,0:T(1,128)S(1)}, u32[]{:S(2)}, u32[]{:S(2)}) %collective-permute-start.9) | collective-permute-done | bytes 544 | tf_op jit(solution)/shard_map/ppermute | solution.py:458
  30.8 0.8 %collective-permute-start.10 = (f32[1,128]{1,0:T(1,128)S(1)}, f32[1,128]{1,0:T(1,128)S(1)}, u32[]{:S(2)}, u32[]{:S(2)}) collective-permute-start(f32[1,128]{1,0:T(1,128)S(1)} %add.18), channel_id=1, source_target_pairs={{0,4},{1,5},{2,6},{3,7},{4,0},{5,1},{6,2},{7,3},{8,12},{9,13},{10,... | collective-permute-start | bytes 1544 | tf_op jit(solution)/shard_map/ppermute | solution.py:458
  31.6 1.1 %shard_map.53 = f32[19,64,128]{2,1,0:T(8,128)} custom-call(f32[19,96,128]{2,1,0:T(8,128)S(1)} %get-tuple-element.14.later, f32[19,96,128]{2,1,0:T(8,128)S(1)} %get-tuple-element.15.later_shifted, f32[3,96,128]{2,1,0:T(8,128)S(1)} %get-tuple-element.16.solid_rows, bf16[2,3,64,128]{3,2,1,0:T(8,128)(2,1)S(1)} %bitcast.10), custom_call_target="tpu_custom_call" | custom-call | flops 4000000 | bytes 4000000 | tf_op jit(solution)/shard_map/pallas_call | solution.py:525
  32.7 2.5 %collective-permute-done.10 = f32[1,128]{1,0:T(1,128)S(1)} collective-permute-done((f32[1,128]{1,0:T(1,128)S(1)}, f32[1,128]{1,0:T(1,128)S(1)}, u32[]{:S(2)}, u32[]{:S(2)}) %collective-permute-start.10) | collective-permute-done | bytes 544 | tf_op jit(solution)/shard_map/ppermute | solution.py:458
  (9 shorter events, 0.0 us)
Async XLA Ops:
  0.6 16.8 %copy-start = (f32[19,16,4,128]{3,2,1,0:T(4,128)S(1)}, f32[19,16,4,128]{3,2,1,0:T(4,128)}, u32[]{:S(2)}) copy-start(f32[19,16,4,128]{3,2,1,0:T(4,128)} %param.4) | copy-start | bytes 1867780
  0.6 16.8 %copy-start.1 = (bf16[2,3,16,4,128]{4,3,2,1,0:T(4,128)(2,1)S(1)}, bf16[2,3,16,4,128]{4,3,2,1,0:T(4,128)(2,1)}, u32[]{:S(2)}) copy-start(bf16[2,3,16,4,128]{4,3,2,1,0:T(4,128)(2,1)} %param.5) | copy-start | bytes 294916
  2.9 14.5 %collective-permute-start = (f32[28,4,128]{2,1,0:T(4,128)}, f32[28,4,128]{2,1,0:T(4,128)S(1)}, u32[]{:S(2)}, u32[]{:S(2)}) collective-permute-start(f32[28,4,128]{2,1,0:T(4,128)} %get-tuple-element.10), channel_id=1, source_target_pairs={{0,8},{8,0},{16,24},{24,16},{1,9},{9,1},{17,25},{25,17},{2,10},{10... | collective-permute-start | bytes 172040 | tf_op jit(solution)/shard_map/ppermute | solution.py:467
  3.4 14.0 %collective-permute-start.1 = (f32[28,4,128]{2,1,0:T(4,128)}, f32[28,4,128]{2,1,0:T(4,128)S(1)}, u32[]{:S(2)}, u32[]{:S(2)}) collective-permute-start(f32[28,4,128]{2,1,0:T(4,128)} %get-tuple-element.11), channel_id=1, source_target_pairs={{0,24},{8,16},{16,8},{24,0},{1,25},{9,17},{17,9},{25,1},{2,26},{10... | collective-permute-start | bytes 172040 | tf_op jit(solution)/shard_map/ppermute | solution.py:467
  6.1 5.1 %collective-permute-start.2 = (f32[3,8,128]{2,1,0:T(8,128)}, f32[3,8,128]{2,1,0:T(8,128)S(1)}, u32[]{:S(2)}, u32[]{:S(2)}) collective-permute-start(f32[3,8,128]{2,1,0:T(8,128)} %get-tuple-element.12.sent_first), channel_id=1, source_target_pairs={{0,1},{1,0},{2,3},{3,2},{4,5},{5,4},{6,7},{7,6},{8,9},{9,8},{10,11... | collective-permute-start | bytes 36872 | tf_op jit(solution)/shard_map/ppermute | solution.py:467
  7.6 9.9 %copy-start.2 = (s32[4,4,32]{2,1,0:T(4,128)S(1)}, s32[4,4,32]{2,1,0:T(4,128)}, u32[]{:S(2)}) copy-start(s32[4,4,32]{2,1,0:T(4,128)} %param.6) | copy-start | bytes 6148
  7.6 9.9 %copy-start.3 = (f32[3,8,128]{2,1,0:T(8,128)S(1)}, f32[3,8,128]{2,1,0:T(8,128)}, u32[]{:S(2)}) copy-start(f32[3,8,128]{2,1,0:T(8,128)} %get-tuple-element.12.sent_first) | copy-start | bytes 36868
  7.6 9.9 %copy-start.4 = (f32[3,8,128]{2,1,0:T(8,128)S(1)}, f32[3,8,128]{2,1,0:T(8,128)}, u32[]{:S(2)}) copy-start(f32[3,8,128]{2,1,0:T(8,128)} %get-tuple-element.13.sent_second) | copy-start | bytes 36868
  7.6 6.6 %collective-permute-start.3 = (f32[3,8,128]{2,1,0:T(8,128)}, f32[3,8,128]{2,1,0:T(8,128)S(1)}, u32[]{:S(2)}, u32[]{:S(2)}) collective-permute-start(f32[3,8,128]{2,1,0:T(8,128)} %get-tuple-element.13.sent_second), channel_id=1, source_target_pairs={{0,7},{1,2},{2,1},{3,4},{4,3},{5,6},{6,5},{7,0},{8,15},{9,10},{10,... | collective-permute-start | bytes 36872 | tf_op jit(solution)/shard_map/ppermute | solution.py:467
  14.2 3.3 %collective-permute-start.5 = (f32[6,8,128]{2,1,0:T(8,128)S(1)}, f32[6,8,128]{2,1,0:T(8,128)S(1)}, u32[]{:S(2)}, u32[]{:S(2)}) collective-permute-start(f32[6,8,128]{2,1,0:T(8,128)S(1)} %shard_map.51), channel_id=1, source_target_pairs={{0,24},{8,16},{16,8},{24,0},{1,25},{9,17},{17,9},{25,1},{2,26},{10... | collective-permute-start | bytes 73736 | tf_op jit(solution)/shard_map/ppermute | solution.py:467
  14.2 3.2 %collective-permute-start.4 = (f32[6,8,128]{2,1,0:T(8,128)S(1)}, f32[6,8,128]{2,1,0:T(8,128)S(1)}, u32[]{:S(2)}, u32[]{:S(2)}) collective-permute-start(f32[6,8,128]{2,1,0:T(8,128)S(1)} %shard_map.51), channel_id=1, source_target_pairs={{0,8},{8,0},{16,24},{24,16},{1,9},{9,1},{17,25},{25,17},{2,10},{10... | collective-permute-start | bytes 73736 | tf_op jit(solution)/shard_map/ppermute | solution.py:467
  18.9 1.2 %collective-permute-start.6 = (f32[1,128]{1,0:T(1,128)S(1)}, f32[1,128]{1,0:T(1,128)S(1)}, u32[]{:S(2)}, u32[]{:S(2)}) collective-permute-start(f32[1,128]{1,0:T(1,128)S(1)} %get-tuple-element.17), channel_id=1, source_target_pairs={{0,8},{8,0},{16,24},{24,16},{1,9},{9,1},{17,25},{25,17},{2,10},{10... | collective-permute-start | bytes 1544 | tf_op jit(solution)/shard_map/ppermute | solution.py:458
  20.1 3.5 %collective-permute-start.7 = (f32[1,128]{1,0:T(1,128)S(1)}, f32[1,128]{1,0:T(1,128)S(1)}, u32[]{:S(2)}, u32[]{:S(2)}) collective-permute-start(f32[1,128]{1,0:T(1,128)S(1)} %add.15), channel_id=1, source_target_pairs={{0,16},{8,24},{16,0},{24,8},{1,17},{9,25},{17,1},{25,9},{2,18},{10... | collective-permute-start | bytes 1544 | tf_op jit(solution)/shard_map/ppermute | solution.py:458
  23.7 3.5 %collective-permute-start.8 = (f32[1,128]{1,0:T(1,128)S(1)}, f32[1,128]{1,0:T(1,128)S(1)}, u32[]{:S(2)}, u32[]{:S(2)}) collective-permute-start(f32[1,128]{1,0:T(1,128)S(1)} %add.16), channel_id=1, source_target_pairs={{0,1},{1,0},{2,3},{3,2},{4,5},{5,4},{6,7},{7,6},{8,9},{9,8},{10,11... | collective-permute-start | bytes 1544 | tf_op jit(solution)/shard_map/ppermute | solution.py:458
  27.2 3.5 %collective-permute-start.9 = (f32[1,128]{1,0:T(1,128)S(1)}, f32[1,128]{1,0:T(1,128)S(1)}, u32[]{:S(2)}, u32[]{:S(2)}) collective-permute-start(f32[1,128]{1,0:T(1,128)S(1)} %add.17), channel_id=1, source_target_pairs={{0,2},{1,3},{2,0},{3,1},{4,6},{5,7},{6,4},{7,5},{8,10},{9,11},{10,... | collective-permute-start | bytes 1544 | tf_op jit(solution)/shard_map/ppermute | solution.py:458
  30.8 4.4 %collective-permute-start.10 = (f32[1,128]{1,0:T(1,128)S(1)}, f32[1,128]{1,0:T(1,128)S(1)}, u32[]{:S(2)}, u32[]{:S(2)}) collective-permute-start(f32[1,128]{1,0:T(1,128)S(1)} %add.18), channel_id=1, source_target_pairs={{0,4},{1,5},{2,6},{3,7},{4,0},{5,1},{6,2},{7,3},{8,12},{9,13},{10,... | collective-permute-start | bytes 1544 | tf_op jit(solution)/shard_map/ppermute | solution.py:458

commit v7 on v6

--- a/solution.py
+++ b/solution.py
@@ -1,3 +1,4 @@
+import functools
 import math
 
 import jax
@@ -106,79 +107,95 @@
     parts[part] = jnp.where(lane == place + ahead, turned, parts[part])
 
 
-def message_kernel(
-    state, velocity, solid, row_first, row_second, column_first, column_second, cells, flow, tiles, arrived
+def row_message_kernel(
+    state, velocity, solid, row_first, row_second, held, flow, tiles, arrived
 ):
     rows = state.shape[1]
-    groups = rows // 8 + 2
-    chunks = ((0, 7), (7, 6), (13, 6))
+    own = pl.ds(GUARD + 8, rows)
     copies = [
-        pltpu.make_async_copy(velocity.at[0], flow, arrived.at[0]),
-        pltpu.make_async_copy(solid, tiles, arrived.at[1]),
+        pltpu.make_async_copy(state, held.at[:, own, :], arrived.at[0]),
+        pltpu.make_async_copy(velocity, flow, arrived.at[1]),
+        pltpu.make_async_copy(solid, tiles, arrived.at[2]),
     ]
-    for number, (first, count) in enumerate(chunks):
-        part = pl.ds(first, count)
-        copies.append(pltpu.make_async_copy(state.at[part], cells.at[part], arrived.at[2 + number]))
     for copy in copies:
         copy.start()
-    x_even, y_even = on_even("gx"), on_even("gy")
+    for copy in copies:
+        copy.wait()
+    even = on_even("gx")
+    low_row, high_row = GUARD + 8, GUARD + 8 + rows - LEVELS
 
     def put(slot, low, high):
-        row_first[slot] = jnp.where(x_even, high, low)
-        row_second[slot] = jnp.where(x_even, low, high)
-
-    count = column_first.shape[0]
-    low_parts = [jnp.zeros((8, LANES), jnp.float32) for _ in range(count)]
-    high_parts = [jnp.zeros((8, LANES), jnp.float32) for _ in range(count)]
-
-    def pack(slot, group, value):
-        part, place = slot_place(slot, group, groups)
-        lane = lane_index()
-        turned = pltpu.roll(value, (place + 1) % LANES, 1)
-        low_parts[part] = jnp.where(lane == place + 1, turned, low_parts[part])
-        high_parts[part] = jnp.where(lane == place, turned, high_parts[part])
-        if slot in y_up:
-            insert_column(low_parts, SECOND + y_up.index(slot), group, groups, value, 1, 1)
-        if slot in y_down:
-            insert_column(high_parts, SECOND + y_down.index(slot), group, groups, value, LANES - 2, 0)
-
-    copies[0].wait()
+        row_first[slot] = jnp.where(even, high, low)
+        row_second[slot] = jnp.where(even, low, high)
+
+    for number in range(19):
+        put(number, held[number, pl.ds(low_row, LEVELS), :], held[number, pl.ds(high_row, LEVELS), :])
     for axis in range(3):
-        blocks = []
-        for pair in range(rows // 16):
-            both = flow[axis, pl.ds(16 * pair, 16), :].astype(jnp.float32)
-            blocks += [both[:8], both[8:]]
-        for group, value in enumerate(blocks):
-            pack(FLOW + axis, group + 1, value)
-        put(FLOW + axis, blocks[0][:LEVELS], blocks[-1][LEVELS:])
-    copies[1].wait()
+        low = flow[0, axis, pl.ds(0, 16), :].astype(jnp.float32)
+        high = flow[0, axis, pl.ds(rows - 16, 16), :].astype(jnp.float32)
+        put(FLOW + axis, low[:LEVELS], high[16 - LEVELS :])
     solid_parts = spread_solid(tiles)
-    for group in range(rows // 8):
-        pack(SOLID, group + 1, solid_parts[8 * group // (LEVELS * TILE)])
     put(SOLID, solid_parts[0][:LEVELS], solid_parts[-1][:LEVELS])
-    for copy, (first, count) in zip(copies[2:], chunks):
-        copy.wait()
-        for number in range(first, first + count):
-            for group in range(rows // 8):
-                pack(number, group + 1, cells[number, pl.ds(8 * group, 8), :])
-            put(number, cells[number, pl.ds(0, LEVELS), :], cells[number, pl.ds(rows - LEVELS, LEVELS), :])
     for slot in range(5):
         put(
             SECOND + slot,
-            cells[x_up[slot], pl.ds(LEVELS, LEVELS), :],
-            cells[x_down[slot], pl.ds(rows - 2 * LEVELS, LEVELS), :],
+            held[x_up[slot], pl.ds(low_row + LEVELS, LEVELS), :],
+            held[x_down[slot], pl.ds(high_row - LEVELS, LEVELS), :],
         )
-    for part in range(len(low_parts)):
-        column_first[part] = jnp.where(y_even, high_parts[part], low_parts[part])
-        column_second[part] = jnp.where(y_even, low_parts[part], high_parts[part])
-
-
-def corner_kernel(column_first, column_second, out):
+
+
+def pack_columns(parts, slot, group, groups, value):
+    low_parts, high_parts = parts
+    part, place = slot_place(slot, group, groups)
+    lane = lane_index()
+    turned = pltpu.roll(value, (place + 1) % LANES, 1)
+    low_parts[part] = jnp.where(lane == place + 1, turned, low_parts[part])
+    high_parts[part] = jnp.where(lane == place, turned, high_parts[part])
+    if slot in y_up:
+        insert_column(low_parts, SECOND + y_up.index(slot), group, groups, value, 1, 1)
+    if slot in y_down:
+        insert_column(high_parts, SECOND + y_down.index(slot), group, groups, value, LANES - 2, 0)
+
+
+def own_columns_kernel(held, velocity, solid, low, high):
+    rows = velocity.shape[2]
+    groups = rows // 8 + 2
+    solid_parts = spread_solid(solid)
+    flow = flow_blocks(velocity, 0, rows)
+    parts = [[jnp.zeros((8, LANES), jnp.float32) for _ in range(low.shape[0])] for _ in range(2)]
+    for group in range(1, groups - 1):
+        for slot in range(19):
+            pack_columns(parts, slot, group, groups, held[slot, pl.ds(GUARD + 8 * group, 8), :])
+        for axis in range(3):
+            pack_columns(parts, FLOW + axis, group, groups, flow[group - 1][axis])
+        pack_columns(parts, SOLID, group, groups, solid_parts[(group - 1) * 8 // (LEVELS * TILE)])
+    for part in range(low.shape[0]):
+        low[part] = parts[0][part]
+        high[part] = parts[1][part]
+
+
+def halo_columns_kernel(groups, own_low, own_high, row_first, row_second, first_out, second_out, ends):
+    count = own_low.shape[0]
+    even = on_even("gx")
+    after, before = Chosen(even, row_first, row_second), Chosen(even, row_second, row_first)
+    parts = [[own_low[part] for part in range(count)], [own_high[part] for part in range(count)]]
+    for slot in range(SECOND):
+        ends[0, slot, pl.ds(LEVELS, LEVELS), :] = before[slot]
+        ends[1, slot, pl.ds(0, LEVELS), :] = after[slot]
+        if slot == SOLID:
+            low_second, high_second = SOLID, SOLID
+        else:
+            low_second = SECOND + x_down.index(slot) if slot in x_down else None
+            high_second = SECOND + x_up.index(slot) if slot in x_up else None
+        blank = jnp.zeros((LEVELS, LANES), jnp.float32)
+        ends[0, slot, pl.ds(0, LEVELS), :] = blank if low_second is None else before[low_second]
+        ends[1, slot, pl.ds(LEVELS, LEVELS), :] = blank if high_second is None else after[high_second]
+        pack_columns(parts, slot, 0, groups, ends[0, slot])
+        pack_columns(parts, slot, groups - 1, groups, ends[1, slot])
     even = on_even("gy")
-    count = column_first.shape[0]
     for part in range(count):
-        out[part] = jnp.where(even, column_first[part], column_second[part])
-        out[count + part] = jnp.where(even, column_second[part], column_first[part])
+        first_out[part] = jnp.where(even, parts[1][part], parts[0][part])
+        second_out[part] = jnp.where(even, parts[0][part], parts[1][part])
 
 
 def collide(moved, flow, fluid):
@@ -265,16 +282,13 @@
     return fluid * sum(speed * part for speed, part in zip(flow, momentum(moved)))
 
 
-def first_step_kernel(
-    state, velocity, solid, row_first, row_second, column_first, column_second,
-    sent_first, sent_second, corner_first, corner_second,
-    later, later_shifted, solid_rows, shared, held, shifted, row_flow,
+def main_kernel(
+    own_held, velocity, solid, row_first, row_second, column_first, column_second,
+    sent_first, sent_second, out, shared, held, shifted, later, solid_rows, row_flow,
 ):
-    rows = state.shape[1]
+    rows = velocity.shape[2]
     even = on_even("gx")
     after, before = Chosen(even, row_first, row_second), Chosen(even, row_second, row_first)
-    corner_after = Chosen(even, corner_first, corner_second)
-    corner_before = Chosen(even, corner_second, corner_first)
     even = on_even("gy")
     parts = range(column_first.shape[0])
 
@@ -282,26 +296,13 @@
         return [jnp.where(even, yes[part], no[part]) for part in parts]
 
     low, high = chosen(sent_second, sent_first), chosen(sent_first, sent_second)
+    y_after, y_before = chosen(column_first, column_second), chosen(column_second, column_first)
     groups = rows // 8 + 2
     own = GUARD + 8
     near, far = own - LEVELS, own + rows
     lane = lane_index()
     solid_parts = spread_solid(solid)
 
-    def with_corners(yes, no, first_part, ahead):
-        whole = []
-        group = lax.rem(lane + groups - ahead, groups)
-        inside = jnp.logical_and(lane >= ahead, lane < LANES // groups * groups + ahead)
-        for part, own_rows in enumerate(chosen(yes, no)):
-            above = pltpu.roll(corner_before[first_part + part], LANES - (groups - 2), 1)
-            below = pltpu.roll(corner_after[first_part + part], groups - 2, 1)
-            own_rows = jnp.where(jnp.logical_and(inside, group == 0), above, own_rows)
-            whole.append(jnp.where(jnp.logical_and(inside, group == groups - 1), below, own_rows))
-        return whole
-
-    y_after = with_corners(column_first, column_second, 0, 1)
-    y_before = with_corners(column_second, column_first, len(parts), 0)
-
     def column(message, slot, lane_first, group=0):
         part, place = slot_place(slot, group, groups)
         ahead = 1 if message is y_after or message is low else 0
@@ -309,7 +310,8 @@
 
     for number in range(19):
         for group in range(rows // 8):
-            held[number, pl.ds(own + 8 * group, 8), :] = state[number, pl.ds(8 * group, 8), :]
+            there = pl.ds(own + 8 * group, 8)
+            held[number, there, :] = own_held[number, there, :]
         held[number, pl.ds(near, LEVELS), :] = before[number]
         held[number, pl.ds(far, LEVELS), :] = after[number]
         if number in x_down:
@@ -342,15 +344,6 @@
         row_flow[axis, pl.ds(LEVELS, LEVELS), :] = after[FLOW + axis]
     row_flow[3, pl.ds(0, LEVELS), :] = before[SOLID]
     row_flow[3, pl.ds(LEVELS, LEVELS), :] = after[SOLID]
-
-    for group in (0, groups - 1):
-        first = GUARD + 8 * group
-        for slot in y_up + [SOLID]:
-            value = solid_rows[0, pl.ds(first, 8), :] if slot == SOLID else held[slot, pl.ds(first, 8), :]
-            insert_column(low, slot, group, groups, value, 0, 1)
-        for slot in y_down + [SOLID]:
-            value = solid_rows[0, pl.ds(first, 8), :] if slot == SOLID else held[slot, pl.ds(first, 8), :]
-            insert_column(high, slot, group, groups, value, LANES - 1, 0)
 
     def both_rows(field, index, shift):
         ends = [field[index, pl.ds(place + shift, LEVELS), :] for place in (near, far)]
@@ -430,34 +423,17 @@
                 edge = pltpu.roll(column_results[number], (LANES - 1 - AFTER_LANE - group) % LANES, 1)
             else:
                 edge = pltpu.roll(column_results[number], (-BEFORE_LANE - group) % LANES, 1)
-            later_shifted[number, pl.ds(GUARD + 8 * group, 8), :] = shift_lanes(value, cy, edge)
+            shifted[number, pl.ds(GUARD + 8 * group, 8), :] = shift_lanes(value, cy, edge)
 
     flow = flow_blocks(velocity, 1, rows)
     for group in range(rows // 8):
         first = 8 * group
-        moved = gather_cells(later, later_shifted, own + first, solid_rows)
+        moved = gather_cells(later, shifted, own + first, solid_rows)
+        results = collide(moved, flow[group], fluid_at(first))
+        for number in range(19):
+            out[number, pl.ds(first, 8), :] = results[number]
         drag_sum = drag_sum + drag_term(moved, flow[group], fluid_at(first))
     shared[...] = jnp.broadcast_to(jnp.sum(drag_sum), shared.shape)
-
-
-def second_step_kernel(later, later_shifted, solid_rows, velocity, out):
-    rows = out.shape[1]
-    flow = flow_blocks(velocity, 1, rows)
-    for group in range(rows // 8):
-        first = GUARD + 8 + 8 * group
-        moved = gather_cells(later, later_shifted, first, solid_rows)
-        results = collide(moved, flow[group], 1.0 - solid_rows[0, pl.ds(first, 8), :])
-        for number in range(19):
-            out[number, pl.ds(8 * group, 8), :] = results[number]
-
-
-def sum_over(value, axis):
-    count = lax.axis_size(axis)
-    distance = 1
-    while distance < count:
-        value = value + lax.ppermute(value, axis, [(i, i ^ distance) for i in range(count)])
-        distance *= 2
-    return value
 
 
 def swap_pairs(first, second, axis):
@@ -482,57 +458,59 @@
 
     params = pltpu.CompilerParams(vmem_limit_bytes=16 * 1024 * 1024)
     anywhere = pl.BlockSpec(memory_space=pl.ANY)
-    sent = pl.pallas_call(
-        message_kernel,
-        out_shape=(shape_of(QUANTITIES, levels, rows_y),) * 2 + (shape_of(parts, 8, rows_y),) * 2,
+    *row_sent, held, flow, tiles = pl.pallas_call(
+        row_message_kernel,
+        out_shape=(
+            pltpu.VMEM((QUANTITIES, levels, rows_y), jnp.float32),
+            pltpu.VMEM((QUANTITIES, levels, rows_y), jnp.float32),
+            pltpu.VMEM((19, padded, rows_y), jnp.float32),
+            pltpu.VMEM(flow.shape, flow.dtype),
+            pltpu.VMEM(solid.shape, solid.dtype),
+        ),
         in_specs=[anywhere] * 3,
-        out_specs=(vmem,) * 4,
-        scratch_shapes=[
-            pltpu.VMEM(state.shape, jnp.float32),
-            pltpu.VMEM(flow.shape[1:], velocity.dtype),
-            pltpu.VMEM(solid.shape, solid.dtype),
-            pltpu.SemaphoreType.DMA((5,)),
-        ],
-        compiler_params=pltpu.CompilerParams(vmem_limit_bytes=60 * 1024 * 1024),
-    )(state, flow, solid)
-    column_sent = sent[2:]
+        out_specs=(vmem,) * 5,
+        scratch_shapes=[pltpu.SemaphoreType.DMA((3,))],
+        compiler_params=params,
+    )(*(pltpu.with_memory_space_constraint(value, pltpu.HBM) for value in (state, flow, solid)))
+    row_got = swap_pairs(*row_sent, "gx")
+    own_columns = pl.pallas_call(
+        own_columns_kernel,
+        out_shape=(shape_of(parts, 8, rows_y),) * 2,
+        in_specs=[vmem] * 3,
+        out_specs=(vmem,) * 2,
+        compiler_params=params,
+        cost_estimate=pl.CostEstimate(flops=2_000_000, bytes_accessed=1_000_000, transcendentals=0),
+    )(held, flow, tiles)
+    column_sent = pl.pallas_call(
+        functools.partial(halo_columns_kernel, groups),
+        out_shape=(shape_of(parts, 8, rows_y),) * 2,
+        in_specs=[vmem] * 4,
+        out_specs=(vmem,) * 2,
+        scratch_shapes=[pltpu.VMEM((2, SECOND, 8, rows_y), jnp.float32)],
+        compiler_params=params,
+    )(*own_columns, *row_got)
     column_got = swap_pairs(*column_sent, "gy")
-    row_got = swap_pairs(*sent[:2], "gx")
-    corners = pl.pallas_call(
-        corner_kernel,
-        out_shape=shape_of(2 * parts, 8, rows_y),
-        in_specs=[vmem] * 2,
-        out_specs=vmem,
-        compiler_params=params,
-    )(*column_got)
-    corner_got = swap_pairs(corners, corners, "gx")
     count = lax.axis_size("gx") * lax.axis_size("gy")
     field = pltpu.VMEM((19, padded, rows_y), jnp.float32)
-    later, later_shifted, solid_rows, own = pl.pallas_call(
-        first_step_kernel,
-        out_shape=(
-            shape_of(19, padded, rows_y),
-            shape_of(19, padded, rows_y),
-            shape_of(3, padded, rows_y),
-            shape_of(1, rows_y),
-        ),
-        in_specs=[vmem] * 11,
-        out_specs=(vmem,) * 4,
-        scratch_shapes=[field, field, pltpu.VMEM((4, 8, rows_y), jnp.float32)],
+    result, own = pl.pallas_call(
+        main_kernel,
+        out_shape=(shape_of(19, rows, rows_y), shape_of(count, 1, rows_y)),
+        in_specs=[vmem] * 9,
+        out_specs=(vmem,) * 2,
+        scratch_shapes=[
+            field,
+            field,
+            field,
+            pltpu.VMEM((3, padded, rows_y), jnp.float32),
+            pltpu.VMEM((4, 8, rows_y), jnp.float32),
+        ],
         compiler_params=params,
-    )(state, flow, solid, *row_got, *column_got, *column_sent, *corner_got)
-    total = sum_over(sum_over(own, "gx"), "gy")
-    result = pl.pallas_call(
-        second_step_kernel,
-        out_shape=shape_of(19, rows, rows_y),
-        in_specs=[vmem] * 4,
-        out_specs=vmem,
-        compiler_params=params,
-        cost_estimate=pl.CostEstimate(flops=4_000_000, bytes_accessed=4_000_000, transcendentals=0),
-    )(later, later_shifted, solid_rows, flow)
+    )(held, flow, tiles, *row_got, *column_got, *column_sent)
+    shared = lax.all_to_all(own, ("gx", "gy"), split_axis=0, concat_axis=0, tiled=True)
     cell_count = rows * rows_y * count
     scale = drag_factor / math.sqrt(cell_count) * 3.0 / 36.0
-    return (result.reshape(adjoint_in.shape), -scale * total[0, :1])
+    total = jnp.sum(shared[:, 0, 0])
+    return (result.reshape(adjoint_in.shape), (-scale * total).reshape(1))
 
 
 def solution(mesh):

time: 36.5 us -> 31.8 us (0.87)
  waiting for transfers between devices: 19.2 us -> 4.65 us
  blocking collectives: 0 us -> 11.8 us
  starting transfers between devices: 10.4 us -> 8.13 us
  Pallas kernels: 4.85 us -> 3.94 us
  other arithmetic: 0.02 us -> 0.63 us
  between operations: 1.9 us -> 2.44 us
    ppermute x5 -> x0, waiting for transfers between devices: 13.5 us -> none  [sum_over(): lax.ppermute(value, axis, [(i, i ^ distance) for i in range(count)])]
    all_to_all x0 -> x1, blocking collectives: none -> 11.8 us  [per_device(): lax.all_to_all(own, ('gx', 'gy'), split_axis=0, concat_axis=0, tiled=True)]
    ppermute x5 -> x0, starting transfers between devices: 1.56 us -> none  [sum_over(): lax.ppermute(value, axis, [(i, i ^ distance) for i in range(count)])]
    ppermute x3 -> x2, waiting for transfers between devices: 5.66 us -> 4.65 us  [swap_pairs(): lax.ppermute(second, axis, across)]
    pallas_call x4, Pallas kernels: 4.85 us -> 3.94 us  [the longest x1 2.2 us: per_device(): pl.pallas_call(main_kernel, out_shape=(shape_of(19, rows, rows_y), shape_...]
    ppermute x3 -> x2, starting transfers between devices: 2.63 us -> 1.91 us  [swap_pairs(): lax.ppermute(first, axis, inside)]
    reduce_sum x0 -> x1, other arithmetic: none -> 0.63 us  [per_device(): total = jnp.sum(shared[:, 0, 0])]
    ppermute x3 -> x2, starting transfers between devices: 6.22 us -> 6.22 us  [swap_pairs(): lax.ppermute(second, axis, across)]
  transfers between devices with their start and end apart: 11 -> 4, of which waited for: 7 -> 2; matrix products, arithmetic and copies ran while one was open for 0% -> 0% of each run, Pallas kernels for 3% -> 1%
where the time goes in v7:
time: 31.8 us; the launch traced here: 31.6 us
  blocking collectives  11.8 us (37%)
  starting transfers between devices  8.13 us (26%)
  waiting for transfers between devices  4.65 us (15%)
  Pallas kernels  3.94 us (12%)
  between operations  2.44 us (8%)
  other arithmetic  0.63 us (2%)
    all_to_all x1, blocking collectives, per_device(): lax.all_to_all(own, ('gx', 'gy'), split_axis=0, concat_axis=0, tiled=True)  11.8 us
    ppermute x2, starting transfers between devices, swap_pairs(): lax.ppermute(second, axis, across)  6.22 us
    ppermute x2, waiting for transfers between devices, swap_pairs(): lax.ppermute(second, axis, across)  4.65 us
    pallas_call x1, Pallas kernels, per_device(): pl.pallas_call(main_kernel, out_shape=(shape_of(19, rows, rows_y), shape_...  2.2 us
    ppermute x2, starting transfers between devices, swap_pairs(): lax.ppermute(first, axis, inside)  1.91 us
    pallas_call x1, Pallas kernels, per_device(): pl.pallas_call(row_message_kernel, out_shape=(pltpu.VMEM((QUANTITIES, lev...  1.24 us
  transfers between devices with their start and end apart: 4, of which 2 were waited for; matrix products, arithmetic and copies ran while one was open for 0% of the time, Pallas kernels for 1%

profile of v7, /device:TPU:0, one launch (start us, length us, event | category | flops | bytes accessed | tf_op | source)
XLA Modules:
  0.0 31.6 jit_solution(15716945287535819235)
XLA Ops:
  0.6 1.2 %shard_map.50 = (f32[28,4,128]{2,1,0:T(4,128)S(1)}, f32[28,4,128]{2,1,0:T(4,128)S(1)}, f32[19,96,128]{2,1,0:T(8,128)S(1)}, bf16[2,3,64,128]{3,2,1,0:T(8,128)(2,1)S(1)}, s32[16,32]{1,0:T(8,128)S(1)}) custom-call(f32[19,64,128]{2,1,0:T(8,128)} %bitcast.5, bf16[2,3,64,128]{3,2,1,0:T(8,128)(2,1)} %bitcast.6, s32[16,32]{1,0:T(8,128)} %bitcast.7), custom_call_target="tpu_custom_call" | custom-call | tf_op jit(solution)/shard_map/pallas_call | solution.py:461
  1.9 0.5 %collective-permute-start = (f32[28,4,128]{2,1,0:T(4,128)S(1)}, f32[28,4,128]{2,1,0:T(4,128)S(1)}, u32[]{:S(2)}, u32[]{:S(2)}) collective-permute-start(f32[28,4,128]{2,1,0:T(4,128)S(1)} %get-tuple-element.16), channel_id=1, source_target_pairs={{0,8},{8,0},{16,24},{24,16},{1,9},{9,1},{17,25},{25,17},{2,10},{10... | collective-permute-start | bytes 172040 | tf_op jit(solution)/shard_map/ppermute | solution.py:443
  2.4 2.6 %collective-permute-start.1 = (f32[28,4,128]{2,1,0:T(4,128)S(1)}, f32[28,4,128]{2,1,0:T(4,128)S(1)}, u32[]{:S(2)}, u32[]{:S(2)}) collective-permute-start(f32[28,4,128]{2,1,0:T(4,128)S(1)} %get-tuple-element.17), channel_id=1, source_target_pairs={{0,24},{8,16},{16,8},{24,0},{1,25},{9,17},{17,9},{25,1},{2,26},{10... | collective-permute-start | bytes 172040 | tf_op jit(solution)/shard_map/ppermute | solution.py:443
  5.0 0.3 %shard_map.51 = (f32[3,8,128]{2,1,0:T(8,128)S(1)}, f32[3,8,128]{2,1,0:T(8,128)S(1)}) custom-call(f32[19,96,128]{2,1,0:T(8,128)S(1)} %get-tuple-element.13.held.own_held, bf16[2,3,64,128]{3,2,1,0:T(8,128)(2,1)S(1)} %get-tuple-element.14.velocity, s32[16,32]{1,0:T(8,128)S(1)} %get-tuple-element.15.solid), custom_call_target="tpu_custom_call" | custom-call | flops 2000000 | bytes 1000000 | tf_op jit(solution)/shard_map/pallas_call | solution.py:476
  5.4 0.0 collective-permute-done.row_first
  5.4 1.8 %collective-permute-done.1.row_second = f32[28,4,128]{2,1,0:T(4,128)S(1)} collective-permute-done((f32[28,4,128]{2,1,0:T(4,128)S(1)}, f32[28,4,128]{2,1,0:T(4,128)S(1)}, u32[]{:S(2)}, u32[]{:S(2)}) %collective-permute-start.1) | collective-permute-done | bytes 57376 | tf_op jit(solution)/shard_map/ppermute | solution.py:443
  7.2 0.2 shard_map.52
  7.4 1.4 %collective-permute-start.2 = (f32[3,8,128]{2,1,0:T(8,128)S(1)}, f32[3,8,128]{2,1,0:T(8,128)S(1)}, u32[]{:S(2)}, u32[]{:S(2)}) collective-permute-start(f32[3,8,128]{2,1,0:T(8,128)S(1)} %get-tuple-element.20.sent_first), channel_id=1, source_target_pairs={{0,1},{1,0},{2,3},{3,2},{4,5},{5,4},{6,7},{7,6},{8,9},{9,8},{10,11... | collective-permute-start | bytes 36872 | tf_op jit(solution)/shard_map/ppermute | solution.py:443
  8.8 3.6 %collective-permute-start.3 = (f32[3,8,128]{2,1,0:T(8,128)S(1)}, f32[3,8,128]{2,1,0:T(8,128)S(1)}, u32[]{:S(2)}, u32[]{:S(2)}) collective-permute-start(f32[3,8,128]{2,1,0:T(8,128)S(1)} %get-tuple-element.21.sent_second), channel_id=1, source_target_pairs={{0,7},{1,2},{2,1},{3,4},{4,3},{5,6},{6,5},{7,0},{8,15},{9,10},{10,... | collective-permute-start | bytes 36872 | tf_op jit(solution)/shard_map/ppermute | solution.py:443
  12.4 0.0 collective-permute-done.2.column_first
  12.4 2.8 %collective-permute-done.3.column_second = f32[3,8,128]{2,1,0:T(8,128)S(1)} collective-permute-done((f32[3,8,128]{2,1,0:T(8,128)S(1)}, f32[3,8,128]{2,1,0:T(8,128)S(1)}, u32[]{:S(2)}, u32[]{:S(2)}) %collective-permute-start.3) | collective-permute-done | bytes 12320 | tf_op jit(solution)/shard_map/ppermute | solution.py:443
  15.2 2.2 %shard_map.53 = (f32[19,64,128]{2,1,0:T(8,128)}, f32[32,1,128]{2,1,0:T(1,128)S(1)}) custom-call(f32[19,96,128]{2,1,0:T(8,128)S(1)} %get-tuple-element.13.held.own_held, bf16[2,3,64,128]{3,2,1,0:T(8,128)(2,1)S(1)} %get-tuple-element.14.velocity, s32[16,32]{1,0:T(8,128)S(1)} %get-tuple-element.15.solid, f32[28,4,128]{2,1,0:T(4,128)S(1)} %collective-permute-done.row_first, ...), custom_call_target="tpu_custom_call" | custom-call | tf_op jit(solution)/shard_map/pallas_call | solution.py:495
  17.4 11.8 %all_to_all.5 = f32[32,1,128]{2,1,0:T(1,128)S(1)} all-to-all(f32[32,1,128]{2,1,0:T(1,128)S(1)} %get-tuple-element.23), channel_id=1, replica_groups=mesh['gx'=4,'gy'=8] {'gx','gy'}, dimensions={0} | all-to-all | bytes 32768 | tf_op jit(solution)/shard_map/all_to_all | solution.py:509
  29.2 0.6 %slice_reduce_fusion = f32[]{:T(128)} fusion(f32[32,1,128]{2,1,0:T(1,128)S(1)} %all_to_all.5), kind=kLoop, calls=%fused_computation | loop fusion | flops 31 | bytes 132 | tf_op jit(solution)/shard_map/reduce_sum | solution.py:512
Async XLA Ops:
  1.9 3.5 %collective-permute-start = (f32[28,4,128]{2,1,0:T(4,128)S(1)}, f32[28,4,128]{2,1,0:T(4,128)S(1)}, u32[]{:S(2)}, u32[]{:S(2)}) collective-permute-start(f32[28,4,128]{2,1,0:T(4,128)S(1)} %get-tuple-element.16), channel_id=1, source_target_pairs={{0,8},{8,0},{16,24},{24,16},{1,9},{9,1},{17,25},{25,17},{2,10},{10... | collective-permute-start | bytes 172040 | tf_op jit(solution)/shard_map/ppermute | solution.py:443
  2.4 4.8 %collective-permute-start.1 = (f32[28,4,128]{2,1,0:T(4,128)S(1)}, f32[28,4,128]{2,1,0:T(4,128)S(1)}, u32[]{:S(2)}, u32[]{:S(2)}) collective-permute-start(f32[28,4,128]{2,1,0:T(4,128)S(1)} %get-tuple-element.17), channel_id=1, source_target_pairs={{0,24},{8,16},{16,8},{24,0},{1,25},{9,17},{17,9},{25,1},{2,26},{10... | collective-permute-start | bytes 172040 | tf_op jit(solution)/shard_map/ppermute | solution.py:443
  7.4 5.0 %collective-permute-start.2 = (f32[3,8,128]{2,1,0:T(8,128)S(1)}, f32[3,8,128]{2,1,0:T(8,128)S(1)}, u32[]{:S(2)}, u32[]{:S(2)}) collective-permute-start(f32[3,8,128]{2,1,0:T(8,128)S(1)} %get-tuple-element.20.sent_first), channel_id=1, source_target_pairs={{0,1},{1,0},{2,3},{3,2},{4,5},{5,4},{6,7},{7,6},{8,9},{9,8},{10,11... | collective-permute-start | bytes 36872 | tf_op jit(solution)/shard_map/ppermute | solution.py:443
  8.8 6.4 %collective-permute-start.3 = (f32[3,8,128]{2,1,0:T(8,128)S(1)}, f32[3,8,128]{2,1,0:T(8,128)S(1)}, u32[]{:S(2)}, u32[]{:S(2)}) collective-permute-start(f32[3,8,128]{2,1,0:T(8,128)S(1)} %get-tuple-element.21.sent_second), channel_id=1, source_target_pairs={{0,7},{1,2},{2,1},{3,4},{4,3},{5,6},{6,5},{7,0},{8,15},{9,10},{10,... | collective-permute-start | bytes 36872 | tf_op jit(solution)/shard_map/ppermute | solution.py:443

commit v8 on v7

--- a/solution.py
+++ b/solution.py
@@ -46,8 +46,11 @@
 
 FLOW = 19
 SOLID = 22
-SECOND = 23
-QUANTITIES = 28
+NEXT = 23
+SECOND = 26
+QUANTITIES = 31
+NEXT_SECOND = 31
+COLUMN_QUANTITIES = 34
 BEFORE_LANE = 16
 AFTER_LANE = 32
 
@@ -130,10 +133,11 @@
 
     for number in range(19):
         put(number, held[number, pl.ds(low_row, LEVELS), :], held[number, pl.ds(high_row, LEVELS), :])
-    for axis in range(3):
-        low = flow[0, axis, pl.ds(0, 16), :].astype(jnp.float32)
-        high = flow[0, axis, pl.ds(rows - 16, 16), :].astype(jnp.float32)
-        put(FLOW + axis, low[:LEVELS], high[16 - LEVELS :])
+    for step, slot in ((0, FLOW), (1, NEXT)):
+        for axis in range(3):
+            low = flow[step, axis, pl.ds(0, 16), :].astype(jnp.float32)
+            high = flow[step, axis, pl.ds(rows - 16, 16), :].astype(jnp.float32)
+            put(slot + axis, low[:LEVELS], high[16 - LEVELS :])
     solid_parts = spread_solid(tiles)
     put(SOLID, solid_parts[0][:LEVELS], solid_parts[-1][:LEVELS])
     for slot in range(5):
@@ -155,26 +159,29 @@
         insert_column(low_parts, SECOND + y_up.index(slot), group, groups, value, 1, 1)
     if slot in y_down:
         insert_column(high_parts, SECOND + y_down.index(slot), group, groups, value, LANES - 2, 0)
+    if NEXT <= slot < NEXT + 3:
+        insert_column(high_parts, NEXT_SECOND + slot - NEXT, group, groups, value, LANES - 2, 0)
 
 
 def own_columns_kernel(held, velocity, solid, low, high):
     rows = velocity.shape[2]
     groups = rows // 8 + 2
     solid_parts = spread_solid(solid)
-    flow = flow_blocks(velocity, 0, rows)
+    flow = [flow_blocks(velocity, step, rows) for step in range(2)]
     parts = [[jnp.zeros((8, LANES), jnp.float32) for _ in range(low.shape[0])] for _ in range(2)]
     for group in range(1, groups - 1):
         for slot in range(19):
             pack_columns(parts, slot, group, groups, held[slot, pl.ds(GUARD + 8 * group, 8), :])
         for axis in range(3):
-            pack_columns(parts, FLOW + axis, group, groups, flow[group - 1][axis])
+            pack_columns(parts, FLOW + axis, group, groups, flow[0][group - 1][axis])
+            pack_columns(parts, NEXT + axis, group, groups, flow[1][group - 1][axis])
         pack_columns(parts, SOLID, group, groups, solid_parts[(group - 1) * 8 // (LEVELS * TILE)])
     for part in range(low.shape[0]):
         low[part] = parts[0][part]
         high[part] = parts[1][part]
 
 
-def halo_columns_kernel(groups, own_low, own_high, row_first, row_second, first_out, second_out, ends):
+def halo_columns_kernel(groups, own_low, own_high, row_first, row_second, low_out, high_out, ends):
     count = own_low.shape[0]
     even = on_even("gx")
     after, before = Chosen(even, row_first, row_second), Chosen(even, row_second, row_first)
@@ -192,10 +199,9 @@
         ends[1, slot, pl.ds(LEVELS, LEVELS), :] = blank if high_second is None else after[high_second]
         pack_columns(parts, slot, 0, groups, ends[0, slot])
         pack_columns(parts, slot, groups - 1, groups, ends[1, slot])
-    even = on_even("gy")
     for part in range(count):
-        first_out[part] = jnp.where(even, parts[1][part], parts[0][part])
-        second_out[part] = jnp.where(even, parts[0][part], parts[1][part])
+        low_out[part] = parts[0][part]
+        high_out[part] = parts[1][part]
 
 
 def collide(moved, flow, fluid):
@@ -249,25 +255,25 @@
 
 def shift_lanes(value, cy, edge_value):
     lane = lane_index(value.shape[0])
-    if cy == 1:
-        return jnp.where(lane == LANES - 1, edge_value, pltpu.roll(value, LANES - 1, 1))
-    return jnp.where(lane == 0, edge_value, pltpu.roll(value, 1, 1))
+    shifted = pltpu.roll(value, -cy % LANES, 1)
+    if edge_value is None:
+        return shifted
+    return jnp.where(lane == (LANES - 1 if cy == 1 else 0), edge_value, shifted)
 
 
 def gather_cells(held, shifted, first, solid_rows):
     here = [held[n, pl.ds(first, 8), :] for n in range(19)]
-    moved = [here[0]]
+    moved, closed = [here[0]], [None]
     for number in range(1, 19):
         cx, cy, cz = lattice_speeds[number]
         field = held if cy == 0 else shifted
         there = pl.ds(first + LEVELS * cx + cz, 8)
-        source = field[number, there, :]
-        closed = link_closed(solid_rows[cy % 3, there, :], cz)
+        closed.append(link_closed(solid_rows[cy % 3, there, :], cz))
         bounced = here[opposite_of(number)]
         if cx != 0:
             bounced = bounced + 2.0 * cx
-        moved.append(jnp.where(closed, bounced, source))
-    return moved
+        moved.append(jnp.where(closed[number], bounced, field[number, there, :]))
+    return moved, closed
 
 
 def momentum(moved):
@@ -282,32 +288,45 @@
     return fluid * sum(speed * part for speed, part in zip(flow, momentum(moved)))
 
 
-def main_kernel(
-    own_held, velocity, solid, row_first, row_second, column_first, column_second,
-    sent_first, sent_second, out, shared, held, shifted, later, solid_rows, row_flow,
-):
-    rows = velocity.shape[2]
-    even = on_even("gx")
-    after, before = Chosen(even, row_first, row_second), Chosen(even, row_second, row_first)
-    even = on_even("gy")
-    parts = range(column_first.shape[0])
-
-    def chosen(yes, no):
-        return [jnp.where(even, yes[part], no[part]) for part in parts]
-
-    low, high = chosen(sent_second, sent_first), chosen(sent_first, sent_second)
-    y_after, y_before = chosen(column_first, column_second), chosen(column_second, column_first)
-    groups = rows // 8 + 2
+def along_link(number, vector):
+    total = None
+    for axis, speed in enumerate(lattice_speeds[number]):
+        if speed == 0:
+            continue
+        part = vector(axis)
+        if total is None:
+            total = part if speed == 1 else -part
+        else:
+            total = total + part if speed == 1 else total - part
+    return total
+
+
+def later_drag(results, closed, weight_here, weight_back):
+    term = None
+    for number in range(1, 19):
+        cx = lattice_speeds[number][0]
+        here = along_link(number, lambda axis: weight_here[axis])
+        back = along_link(number, lambda axis: weight_back(number, axis))
+        part = jnp.where(closed[opposite_of(number)], -here, back) * results[number]
+        if cx != 0:
+            part = part + jnp.where(closed[number], (2.0 * cx) * here, 0.0)
+        if number < 7:
+            part = 2.0 * part
+        term = part if term is None else term + part
+    return term
+
+
+def column_reader(groups):
+    def column(message, ahead, slot, lane_first, group=0):
+        part, place = slot_place(slot, group, groups)
+        return pltpu.roll(message[part], (lane_first - place - ahead) % LANES, 1)
+
+    return column
+
+
+def fill_held(own_held, before, after, held, rows):
     own = GUARD + 8
     near, far = own - LEVELS, own + rows
-    lane = lane_index()
-    solid_parts = spread_solid(solid)
-
-    def column(message, slot, lane_first, group=0):
-        part, place = slot_place(slot, group, groups)
-        ahead = 1 if message is y_after or message is low else 0
-        return pltpu.roll(message[part], (lane_first - place - ahead) % LANES, 1)
-
     for number in range(19):
         for group in range(rows // 8):
             there = pl.ds(own + 8 * group, 8)
@@ -318,16 +337,17 @@
             held[number, pl.ds(near - LEVELS, LEVELS), :] = before[SECOND + x_down.index(number)]
         if number in x_up:
             held[number, pl.ds(far + LEVELS, LEVELS), :] = after[SECOND + x_up.index(number)]
+
+
+def fill_shifted(field, shifted, groups, edge_of):
     for number in y_up + y_down:
         cy = lattice_speeds[number][1]
         for group in range(groups):
-            value = held[number, pl.ds(GUARD + 8 * group, 8), :]
-            if cy == 1:
-                edge = column(y_after, number, LANES - 1, group)
-            else:
-                edge = column(y_before, number, 0, group)
-            shifted[number, pl.ds(GUARD + 8 * group, 8), :] = shift_lanes(value, cy, edge)
-
+            there = pl.ds(GUARD + 8 * group, 8)
+            shifted[number, there, :] = shift_lanes(field[number, there, :], cy, edge_of(number, cy, group))
+
+
+def fill_solid(solid_parts, before, after, solid_rows, groups, edge_of):
     for group in range(groups):
         first = GUARD + 8 * group
         if group in (0, groups - 1):
@@ -337,13 +357,138 @@
         else:
             solid_rows[0, pl.ds(first, 8), :] = solid_parts[(group - 1) * 8 // (LEVELS * TILE)]
         value = solid_rows[0, pl.ds(first, 8), :]
-        solid_rows[1, pl.ds(first, 8), :] = shift_lanes(value, 1, column(y_after, SOLID, LANES - 1, group))
-        solid_rows[2, pl.ds(first, 8), :] = shift_lanes(value, -1, column(y_before, SOLID, 0, group))
+        for cy in (1, -1):
+            solid_rows[cy % 3, pl.ds(first, 8), :] = shift_lanes(value, cy, edge_of(SOLID, cy, group))
+
+
+def shift_rows(value, cx, cz):
+    if cx != 0:
+        upper = lax.broadcasted_iota(jnp.int32, (8, LANES), 0) < LEVELS
+        swapped = pltpu.roll(value, LEVELS, 0)
+        if cx == 1:
+            value = jnp.where(upper, swapped, pltpu.roll(swapped, LANES - 1, 1))
+        else:
+            value = jnp.where(upper, pltpu.roll(swapped, 1, 1), swapped)
+    if cz != 0:
+        value = pltpu.roll(value, (-cz) % 8, 0)
+    return value
+
+
+def gather_columns(neighbours):
+    here = [neighbours(n, 0) for n in range(19)]
+    solid = {cy: neighbours(SOLID, cy) for cy in (0, 1, -1)}
+    moved, closed = [here[0]], [None]
+    for number in range(1, 19):
+        cx, cy, cz = lattice_speeds[number]
+        source = shift_rows(here[number] if cy == 0 else neighbours(number, cy), cx, cz)
+        closed.append(link_closed(shift_rows(solid[cy], cx, cz), cz))
+        moved.append(jnp.where(closed[number], here[opposite_of(number)] + 2.0 * cx, source))
+    return moved, closed, solid
+
+
+def drag_kernel(
+    own_held, velocity, solid, row_first, row_second, y_before, low, shared,
+    held, shifted, solid_rows, weights,
+):
+    rows = velocity.shape[2]
+    groups = rows // 8 + 2
+    own = GUARD + 8
+    near, far = own - LEVELS, own + rows
+    even = on_even("gx")
+    after, before = Chosen(even, row_first, row_second), Chosen(even, row_second, row_first)
+    lane = lane_index()
+    solid_parts = spread_solid(solid)
+    column = column_reader(groups)
+
+    def edge_of(slot, cy, group):
+        return None if cy == 1 else column(y_before, 0, slot, 0, group)
+
+    fill_held(own_held, before, after, held, rows)
+    fill_shifted(held, shifted, groups, edge_of)
+    fill_solid(solid_parts, before, after, solid_rows, groups, edge_of)
+
+    flow = flow_blocks(velocity, 1, rows)
     for axis in range(3):
-        row_flow[axis, pl.ds(0, LEVELS), :] = before[FLOW + axis]
-        row_flow[axis, pl.ds(LEVELS, LEVELS), :] = after[FLOW + axis]
-    row_flow[3, pl.ds(0, LEVELS), :] = before[SOLID]
-    row_flow[3, pl.ds(LEVELS, LEVELS), :] = after[SOLID]
+        for group in range(rows // 8):
+            there = pl.ds(own + 8 * group, 8)
+            weights[axis, there, :] = (1.0 - solid_rows[0, there, :]) * flow[group][axis]
+        for row, message in ((near, before), (far, after)):
+            weights[axis, pl.ds(row, LEVELS), :] = (1.0 - message[SOLID]) * message[NEXT + axis]
+        for group in range(groups):
+            there = pl.ds(GUARD + 8 * group, 8)
+            value = weights[axis, there, :]
+            edge = (1.0 - column(y_before, 0, SOLID, 0, group)) * column(y_before, 0, NEXT + axis, 0, group)
+            weights[3 + axis, there, :] = shift_lanes(value, 1, None)
+            weights[6 + axis, there, :] = shift_lanes(value, -1, edge)
+
+    total = jnp.zeros((8, LANES), jnp.float32)
+    flow = flow_blocks(velocity, 0, rows)
+    for group in range(rows // 8):
+        first = own + 8 * group
+        moved, closed = gather_cells(held, shifted, first, solid_rows)
+        fluid = 1.0 - solid_parts[8 * group // (LEVELS * TILE)]
+        results = collide(moved, flow[group], fluid)
+
+        def back(number, axis):
+            cx, cy, cz = lattice_speeds[number]
+            return weights[3 * (-cy % 3) + axis, pl.ds(first - LEVELS * cx - cz, 8), :]
+
+        here = [weights[axis, pl.ds(first, 8), :] for axis in range(3)]
+        total = total + drag_term(moved, flow[group], fluid) + later_drag(results, closed, here, back)
+    total = jnp.where(lane < LANES - 1, total, 0.0)
+
+    def neighbours(slot, cy):
+        if cy == 1:
+            return column(low, 1, slot, BEFORE_LANE)
+        if cy == -1 and slot != SOLID:
+            slot = SECOND + y_down.index(slot)
+        return column(y_before, 0, slot, BEFORE_LANE)
+
+    moved, closed, solid_columns = gather_columns(neighbours)
+    fluid = {cy: 1.0 - solid_columns[cy] for cy in (0, 1, -1)}
+    column_flow = [neighbours(FLOW + axis, 0) for axis in range(3)]
+    results = collide(moved, column_flow, fluid[0])
+    weight = {
+        0: [fluid[0] * neighbours(NEXT + axis, 0) for axis in range(3)],
+        1: [fluid[1] * neighbours(NEXT + axis, 1) for axis in range(3)],
+        -1: [fluid[-1] * neighbours(NEXT_SECOND + axis, 0) for axis in range(3)],
+    }
+
+    def back_column(number, axis):
+        cx, cy, cz = lattice_speeds[number]
+        return shift_rows(weight[-cy][axis], -cx, -cz)
+
+    term = drag_term(moved, column_flow, fluid[0]) + later_drag(results, closed, weight[0], back_column)
+    inside = jnp.logical_and(lane > BEFORE_LANE, lane < BEFORE_LANE + groups - 1)
+    total = total + jnp.where(inside, term, 0.0)
+    shared[...] = jnp.broadcast_to(jnp.sum(total), shared.shape)
+
+
+def main_kernel(
+    own_held, velocity, solid, row_first, row_second, y_after, y_before, low, high, out,
+    held, shifted, later, solid_rows, row_flow,
+):
+    rows = velocity.shape[2]
+    groups = rows // 8 + 2
+    own = GUARD + 8
+    near, far = own - LEVELS, own + rows
+    even = on_even("gx")
+    after, before = Chosen(even, row_first, row_second), Chosen(even, row_second, row_first)
+    lane = lane_index()
+    solid_parts = spread_solid(solid)
+    column = column_reader(groups)
+
+    def edge_of(slot, cy, group):
+        if cy == 1:
+            return column(y_after, 1, slot, LANES - 1, group)
+        return column(y_before, 0, slot, 0, group)
+
+    fill_held(own_held, before, after, held, rows)
+    fill_shifted(held, shifted, groups, edge_of)
+    fill_solid(solid_parts, before, after, solid_rows, groups, edge_of)
+    for slot, place in ((FLOW, 0), (FLOW + 1, 1), (FLOW + 2, 2), (SOLID, 3)):
+        row_flow[place, pl.ds(0, LEVELS), :] = before[slot]
+        row_flow[place, pl.ds(LEVELS, LEVELS), :] = after[slot]
 
     def both_rows(field, index, shift):
         ends = [field[index, pl.ds(place + shift, LEVELS), :] for place in (near, far)]
@@ -359,88 +504,53 @@
         moved.append(jnp.where(closed, here[opposite_of(number)] + 2.0 * cx, source))
     row_results = collide(moved, [row_flow[axis] for axis in range(3)], 1.0 - row_flow[3])
 
-    def columns(number_before, number_after, message_before, message_after):
-        return jnp.where(
-            lane < AFTER_LANE,
-            column(message_before, number_before, BEFORE_LANE),
-            column(message_after, number_after, AFTER_LANE),
-        )
-
     def neighbours(slot, cy):
-        if cy == 0:
-            return columns(slot, slot, y_before, y_after)
+        beyond = slot if cy == 0 or slot == SOLID else SECOND + (y_up if cy == 1 else y_down).index(slot)
         if cy == 1:
-            beyond = SOLID if slot == SOLID else SECOND + y_up.index(slot)
-            return columns(slot, beyond, low, y_after)
-        beyond = SOLID if slot == SOLID else SECOND + y_down.index(slot)
-        return columns(beyond, slot, y_before, high)
-
-    upper = lax.broadcasted_iota(jnp.int32, (8, LANES), 0) < LEVELS
-
-    def shift_rows(value, cx, cz):
-        if cx != 0:
-            swapped = pltpu.roll(value, LEVELS, 0)
-            if cx == 1:
-                value = jnp.where(upper, swapped, pltpu.roll(swapped, LANES - 1, 1))
-            else:
-                value = jnp.where(upper, pltpu.roll(swapped, 1, 1), swapped)
-        if cz != 0:
-            value = pltpu.roll(value, (-cz) % 8, 0)
-        return value
-
-    here = [neighbours(n, 0) for n in range(19)]
-    solid_columns = [neighbours(SOLID, cy) for cy in (0, 1, -1)]
-    moved = [here[0]]
-    for number in range(1, 19):
-        cx, cy, cz = lattice_speeds[number]
-        source = shift_rows(here[number] if cy == 0 else neighbours(number, cy), cx, cz)
-        closed = link_closed(shift_rows(solid_columns[cy % 3], cx, cz), cz)
-        moved.append(jnp.where(closed, here[opposite_of(number)] + 2.0 * cx, source))
+            first, second = column(low, 1, slot, BEFORE_LANE), column(y_after, 1, beyond, AFTER_LANE)
+        elif cy == -1:
+            first, second = column(y_before, 0, beyond, BEFORE_LANE), column(high, 0, slot, AFTER_LANE)
+        else:
+            first, second = column(y_before, 0, slot, BEFORE_LANE), column(y_after, 1, slot, AFTER_LANE)
+        return jnp.where(lane < AFTER_LANE, first, second)
+
+    moved, _, solid_columns = gather_columns(neighbours)
     column_flow = [neighbours(FLOW + axis, 0) for axis in range(3)]
     column_results = collide(moved, column_flow, 1.0 - solid_columns[0])
 
-    def fluid_at(first):
-        return 1.0 - solid_parts[first // (LEVELS * TILE)]
-
-    drag_sum = jnp.zeros((8, LANES), jnp.float32)
     flow = flow_blocks(velocity, 0, rows)
     for group in range(rows // 8):
-        first = 8 * group
-        moved = gather_cells(held, shifted, own + first, solid_rows)
-        results = collide(moved, flow[group], fluid_at(first))
+        first = own + 8 * group
+        moved, _ = gather_cells(held, shifted, first, solid_rows)
+        results = collide(moved, flow[group], 1.0 - solid_parts[8 * group // (LEVELS * TILE)])
         for number in range(19):
-            later[number, pl.ds(own + first, 8), :] = results[number]
-        drag_sum = drag_sum + drag_term(moved, flow[group], fluid_at(first))
+            later[number, pl.ds(first, 8), :] = results[number]
     for number in x_down:
         later[number, pl.ds(near, LEVELS), :] = row_results[number][:LEVELS]
     for number in x_up:
         later[number, pl.ds(far, LEVELS), :] = row_results[number][LEVELS:]
-    for number in y_up + y_down:
-        cy = lattice_speeds[number][1]
-        for group in range(groups):
-            value = later[number, pl.ds(GUARD + 8 * group, 8), :]
-            if cy == 1:
-                edge = pltpu.roll(column_results[number], (LANES - 1 - AFTER_LANE - group) % LANES, 1)
-            else:
-                edge = pltpu.roll(column_results[number], (-BEFORE_LANE - group) % LANES, 1)
-            shifted[number, pl.ds(GUARD + 8 * group, 8), :] = shift_lanes(value, cy, edge)
+
+    def later_edge(number, cy, group):
+        shift = LANES - 1 - AFTER_LANE - group if cy == 1 else -BEFORE_LANE - group
+        return pltpu.roll(column_results[number], shift % LANES, 1)
+
+    fill_shifted(later, shifted, groups, later_edge)
 
     flow = flow_blocks(velocity, 1, rows)
     for group in range(rows // 8):
         first = 8 * group
-        moved = gather_cells(later, shifted, own + first, solid_rows)
-        results = collide(moved, flow[group], fluid_at(first))
+        moved, _ = gather_cells(later, shifted, own + first, solid_rows)
+        results = collide(moved, flow[group], 1.0 - solid_parts[first // (LEVELS * TILE)])
         for number in range(19):
             out[number, pl.ds(first, 8), :] = results[number]
-        drag_sum = drag_sum + drag_term(moved, flow[group], fluid_at(first))
-    shared[...] = jnp.broadcast_to(jnp.sum(drag_sum), shared.shape)
 
 
 def swap_pairs(first, second, axis):
     count = lax.axis_size(axis)
     inside = [(i, i ^ 1) for i in range(count)]
     across = [(i, (i + 1) % count if i % 2 == 1 else (i - 1) % count) for i in range(count)]
-    return lax.ppermute(first, axis, inside), lax.ppermute(second, axis, across)
+    second = lax.ppermute(second, axis, across)
+    return lax.ppermute(first, axis, inside), second
 
 
 def per_device(adjoint_in, velocity, solid_tiles, link_blocked):
@@ -448,7 +558,7 @@
     rows = rows_x * levels
     padded = rows + 16 + 2 * GUARD
     groups = rows // 8 + 2
-    parts = -(-QUANTITIES // (LANES // groups))
+    parts = -(-COLUMN_QUANTITIES // (LANES // groups))
     state = adjoint_in.reshape(19, rows, rows_y)
     flow = velocity.reshape(STEPS, 3, rows, rows_y)
     solid = solid_tiles.reshape(-1, solid_tiles.shape[2])
@@ -481,7 +591,7 @@
         compiler_params=params,
         cost_estimate=pl.CostEstimate(flops=2_000_000, bytes_accessed=1_000_000, transcendentals=0),
     )(held, flow, tiles)
-    column_sent = pl.pallas_call(
+    low, high = pl.pallas_call(
         functools.partial(halo_columns_kernel, groups),
         out_shape=(shape_of(parts, 8, rows_y),) * 2,
         in_specs=[vmem] * 4,
@@ -489,24 +599,30 @@
         scratch_shapes=[pltpu.VMEM((2, SECOND, 8, rows_y), jnp.float32)],
         compiler_params=params,
     )(*own_columns, *row_got)
-    column_got = swap_pairs(*column_sent, "gy")
-    count = lax.axis_size("gx") * lax.axis_size("gy")
+    size = lax.axis_size("gy")
+    y_before = lax.ppermute(high, "gy", [(i, (i + 1) % size) for i in range(size)])
+    y_after = lax.ppermute(low, "gy", [((i + 1) % size, i) for i in range(size)])
+    count = lax.axis_size("gx") * size
     field = pltpu.VMEM((19, padded, rows_y), jnp.float32)
-    result, own = pl.pallas_call(
+    solid_field = pltpu.VMEM((3, padded, rows_y), jnp.float32)
+    own = pl.pallas_call(
+        drag_kernel,
+        out_shape=pltpu.VMEM((count, 1, rows_y), jnp.float32),
+        in_specs=[vmem] * 7,
+        out_specs=vmem,
+        scratch_shapes=[field, field, solid_field, pltpu.VMEM((9, padded, rows_y), jnp.float32)],
+        compiler_params=params,
+    )(held, flow, tiles, *row_got, y_before, low)
+    shared = lax.all_to_all(own, ("gx", "gy"), split_axis=0, concat_axis=0, tiled=True)
+    result = pl.pallas_call(
         main_kernel,
-        out_shape=(shape_of(19, rows, rows_y), shape_of(count, 1, rows_y)),
+        out_shape=shape_of(19, rows, rows_y),
         in_specs=[vmem] * 9,
-        out_specs=(vmem,) * 2,
-        scratch_shapes=[
-            field,
-            field,
-            field,
-            pltpu.VMEM((3, padded, rows_y), jnp.float32),
-            pltpu.VMEM((4, 8, rows_y), jnp.float32),
-        ],
+        out_specs=vmem,
+        scratch_shapes=[field, field, field, solid_field, pltpu.VMEM((4, 8, rows_y), jnp.float32)],
         compiler_params=params,
-    )(held, flow, tiles, *row_got, *column_got, *column_sent)
-    shared = lax.all_to_all(own, ("gx", "gy"), split_axis=0, concat_axis=0, tiled=True)
+        cost_estimate=pl.CostEstimate(flops=8_000_000, bytes_accessed=4_000_000, transcendentals=0),
+    )(held, flow, tiles, *row_got, y_after, y_before, low, high)
     cell_count = rows * rows_y * count
     scale = drag_factor / math.sqrt(cell_count) * 3.0 / 36.0
     total = jnp.sum(shared[:, 0, 0])

time: 31.8 us -> 29.4 us (0.925)
  blocking collectives: 11.8 us -> 0 us
  starting transfers between devices: 8.13 us -> 12.3 us
  waiting for transfers between devices: 4.65 us -> 8.33 us
  Pallas kernels: 3.94 us -> 5.5 us
    all_to_all x1 -> x0, blocking collectives: 11.8 us -> none  [per_device(): lax.all_to_all(own, ('gx', 'gy'), split_axis=0, concat_axis=0, tiled=True)]
    ppermute x4, waiting for transfers between devices: 4.65 us -> 8.33 us  [the longest x1 4.99 us: per_device(): lax.ppermute(high, 'gy', [(i, (i + 1) % size) for i in range(size)])]
    all_to_all x0 -> x1, starting transfers between devices: none -> 3.06 us  [per_device(): lax.all_to_all(own, ('gx', 'gy'), split_axis=0, concat_axis=0, tiled=True)]
    pallas_call x1 -> x2, Pallas kernels: 2.2 us -> 3.72 us  [the longest x1 2.22 us: per_device(): pl.pallas_call(main_kernel, out_shape=shape_of(19, rows, rows_y), in_spec...]
    ppermute x4, starting transfers between devices: 8.13 us -> 9.2 us  [the longest x1 4.59 us: per_device(): lax.ppermute(low, 'gy', [((i + 1) % size, i) for i in range(size)])]
  transfers between devices with their start and end apart: 4 -> 5, of which waited for: 2 -> 3; matrix products, arithmetic and copies ran while one was open for 0% -> 0% of each run, Pallas kernels for 1% -> 9%
where the time goes in v8:
time: 29.4 us; the launch traced here: 29.2 us
  starting transfers between devices  12.3 us (42%)
  waiting for transfers between devices  8.33 us (28%)
  Pallas kernels  5.5 us (19%)
  between operations  2.45 us (8%)
  other arithmetic  0.63 us (2%)
    ppermute x1, waiting for transfers between devices, per_device(): lax.ppermute(high, 'gy', [(i, (i + 1) % size) for i in range(size)])  4.99 us
    ppermute x1, starting transfers between devices, per_device(): lax.ppermute(low, 'gy', [((i + 1) % size, i) for i in range(size)])  4.59 us
    all_to_all x1, starting transfers between devices, per_device(): lax.all_to_all(own, ('gx', 'gy'), split_axis=0, concat_axis=0, tiled=True)  3.06 us
    ppermute x1, starting transfers between devices, swap_pairs(): second = lax.ppermute(second, axis, across)  2.64 us
    pallas_call x1, Pallas kernels, per_device(): pl.pallas_call(main_kernel, out_shape=shape_of(19, rows, rows_y), in_spec...  2.22 us
    ppermute x1, waiting for transfers between devices, swap_pairs(): second = lax.ppermute(second, axis, across)  1.93 us
    pallas_call x1, Pallas kernels, per_device(): pl.pallas_call(drag_kernel, out_shape=pltpu.VMEM((count, 1, rows_y), jnp....  1.49 us
    ppermute x1, starting transfers between devices, per_device(): lax.ppermute(high, 'gy', [(i, (i + 1) % size) for i in range(size)])  1.45 us
  transfers between devices with their start and end apart: 5, of which 3 were waited for; matrix products, arithmetic and copies ran while one was open for 0% of the time, Pallas kernels for 9%

profile of v8, /device:TPU:0, one launch (start us, length us, event | category | flops | bytes accessed | tf_op | source)
XLA Modules:
  0.0 29.2 jit_solution(14639492672343685817)
XLA Ops:
  0.6 1.2 %shard_map.50 = (f32[31,4,128]{2,1,0:T(4,128)S(1)}, f32[31,4,128]{2,1,0:T(4,128)S(1)}, f32[19,96,128]{2,1,0:T(8,128)S(1)}, bf16[2,3,64,128]{3,2,1,0:T(8,128)(2,1)S(1)}, s32[16,32]{1,0:T(8,128)S(1)}) custom-call(f32[19,64,128]{2,1,0:T(8,128)} %bitcast.6, bf16[2,3,64,128]{3,2,1,0:T(8,128)(2,1)} %bitcast.7, s32[16,32]{1,0:T(8,128)} %bitcast.8), custom_call_target="tpu_custom_call" | custom-call | tf_op jit(solution)/shard_map/pallas_call | solution.py:571
  1.9 0.5 %collective-permute-start = (f32[31,4,128]{2,1,0:T(4,128)S(1)}, f32[31,4,128]{2,1,0:T(4,128)S(1)}, u32[]{:S(2)}, u32[]{:S(2)}) collective-permute-start(f32[31,4,128]{2,1,0:T(4,128)S(1)} %get-tuple-element.14), channel_id=1, source_target_pairs={{0,8},{8,0},{16,24},{24,16},{1,9},{9,1},{17,25},{25,17},{2,10},{10... | collective-permute-start | bytes 190472 | tf_op jit(solution)/shard_map/ppermute | solution.py:553
  2.4 2.6 %collective-permute-start.1 = (f32[31,4,128]{2,1,0:T(4,128)S(1)}, f32[31,4,128]{2,1,0:T(4,128)S(1)}, u32[]{:S(2)}, u32[]{:S(2)}) collective-permute-start(f32[31,4,128]{2,1,0:T(4,128)S(1)} %get-tuple-element.15), channel_id=1, source_target_pairs={{0,24},{8,16},{16,8},{24,0},{1,25},{9,17},{17,9},{25,1},{2,26},{10... | collective-permute-start | bytes 190472 | tf_op jit(solution)/shard_map/ppermute | solution.py:552
  5.0 0.4 %shard_map.51 = (f32[3,8,128]{2,1,0:T(8,128)S(1)}, f32[3,8,128]{2,1,0:T(8,128)S(1)}) custom-call(f32[19,96,128]{2,1,0:T(8,128)S(1)} %get-tuple-element.11.held.own_held, bf16[2,3,64,128]{3,2,1,0:T(8,128)(2,1)S(1)} %get-tuple-element.12.velocity, s32[16,32]{1,0:T(8,128)S(1)} %get-tuple-element.13.solid), custom_call_target="tpu_custom_call" | custom-call | flops 2000000 | bytes 1000000 | tf_op jit(solution)/shard_map/pallas_call | solution.py:586
  5.4 0.0 collective-permute-done.row_first
  5.4 1.9 %collective-permute-done.1.row_second = f32[31,4,128]{2,1,0:T(4,128)S(1)} collective-permute-done((f32[31,4,128]{2,1,0:T(4,128)S(1)}, f32[31,4,128]{2,1,0:T(4,128)S(1)}, u32[]{:S(2)}, u32[]{:S(2)}) %collective-permute-start.1) | collective-permute-done | bytes 63520 | tf_op jit(solution)/shard_map/ppermute | solution.py:552
  7.4 0.2 shard_map.52
  7.5 1.5 %collective-permute-start.3 = (f32[3,8,128]{2,1,0:T(8,128)S(1)}, f32[3,8,128]{2,1,0:T(8,128)S(1)}, u32[]{:S(2)}, u32[]{:S(2)}) collective-permute-start(f32[3,8,128]{2,1,0:T(8,128)S(1)} %get-tuple-element.19.high), channel_id=1, source_target_pairs={{0,1},{1,2},{2,3},{3,4},{4,5},{5,6},{6,7},{7,0},{8,9},{9,10},{10,1... | collective-permute-start | bytes 36872 | tf_op jit(solution)/shard_map/ppermute | solution.py:603
  9.0 5.0 %collective-permute-done.3.y_before = f32[3,8,128]{2,1,0:T(8,128)S(1)} collective-permute-done((f32[3,8,128]{2,1,0:T(8,128)S(1)}, f32[3,8,128]{2,1,0:T(8,128)S(1)}, u32[]{:S(2)}, u32[]{:S(2)}) %collective-permute-start.3) | collective-permute-done | bytes 12320 | tf_op jit(solution)/shard_map/ppermute | solution.py:603
  14.0 1.5 %shard_map.54 = f32[32,1,128]{2,1,0:T(1,128)} custom-call(f32[19,96,128]{2,1,0:T(8,128)S(1)} %get-tuple-element.11.held.own_held, bf16[2,3,64,128]{3,2,1,0:T(8,128)(2,1)S(1)} %get-tuple-element.12.velocity, s32[16,32]{1,0:T(8,128)S(1)} %get-tuple-element.13.solid, f32[31,4,128]{2,1,0:T(4,128)S(1)} %collective-permute-done.row_first, ...), custom_call_target="tpu_custom_call" | custom-call | tf_op jit(solution)/shard_map/pallas_call | solution.py:608
  15.5 3.1 %all-to-all-start = ((f32[32,1,128]{2,1,0:T(1,128)}), f32[32,1,128]{2,1,0:T(1,128)S(1)}, u32[]{:S(2)}, u32[]{:S(2)}) async-start(f32[32,1,128]{2,1,0:T(1,128)} %shard_map.54), calls=%async_computation | async-start | bytes 32768 | tf_op jit(solution)/shard_map/all_to_all | solution.py:616
  18.5 4.6 %collective-permute-start.2 = (f32[3,8,128]{2,1,0:T(8,128)S(1)}, f32[3,8,128]{2,1,0:T(8,128)S(1)}, u32[]{:S(2)}, u32[]{:S(2)}) collective-permute-start(f32[3,8,128]{2,1,0:T(8,128)S(1)} %get-tuple-element.18.low), channel_id=1, source_target_pairs={{1,0},{2,1},{3,2},{4,3},{5,4},{6,5},{7,6},{0,7},{9,8},{10,9},{11,1... | collective-permute-start | bytes 36872 | tf_op jit(solution)/shard_map/ppermute | solution.py:604
  23.1 1.4 %collective-permute-done.2.y_after = f32[3,8,128]{2,1,0:T(8,128)S(1)} collective-permute-done((f32[3,8,128]{2,1,0:T(8,128)S(1)}, f32[3,8,128]{2,1,0:T(8,128)S(1)}, u32[]{:S(2)}, u32[]{:S(2)}) %collective-permute-start.2) | collective-permute-done | bytes 12320 | tf_op jit(solution)/shard_map/ppermute | solution.py:604
  24.5 2.2 %shard_map.53 = f32[19,64,128]{2,1,0:T(8,128)} custom-call(f32[19,96,128]{2,1,0:T(8,128)S(1)} %get-tuple-element.11.held.own_held, bf16[2,3,64,128]{3,2,1,0:T(8,128)(2,1)S(1)} %get-tuple-element.12.velocity, s32[16,32]{1,0:T(8,128)S(1)} %get-tuple-element.13.solid, f32[31,4,128]{2,1,0:T(4,128)S(1)} %collective-permute-done.row_first, ...), custom_call_target="tpu_custom_call" | custom-call | flops 8000000 | bytes 4000000 | tf_op jit(solution)/shard_map/pallas_call | solution.py:617
  26.8 0.0 all-to-all-done
  26.8 0.6 %slice_reduce_fusion = f32[]{:T(128)} fusion(f32[32,1,128]{2,1,0:T(1,128)S(1)} %all-to-all-done), kind=kLoop, calls=%fused_computation | loop fusion | flops 31 | bytes 132 | tf_op jit(solution)/shard_map/reduce_sum | solution.py:628
Async XLA Ops:
  1.9 3.6 %collective-permute-start = (f32[31,4,128]{2,1,0:T(4,128)S(1)}, f32[31,4,128]{2,1,0:T(4,128)S(1)}, u32[]{:S(2)}, u32[]{:S(2)}) collective-permute-start(f32[31,4,128]{2,1,0:T(4,128)S(1)} %get-tuple-element.14), channel_id=1, source_target_pairs={{0,8},{8,0},{16,24},{24,16},{1,9},{9,1},{17,25},{25,17},{2,10},{10... | collective-permute-start | bytes 190472 | tf_op jit(solution)/shard_map/ppermute | solution.py:553
  2.4 5.0 %collective-permute-start.1 = (f32[31,4,128]{2,1,0:T(4,128)S(1)}, f32[31,4,128]{2,1,0:T(4,128)S(1)}, u32[]{:S(2)}, u32[]{:S(2)}) collective-permute-start(f32[31,4,128]{2,1,0:T(4,128)S(1)} %get-tuple-element.15), channel_id=1, source_target_pairs={{0,24},{8,16},{16,8},{24,0},{1,25},{9,17},{17,9},{25,1},{2,26},{10... | collective-permute-start | bytes 190472 | tf_op jit(solution)/shard_map/ppermute | solution.py:552
  7.5 6.4 %collective-permute-start.3 = (f32[3,8,128]{2,1,0:T(8,128)S(1)}, f32[3,8,128]{2,1,0:T(8,128)S(1)}, u32[]{:S(2)}, u32[]{:S(2)}) collective-permute-start(f32[3,8,128]{2,1,0:T(8,128)S(1)} %get-tuple-element.19.high), channel_id=1, source_target_pairs={{0,1},{1,2},{2,3},{3,4},{4,5},{5,6},{6,7},{7,0},{8,9},{9,10},{10,1... | collective-permute-start | bytes 36872 | tf_op jit(solution)/shard_map/ppermute | solution.py:603
  15.5 11.3 %all-to-all-start = ((f32[32,1,128]{2,1,0:T(1,128)}), f32[32,1,128]{2,1,0:T(1,128)S(1)}, u32[]{:S(2)}, u32[]{:S(2)}) async-start(f32[32,1,128]{2,1,0:T(1,128)} %shard_map.54), calls=%async_computation | async-start | bytes 32768 | tf_op jit(solution)/shard_map/all_to_all | solution.py:616
  18.5 6.0 %collective-permute-start.2 = (f32[3,8,128]{2,1,0:T(8,128)S(1)}, f32[3,8,128]{2,1,0:T(8,128)S(1)}, u32[]{:S(2)}, u32[]{:S(2)}) collective-permute-start(f32[3,8,128]{2,1,0:T(8,128)S(1)} %get-tuple-element.18.low), channel_id=1, source_target_pairs={{1,0},{2,1},{3,2},{4,3},{5,4},{6,5},{7,6},{0,7},{9,8},{10,9},{11,1... | collective-permute-start | bytes 36872 | tf_op jit(solution)/shard_map/ppermute | solution.py:604

commit v9 on v8

--- a/solution.py
+++ b/solution.py
@@ -612,6 +612,7 @@
         out_specs=vmem,
         scratch_shapes=[field, field, solid_field, pltpu.VMEM((9, padded, rows_y), jnp.float32)],
         compiler_params=params,
+        cost_estimate=pl.CostEstimate(flops=8_000_000, bytes_accessed=100_000_000, transcendentals=0),
     )(held, flow, tiles, *row_got, y_before, low)
     shared = lax.all_to_all(own, ("gx", "gy"), split_axis=0, concat_axis=0, tiled=True)
     result = pl.pallas_call(
@@ -621,7 +622,7 @@
         out_specs=vmem,
         scratch_shapes=[field, field, field, solid_field, pltpu.VMEM((4, 8, rows_y), jnp.float32)],
         compiler_params=params,
-        cost_estimate=pl.CostEstimate(flops=8_000_000, bytes_accessed=4_000_000, transcendentals=0),
+        cost_estimate=pl.CostEstimate(flops=8_000_000, bytes_accessed=200_000_000, transcendentals=0),
     )(held, flow, tiles, *row_got, y_after, y_before, low, high)
     cell_count = rows * rows_y * count
     scale = drag_factor / math.sqrt(cell_count) * 3.0 / 36.0

time: 29.4 us -> 29.4 us (level)
  no operation moved by 1% of the time
where the time goes in v9:
time: 29.4 us; the launch traced here: 29.2 us
  starting transfers between devices  12.3 us (42%)
  waiting for transfers between devices  8.33 us (28%)
  Pallas kernels  5.5 us (19%)
  between operations  2.45 us (8%)
  other arithmetic  0.63 us (2%)
    ppermute x1, waiting for transfers between devices, per_device(): lax.ppermute(high, 'gy', [(i, (i + 1) % size) for i in range(size)])  4.99 us
    ppermute x1, starting transfers between devices, per_device(): lax.ppermute(low, 'gy', [((i + 1) % size, i) for i in range(size)])  4.59 us
    all_to_all x1, starting transfers between devices, per_device(): lax.all_to_all(own, ('gx', 'gy'), split_axis=0, concat_axis=0, tiled=True)  3.06 us
    ppermute x1, starting transfers between devices, swap_pairs(): second = lax.ppermute(second, axis, across)  2.64 us
    pallas_call x1, Pallas kernels, per_device(): pl.pallas_call(main_kernel, out_shape=shape_of(19, rows, rows_y), in_spec...  2.22 us
    ppermute x1, waiting for transfers between devices, swap_pairs(): second = lax.ppermute(second, axis, across)  1.93 us
    pallas_call x1, Pallas kernels, per_device(): pl.pallas_call(drag_kernel, out_shape=pltpu.VMEM((count, 1, rows_y), jnp....  1.49 us
    ppermute x1, starting transfers between devices, per_device(): lax.ppermute(high, 'gy', [(i, (i + 1) % size) for i in range(size)])  1.45 us
  transfers between devices with their start and end apart: 5, of which 3 were waited for; matrix products, arithmetic and copies ran while one was open for 0% of the time, Pallas kernels for 9%

profile of v9, /device:TPU:0, one launch (start us, length us, event | category | flops | bytes accessed | tf_op | source)
XLA Modules:
  0.0 29.2 jit_solution(14639492672343685817)
XLA Ops:
  0.6 1.2 %shard_map.50 = (f32[31,4,128]{2,1,0:T(4,128)S(1)}, f32[31,4,128]{2,1,0:T(4,128)S(1)}, f32[19,96,128]{2,1,0:T(8,128)S(1)}, bf16[2,3,64,128]{3,2,1,0:T(8,128)(2,1)S(1)}, s32[16,32]{1,0:T(8,128)S(1)}) custom-call(f32[19,64,128]{2,1,0:T(8,128)} %bitcast.6, bf16[2,3,64,128]{3,2,1,0:T(8,128)(2,1)} %bitcast.7, s32[16,32]{1,0:T(8,128)} %bitcast.8), custom_call_target="tpu_custom_call" | custom-call | tf_op jit(solution)/shard_map/pallas_call | solution.py:571
  1.9 0.5 %collective-permute-start = (f32[31,4,128]{2,1,0:T(4,128)S(1)}, f32[31,4,128]{2,1,0:T(4,128)S(1)}, u32[]{:S(2)}, u32[]{:S(2)}) collective-permute-start(f32[31,4,128]{2,1,0:T(4,128)S(1)} %get-tuple-element.14), channel_id=1, source_target_pairs={{0,8},{8,0},{16,24},{24,16},{1,9},{9,1},{17,25},{25,17},{2,10},{10... | collective-permute-start | bytes 190472 | tf_op jit(solution)/shard_map/ppermute | solution.py:553
  2.4 2.6 %collective-permute-start.1 = (f32[31,4,128]{2,1,0:T(4,128)S(1)}, f32[31,4,128]{2,1,0:T(4,128)S(1)}, u32[]{:S(2)}, u32[]{:S(2)}) collective-permute-start(f32[31,4,128]{2,1,0:T(4,128)S(1)} %get-tuple-element.15), channel_id=1, source_target_pairs={{0,24},{8,16},{16,8},{24,0},{1,25},{9,17},{17,9},{25,1},{2,26},{10... | collective-permute-start | bytes 190472 | tf_op jit(solution)/shard_map/ppermute | solution.py:552
  5.0 0.4 %shard_map.51 = (f32[3,8,128]{2,1,0:T(8,128)S(1)}, f32[3,8,128]{2,1,0:T(8,128)S(1)}) custom-call(f32[19,96,128]{2,1,0:T(8,128)S(1)} %get-tuple-element.11.held.own_held, bf16[2,3,64,128]{3,2,1,0:T(8,128)(2,1)S(1)} %get-tuple-element.12.velocity, s32[16,32]{1,0:T(8,128)S(1)} %get-tuple-element.13.solid), custom_call_target="tpu_custom_call" | custom-call | flops 2000000 | bytes 1000000 | tf_op jit(solution)/shard_map/pallas_call | solution.py:586
  5.4 0.0 collective-permute-done.row_first
  5.4 1.9 %collective-permute-done.1.row_second = f32[31,4,128]{2,1,0:T(4,128)S(1)} collective-permute-done((f32[31,4,128]{2,1,0:T(4,128)S(1)}, f32[31,4,128]{2,1,0:T(4,128)S(1)}, u32[]{:S(2)}, u32[]{:S(2)}) %collective-permute-start.1) | collective-permute-done | bytes 63520 | tf_op jit(solution)/shard_map/ppermute | solution.py:552
  7.4 0.2 shard_map.52
  7.5 1.5 %collective-permute-start.3 = (f32[3,8,128]{2,1,0:T(8,128)S(1)}, f32[3,8,128]{2,1,0:T(8,128)S(1)}, u32[]{:S(2)}, u32[]{:S(2)}) collective-permute-start(f32[3,8,128]{2,1,0:T(8,128)S(1)} %get-tuple-element.19.high), channel_id=1, source_target_pairs={{0,1},{1,2},{2,3},{3,4},{4,5},{5,6},{6,7},{7,0},{8,9},{9,10},{10,1... | collective-permute-start | bytes 36872 | tf_op jit(solution)/shard_map/ppermute | solution.py:603
  9.0 5.0 %collective-permute-done.3.y_before = f32[3,8,128]{2,1,0:T(8,128)S(1)} collective-permute-done((f32[3,8,128]{2,1,0:T(8,128)S(1)}, f32[3,8,128]{2,1,0:T(8,128)S(1)}, u32[]{:S(2)}, u32[]{:S(2)}) %collective-permute-start.3) | collective-permute-done | bytes 12320 | tf_op jit(solution)/shard_map/ppermute | solution.py:603
  14.0 1.5 %shard_map.54 = f32[32,1,128]{2,1,0:T(1,128)} custom-call(f32[19,96,128]{2,1,0:T(8,128)S(1)} %get-tuple-element.11.held.own_held, bf16[2,3,64,128]{3,2,1,0:T(8,128)(2,1)S(1)} %get-tuple-element.12.velocity, s32[16,32]{1,0:T(8,128)S(1)} %get-tuple-element.13.solid, f32[31,4,128]{2,1,0:T(4,128)S(1)} %collective-permute-done.row_first, ...), custom_call_target="tpu_custom_call" | custom-call | flops 8000000 | bytes 100000000 | tf_op jit(solution)/shard_map/pallas_call | solution.py:608
  15.5 3.1 %all-to-all-start = ((f32[32,1,128]{2,1,0:T(1,128)}), f32[32,1,128]{2,1,0:T(1,128)S(1)}, u32[]{:S(2)}, u32[]{:S(2)}) async-start(f32[32,1,128]{2,1,0:T(1,128)} %shard_map.54), calls=%async_computation | async-start | bytes 32768 | tf_op jit(solution)/shard_map/all_to_all | solution.py:617
  18.5 4.6 %collective-permute-start.2 = (f32[3,8,128]{2,1,0:T(8,128)S(1)}, f32[3,8,128]{2,1,0:T(8,128)S(1)}, u32[]{:S(2)}, u32[]{:S(2)}) collective-permute-start(f32[3,8,128]{2,1,0:T(8,128)S(1)} %get-tuple-element.18.low), channel_id=1, source_target_pairs={{1,0},{2,1},{3,2},{4,3},{5,4},{6,5},{7,6},{0,7},{9,8},{10,9},{11,1... | collective-permute-start | bytes 36872 | tf_op jit(solution)/shard_map/ppermute | solution.py:604
  23.1 1.4 %collective-permute-done.2.y_after = f32[3,8,128]{2,1,0:T(8,128)S(1)} collective-permute-done((f32[3,8,128]{2,1,0:T(8,128)S(1)}, f32[3,8,128]{2,1,0:T(8,128)S(1)}, u32[]{:S(2)}, u32[]{:S(2)}) %collective-permute-start.2) | collective-permute-done | bytes 12320 | tf_op jit(solution)/shard_map/ppermute | solution.py:604
  24.5 2.2 %shard_map.53 = f32[19,64,128]{2,1,0:T(8,128)} custom-call(f32[19,96,128]{2,1,0:T(8,128)S(1)} %get-tuple-element.11.held.own_held, bf16[2,3,64,128]{3,2,1,0:T(8,128)(2,1)S(1)} %get-tuple-element.12.velocity, s32[16,32]{1,0:T(8,128)S(1)} %get-tuple-element.13.solid, f32[31,4,128]{2,1,0:T(4,128)S(1)} %collective-permute-done.row_first, ...), custom_call_target="tpu_custom_call" | custom-call | flops 8000000 | bytes 200000000 | tf_op jit(solution)/shard_map/pallas_call | solution.py:618
  26.8 0.0 all-to-all-done
  26.8 0.6 %slice_reduce_fusion = f32[]{:T(128)} fusion(f32[32,1,128]{2,1,0:T(1,128)S(1)} %all-to-all-done), kind=kLoop, calls=%fused_computation | loop fusion | flops 31 | bytes 132 | tf_op jit(solution)/shard_map/reduce_sum | solution.py:629
Async XLA Ops:
  1.9 3.6 %collective-permute-start = (f32[31,4,128]{2,1,0:T(4,128)S(1)}, f32[31,4,128]{2,1,0:T(4,128)S(1)}, u32[]{:S(2)}, u32[]{:S(2)}) collective-permute-start(f32[31,4,128]{2,1,0:T(4,128)S(1)} %get-tuple-element.14), channel_id=1, source_target_pairs={{0,8},{8,0},{16,24},{24,16},{1,9},{9,1},{17,25},{25,17},{2,10},{10... | collective-permute-start | bytes 190472 | tf_op jit(solution)/shard_map/ppermute | solution.py:553
  2.4 5.0 %collective-permute-start.1 = (f32[31,4,128]{2,1,0:T(4,128)S(1)}, f32[31,4,128]{2,1,0:T(4,128)S(1)}, u32[]{:S(2)}, u32[]{:S(2)}) collective-permute-start(f32[31,4,128]{2,1,0:T(4,128)S(1)} %get-tuple-element.15), channel_id=1, source_target_pairs={{0,24},{8,16},{16,8},{24,0},{1,25},{9,17},{17,9},{25,1},{2,26},{10... | collective-permute-start | bytes 190472 | tf_op jit(solution)/shard_map/ppermute | solution.py:552
  7.5 6.4 %collective-permute-start.3 = (f32[3,8,128]{2,1,0:T(8,128)S(1)}, f32[3,8,128]{2,1,0:T(8,128)S(1)}, u32[]{:S(2)}, u32[]{:S(2)}) collective-permute-start(f32[3,8,128]{2,1,0:T(8,128)S(1)} %get-tuple-element.19.high), channel_id=1, source_target_pairs={{0,1},{1,2},{2,3},{3,4},{4,5},{5,6},{6,7},{7,0},{8,9},{9,10},{10,1... | collective-permute-start | bytes 36872 | tf_op jit(solution)/shard_map/ppermute | solution.py:603
  15.5 11.3 %all-to-all-start = ((f32[32,1,128]{2,1,0:T(1,128)}), f32[32,1,128]{2,1,0:T(1,128)S(1)}, u32[]{:S(2)}, u32[]{:S(2)}) async-start(f32[32,1,128]{2,1,0:T(1,128)} %shard_map.54), calls=%async_computation | async-start | bytes 32768 | tf_op jit(solution)/shard_map/all_to_all | solution.py:617
  18.5 6.0 %collective-permute-start.2 = (f32[3,8,128]{2,1,0:T(8,128)S(1)}, f32[3,8,128]{2,1,0:T(8,128)S(1)}, u32[]{:S(2)}, u32[]{:S(2)}) collective-permute-start(f32[3,8,128]{2,1,0:T(8,128)S(1)} %get-tuple-element.18.low), channel_id=1, source_target_pairs={{1,0},{2,1},{3,2},{4,3},{5,4},{6,5},{7,6},{0,7},{9,8},{10,9},{11,1... | collective-permute-start | bytes 36872 | tf_op jit(solution)/shard_map/ppermute | solution.py:604

commit v10 on v8

--- a/solution.py
+++ b/solution.py
@@ -160,6 +160,7 @@
     if slot in y_down:
         insert_column(high_parts, SECOND + y_down.index(slot), group, groups, value, LANES - 2, 0)
     if NEXT <= slot < NEXT + 3:
+        insert_column(low_parts, NEXT_SECOND + slot - NEXT, group, groups, value, 1, 1)
         insert_column(high_parts, NEXT_SECOND + slot - NEXT, group, groups, value, LANES - 2, 0)
 
 
@@ -386,9 +387,8 @@
     return moved, closed, solid
 
 
-def drag_kernel(
-    own_held, velocity, solid, row_first, row_second, y_before, low, shared,
-    held, shifted, solid_rows, weights,
+def inner_drag_kernel(
+    own_held, velocity, solid, row_first, row_second, partial, held, shifted, solid_rows, weights
 ):
     rows = velocity.shape[2]
     groups = rows // 8 + 2
@@ -398,14 +398,13 @@
     after, before = Chosen(even, row_first, row_second), Chosen(even, row_second, row_first)
     lane = lane_index()
     solid_parts = spread_solid(solid)
-    column = column_reader(groups)
-
-    def edge_of(slot, cy, group):
-        return None if cy == 1 else column(y_before, 0, slot, 0, group)
+
+    def no_edge(slot, cy, group):
+        return None
 
     fill_held(own_held, before, after, held, rows)
-    fill_shifted(held, shifted, groups, edge_of)
-    fill_solid(solid_parts, before, after, solid_rows, groups, edge_of)
+    fill_shifted(held, shifted, groups, no_edge)
+    fill_solid(solid_parts, before, after, solid_rows, groups, no_edge)
 
     flow = flow_blocks(velocity, 1, rows)
     for axis in range(3):
@@ -417,9 +416,8 @@
         for group in range(groups):
             there = pl.ds(GUARD + 8 * group, 8)
             value = weights[axis, there, :]
-            edge = (1.0 - column(y_before, 0, SOLID, 0, group)) * column(y_before, 0, NEXT + axis, 0, group)
             weights[3 + axis, there, :] = shift_lanes(value, 1, None)
-            weights[6 + axis, there, :] = shift_lanes(value, -1, edge)
+            weights[6 + axis, there, :] = shift_lanes(value, -1, None)
 
     total = jnp.zeros((8, LANES), jnp.float32)
     flow = flow_blocks(velocity, 0, rows)
@@ -435,32 +433,45 @@
 
         here = [weights[axis, pl.ds(first, 8), :] for axis in range(3)]
         total = total + drag_term(moved, flow[group], fluid) + later_drag(results, closed, here, back)
-    total = jnp.where(lane < LANES - 1, total, 0.0)
+    inside = jnp.logical_and(lane > 0, lane < LANES - 1)
+    partial[...] = jnp.where(inside, total, 0.0)
+
+
+def edge_drag_kernel(groups, y_before, low, partial, shared):
+    lane = lane_index()
+    column = column_reader(groups)
 
     def neighbours(slot, cy):
-        if cy == 1:
-            return column(low, 1, slot, BEFORE_LANE)
-        if cy == -1 and slot != SOLID:
-            slot = SECOND + y_down.index(slot)
-        return column(y_before, 0, slot, BEFORE_LANE)
+        ahead = slot
+        behind = slot
+        if slot < 19 and cy == 1:
+            ahead = SECOND + y_up.index(slot)
+        if slot < 19 and cy == -1:
+            behind = SECOND + y_down.index(slot)
+        if NEXT <= slot < NEXT + 3:
+            ahead = behind = NEXT_SECOND + slot - NEXT
+        if cy == 0:
+            first, second = column(y_before, 0, slot, BEFORE_LANE), column(low, 1, slot, AFTER_LANE)
+        elif cy == 1:
+            first, second = column(low, 1, slot, BEFORE_LANE), column(low, 1, ahead, AFTER_LANE)
+        else:
+            first, second = column(y_before, 0, behind, BEFORE_LANE), column(y_before, 0, slot, AFTER_LANE)
+        return jnp.where(lane < AFTER_LANE, first, second)
 
     moved, closed, solid_columns = gather_columns(neighbours)
     fluid = {cy: 1.0 - solid_columns[cy] for cy in (0, 1, -1)}
-    column_flow = [neighbours(FLOW + axis, 0) for axis in range(3)]
-    results = collide(moved, column_flow, fluid[0])
-    weight = {
-        0: [fluid[0] * neighbours(NEXT + axis, 0) for axis in range(3)],
-        1: [fluid[1] * neighbours(NEXT + axis, 1) for axis in range(3)],
-        -1: [fluid[-1] * neighbours(NEXT_SECOND + axis, 0) for axis in range(3)],
-    }
-
-    def back_column(number, axis):
+    flow = [neighbours(FLOW + axis, 0) for axis in range(3)]
+    results = collide(moved, flow, fluid[0])
+    weight = {cy: [fluid[cy] * neighbours(NEXT + axis, cy) for axis in range(3)] for cy in (0, 1, -1)}
+
+    def back(number, axis):
         cx, cy, cz = lattice_speeds[number]
         return shift_rows(weight[-cy][axis], -cx, -cz)
 
-    term = drag_term(moved, column_flow, fluid[0]) + later_drag(results, closed, weight[0], back_column)
-    inside = jnp.logical_and(lane > BEFORE_LANE, lane < BEFORE_LANE + groups - 1)
-    total = total + jnp.where(inside, term, 0.0)
+    term = drag_term(moved, flow, fluid[0]) + later_drag(results, closed, weight[0], back)
+    place = jnp.where(lane < AFTER_LANE, lane - BEFORE_LANE, lane - AFTER_LANE)
+    inside = jnp.logical_and(place > 0, place < groups - 1)
+    total = partial[...] + jnp.where(inside, term, 0.0)
     shared[...] = jnp.broadcast_to(jnp.sum(total), shared.shape)
 
 
@@ -605,14 +616,23 @@
     count = lax.axis_size("gx") * size
     field = pltpu.VMEM((19, padded, rows_y), jnp.float32)
     solid_field = pltpu.VMEM((3, padded, rows_y), jnp.float32)
-    own = pl.pallas_call(
-        drag_kernel,
-        out_shape=pltpu.VMEM((count, 1, rows_y), jnp.float32),
-        in_specs=[vmem] * 7,
+    partial = pl.pallas_call(
+        inner_drag_kernel,
+        out_shape=pltpu.VMEM((8, rows_y), jnp.float32),
+        in_specs=[vmem] * 5,
         out_specs=vmem,
         scratch_shapes=[field, field, solid_field, pltpu.VMEM((9, padded, rows_y), jnp.float32)],
         compiler_params=params,
-    )(held, flow, tiles, *row_got, y_before, low)
+        cost_estimate=pl.CostEstimate(flops=2_000_000_000, bytes_accessed=10_000_000, transcendentals=0),
+    )(held, flow, tiles, *row_got)
+    own = pl.pallas_call(
+        functools.partial(edge_drag_kernel, groups),
+        out_shape=pltpu.VMEM((count, 1, rows_y), jnp.float32),
+        in_specs=[vmem] * 3,
+        out_specs=vmem,
+        compiler_params=params,
+        cost_estimate=pl.CostEstimate(flops=20_000_000_000, bytes_accessed=10_000_000, transcendentals=0),
+    )(y_before, low, partial)
     shared = lax.all_to_all(own, ("gx", "gy"), split_axis=0, concat_axis=0, tiled=True)
     result = pl.pallas_call(
         main_kernel,
@@ -621,7 +641,7 @@
         out_specs=vmem,
         scratch_shapes=[field, field, field, solid_field, pltpu.VMEM((4, 8, rows_y), jnp.float32)],
         compiler_params=params,
-        cost_estimate=pl.CostEstimate(flops=8_000_000, bytes_accessed=4_000_000, transcendentals=0),
+        cost_estimate=pl.CostEstimate(flops=200_000_000_000, bytes_accessed=200_000_000, transcendentals=0),
     )(held, flow, tiles, *row_got, y_after, y_before, low, high)
     cell_count = rows * rows_y * count
     scale = drag_factor / math.sqrt(cell_count) * 3.0 / 36.0

time: 29.4 us -> 33 us (1.12)
  waiting for transfers between devices: 8.33 us -> 12.4 us
  starting transfers between devices: 12.3 us -> 10.9 us
  other arithmetic: 0.63 us -> 1.36 us
    all_to_all x1, waiting for transfers between devices: 0.01 us -> 4.7 us  [per_device(): lax.all_to_all(own, ('gx', 'gy'), split_axis=0, concat_axis=0, tiled=True)]
    ppermute x1, starting transfers between devices: 1.45 us -> 0.01 us  [per_device(): lax.ppermute(high, 'gy', [(i, (i + 1) % size) for i in range(size)])]
    ppermute x1, waiting for transfers between devices: 1.41 us -> 0.01 us  [per_device(): lax.ppermute(low, 'gy', [((i + 1) % size, i) for i in range(size)])]
    ppermute x1, waiting for transfers between devices: 4.99 us -> 5.76 us  [per_device(): lax.ppermute(high, 'gy', [(i, (i + 1) % size) for i in range(size)])]
    reduce_sum x1, other arithmetic: 0.63 us -> 1.36 us  [per_device(): total = jnp.sum(shared[:, 0, 0])]
    pallas_call x1 -> x2, Pallas kernels: 1.49 us -> 1.58 us  [the longest x1 0.95 us: per_device(): pl.pallas_call(functools.partial(edge_drag_kernel, groups), out_shape=plt...]
  transfers between devices with their start and end apart: 5 -> 5, of which waited for: 3 -> 3; matrix products, arithmetic and copies ran while one was open for 0% -> 0% of each run, Pallas kernels for 9% -> 13%
where the time goes in v10:
time: 33 us; the launch traced here: 32.7 us
  waiting for transfers between devices  12.4 us (38%)
  starting transfers between devices  10.9 us (33%)
  Pallas kernels  5.62 us (17%)
  between operations  2.46 us (7%)
  other arithmetic  1.36 us (4%)
    ppermute x1, waiting for transfers between devices, per_device(): lax.ppermute(high, 'gy', [(i, (i + 1) % size) for i in range(size)])  5.76 us
    all_to_all x1, waiting for transfers between devices, per_device(): lax.all_to_all(own, ('gx', 'gy'), split_axis=0, concat_axis=0, tiled=True)  4.7 us
    ppermute x1, starting transfers between devices, per_device(): lax.ppermute(low, 'gy', [((i + 1) % size, i) for i in range(size)])  4.49 us
    all_to_all x1, starting transfers between devices, per_device(): lax.all_to_all(own, ('gx', 'gy'), split_axis=0, concat_axis=0, tiled=True)  3.2 us
    ppermute x1, starting transfers between devices, swap_pairs(): second = lax.ppermute(second, axis, across)  2.64 us
    pallas_call x1, Pallas kernels, per_device(): pl.pallas_call(main_kernel, out_shape=shape_of(19, rows, rows_y), in_spec...  2.23 us
    ppermute x1, waiting for transfers between devices, swap_pairs(): second = lax.ppermute(second, axis, across)  1.91 us
    reduce_sum x1, other arithmetic, per_device(): total = jnp.sum(shared[:, 0, 0])  1.36 us
  transfers between devices with their start and end apart: 5, of which 3 were waited for; matrix products, arithmetic and copies ran while one was open for 0% of the time, Pallas kernels for 13%

profile of v10, /device:TPU:0, one launch (start us, length us, event | category | flops | bytes accessed | tf_op | source)
XLA Modules:
  0.0 32.7 jit_solution(8523620980532470491)
XLA Ops:
  0.6 1.2 %shard_map.50 = (f32[31,4,128]{2,1,0:T(4,128)S(1)}, f32[31,4,128]{2,1,0:T(4,128)S(1)}, f32[19,96,128]{2,1,0:T(8,128)S(1)}, bf16[2,3,64,128]{3,2,1,0:T(8,128)(2,1)S(1)}, s32[16,32]{1,0:T(8,128)S(1)}) custom-call(f32[19,64,128]{2,1,0:T(8,128)} %bitcast.5, bf16[2,3,64,128]{3,2,1,0:T(8,128)(2,1)} %bitcast.6, s32[16,32]{1,0:T(8,128)} %bitcast.7), custom_call_target="tpu_custom_call" | custom-call | tf_op jit(solution)/shard_map/pallas_call | solution.py:582
  1.9 0.5 %collective-permute-start = (f32[31,4,128]{2,1,0:T(4,128)S(1)}, f32[31,4,128]{2,1,0:T(4,128)S(1)}, u32[]{:S(2)}, u32[]{:S(2)}) collective-permute-start(f32[31,4,128]{2,1,0:T(4,128)S(1)} %get-tuple-element.14), channel_id=1, source_target_pairs={{0,8},{8,0},{16,24},{24,16},{1,9},{9,1},{17,25},{25,17},{2,10},{10... | collective-permute-start | bytes 190472 | tf_op jit(solution)/shard_map/ppermute | solution.py:564
  2.4 2.6 %collective-permute-start.1 = (f32[31,4,128]{2,1,0:T(4,128)S(1)}, f32[31,4,128]{2,1,0:T(4,128)S(1)}, u32[]{:S(2)}, u32[]{:S(2)}) collective-permute-start(f32[31,4,128]{2,1,0:T(4,128)S(1)} %get-tuple-element.15), channel_id=1, source_target_pairs={{0,24},{8,16},{16,8},{24,0},{1,25},{9,17},{17,9},{25,1},{2,26},{10... | collective-permute-start | bytes 190472 | tf_op jit(solution)/shard_map/ppermute | solution.py:563
  5.0 0.4 %shard_map.51 = (f32[3,8,128]{2,1,0:T(8,128)S(1)}, f32[3,8,128]{2,1,0:T(8,128)S(1)}) custom-call(f32[19,96,128]{2,1,0:T(8,128)S(1)} %get-tuple-element.11.held.own_held, bf16[2,3,64,128]{3,2,1,0:T(8,128)(2,1)S(1)} %get-tuple-element.12.velocity, s32[16,32]{1,0:T(8,128)S(1)} %get-tuple-element.13.solid), custom_call_target="tpu_custom_call" | custom-call | flops 2000000 | bytes 1000000 | tf_op jit(solution)/shard_map/pallas_call | solution.py:597
  5.4 0.0 collective-permute-done.row_first
  5.5 1.9 %collective-permute-done.1.row_second = f32[31,4,128]{2,1,0:T(4,128)S(1)} collective-permute-done((f32[31,4,128]{2,1,0:T(4,128)S(1)}, f32[31,4,128]{2,1,0:T(4,128)S(1)}, u32[]{:S(2)}, u32[]{:S(2)}) %collective-permute-start.1) | collective-permute-done | bytes 63520 | tf_op jit(solution)/shard_map/ppermute | solution.py:563
  7.4 0.2 shard_map.52
  7.5 4.5 %collective-permute-start.2 = (f32[3,8,128]{2,1,0:T(8,128)S(1)}, f32[3,8,128]{2,1,0:T(8,128)S(1)}, u32[]{:S(2)}, u32[]{:S(2)}) collective-permute-start(f32[3,8,128]{2,1,0:T(8,128)S(1)} %get-tuple-element.18.low), channel_id=1, source_target_pairs={{1,0},{2,1},{3,2},{4,3},{5,4},{6,5},{7,6},{0,7},{9,8},{10,9},{11,1... | collective-permute-start | bytes 36872 | tf_op jit(solution)/shard_map/ppermute | solution.py:615
  12.0 0.0 collective-permute-start.3
  12.0 0.6 %shard_map.54.partial = f32[8,128]{1,0:T(8,128)S(1)} custom-call(f32[19,96,128]{2,1,0:T(8,128)S(1)} %get-tuple-element.11.held.own_held, bf16[2,3,64,128]{3,2,1,0:T(8,128)(2,1)S(1)} %get-tuple-element.12.velocity, s32[16,32]{1,0:T(8,128)S(1)} %get-tuple-element.13.solid, f32[31,4,128]{2,1,0:T(4,128)S(1)} %collective-permute-done.row_first, ...), custom_call_target="tpu_custom_call" | custom-call | flops 2000000000 | bytes 10000000 | tf_op jit(solution)/shard_map/pallas_call | solution.py:619
  12.7 5.8 %collective-permute-done.3.y_before = f32[3,8,128]{2,1,0:T(8,128)S(1)} collective-permute-done((f32[3,8,128]{2,1,0:T(8,128)S(1)}, f32[3,8,128]{2,1,0:T(8,128)S(1)}, u32[]{:S(2)}, u32[]{:S(2)}) %collective-permute-start.3) | collective-permute-done | bytes 12320 | tf_op jit(solution)/shard_map/ppermute | solution.py:614
  18.4 1.0 %shard_map.55 = f32[32,1,128]{2,1,0:T(1,128)} custom-call(f32[3,8,128]{2,1,0:T(8,128)S(1)} %collective-permute-done.3.y_before, f32[3,8,128]{2,1,0:T(8,128)S(1)} %get-tuple-element.18.low, f32[8,128]{1,0:T(8,128)S(1)} %shard_map.54.partial), custom_call_target="tpu_custom_call" | custom-call | flops 20000000000 | bytes 10000000 | tf_op jit(solution)/shard_map/pallas_call | solution.py:628
  19.4 3.2 %all-to-all-start = ((f32[32,1,128]{2,1,0:T(1,128)}), f32[32,1,128]{2,1,0:T(1,128)}, u32[]{:S(2)}, u32[]{:S(2)}) async-start(f32[32,1,128]{2,1,0:T(1,128)} %shard_map.55), calls=%async_computation | async-start | bytes 32768 | tf_op jit(solution)/shard_map/all_to_all | solution.py:636
  22.6 0.0 collective-permute-done.2.y_after
  22.6 2.2 %shard_map.53 = f32[19,64,128]{2,1,0:T(8,128)} custom-call(f32[19,96,128]{2,1,0:T(8,128)S(1)} %get-tuple-element.11.held.own_held, bf16[2,3,64,128]{3,2,1,0:T(8,128)(2,1)S(1)} %get-tuple-element.12.velocity, s32[16,32]{1,0:T(8,128)S(1)} %get-tuple-element.13.solid, f32[31,4,128]{2,1,0:T(4,128)S(1)} %collective-permute-done.row_first, ...), custom_call_target="tpu_custom_call" | custom-call | flops 199999995904 | bytes 200000000 | tf_op jit(solution)/shard_map/pallas_call | solution.py:637
  24.8 4.7 %all-to-all-done = f32[32,1,128]{2,1,0:T(1,128)} async-done(((f32[32,1,128]{2,1,0:T(1,128)}), f32[32,1,128]{2,1,0:T(1,128)}, u32[]{:S(2)}, u32[]{:S(2)}) %all-to-all-start) | async-done | bytes 16416 | tf_op jit(solution)/shard_map/all_to_all | solution.py:636
  29.5 1.4 %slice_reduce_fusion = f32[]{:T(128)} fusion(f32[32,1,128]{2,1,0:T(1,128)} %all-to-all-done), kind=kLoop, calls=%fused_computation | loop fusion | flops 31 | bytes 132 | tf_op jit(solution)/shard_map/reduce_sum | solution.py:648
Async XLA Ops:
  1.9 3.6 %collective-permute-start = (f32[31,4,128]{2,1,0:T(4,128)S(1)}, f32[31,4,128]{2,1,0:T(4,128)S(1)}, u32[]{:S(2)}, u32[]{:S(2)}) collective-permute-start(f32[31,4,128]{2,1,0:T(4,128)S(1)} %get-tuple-element.14), channel_id=1, source_target_pairs={{0,8},{8,0},{16,24},{24,16},{1,9},{9,1},{17,25},{25,17},{2,10},{10... | collective-permute-start | bytes 190472 | tf_op jit(solution)/shard_map/ppermute | solution.py:564
  2.4 5.0 %collective-permute-start.1 = (f32[31,4,128]{2,1,0:T(4,128)S(1)}, f32[31,4,128]{2,1,0:T(4,128)S(1)}, u32[]{:S(2)}, u32[]{:S(2)}) collective-permute-start(f32[31,4,128]{2,1,0:T(4,128)S(1)} %get-tuple-element.15), channel_id=1, source_target_pairs={{0,24},{8,16},{16,8},{24,0},{1,25},{9,17},{17,9},{25,1},{2,26},{10... | collective-permute-start | bytes 190472 | tf_op jit(solution)/shard_map/ppermute | solution.py:563
  7.5 15.1 %collective-permute-start.2 = (f32[3,8,128]{2,1,0:T(8,128)S(1)}, f32[3,8,128]{2,1,0:T(8,128)S(1)}, u32[]{:S(2)}, u32[]{:S(2)}) collective-permute-start(f32[3,8,128]{2,1,0:T(8,128)S(1)} %get-tuple-element.18.low), channel_id=1, source_target_pairs={{1,0},{2,1},{3,2},{4,3},{5,4},{6,5},{7,6},{0,7},{9,8},{10,9},{11,1... | collective-permute-start | bytes 36872 | tf_op jit(solution)/shard_map/ppermute | solution.py:615
  12.0 6.4 %collective-permute-start.3 = (f32[3,8,128]{2,1,0:T(8,128)S(1)}, f32[3,8,128]{2,1,0:T(8,128)S(1)}, u32[]{:S(2)}, u32[]{:S(2)}) collective-permute-start(f32[3,8,128]{2,1,0:T(8,128)S(1)} %get-tuple-element.19.high), channel_id=1, source_target_pairs={{0,1},{1,2},{2,3},{3,4},{4,5},{5,6},{6,7},{7,0},{8,9},{9,10},{10,1... | collective-permute-start | bytes 36872 | tf_op jit(solution)/shard_map/ppermute | solution.py:614
  19.4 10.2 %all-to-all-start = ((f32[32,1,128]{2,1,0:T(1,128)}), f32[32,1,128]{2,1,0:T(1,128)}, u32[]{:S(2)}, u32[]{:S(2)}) async-start(f32[32,1,128]{2,1,0:T(1,128)} %shard_map.55), calls=%async_computation | async-start | bytes 32768 | tf_op jit(solution)/shard_map/all_to_all | solution.py:636

commit v11 on v10

--- a/solution.py
+++ b/solution.py
@@ -623,7 +623,7 @@
         out_specs=vmem,
         scratch_shapes=[field, field, solid_field, pltpu.VMEM((9, padded, rows_y), jnp.float32)],
         compiler_params=params,
-        cost_estimate=pl.CostEstimate(flops=2_000_000_000, bytes_accessed=10_000_000, transcendentals=0),
+        cost_estimate=pl.CostEstimate(flops=1_000_000, bytes_accessed=1_000_000, transcendentals=0),
     )(held, flow, tiles, *row_got)
     own = pl.pallas_call(
         functools.partial(edge_drag_kernel, groups),

time: 33 us -> 28.5 us (0.86)
  waiting for transfers between devices: 12.4 us -> 7.66 us
    ppermute x1, waiting for transfers between devices: 5.76 us -> 1.04 us  [per_device(): lax.ppermute(high, 'gy', [(i, (i + 1) % size) for i in range(size)])]
    ppermute x1, starting transfers between devices: 0.01 us -> 1.45 us  [per_device(): lax.ppermute(high, 'gy', [(i, (i + 1) % size) for i in range(size)])]
    ppermute x1, starting transfers between devices: 4.49 us -> 3.32 us  [per_device(): lax.ppermute(low, 'gy', [((i + 1) % size, i) for i in range(size)])]
  transfers between devices with their start and end apart: 5 -> 5, of which waited for: 3 -> 3; matrix products, arithmetic and copies ran while one was open for 0% -> 0% of each run, Pallas kernels for 13% -> 15%
where the time goes in v11:
time: 28.5 us; the launch traced here: 28.2 us
  starting transfers between devices  11.1 us (39%)
  waiting for transfers between devices  7.66 us (27%)
  Pallas kernels  5.62 us (20%)
  between operations  2.46 us (9%)
  other arithmetic  1.36 us (5%)
    all_to_all x1, waiting for transfers between devices, per_device(): lax.all_to_all(own, ('gx', 'gy'), split_axis=0, concat_axis=0, tiled=True)  4.7 us
    ppermute x1, starting transfers between devices, per_device(): lax.ppermute(low, 'gy', [((i + 1) % size, i) for i in range(size)])  3.32 us
    all_to_all x1, starting transfers between devices, per_device(): lax.all_to_all(own, ('gx', 'gy'), split_axis=0, concat_axis=0, tiled=True)  3.21 us
    ppermute x1, starting transfers between devices, swap_pairs(): second = lax.ppermute(second, axis, across)  2.64 us
    pallas_call x1, Pallas kernels, per_device(): pl.pallas_call(main_kernel, out_shape=shape_of(19, rows, rows_y), in_spec...  2.23 us
    ppermute x1, waiting for transfers between devices, swap_pairs(): second = lax.ppermute(second, axis, across)  1.91 us
    ppermute x1, starting transfers between devices, per_device(): lax.ppermute(high, 'gy', [(i, (i + 1) % size) for i in range(size)])  1.45 us
    reduce_sum x1, other arithmetic, per_device(): total = jnp.sum(shared[:, 0, 0])  1.36 us
  transfers between devices with their start and end apart: 5, of which 3 were waited for; matrix products, arithmetic and copies ran while one was open for 0% of the time, Pallas kernels for 15%

profile of v11, /device:TPU:0, one launch (start us, length us, event | category | flops | bytes accessed | tf_op | source)
XLA Modules:
  0.0 28.2 jit_solution(18149212302731911454)
XLA Ops:
  0.6 1.2 %shard_map.50 = (f32[31,4,128]{2,1,0:T(4,128)S(1)}, f32[31,4,128]{2,1,0:T(4,128)S(1)}, f32[19,96,128]{2,1,0:T(8,128)S(1)}, bf16[2,3,64,128]{3,2,1,0:T(8,128)(2,1)S(1)}, s32[16,32]{1,0:T(8,128)S(1)}) custom-call(f32[19,64,128]{2,1,0:T(8,128)} %bitcast.5, bf16[2,3,64,128]{3,2,1,0:T(8,128)(2,1)} %bitcast.6, s32[16,32]{1,0:T(8,128)} %bitcast.7), custom_call_target="tpu_custom_call" | custom-call | tf_op jit(solution)/shard_map/pallas_call | solution.py:582
  1.9 0.5 %collective-permute-start = (f32[31,4,128]{2,1,0:T(4,128)S(1)}, f32[31,4,128]{2,1,0:T(4,128)S(1)}, u32[]{:S(2)}, u32[]{:S(2)}) collective-permute-start(f32[31,4,128]{2,1,0:T(4,128)S(1)} %get-tuple-element.14), channel_id=1, source_target_pairs={{0,8},{8,0},{16,24},{24,16},{1,9},{9,1},{17,25},{25,17},{2,10},{10... | collective-permute-start | bytes 190472 | tf_op jit(solution)/shard_map/ppermute | solution.py:564
  2.4 2.6 %collective-permute-start.1 = (f32[31,4,128]{2,1,0:T(4,128)S(1)}, f32[31,4,128]{2,1,0:T(4,128)S(1)}, u32[]{:S(2)}, u32[]{:S(2)}) collective-permute-start(f32[31,4,128]{2,1,0:T(4,128)S(1)} %get-tuple-element.15), channel_id=1, source_target_pairs={{0,24},{8,16},{16,8},{24,0},{1,25},{9,17},{17,9},{25,1},{2,26},{10... | collective-permute-start | bytes 190472 | tf_op jit(solution)/shard_map/ppermute | solution.py:563
  5.0 0.4 %shard_map.51 = (f32[3,8,128]{2,1,0:T(8,128)S(1)}, f32[3,8,128]{2,1,0:T(8,128)S(1)}) custom-call(f32[19,96,128]{2,1,0:T(8,128)S(1)} %get-tuple-element.11.held.own_held, bf16[2,3,64,128]{3,2,1,0:T(8,128)(2,1)S(1)} %get-tuple-element.12.velocity, s32[16,32]{1,0:T(8,128)S(1)} %get-tuple-element.13.solid), custom_call_target="tpu_custom_call" | custom-call | flops 2000000 | bytes 1000000 | tf_op jit(solution)/shard_map/pallas_call | solution.py:597
  5.4 0.0 collective-permute-done.row_first
  5.5 1.9 %collective-permute-done.1.row_second = f32[31,4,128]{2,1,0:T(4,128)S(1)} collective-permute-done((f32[31,4,128]{2,1,0:T(4,128)S(1)}, f32[31,4,128]{2,1,0:T(4,128)S(1)}, u32[]{:S(2)}, u32[]{:S(2)}) %collective-permute-start.1) | collective-permute-done | bytes 63520 | tf_op jit(solution)/shard_map/ppermute | solution.py:563
  7.4 0.2 shard_map.52
  7.5 1.5 %collective-permute-start.3 = (f32[3,8,128]{2,1,0:T(8,128)S(1)}, f32[3,8,128]{2,1,0:T(8,128)S(1)}, u32[]{:S(2)}, u32[]{:S(2)}) collective-permute-start(f32[3,8,128]{2,1,0:T(8,128)S(1)} %get-tuple-element.19.high), channel_id=1, source_target_pairs={{0,1},{1,2},{2,3},{3,4},{4,5},{5,6},{6,7},{7,0},{8,9},{9,10},{10,1... | collective-permute-start | bytes 36872 | tf_op jit(solution)/shard_map/ppermute | solution.py:614
  9.0 3.3 %collective-permute-start.2 = (f32[3,8,128]{2,1,0:T(8,128)S(1)}, f32[3,8,128]{2,1,0:T(8,128)S(1)}, u32[]{:S(2)}, u32[]{:S(2)}) collective-permute-start(f32[3,8,128]{2,1,0:T(8,128)S(1)} %get-tuple-element.18.low), channel_id=1, source_target_pairs={{1,0},{2,1},{3,2},{4,3},{5,4},{6,5},{7,6},{0,7},{9,8},{10,9},{11,1... | collective-permute-start | bytes 36872 | tf_op jit(solution)/shard_map/ppermute | solution.py:615
  12.3 0.6 %shard_map.54.partial = f32[8,128]{1,0:T(8,128)S(1)} custom-call(f32[19,96,128]{2,1,0:T(8,128)S(1)} %get-tuple-element.11.held.own_held, bf16[2,3,64,128]{3,2,1,0:T(8,128)(2,1)S(1)} %get-tuple-element.12.velocity, s32[16,32]{1,0:T(8,128)S(1)} %get-tuple-element.13.solid, f32[31,4,128]{2,1,0:T(4,128)S(1)} %collective-permute-done.row_first, ...), custom_call_target="tpu_custom_call" | custom-call | flops 1000000 | bytes 1000000 | tf_op jit(solution)/shard_map/pallas_call | solution.py:619
  12.9 1.0 %collective-permute-done.3.y_before = f32[3,8,128]{2,1,0:T(8,128)S(1)} collective-permute-done((f32[3,8,128]{2,1,0:T(8,128)S(1)}, f32[3,8,128]{2,1,0:T(8,128)S(1)}, u32[]{:S(2)}, u32[]{:S(2)}) %collective-permute-start.3) | collective-permute-done | bytes 12320 | tf_op jit(solution)/shard_map/ppermute | solution.py:614
  14.0 1.0 %shard_map.55 = f32[32,1,128]{2,1,0:T(1,128)} custom-call(f32[3,8,128]{2,1,0:T(8,128)S(1)} %collective-permute-done.3.y_before, f32[3,8,128]{2,1,0:T(8,128)S(1)} %get-tuple-element.18.low, f32[8,128]{1,0:T(8,128)S(1)} %shard_map.54.partial), custom_call_target="tpu_custom_call" | custom-call | flops 20000000000 | bytes 10000000 | tf_op jit(solution)/shard_map/pallas_call | solution.py:628
  14.9 3.2 %all-to-all-start = ((f32[32,1,128]{2,1,0:T(1,128)}), f32[32,1,128]{2,1,0:T(1,128)}, u32[]{:S(2)}, u32[]{:S(2)}) async-start(f32[32,1,128]{2,1,0:T(1,128)} %shard_map.55), calls=%async_computation | async-start | bytes 32768 | tf_op jit(solution)/shard_map/all_to_all | solution.py:636
  18.2 0.0 collective-permute-done.2.y_after
  18.2 2.2 %shard_map.53 = f32[19,64,128]{2,1,0:T(8,128)} custom-call(f32[19,96,128]{2,1,0:T(8,128)S(1)} %get-tuple-element.11.held.own_held, bf16[2,3,64,128]{3,2,1,0:T(8,128)(2,1)S(1)} %get-tuple-element.12.velocity, s32[16,32]{1,0:T(8,128)S(1)} %get-tuple-element.13.solid, f32[31,4,128]{2,1,0:T(4,128)S(1)} %collective-permute-done.row_first, ...), custom_call_target="tpu_custom_call" | custom-call | flops 199999995904 | bytes 200000000 | tf_op jit(solution)/shard_map/pallas_call | solution.py:637
  20.4 4.7 %all-to-all-done = f32[32,1,128]{2,1,0:T(1,128)} async-done(((f32[32,1,128]{2,1,0:T(1,128)}), f32[32,1,128]{2,1,0:T(1,128)}, u32[]{:S(2)}, u32[]{:S(2)}) %all-to-all-start) | async-done | bytes 16416 | tf_op jit(solution)/shard_map/all_to_all | solution.py:636
  25.1 1.4 %slice_reduce_fusion = f32[]{:T(128)} fusion(f32[32,1,128]{2,1,0:T(1,128)} %all-to-all-done), kind=kLoop, calls=%fused_computation | loop fusion | flops 31 | bytes 132 | tf_op jit(solution)/shard_map/reduce_sum | solution.py:648
Async XLA Ops:
  1.9 3.6 %collective-permute-start = (f32[31,4,128]{2,1,0:T(4,128)S(1)}, f32[31,4,128]{2,1,0:T(4,128)S(1)}, u32[]{:S(2)}, u32[]{:S(2)}) collective-permute-start(f32[31,4,128]{2,1,0:T(4,128)S(1)} %get-tuple-element.14), channel_id=1, source_target_pairs={{0,8},{8,0},{16,24},{24,16},{1,9},{9,1},{17,25},{25,17},{2,10},{10... | collective-permute-start | bytes 190472 | tf_op jit(solution)/shard_map/ppermute | solution.py:564
  2.4 5.0 %collective-permute-start.1 = (f32[31,4,128]{2,1,0:T(4,128)S(1)}, f32[31,4,128]{2,1,0:T(4,128)S(1)}, u32[]{:S(2)}, u32[]{:S(2)}) collective-permute-start(f32[31,4,128]{2,1,0:T(4,128)S(1)} %get-tuple-element.15), channel_id=1, source_target_pairs={{0,24},{8,16},{16,8},{24,0},{1,25},{9,17},{17,9},{25,1},{2,26},{10... | collective-permute-start | bytes 190472 | tf_op jit(solution)/shard_map/ppermute | solution.py:563
  7.5 6.4 %collective-permute-start.3 = (f32[3,8,128]{2,1,0:T(8,128)S(1)}, f32[3,8,128]{2,1,0:T(8,128)S(1)}, u32[]{:S(2)}, u32[]{:S(2)}) collective-permute-start(f32[3,8,128]{2,1,0:T(8,128)S(1)} %get-tuple-element.19.high), channel_id=1, source_target_pairs={{0,1},{1,2},{2,3},{3,4},{4,5},{5,6},{6,7},{7,0},{8,9},{9,10},{10,1... | collective-permute-start | bytes 36872 | tf_op jit(solution)/shard_map/ppermute | solution.py:614
  9.0 9.2 %collective-permute-start.2 = (f32[3,8,128]{2,1,0:T(8,128)S(1)}, f32[3,8,128]{2,1,0:T(8,128)S(1)}, u32[]{:S(2)}, u32[]{:S(2)}) collective-permute-start(f32[3,8,128]{2,1,0:T(8,128)S(1)} %get-tuple-element.18.low), channel_id=1, source_target_pairs={{1,0},{2,1},{3,2},{4,3},{5,4},{6,5},{7,6},{0,7},{9,8},{10,9},{11,1... | collective-permute-start | bytes 36872 | tf_op jit(solution)/shard_map/ppermute | solution.py:615
  14.9 10.2 %all-to-all-start = ((f32[32,1,128]{2,1,0:T(1,128)}), f32[32,1,128]{2,1,0:T(1,128)}, u32[]{:S(2)}, u32[]{:S(2)}) async-start(f32[32,1,128]{2,1,0:T(1,128)} %shard_map.55), calls=%async_computation | async-start | bytes 32768 | tf_op jit(solution)/shard_map/all_to_all | solution.py:636

commit v12 on v11

--- a/solution.py
+++ b/solution.py
@@ -307,8 +307,7 @@
     for number in range(1, 19):
         cx = lattice_speeds[number][0]
         here = along_link(number, lambda axis: weight_here[axis])
-        back = along_link(number, lambda axis: weight_back(number, axis))
-        part = jnp.where(closed[opposite_of(number)], -here, back) * results[number]
+        part = jnp.where(closed[opposite_of(number)], -here, weight_back(number)) * results[number]
         if cx != 0:
             part = part + jnp.where(closed[number], (2.0 * cx) * here, 0.0)
         if number < 7:
@@ -388,7 +387,8 @@
 
 
 def inner_drag_kernel(
-    own_held, velocity, solid, row_first, row_second, partial, held, shifted, solid_rows, weights
+    own_held, velocity, solid, row_first, row_second, low, partial, own_blocks,
+    held, shifted, solid_rows, weights,
 ):
     rows = velocity.shape[2]
     groups = rows // 8 + 2
@@ -427,35 +427,46 @@
         fluid = 1.0 - solid_parts[8 * group // (LEVELS * TILE)]
         results = collide(moved, flow[group], fluid)
 
-        def back(number, axis):
+        def back(number):
             cx, cy, cz = lattice_speeds[number]
-            return weights[3 * (-cy % 3) + axis, pl.ds(first - LEVELS * cx - cz, 8), :]
+            there = pl.ds(first - LEVELS * cx - cz, 8)
+            return along_link(number, lambda axis: weights[3 * (-cy % 3) + axis, there, :])
 
         here = [weights[axis, pl.ds(first, 8), :] for axis in range(3)]
         total = total + drag_term(moved, flow[group], fluid) + later_drag(results, closed, here, back)
     inside = jnp.logical_and(lane > 0, lane < LANES - 1)
     partial[...] = jnp.where(inside, total, 0.0)
 
-
-def edge_drag_kernel(groups, y_before, low, partial, shared):
+    column = column_reader(groups)
+    for slot in range(SECOND):
+        own_blocks[slot] = column(low, 1, slot, AFTER_LANE)
+    for place, slot in enumerate(ahead_slots):
+        here = column(low, 1, slot, BEFORE_LANE)
+        ahead = column(low, 1, second_slot(slot, y_up), AFTER_LANE)
+        own_blocks[SECOND + place] = jnp.where(lane < AFTER_LANE, here, ahead)
+
+
+ahead_slots = y_up + [SOLID, NEXT, NEXT + 1, NEXT + 2]
+
+
+def second_slot(slot, moving):
+    if slot in moving:
+        return SECOND + moving.index(slot)
+    return NEXT_SECOND + slot - NEXT if NEXT <= slot < NEXT + 3 else slot
+
+
+def edge_drag_kernel(groups, y_before, own_blocks, partial, shared):
     lane = lane_index()
     column = column_reader(groups)
 
     def neighbours(slot, cy):
-        ahead = slot
-        behind = slot
-        if slot < 19 and cy == 1:
-            ahead = SECOND + y_up.index(slot)
-        if slot < 19 and cy == -1:
-            behind = SECOND + y_down.index(slot)
-        if NEXT <= slot < NEXT + 3:
-            ahead = behind = NEXT_SECOND + slot - NEXT
+        if cy == 1:
+            return own_blocks[SECOND + ahead_slots.index(slot)]
         if cy == 0:
-            first, second = column(y_before, 0, slot, BEFORE_LANE), column(low, 1, slot, AFTER_LANE)
-        elif cy == 1:
-            first, second = column(low, 1, slot, BEFORE_LANE), column(low, 1, ahead, AFTER_LANE)
+            first, second = column(y_before, 0, slot, BEFORE_LANE), own_blocks[slot]
         else:
-            first, second = column(y_before, 0, behind, BEFORE_LANE), column(y_before, 0, slot, AFTER_LANE)
+            first = column(y_before, 0, second_slot(slot, y_down), BEFORE_LANE)
+            second = column(y_before, 0, slot, AFTER_LANE)
         return jnp.where(lane < AFTER_LANE, first, second)
 
     moved, closed, solid_columns = gather_columns(neighbours)
@@ -464,9 +475,9 @@
     results = collide(moved, flow, fluid[0])
     weight = {cy: [fluid[cy] * neighbours(NEXT + axis, cy) for axis in range(3)] for cy in (0, 1, -1)}
 
-    def back(number, axis):
+    def back(number):
         cx, cy, cz = lattice_speeds[number]
-        return shift_rows(weight[-cy][axis], -cx, -cz)
+        return shift_rows(along_link(number, lambda axis: weight[-cy][axis]), -cx, -cz)
 
     term = drag_term(moved, flow, fluid[0]) + later_drag(results, closed, weight[0], back)
     place = jnp.where(lane < AFTER_LANE, lane - BEFORE_LANE, lane - AFTER_LANE)
@@ -616,15 +627,18 @@
     count = lax.axis_size("gx") * size
     field = pltpu.VMEM((19, padded, rows_y), jnp.float32)
     solid_field = pltpu.VMEM((3, padded, rows_y), jnp.float32)
-    partial = pl.pallas_call(
+    partial, own_blocks = pl.pallas_call(
         inner_drag_kernel,
-        out_shape=pltpu.VMEM((8, rows_y), jnp.float32),
-        in_specs=[vmem] * 5,
-        out_specs=vmem,
+        out_shape=(
+            pltpu.VMEM((8, rows_y), jnp.float32),
+            pltpu.VMEM((SECOND + len(ahead_slots), 8, rows_y), jnp.float32),
+        ),
+        in_specs=[vmem] * 6,
+        out_specs=(vmem,) * 2,
         scratch_shapes=[field, field, solid_field, pltpu.VMEM((9, padded, rows_y), jnp.float32)],
         compiler_params=params,
         cost_estimate=pl.CostEstimate(flops=1_000_000, bytes_accessed=1_000_000, transcendentals=0),
-    )(held, flow, tiles, *row_got)
+    )(held, flow, tiles, *row_got, low)
     own = pl.pallas_call(
         functools.partial(edge_drag_kernel, groups),
         out_shape=pltpu.VMEM((count, 1, rows_y), jnp.float32),
@@ -632,7 +646,7 @@
         out_specs=vmem,
         compiler_params=params,
         cost_estimate=pl.CostEstimate(flops=20_000_000_000, bytes_accessed=10_000_000, transcendentals=0),
-    )(y_before, low, partial)
+    )(y_before, own_blocks, partial)
     shared = lax.all_to_all(own, ("gx", "gy"), split_axis=0, concat_axis=0, tiled=True)
     result = pl.pallas_call(
         main_kernel,
@@ -641,7 +655,7 @@
         out_specs=vmem,
         scratch_shapes=[field, field, field, solid_field, pltpu.VMEM((4, 8, rows_y), jnp.float32)],
         compiler_params=params,
-        cost_estimate=pl.CostEstimate(flops=200_000_000_000, bytes_accessed=200_000_000, transcendentals=0),
+        cost_estimate=pl.CostEstimate(flops=20_000_000_000, bytes_accessed=4_000_000, transcendentals=0),
     )(held, flow, tiles, *row_got, y_after, y_before, low, high)
     cell_count = rows * rows_y * count
     scale = drag_factor / math.sqrt(cell_count) * 3.0 / 36.0

time: 28.5 us -> 27.7 us (0.972)
  other arithmetic: 1.36 us -> 0.63 us
    reduce_sum x1, other arithmetic: 1.36 us -> 0.63 us  [per_device(): total = jnp.sum(shared[:, 0, 0])]
where the time goes in v12:
time: 27.7 us; the launch traced here: 27.5 us
  starting transfers between devices  11 us (40%)
  waiting for transfers between devices  7.83 us (28%)
  Pallas kernels  5.58 us (20%)
  between operations  2.46 us (9%)
  other arithmetic  0.63 us (2%)
    all_to_all x1, waiting for transfers between devices, per_device(): lax.all_to_all(own, ('gx', 'gy'), split_axis=0, concat_axis=0, tiled=True)  4.88 us
    ppermute x1, starting transfers between devices, per_device(): lax.ppermute(low, 'gy', [((i + 1) % size, i) for i in range(size)])  3.32 us
    all_to_all x1, starting transfers between devices, per_device(): lax.all_to_all(own, ('gx', 'gy'), split_axis=0, concat_axis=0, tiled=True)  3.06 us
    ppermute x1, starting transfers between devices, swap_pairs(): second = lax.ppermute(second, axis, across)  2.64 us
    pallas_call x1, Pallas kernels, per_device(): pl.pallas_call(main_kernel, out_shape=shape_of(19, rows, rows_y), in_spec...  2.23 us
    ppermute x1, waiting for transfers between devices, swap_pairs(): second = lax.ppermute(second, axis, across)  1.91 us
    ppermute x1, starting transfers between devices, per_device(): lax.ppermute(high, 'gy', [(i, (i + 1) % size) for i in range(size)])  1.45 us
    pallas_call x1, Pallas kernels, per_device(): pl.pallas_call(row_message_kernel, out_shape=(pltpu.VMEM((QUANTITIES, lev...  1.24 us
  transfers between devices with their start and end apart: 5, of which 3 were waited for; matrix products, arithmetic and copies ran while one was open for 0% of the time, Pallas kernels for 15%

profile of v12, /device:TPU:0, one launch (start us, length us, event | category | flops | bytes accessed | tf_op | source)
XLA Modules:
  0.0 27.5 jit_solution(17411045318744615233)
XLA Ops:
  0.6 1.2 %shard_map.50 = (f32[31,4,128]{2,1,0:T(4,128)S(1)}, f32[31,4,128]{2,1,0:T(4,128)S(1)}, f32[19,96,128]{2,1,0:T(8,128)S(1)}, bf16[2,3,64,128]{3,2,1,0:T(8,128)(2,1)S(1)}, s32[16,32]{1,0:T(8,128)S(1)}) custom-call(f32[19,64,128]{2,1,0:T(8,128)} %bitcast.5, bf16[2,3,64,128]{3,2,1,0:T(8,128)(2,1)} %bitcast.6, s32[16,32]{1,0:T(8,128)} %bitcast.7), custom_call_target="tpu_custom_call" | custom-call | tf_op jit(solution)/shard_map/pallas_call | solution.py:593
  1.9 0.5 %collective-permute-start = (f32[31,4,128]{2,1,0:T(4,128)S(1)}, f32[31,4,128]{2,1,0:T(4,128)S(1)}, u32[]{:S(2)}, u32[]{:S(2)}) collective-permute-start(f32[31,4,128]{2,1,0:T(4,128)S(1)} %get-tuple-element.16), channel_id=1, source_target_pairs={{0,8},{8,0},{16,24},{24,16},{1,9},{9,1},{17,25},{25,17},{2,10},{10... | collective-permute-start | bytes 190472 | tf_op jit(solution)/shard_map/ppermute | solution.py:575
  2.4 2.6 %collective-permute-start.1 = (f32[31,4,128]{2,1,0:T(4,128)S(1)}, f32[31,4,128]{2,1,0:T(4,128)S(1)}, u32[]{:S(2)}, u32[]{:S(2)}) collective-permute-start(f32[31,4,128]{2,1,0:T(4,128)S(1)} %get-tuple-element.17), channel_id=1, source_target_pairs={{0,24},{8,16},{16,8},{24,0},{1,25},{9,17},{17,9},{25,1},{2,26},{10... | collective-permute-start | bytes 190472 | tf_op jit(solution)/shard_map/ppermute | solution.py:574
  5.0 0.4 %shard_map.51 = (f32[3,8,128]{2,1,0:T(8,128)S(1)}, f32[3,8,128]{2,1,0:T(8,128)S(1)}) custom-call(f32[19,96,128]{2,1,0:T(8,128)S(1)} %get-tuple-element.13.held.own_held, bf16[2,3,64,128]{3,2,1,0:T(8,128)(2,1)S(1)} %get-tuple-element.14.velocity, s32[16,32]{1,0:T(8,128)S(1)} %get-tuple-element.15.solid), custom_call_target="tpu_custom_call" | custom-call | flops 2000000 | bytes 1000000 | tf_op jit(solution)/shard_map/pallas_call | solution.py:608
  5.4 0.0 collective-permute-done.row_first
  5.5 1.9 %collective-permute-done.1.row_second = f32[31,4,128]{2,1,0:T(4,128)S(1)} collective-permute-done((f32[31,4,128]{2,1,0:T(4,128)S(1)}, f32[31,4,128]{2,1,0:T(4,128)S(1)}, u32[]{:S(2)}, u32[]{:S(2)}) %collective-permute-start.1) | collective-permute-done | bytes 63520 | tf_op jit(solution)/shard_map/ppermute | solution.py:574
  7.4 0.2 shard_map.52
  7.5 1.5 %collective-permute-start.3 = (f32[3,8,128]{2,1,0:T(8,128)S(1)}, f32[3,8,128]{2,1,0:T(8,128)S(1)}, u32[]{:S(2)}, u32[]{:S(2)}) collective-permute-start(f32[3,8,128]{2,1,0:T(8,128)S(1)} %get-tuple-element.21.high), channel_id=1, source_target_pairs={{0,1},{1,2},{2,3},{3,4},{4,5},{5,6},{6,7},{7,0},{8,9},{9,10},{10,1... | collective-permute-start | bytes 36872 | tf_op jit(solution)/shard_map/ppermute | solution.py:625
  9.0 3.3 %collective-permute-start.2 = (f32[3,8,128]{2,1,0:T(8,128)S(1)}, f32[3,8,128]{2,1,0:T(8,128)S(1)}, u32[]{:S(2)}, u32[]{:S(2)}) collective-permute-start(f32[3,8,128]{2,1,0:T(8,128)S(1)} %get-tuple-element.20.low), channel_id=1, source_target_pairs={{1,0},{2,1},{3,2},{4,3},{5,4},{6,5},{7,6},{0,7},{9,8},{10,9},{11,1... | collective-permute-start | bytes 36872 | tf_op jit(solution)/shard_map/ppermute | solution.py:626
  12.3 0.6 %shard_map.54 = (f32[8,128]{1,0:T(8,128)S(1)}, f32[35,8,128]{2,1,0:T(8,128)S(1)}) custom-call(f32[19,96,128]{2,1,0:T(8,128)S(1)} %get-tuple-element.13.held.own_held, bf16[2,3,64,128]{3,2,1,0:T(8,128)(2,1)S(1)} %get-tuple-element.14.velocity, s32[16,32]{1,0:T(8,128)S(1)} %get-tuple-element.15.solid, f32[31,4,128]{2,1,0:T(4,128)S(1)} %collective-permute-done.row_first, ...), custom_call_target="tpu_custom_call" | custom-call | flops 1000000 | bytes 1000000 | tf_op jit(solution)/shard_map/pallas_call | solution.py:630
  12.9 1.0 %collective-permute-done.3.y_before = f32[3,8,128]{2,1,0:T(8,128)S(1)} collective-permute-done((f32[3,8,128]{2,1,0:T(8,128)S(1)}, f32[3,8,128]{2,1,0:T(8,128)S(1)}, u32[]{:S(2)}, u32[]{:S(2)}) %collective-permute-start.3) | collective-permute-done | bytes 12320 | tf_op jit(solution)/shard_map/ppermute | solution.py:625
  14.0 0.9 %shard_map.55 = f32[32,1,128]{2,1,0:T(1,128)} custom-call(f32[3,8,128]{2,1,0:T(8,128)S(1)} %collective-permute-done.3.y_before, f32[35,8,128]{2,1,0:T(8,128)S(1)} %get-tuple-element.22.own_blocks, f32[8,128]{1,0:T(8,128)S(1)} %get-tuple-element.23.partial), custom_call_target="tpu_custom_call" | custom-call | flops 20000000000 | bytes 10000000 | tf_op jit(solution)/shard_map/pallas_call | solution.py:642
  14.9 3.1 %all-to-all-start = ((f32[32,1,128]{2,1,0:T(1,128)}), f32[32,1,128]{2,1,0:T(1,128)S(1)}, u32[]{:S(2)}, u32[]{:S(2)}) async-start(f32[32,1,128]{2,1,0:T(1,128)} %shard_map.55), calls=%async_computation | async-start | bytes 32768 | tf_op jit(solution)/shard_map/all_to_all | solution.py:650
  18.0 0.0 collective-permute-done.2.y_after
  18.0 2.2 %shard_map.53 = f32[19,64,128]{2,1,0:T(8,128)} custom-call(f32[19,96,128]{2,1,0:T(8,128)S(1)} %get-tuple-element.13.held.own_held, bf16[2,3,64,128]{3,2,1,0:T(8,128)(2,1)S(1)} %get-tuple-element.14.velocity, s32[16,32]{1,0:T(8,128)S(1)} %get-tuple-element.15.solid, f32[31,4,128]{2,1,0:T(4,128)S(1)} %collective-permute-done.row_first, ...), custom_call_target="tpu_custom_call" | custom-call | flops 20000000000 | bytes 4000000 | tf_op jit(solution)/shard_map/pallas_call | solution.py:651
  20.2 4.9 %all-to-all-done = f32[32,1,128]{2,1,0:T(1,128)S(1)} async-done(((f32[32,1,128]{2,1,0:T(1,128)}), f32[32,1,128]{2,1,0:T(1,128)S(1)}, u32[]{:S(2)}, u32[]{:S(2)}) %all-to-all-start) | async-done | bytes 16416 | tf_op jit(solution)/shard_map/all_to_all | solution.py:650
  25.1 0.6 %slice_reduce_fusion = f32[]{:T(128)} fusion(f32[32,1,128]{2,1,0:T(1,128)S(1)} %all-to-all-done), kind=kLoop, calls=%fused_computation | loop fusion | flops 31 | bytes 132 | tf_op jit(solution)/shard_map/reduce_sum | solution.py:662
Async XLA Ops:
  1.9 3.6 %collective-permute-start = (f32[31,4,128]{2,1,0:T(4,128)S(1)}, f32[31,4,128]{2,1,0:T(4,128)S(1)}, u32[]{:S(2)}, u32[]{:S(2)}) collective-permute-start(f32[31,4,128]{2,1,0:T(4,128)S(1)} %get-tuple-element.16), channel_id=1, source_target_pairs={{0,8},{8,0},{16,24},{24,16},{1,9},{9,1},{17,25},{25,17},{2,10},{10... | collective-permute-start | bytes 190472 | tf_op jit(solution)/shard_map/ppermute | solution.py:575
  2.4 5.0 %collective-permute-start.1 = (f32[31,4,128]{2,1,0:T(4,128)S(1)}, f32[31,4,128]{2,1,0:T(4,128)S(1)}, u32[]{:S(2)}, u32[]{:S(2)}) collective-permute-start(f32[31,4,128]{2,1,0:T(4,128)S(1)} %get-tuple-element.17), channel_id=1, source_target_pairs={{0,24},{8,16},{16,8},{24,0},{1,25},{9,17},{17,9},{25,1},{2,26},{10... | collective-permute-start | bytes 190472 | tf_op jit(solution)/shard_map/ppermute | solution.py:574
  7.5 6.4 %collective-permute-start.3 = (f32[3,8,128]{2,1,0:T(8,128)S(1)}, f32[3,8,128]{2,1,0:T(8,128)S(1)}, u32[]{:S(2)}, u32[]{:S(2)}) collective-permute-start(f32[3,8,128]{2,1,0:T(8,128)S(1)} %get-tuple-element.21.high), channel_id=1, source_target_pairs={{0,1},{1,2},{2,3},{3,4},{4,5},{5,6},{6,7},{7,0},{8,9},{9,10},{10,1... | collective-permute-start | bytes 36872 | tf_op jit(solution)/shard_map/ppermute | solution.py:625
  9.0 9.0 %collective-permute-start.2 = (f32[3,8,128]{2,1,0:T(8,128)S(1)}, f32[3,8,128]{2,1,0:T(8,128)S(1)}, u32[]{:S(2)}, u32[]{:S(2)}) collective-permute-start(f32[3,8,128]{2,1,0:T(8,128)S(1)} %get-tuple-element.20.low), channel_id=1, source_target_pairs={{1,0},{2,1},{3,2},{4,3},{5,4},{6,5},{7,6},{0,7},{9,8},{10,9},{11,1... | collective-permute-start | bytes 36872 | tf_op jit(solution)/shard_map/ppermute | solution.py:626
  14.9 10.2 %all-to-all-start = ((f32[32,1,128]{2,1,0:T(1,128)}), f32[32,1,128]{2,1,0:T(1,128)S(1)}, u32[]{:S(2)}, u32[]{:S(2)}) async-start(f32[32,1,128]{2,1,0:T(1,128)} %shard_map.55), calls=%async_computation | async-start | bytes 32768 | tf_op jit(solution)/shard_map/all_to_all | solution.py:650

commit v13 on v12

--- a/solution.py
+++ b/solution.py
@@ -455,9 +455,23 @@
     return NEXT_SECOND + slot - NEXT if NEXT <= slot < NEXT + 3 else slot
 
 
-def edge_drag_kernel(groups, y_before, own_blocks, partial, shared):
+def with_halo_rows(columns, diagonal_before, diagonal_after, groups):
+    lane = lane_index()
+    group = lax.rem(lane, groups)
+    used = lane < LANES // groups * groups
+    whole = []
+    for part in range(columns.shape[0]):
+        above = pltpu.roll(diagonal_before[part], LANES - (groups - 2), 1)
+        below = pltpu.roll(diagonal_after[part], groups - 2, 1)
+        value = jnp.where(jnp.logical_and(used, group == 0), above, columns[part])
+        whole.append(jnp.where(jnp.logical_and(used, group == groups - 1), below, value))
+    return whole
+
+
+def edge_drag_kernel(groups, columns, diagonal_before, diagonal_after, own_blocks, partial, shared):
     lane = lane_index()
     column = column_reader(groups)
+    y_before = with_halo_rows(columns, diagonal_before, diagonal_after, groups)
 
     def neighbours(slot, cy):
         if cy == 1:
@@ -487,8 +501,8 @@
 
 
 def main_kernel(
-    own_held, velocity, solid, row_first, row_second, y_after, y_before, low, high, out,
-    held, shifted, later, solid_rows, row_flow,
+    own_held, velocity, solid, row_first, row_second, y_after, columns, diagonal_before, diagonal_after,
+    low, high, out, held, shifted, later, solid_rows, row_flow,
 ):
     rows = velocity.shape[2]
     groups = rows // 8 + 2
@@ -499,6 +513,7 @@
     lane = lane_index()
     solid_parts = spread_solid(solid)
     column = column_reader(groups)
+    y_before = with_halo_rows(columns, diagonal_before, diagonal_after, groups)
 
     def edge_of(slot, cy, group):
         if cy == 1:
@@ -573,6 +588,14 @@
     across = [(i, (i + 1) % count if i % 2 == 1 else (i - 1) % count) for i in range(count)]
     second = lax.ppermute(second, axis, across)
     return lax.ppermute(first, axis, inside), second
+
+
+def from_diagonal(value, side):
+    nx, ny = lax.axis_size("gx"), lax.axis_size("gy")
+    pairs = [
+        (i * ny + j, (i + side) % nx * ny + (j + 1) % ny) for i in range(nx) for j in range(ny)
+    ]
+    return lax.ppermute(value, ("gx", "gy"), pairs)
 
 
 def per_device(adjoint_in, velocity, solid_tiles, link_blocked):
@@ -622,7 +645,8 @@
         compiler_params=params,
     )(*own_columns, *row_got)
     size = lax.axis_size("gy")
-    y_before = lax.ppermute(high, "gy", [(i, (i + 1) % size) for i in range(size)])
+    y_before = lax.ppermute(own_columns[1], "gy", [(i, (i + 1) % size) for i in range(size)])
+    diagonals = [from_diagonal(own_columns[1], side) for side in (1, -1)]
     y_after = lax.ppermute(low, "gy", [((i + 1) % size, i) for i in range(size)])
     count = lax.axis_size("gx") * size
     field = pltpu.VMEM((19, padded, rows_y), jnp.float32)
@@ -642,21 +666,21 @@
     own = pl.pallas_call(
         functools.partial(edge_drag_kernel, groups),
         out_shape=pltpu.VMEM((count, 1, rows_y), jnp.float32),
-        in_specs=[vmem] * 3,
+        in_specs=[vmem] * 5,
         out_specs=vmem,
         compiler_params=params,
         cost_estimate=pl.CostEstimate(flops=20_000_000_000, bytes_accessed=10_000_000, transcendentals=0),
-    )(y_before, own_blocks, partial)
+    )(y_before, *diagonals, own_blocks, partial)
     shared = lax.all_to_all(own, ("gx", "gy"), split_axis=0, concat_axis=0, tiled=True)
     result = pl.pallas_call(
         main_kernel,
         out_shape=shape_of(19, rows, rows_y),
-        in_specs=[vmem] * 9,
+        in_specs=[vmem] * 11,
         out_specs=vmem,
         scratch_shapes=[field, field, field, solid_field, pltpu.VMEM((4, 8, rows_y), jnp.float32)],
         compiler_params=params,
         cost_estimate=pl.CostEstimate(flops=20_000_000_000, bytes_accessed=4_000_000, transcendentals=0),
-    )(held, flow, tiles, *row_got, y_after, y_before, low, high)
+    )(held, flow, tiles, *row_got, y_after, y_before, *diagonals, low, high)
     cell_count = rows * rows_y * count
     scale = drag_factor / math.sqrt(cell_count) * 3.0 / 36.0
     total = jnp.sum(shared[:, 0, 0])

time: 27.7 us -> 28 us (1.011)
  starting transfers between devices: 11 us -> 14.2 us
  waiting for transfers between devices: 7.83 us -> 4.89 us
    ppermute x1 -> x3, starting transfers between devices: 1.45 us -> 5.2 us  [the longest x2 3.66 us: from_diagonal(): return lax.ppermute(value, ('gx', 'gy'), pairs)]
    ppermute x1, waiting for transfers between devices: 1.91 us -> 0.01 us  [swap_pairs(): second = lax.ppermute(second, axis, across)]
    ppermute x1 -> x3, waiting for transfers between devices: 1.04 us -> 0.01 us  [the longest x2 0.01 us: from_diagonal(): return lax.ppermute(value, ('gx', 'gy'), pairs)]
    all_to_all x1, starting transfers between devices: 3.06 us -> 2.54 us  [per_device(): lax.all_to_all(own, ('gx', 'gy'), split_axis=0, concat_axis=0, tiled=True)]
  transfers between devices with their start and end apart: 5 -> 7, of which waited for: 3 -> 1; matrix products, arithmetic and copies ran while one was open for 0% -> 0% of each run, Pallas kernels for 15% -> 16%
where the time goes in v13:
time: 28 us; the launch traced here: 27.8 us
  starting transfers between devices  14.2 us (51%)
  Pallas kernels  5.66 us (20%)
  waiting for transfers between devices  4.89 us (17%)
  between operations  2.48 us (9%)
  other arithmetic  0.63 us (2%)
    all_to_all x1, waiting for transfers between devices, per_device(): lax.all_to_all(own, ('gx', 'gy'), split_axis=0, concat_axis=0, tiled=True)  4.87 us
    ppermute x2, starting transfers between devices, from_diagonal(): return lax.ppermute(value, ('gx', 'gy'), pairs)  3.66 us
    ppermute x1, starting transfers between devices, per_device(): lax.ppermute(low, 'gy', [((i + 1) % size, i) for i in range(size)])  3.28 us
    ppermute x1, starting transfers between devices, swap_pairs(): second = lax.ppermute(second, axis, across)  2.64 us
    all_to_all x1, starting transfers between devices, per_device(): lax.all_to_all(own, ('gx', 'gy'), split_axis=0, concat_axis=0, tiled=True)  2.54 us
    pallas_call x1, Pallas kernels, per_device(): pl.pallas_call(main_kernel, out_shape=shape_of(19, rows, rows_y), in_spec...  2.23 us
    ppermute x1, starting transfers between devices, per_device(): lax.ppermute(own_columns[1], 'gy', [(i, (i + 1) % size) for i in range(si...  1.54 us
    pallas_call x1, Pallas kernels, per_device(): pl.pallas_call(row_message_kernel, out_shape=(pltpu.VMEM((QUANTITIES, lev...  1.24 us
  transfers between devices with their start and end apart: 7, of which 1 were waited for; matrix products, arithmetic and copies ran while one was open for 0% of the time, Pallas kernels for 16%

profile of v13, /device:TPU:0, one launch (start us, length us, event | category | flops | bytes accessed | tf_op | source)
XLA Modules:
  0.0 27.8 jit_solution(9645635025636540684)
XLA Ops:
  0.6 1.2 %shard_map.50 = (f32[31,4,128]{2,1,0:T(4,128)S(1)}, f32[31,4,128]{2,1,0:T(4,128)S(1)}, f32[19,96,128]{2,1,0:T(8,128)S(1)}, bf16[2,3,64,128]{3,2,1,0:T(8,128)(2,1)S(1)}, s32[16,32]{1,0:T(8,128)S(1)}) custom-call(f32[19,64,128]{2,1,0:T(8,128)} %bitcast.5, bf16[2,3,64,128]{3,2,1,0:T(8,128)(2,1)} %bitcast.6, s32[16,32]{1,0:T(8,128)} %bitcast.7), custom_call_target="tpu_custom_call" | custom-call | tf_op jit(solution)/shard_map/pallas_call | solution.py:616
  1.9 0.5 %collective-permute-start = (f32[31,4,128]{2,1,0:T(4,128)S(1)}, f32[31,4,128]{2,1,0:T(4,128)S(1)}, u32[]{:S(2)}, u32[]{:S(2)}) collective-permute-start(f32[31,4,128]{2,1,0:T(4,128)S(1)} %get-tuple-element.16), channel_id=1, source_target_pairs={{0,8},{8,0},{16,24},{24,16},{1,9},{9,1},{17,25},{25,17},{2,10},{10... | collective-permute-start | bytes 190472 | tf_op jit(solution)/shard_map/ppermute | solution.py:590
  2.4 2.6 %collective-permute-start.1 = (f32[31,4,128]{2,1,0:T(4,128)S(1)}, f32[31,4,128]{2,1,0:T(4,128)S(1)}, u32[]{:S(2)}, u32[]{:S(2)}) collective-permute-start(f32[31,4,128]{2,1,0:T(4,128)S(1)} %get-tuple-element.17), channel_id=1, source_target_pairs={{0,24},{8,16},{16,8},{24,0},{1,25},{9,17},{17,9},{25,1},{2,26},{10... | collective-permute-start | bytes 190472 | tf_op jit(solution)/shard_map/ppermute | solution.py:589
  5.0 0.4 %shard_map.51 = (f32[3,8,128]{2,1,0:T(8,128)S(1)}, f32[3,8,128]{2,1,0:T(8,128)S(1)}) custom-call(f32[19,96,128]{2,1,0:T(8,128)S(1)} %get-tuple-element.13.held.own_held, bf16[2,3,64,128]{3,2,1,0:T(8,128)(2,1)S(1)} %get-tuple-element.14.velocity, s32[16,32]{1,0:T(8,128)S(1)} %get-tuple-element.15.solid), custom_call_target="tpu_custom_call" | custom-call | flops 2000000 | bytes 1000000 | tf_op jit(solution)/shard_map/pallas_call | solution.py:631
  5.4 1.5 %collective-permute-start.3 = (f32[3,8,128]{2,1,0:T(8,128)S(1)}, f32[3,8,128]{2,1,0:T(8,128)S(1)}, u32[]{:S(2)}, u32[]{:S(2)}) collective-permute-start(f32[3,8,128]{2,1,0:T(8,128)S(1)} %get-tuple-element.19.own_high), channel_id=1, source_target_pairs={{0,1},{1,2},{2,3},{3,4},{4,5},{5,6},{6,7},{7,0},{8,9},{9,10},{10,1... | collective-permute-start | bytes 36872 | tf_op jit(solution)/shard_map/ppermute | solution.py:648
  7.0 0.9 %collective-permute-start.4 = (f32[3,8,128]{2,1,0:T(8,128)S(1)}, f32[3,8,128]{2,1,0:T(8,128)S(1)}, u32[]{:S(2)}, u32[]{:S(2)}) collective-permute-start(f32[3,8,128]{2,1,0:T(8,128)S(1)} %get-tuple-element.19.own_high), channel_id=1, source_target_pairs={{0,9},{1,10},{2,11},{3,12},{4,13},{5,14},{6,15},{7,8},{8,17},{9,18... | collective-permute-start | bytes 36872 | tf_op jit(solution)/shard_map/ppermute | solution.py:598
  7.9 2.7 %collective-permute-start.5 = (f32[3,8,128]{2,1,0:T(8,128)S(1)}, f32[3,8,128]{2,1,0:T(8,128)S(1)}, u32[]{:S(2)}, u32[]{:S(2)}) collective-permute-start(f32[3,8,128]{2,1,0:T(8,128)S(1)} %get-tuple-element.19.own_high), channel_id=1, source_target_pairs={{0,25},{1,26},{2,27},{3,28},{4,29},{5,30},{6,31},{7,24},{8,1},{9,2... | collective-permute-start | bytes 36872 | tf_op jit(solution)/shard_map/ppermute | solution.py:598
  10.6 0.0 collective-permute-done.row_first
  10.7 0.0 collective-permute-done.1.row_second
  10.7 0.2 shard_map.52
  10.8 3.3 %collective-permute-start.2 = (f32[3,8,128]{2,1,0:T(8,128)S(1)}, f32[3,8,128]{2,1,0:T(8,128)S(1)}, u32[]{:S(2)}, u32[]{:S(2)}) collective-permute-start(f32[3,8,128]{2,1,0:T(8,128)S(1)} %get-tuple-element.20.low), channel_id=1, source_target_pairs={{1,0},{2,1},{3,2},{4,3},{5,4},{6,5},{7,6},{0,7},{9,8},{10,9},{11,1... | collective-permute-start | bytes 36872 | tf_op jit(solution)/shard_map/ppermute | solution.py:650
  14.1 0.6 %shard_map.54 = (f32[8,128]{1,0:T(8,128)S(1)}, f32[35,8,128]{2,1,0:T(8,128)S(1)}) custom-call(f32[19,96,128]{2,1,0:T(8,128)S(1)} %get-tuple-element.13.held.own_held, bf16[2,3,64,128]{3,2,1,0:T(8,128)(2,1)S(1)} %get-tuple-element.14.velocity, s32[16,32]{1,0:T(8,128)S(1)} %get-tuple-element.15.solid, f32[31,4,128]{2,1,0:T(4,128)S(1)} %collective-permute-done.row_first, ...), custom_call_target="tpu_custom_call" | custom-call | flops 1000000 | bytes 1000000 | tf_op jit(solution)/shard_map/pallas_call | solution.py:654
  14.7 0.0 collective-permute-done.3.columns
  14.8 0.0 collective-permute-done.4.diagonal_before
  14.8 0.0 collective-permute-done.5.diagonal_after
  14.8 1.0 %shard_map.55 = f32[32,1,128]{2,1,0:T(1,128)} custom-call(f32[3,8,128]{2,1,0:T(8,128)S(1)} %collective-permute-done.3.columns, f32[3,8,128]{2,1,0:T(8,128)S(1)} %collective-permute-done.4.diagonal_before, f32[3,8,128]{2,1,0:T(8,128)S(1)} %collective-permute-done.5.diagonal_after, f32[35,8,128]{2,1,0:T(8,128)S(1)} %get-tuple-element.22.own_blocks, ...), custom_call_target="tpu_custom_call" | custom-call | flops 20000000000 | bytes 10000000 | tf_op jit(solution)/shard_map/pallas_call | solution.py:666
  15.8 2.5 %all-to-all-start = ((f32[32,1,128]{2,1,0:T(1,128)}), f32[32,1,128]{2,1,0:T(1,128)S(1)}, u32[]{:S(2)}, u32[]{:S(2)}) async-start(f32[32,1,128]{2,1,0:T(1,128)} %shard_map.55), calls=%async_computation | async-start | bytes 32768 | tf_op jit(solution)/shard_map/all_to_all | solution.py:674
  18.3 0.0 collective-permute-done.2.y_after
  18.3 2.2 %shard_map.53 = f32[19,64,128]{2,1,0:T(8,128)} custom-call(f32[19,96,128]{2,1,0:T(8,128)S(1)} %get-tuple-element.13.held.own_held, bf16[2,3,64,128]{3,2,1,0:T(8,128)(2,1)S(1)} %get-tuple-element.14.velocity, s32[16,32]{1,0:T(8,128)S(1)} %get-tuple-element.15.solid, f32[31,4,128]{2,1,0:T(4,128)S(1)} %collective-permute-done.row_first, ...), custom_call_target="tpu_custom_call" | custom-call | flops 20000000000 | bytes 4000000 | tf_op jit(solution)/shard_map/pallas_call | solution.py:675
  20.6 4.9 %all-to-all-done = f32[32,1,128]{2,1,0:T(1,128)S(1)} async-done(((f32[32,1,128]{2,1,0:T(1,128)}), f32[32,1,128]{2,1,0:T(1,128)S(1)}, u32[]{:S(2)}, u32[]{:S(2)}) %all-to-all-start) | async-done | bytes 16416 | tf_op jit(solution)/shard_map/all_to_all | solution.py:674
  25.4 0.6 %slice_reduce_fusion = f32[]{:T(128)} fusion(f32[32,1,128]{2,1,0:T(1,128)S(1)} %all-to-all-done), kind=kLoop, calls=%fused_computation | loop fusion | flops 31 | bytes 132 | tf_op jit(solution)/shard_map/reduce_sum | solution.py:686
Async XLA Ops:
  1.9 8.8 %collective-permute-start = (f32[31,4,128]{2,1,0:T(4,128)S(1)}, f32[31,4,128]{2,1,0:T(4,128)S(1)}, u32[]{:S(2)}, u32[]{:S(2)}) collective-permute-start(f32[31,4,128]{2,1,0:T(4,128)S(1)} %get-tuple-element.16), channel_id=1, source_target_pairs={{0,8},{8,0},{16,24},{24,16},{1,9},{9,1},{17,25},{25,17},{2,10},{10... | collective-permute-start | bytes 190472 | tf_op jit(solution)/shard_map/ppermute | solution.py:590
  2.4 8.3 %collective-permute-start.1 = (f32[31,4,128]{2,1,0:T(4,128)S(1)}, f32[31,4,128]{2,1,0:T(4,128)S(1)}, u32[]{:S(2)}, u32[]{:S(2)}) collective-permute-start(f32[31,4,128]{2,1,0:T(4,128)S(1)} %get-tuple-element.17), channel_id=1, source_target_pairs={{0,24},{8,16},{16,8},{24,0},{1,25},{9,17},{17,9},{25,1},{2,26},{10... | collective-permute-start | bytes 190472 | tf_op jit(solution)/shard_map/ppermute | solution.py:589
  5.4 9.3 %collective-permute-start.3 = (f32[3,8,128]{2,1,0:T(8,128)S(1)}, f32[3,8,128]{2,1,0:T(8,128)S(1)}, u32[]{:S(2)}, u32[]{:S(2)}) collective-permute-start(f32[3,8,128]{2,1,0:T(8,128)S(1)} %get-tuple-element.19.own_high), channel_id=1, source_target_pairs={{0,1},{1,2},{2,3},{3,4},{4,5},{5,6},{6,7},{7,0},{8,9},{9,10},{10,1... | collective-permute-start | bytes 36872 | tf_op jit(solution)/shard_map/ppermute | solution.py:648
  7.0 7.8 %collective-permute-start.4 = (f32[3,8,128]{2,1,0:T(8,128)S(1)}, f32[3,8,128]{2,1,0:T(8,128)S(1)}, u32[]{:S(2)}, u32[]{:S(2)}) collective-permute-start(f32[3,8,128]{2,1,0:T(8,128)S(1)} %get-tuple-element.19.own_high), channel_id=1, source_target_pairs={{0,9},{1,10},{2,11},{3,12},{4,13},{5,14},{6,15},{7,8},{8,17},{9,18... | collective-permute-start | bytes 36872 | tf_op jit(solution)/shard_map/ppermute | solution.py:598
  7.9 6.8 %collective-permute-start.5 = (f32[3,8,128]{2,1,0:T(8,128)S(1)}, f32[3,8,128]{2,1,0:T(8,128)S(1)}, u32[]{:S(2)}, u32[]{:S(2)}) collective-permute-start(f32[3,8,128]{2,1,0:T(8,128)S(1)} %get-tuple-element.19.own_high), channel_id=1, source_target_pairs={{0,25},{1,26},{2,27},{3,28},{4,29},{5,30},{6,31},{7,24},{8,1},{9,2... | collective-permute-start | bytes 36872 | tf_op jit(solution)/shard_map/ppermute | solution.py:598
  10.8 7.5 %collective-permute-start.2 = (f32[3,8,128]{2,1,0:T(8,128)S(1)}, f32[3,8,128]{2,1,0:T(8,128)S(1)}, u32[]{:S(2)}, u32[]{:S(2)}) collective-permute-start(f32[3,8,128]{2,1,0:T(8,128)S(1)} %get-tuple-element.20.low), channel_id=1, source_target_pairs={{1,0},{2,1},{3,2},{4,3},{5,4},{6,5},{7,6},{0,7},{9,8},{10,9},{11,1... | collective-permute-start | bytes 36872 | tf_op jit(solution)/shard_map/ppermute | solution.py:650
  15.8 9.7 %all-to-all-start = ((f32[32,1,128]{2,1,0:T(1,128)}), f32[32,1,128]{2,1,0:T(1,128)S(1)}, u32[]{:S(2)}, u32[]{:S(2)}) async-start(f32[32,1,128]{2,1,0:T(1,128)} %shard_map.55), calls=%async_computation | async-start | bytes 32768 | tf_op jit(solution)/shard_map/all_to_all | solution.py:674

commit v14 on v13

--- a/solution.py
+++ b/solution.py
@@ -455,23 +455,37 @@
     return NEXT_SECOND + slot - NEXT if NEXT <= slot < NEXT + 3 else slot
 
 
-def with_halo_rows(columns, diagonal_before, diagonal_after, groups):
+def halo_lanes(groups):
     lane = lane_index()
     group = lax.rem(lane, groups)
     used = lane < LANES // groups * groups
+    return jnp.logical_and(used, group == 0), jnp.logical_and(used, group == groups - 1)
+
+
+def hand_on_kernel(groups, columns, out):
+    above, _ = halo_lanes(groups)
+    for part in range(columns.shape[0]):
+        value = columns[part]
+        last = pltpu.roll(value, LANES - (groups - 2), 1)
+        out[part] = jnp.where(above, last, pltpu.roll(value, groups - 2, 1))
+
+
+def with_halo_rows(columns, handed_first, handed_second, groups):
+    even = on_even("gx")
+    from_before = Chosen(even, handed_second, handed_first)
+    from_after = Chosen(even, handed_first, handed_second)
+    above, below = halo_lanes(groups)
     whole = []
     for part in range(columns.shape[0]):
-        above = pltpu.roll(diagonal_before[part], LANES - (groups - 2), 1)
-        below = pltpu.roll(diagonal_after[part], groups - 2, 1)
-        value = jnp.where(jnp.logical_and(used, group == 0), above, columns[part])
-        whole.append(jnp.where(jnp.logical_and(used, group == groups - 1), below, value))
+        value = jnp.where(above, from_before[part], columns[part])
+        whole.append(jnp.where(below, from_after[part], value))
     return whole
 
 
-def edge_drag_kernel(groups, columns, diagonal_before, diagonal_after, own_blocks, partial, shared):
+def edge_drag_kernel(groups, columns, handed_first, handed_second, own_blocks, partial, shared):
     lane = lane_index()
     column = column_reader(groups)
-    y_before = with_halo_rows(columns, diagonal_before, diagonal_after, groups)
+    y_before = with_halo_rows(columns, handed_first, handed_second, groups)
 
     def neighbours(slot, cy):
         if cy == 1:
@@ -501,7 +515,7 @@
 
 
 def main_kernel(
-    own_held, velocity, solid, row_first, row_second, y_after, columns, diagonal_before, diagonal_after,
+    own_held, velocity, solid, row_first, row_second, y_after, columns, handed_first, handed_second,
     low, high, out, held, shifted, later, solid_rows, row_flow,
 ):
     rows = velocity.shape[2]
@@ -513,7 +527,7 @@
     lane = lane_index()
     solid_parts = spread_solid(solid)
     column = column_reader(groups)
-    y_before = with_halo_rows(columns, diagonal_before, diagonal_after, groups)
+    y_before = with_halo_rows(columns, handed_first, handed_second, groups)
 
     def edge_of(slot, cy, group):
         if cy == 1:
@@ -588,14 +602,6 @@
     across = [(i, (i + 1) % count if i % 2 == 1 else (i - 1) % count) for i in range(count)]
     second = lax.ppermute(second, axis, across)
     return lax.ppermute(first, axis, inside), second
-
-
-def from_diagonal(value, side):
-    nx, ny = lax.axis_size("gx"), lax.axis_size("gy")
-    pairs = [
-        (i * ny + j, (i + side) % nx * ny + (j + 1) % ny) for i in range(nx) for j in range(ny)
-    ]
-    return lax.ppermute(value, ("gx", "gy"), pairs)
 
 
 def per_device(adjoint_in, velocity, solid_tiles, link_blocked):
@@ -646,7 +652,15 @@
     )(*own_columns, *row_got)
     size = lax.axis_size("gy")
     y_before = lax.ppermute(own_columns[1], "gy", [(i, (i + 1) % size) for i in range(size)])
-    diagonals = [from_diagonal(own_columns[1], side) for side in (1, -1)]
+    handed = pl.pallas_call(
+        functools.partial(hand_on_kernel, groups),
+        out_shape=shape_of(parts, 8, rows_y),
+        in_specs=[vmem],
+        out_specs=vmem,
+        compiler_params=params,
+        cost_estimate=pl.CostEstimate(flops=10_000_000_000, bytes_accessed=100_000, transcendentals=0),
+    )(y_before)
+    handed = swap_pairs(handed, handed, "gx")
     y_after = lax.ppermute(low, "gy", [((i + 1) % size, i) for i in range(size)])
     count = lax.axis_size("gx") * size
     field = pltpu.VMEM((19, padded, rows_y), jnp.float32)
@@ -670,7 +684,7 @@
         out_specs=vmem,
         compiler_params=params,
         cost_estimate=pl.CostEstimate(flops=20_000_000_000, bytes_accessed=10_000_000, transcendentals=0),
-    )(y_before, *diagonals, own_blocks, partial)
+    )(y_before, *handed, own_blocks, partial)
     shared = lax.all_to_all(own, ("gx", "gy"), split_axis=0, concat_axis=0, tiled=True)
     result = pl.pallas_call(
         main_kernel,
@@ -680,7 +694,7 @@
         scratch_shapes=[field, field, field, solid_field, pltpu.VMEM((4, 8, rows_y), jnp.float32)],
         compiler_params=params,
         cost_estimate=pl.CostEstimate(flops=20_000_000_000, bytes_accessed=4_000_000, transcendentals=0),
-    )(held, flow, tiles, *row_got, y_after, y_before, *diagonals, low, high)
+    )(held, flow, tiles, *row_got, y_after, y_before, *handed, low, high)
     cell_count = rows * rows_y * count
     scale = drag_factor / math.sqrt(cell_count) * 3.0 / 36.0
     total = jnp.sum(shared[:, 0, 0])

time: 28 us -> 27.8 us (level)
  starting transfers between devices: 14.2 us -> 10.9 us
  waiting for transfers between devices: 4.89 us -> 7.96 us
    ppermute x2 -> x0, starting transfers between devices: 3.66 us -> none  [from_diagonal(): return lax.ppermute(value, ('gx', 'gy'), pairs)]
    ppermute x1, waiting for transfers between devices: 0.01 us -> 3.08 us  [per_device(): lax.ppermute(own_columns[1], 'gy', [(i, (i + 1) % size) for i in range(si...]
    ppermute x1, starting transfers between devices: 1.54 us -> 2.99 us  [per_device(): lax.ppermute(own_columns[1], 'gy', [(i, (i + 1) % size) for i in range(si...]
    ppermute x1, starting transfers between devices: 3.28 us -> 1.88 us  [per_device(): lax.ppermute(low, 'gy', [((i + 1) % size, i) for i in range(size)])]
    ppermute x1 -> x2, starting transfers between devices: 2.64 us -> 3.45 us  [swap_pairs(): second = lax.ppermute(second, axis, across)]
    ppermute x1 -> x2, starting transfers between devices: 0.52 us -> 0.01 us  [swap_pairs(): return (lax.ppermute(first, axis, inside), second)]
  transfers between devices with their start and end apart: 7 -> 7, of which waited for: 1 -> 2; matrix products, arithmetic and copies ran while one was open for 0% -> 0% of each run, Pallas kernels for 16% -> 15%
where the time goes in v14:
time: 27.8 us; the launch traced here: 27.6 us
  starting transfers between devices  10.9 us (39%)
  waiting for transfers between devices  7.96 us (29%)
  Pallas kernels  5.68 us (20%)
  between operations  2.48 us (9%)
  other arithmetic  0.63 us (2%)
    all_to_all x1, waiting for transfers between devices, per_device(): lax.all_to_all(own, ('gx', 'gy'), split_axis=0, concat_axis=0, tiled=True)  4.87 us
    ppermute x2, starting transfers between devices, swap_pairs(): second = lax.ppermute(second, axis, across)  3.45 us
    ppermute x1, waiting for transfers between devices, per_device(): lax.ppermute(own_columns[1], 'gy', [(i, (i + 1) % size) for i in range(si...  3.08 us
    ppermute x1, starting transfers between devices, per_device(): lax.ppermute(own_columns[1], 'gy', [(i, (i + 1) % size) for i in range(si...  2.99 us
    all_to_all x1, starting transfers between devices, per_device(): lax.all_to_all(own, ('gx', 'gy'), split_axis=0, concat_axis=0, tiled=True)  2.54 us
    pallas_call x1, Pallas kernels, per_device(): pl.pallas_call(main_kernel, out_shape=shape_of(19, rows, rows_y), in_spec...  2.23 us
    ppermute x1, starting transfers between devices, per_device(): lax.ppermute(low, 'gy', [((i + 1) % size, i) for i in range(size)])  1.88 us
    pallas_call x1, Pallas kernels, per_device(): pl.pallas_call(row_message_kernel, out_shape=(pltpu.VMEM((QUANTITIES, lev...  1.24 us
  transfers between devices with their start and end apart: 7, of which 2 were waited for; matrix products, arithmetic and copies ran while one was open for 0% of the time, Pallas kernels for 15%

profile of v14, /device:TPU:0, one launch (start us, length us, event | category | flops | bytes accessed | tf_op | source)
XLA Modules:
  0.0 27.6 jit_solution(2581534028159177051)
XLA Ops:
  0.6 1.2 %shard_map.50 = (f32[31,4,128]{2,1,0:T(4,128)S(1)}, f32[31,4,128]{2,1,0:T(4,128)S(1)}, f32[19,96,128]{2,1,0:T(8,128)S(1)}, bf16[2,3,64,128]{3,2,1,0:T(8,128)(2,1)S(1)}, s32[16,32]{1,0:T(8,128)S(1)}) custom-call(f32[19,64,128]{2,1,0:T(8,128)} %bitcast.5, bf16[2,3,64,128]{3,2,1,0:T(8,128)(2,1)} %bitcast.6, s32[16,32]{1,0:T(8,128)} %bitcast.7), custom_call_target="tpu_custom_call" | custom-call | tf_op jit(solution)/shard_map/pallas_call | solution.py:622
  1.9 0.4 %shard_map.51 = (f32[3,8,128]{2,1,0:T(8,128)S(1)}, f32[3,8,128]{2,1,0:T(8,128)S(1)}) custom-call(f32[19,96,128]{2,1,0:T(8,128)S(1)} %get-tuple-element.13.held.own_held, bf16[2,3,64,128]{3,2,1,0:T(8,128)(2,1)S(1)} %get-tuple-element.14.velocity, s32[16,32]{1,0:T(8,128)S(1)} %get-tuple-element.15.solid), custom_call_target="tpu_custom_call" | custom-call | flops 2000000 | bytes 1000000 | tf_op jit(solution)/shard_map/pallas_call | solution.py:637
  2.3 3.0 %collective-permute-start.3 = (f32[3,8,128]{2,1,0:T(8,128)S(1)}, f32[3,8,128]{2,1,0:T(8,128)S(1)}, u32[]{:S(2)}, u32[]{:S(2)}) collective-permute-start(f32[3,8,128]{2,1,0:T(8,128)S(1)} %get-tuple-element.19.own_high), channel_id=1, source_target_pairs={{0,1},{1,2},{2,3},{3,4},{4,5},{5,6},{6,7},{7,0},{8,9},{9,10},{10,1... | collective-permute-start | bytes 36872 | tf_op jit(solution)/shard_map/ppermute | solution.py:654
  5.3 0.0 collective-permute-start
  5.3 1.6 %collective-permute-start.1 = (f32[31,4,128]{2,1,0:T(4,128)S(1)}, f32[31,4,128]{2,1,0:T(4,128)S(1)}, u32[]{:S(2)}, u32[]{:S(2)}) collective-permute-start(f32[31,4,128]{2,1,0:T(4,128)S(1)} %get-tuple-element.17), channel_id=1, source_target_pairs={{0,24},{8,16},{16,8},{24,0},{1,25},{9,17},{17,9},{25,1},{2,26},{10... | collective-permute-start | bytes 190472 | tf_op jit(solution)/shard_map/ppermute | solution.py:603
  6.9 3.1 %collective-permute-done.3.columns = f32[3,8,128]{2,1,0:T(8,128)S(1)} collective-permute-done((f32[3,8,128]{2,1,0:T(8,128)S(1)}, f32[3,8,128]{2,1,0:T(8,128)S(1)}, u32[]{:S(2)}, u32[]{:S(2)}) %collective-permute-start.3) | collective-permute-done | bytes 12320 | tf_op jit(solution)/shard_map/ppermute | solution.py:654
  10.0 0.1 shard_map.53
  10.1 0.0 collective-permute-start.4
  10.1 1.8 %collective-permute-start.5 = (f32[3,8,128]{2,1,0:T(8,128)S(1)}, f32[3,8,128]{2,1,0:T(8,128)S(1)}, u32[]{:S(2)}, u32[]{:S(2)}) collective-permute-start(f32[3,8,128]{2,1,0:T(8,128)S(1)} %shard_map.53), channel_id=1, source_target_pairs={{0,24},{8,16},{16,8},{24,0},{1,25},{9,17},{17,9},{25,1},{2,26},{10... | collective-permute-start | bytes 36872 | tf_op jit(solution)/shard_map/ppermute | solution.py:603
  11.9 0.0 collective-permute-done.row_first
  11.9 0.0 collective-permute-done.1.row_second
  11.9 0.2 shard_map.52
  12.1 1.9 %collective-permute-start.2 = (f32[3,8,128]{2,1,0:T(8,128)S(1)}, f32[3,8,128]{2,1,0:T(8,128)S(1)}, u32[]{:S(2)}, u32[]{:S(2)}) collective-permute-start(f32[3,8,128]{2,1,0:T(8,128)S(1)} %get-tuple-element.20.low), channel_id=1, source_target_pairs={{1,0},{2,1},{3,2},{4,3},{5,4},{6,5},{7,6},{0,7},{9,8},{10,9},{11,1... | collective-permute-start | bytes 36872 | tf_op jit(solution)/shard_map/ppermute | solution.py:664
  14.0 0.6 %shard_map.55 = (f32[8,128]{1,0:T(8,128)S(1)}, f32[35,8,128]{2,1,0:T(8,128)S(1)}) custom-call(f32[19,96,128]{2,1,0:T(8,128)S(1)} %get-tuple-element.13.held.own_held, bf16[2,3,64,128]{3,2,1,0:T(8,128)(2,1)S(1)} %get-tuple-element.14.velocity, s32[16,32]{1,0:T(8,128)S(1)} %get-tuple-element.15.solid, f32[31,4,128]{2,1,0:T(4,128)S(1)} %collective-permute-done.row_first, ...), custom_call_target="tpu_custom_call" | custom-call | flops 1000000 | bytes 1000000 | tf_op jit(solution)/shard_map/pallas_call | solution.py:668
  14.6 0.0 collective-permute-done.4.handed_first
  14.6 0.0 collective-permute-done.5.handed_second
  14.6 0.9 %shard_map.56 = f32[32,1,128]{2,1,0:T(1,128)} custom-call(f32[3,8,128]{2,1,0:T(8,128)S(1)} %collective-permute-done.3.columns, f32[3,8,128]{2,1,0:T(8,128)S(1)} %collective-permute-done.4.handed_first, f32[3,8,128]{2,1,0:T(8,128)S(1)} %collective-permute-done.5.handed_second, f32[35,8,128]{2,1,0:T(8,128)S(1)} %get-tuple-element.22.own_blocks, ...), custom_call_target="tpu_custom_call" | custom-call | flops 20000000000 | bytes 10000000 | tf_op jit(solution)/shard_map/pallas_call | solution.py:680
  15.6 2.5 %all-to-all-start = ((f32[32,1,128]{2,1,0:T(1,128)}), f32[32,1,128]{2,1,0:T(1,128)S(1)}, u32[]{:S(2)}, u32[]{:S(2)}) async-start(f32[32,1,128]{2,1,0:T(1,128)} %shard_map.56), calls=%async_computation | async-start | bytes 32768 | tf_op jit(solution)/shard_map/all_to_all | solution.py:688
  18.1 0.0 collective-permute-done.2.y_after
  18.1 2.2 %shard_map.54 = f32[19,64,128]{2,1,0:T(8,128)} custom-call(f32[19,96,128]{2,1,0:T(8,128)S(1)} %get-tuple-element.13.held.own_held, bf16[2,3,64,128]{3,2,1,0:T(8,128)(2,1)S(1)} %get-tuple-element.14.velocity, s32[16,32]{1,0:T(8,128)S(1)} %get-tuple-element.15.solid, f32[31,4,128]{2,1,0:T(4,128)S(1)} %collective-permute-done.row_first, ...), custom_call_target="tpu_custom_call" | custom-call | flops 20000000000 | bytes 4000000 | tf_op jit(solution)/shard_map/pallas_call | solution.py:689
  20.4 4.9 %all-to-all-done = f32[32,1,128]{2,1,0:T(1,128)S(1)} async-done(((f32[32,1,128]{2,1,0:T(1,128)}), f32[32,1,128]{2,1,0:T(1,128)S(1)}, u32[]{:S(2)}, u32[]{:S(2)}) %all-to-all-start) | async-done | bytes 16416 | tf_op jit(solution)/shard_map/all_to_all | solution.py:688
  25.2 0.6 %slice_reduce_fusion = f32[]{:T(128)} fusion(f32[32,1,128]{2,1,0:T(1,128)S(1)} %all-to-all-done), kind=kLoop, calls=%fused_computation | loop fusion | flops 31 | bytes 132 | tf_op jit(solution)/shard_map/reduce_sum | solution.py:700
Async XLA Ops:
  2.3 7.7 %collective-permute-start.3 = (f32[3,8,128]{2,1,0:T(8,128)S(1)}, f32[3,8,128]{2,1,0:T(8,128)S(1)}, u32[]{:S(2)}, u32[]{:S(2)}) collective-permute-start(f32[3,8,128]{2,1,0:T(8,128)S(1)} %get-tuple-element.19.own_high), channel_id=1, source_target_pairs={{0,1},{1,2},{2,3},{3,4},{4,5},{5,6},{6,7},{7,0},{8,9},{9,10},{10,1... | collective-permute-start | bytes 36872 | tf_op jit(solution)/shard_map/ppermute | solution.py:654
  5.3 6.6 %collective-permute-start = (f32[31,4,128]{2,1,0:T(4,128)S(1)}, f32[31,4,128]{2,1,0:T(4,128)S(1)}, u32[]{:S(2)}, u32[]{:S(2)}) collective-permute-start(f32[31,4,128]{2,1,0:T(4,128)S(1)} %get-tuple-element.16), channel_id=1, source_target_pairs={{0,8},{8,0},{16,24},{24,16},{1,9},{9,1},{17,25},{25,17},{2,10},{10... | collective-permute-start | bytes 190472 | tf_op jit(solution)/shard_map/ppermute | solution.py:604
  5.3 6.6 %collective-permute-start.1 = (f32[31,4,128]{2,1,0:T(4,128)S(1)}, f32[31,4,128]{2,1,0:T(4,128)S(1)}, u32[]{:S(2)}, u32[]{:S(2)}) collective-permute-start(f32[31,4,128]{2,1,0:T(4,128)S(1)} %get-tuple-element.17), channel_id=1, source_target_pairs={{0,24},{8,16},{16,8},{24,0},{1,25},{9,17},{17,9},{25,1},{2,26},{10... | collective-permute-start | bytes 190472 | tf_op jit(solution)/shard_map/ppermute | solution.py:603
  10.1 4.5 %collective-permute-start.4 = (f32[3,8,128]{2,1,0:T(8,128)S(1)}, f32[3,8,128]{2,1,0:T(8,128)S(1)}, u32[]{:S(2)}, u32[]{:S(2)}) collective-permute-start(f32[3,8,128]{2,1,0:T(8,128)S(1)} %shard_map.53), channel_id=1, source_target_pairs={{0,8},{8,0},{16,24},{24,16},{1,9},{9,1},{17,25},{25,17},{2,10},{10... | collective-permute-start | bytes 36872 | tf_op jit(solution)/shard_map/ppermute | solution.py:604
  10.1 4.5 %collective-permute-start.5 = (f32[3,8,128]{2,1,0:T(8,128)S(1)}, f32[3,8,128]{2,1,0:T(8,128)S(1)}, u32[]{:S(2)}, u32[]{:S(2)}) collective-permute-start(f32[3,8,128]{2,1,0:T(8,128)S(1)} %shard_map.53), channel_id=1, source_target_pairs={{0,24},{8,16},{16,8},{24,0},{1,25},{9,17},{17,9},{25,1},{2,26},{10... | collective-permute-start | bytes 36872 | tf_op jit(solution)/shard_map/ppermute | solution.py:603
  12.1 6.0 %collective-permute-start.2 = (f32[3,8,128]{2,1,0:T(8,128)S(1)}, f32[3,8,128]{2,1,0:T(8,128)S(1)}, u32[]{:S(2)}, u32[]{:S(2)}) collective-permute-start(f32[3,8,128]{2,1,0:T(8,128)S(1)} %get-tuple-element.20.low), channel_id=1, source_target_pairs={{1,0},{2,1},{3,2},{4,3},{5,4},{6,5},{7,6},{0,7},{9,8},{10,9},{11,1... | collective-permute-start | bytes 36872 | tf_op jit(solution)/shard_map/ppermute | solution.py:664
  15.6 9.7 %all-to-all-start = ((f32[32,1,128]{2,1,0:T(1,128)}), f32[32,1,128]{2,1,0:T(1,128)S(1)}, u32[]{:S(2)}, u32[]{:S(2)}) async-start(f32[32,1,128]{2,1,0:T(1,128)} %shard_map.56), calls=%async_computation | async-start | bytes 32768 | tf_op jit(solution)/shard_map/all_to_all | solution.py:688

commit v15 on v14

--- a/solution.py
+++ b/solution.py
@@ -455,26 +455,27 @@
     return NEXT_SECOND + slot - NEXT if NEXT <= slot < NEXT + 3 else slot
 
 
-def halo_lanes(groups):
+def halo_lanes(groups, ahead):
     lane = lane_index()
-    group = lax.rem(lane, groups)
-    used = lane < LANES // groups * groups
+    group = lax.rem(lane + groups - ahead, groups)
+    used = jnp.logical_and(lane >= ahead, lane < LANES // groups * groups + ahead)
     return jnp.logical_and(used, group == 0), jnp.logical_and(used, group == groups - 1)
 
 
-def hand_on_kernel(groups, columns, out):
-    above, _ = halo_lanes(groups)
+def hand_on_kernel(groups, ahead, columns, *rest):
+    out = rest[-1]
+    above, _ = halo_lanes(groups, ahead)
     for part in range(columns.shape[0]):
         value = columns[part]
         last = pltpu.roll(value, LANES - (groups - 2), 1)
         out[part] = jnp.where(above, last, pltpu.roll(value, groups - 2, 1))
 
 
-def with_halo_rows(columns, handed_first, handed_second, groups):
+def with_halo_rows(columns, handed_first, handed_second, groups, ahead):
     even = on_even("gx")
     from_before = Chosen(even, handed_second, handed_first)
     from_after = Chosen(even, handed_first, handed_second)
-    above, below = halo_lanes(groups)
+    above, below = halo_lanes(groups, ahead)
     whole = []
     for part in range(columns.shape[0]):
         value = jnp.where(above, from_before[part], columns[part])
@@ -485,7 +486,7 @@
 def edge_drag_kernel(groups, columns, handed_first, handed_second, own_blocks, partial, shared):
     lane = lane_index()
     column = column_reader(groups)
-    y_before = with_halo_rows(columns, handed_first, handed_second, groups)
+    y_before = with_halo_rows(columns, handed_first, handed_second, groups, 0)
 
     def neighbours(slot, cy):
         if cy == 1:
@@ -515,8 +516,8 @@
 
 
 def main_kernel(
-    own_held, velocity, solid, row_first, row_second, y_after, columns, handed_first, handed_second,
-    low, high, out, held, shifted, later, solid_rows, row_flow,
+    own_held, velocity, solid, row_first, row_second, columns, handed_first, handed_second,
+    columns_after, after_first, after_second, low, high, out, held, shifted, later, solid_rows, row_flow,
 ):
     rows = velocity.shape[2]
     groups = rows // 8 + 2
@@ -527,7 +528,8 @@
     lane = lane_index()
     solid_parts = spread_solid(solid)
     column = column_reader(groups)
-    y_before = with_halo_rows(columns, handed_first, handed_second, groups)
+    y_before = with_halo_rows(columns, handed_first, handed_second, groups, 0)
+    y_after = with_halo_rows(columns_after, after_first, after_second, groups, 1)
 
     def edge_of(slot, cy, group):
         if cy == 1:
@@ -652,16 +654,19 @@
     )(*own_columns, *row_got)
     size = lax.axis_size("gy")
     y_before = lax.ppermute(own_columns[1], "gy", [(i, (i + 1) % size) for i in range(size)])
-    handed = pl.pallas_call(
-        functools.partial(hand_on_kernel, groups),
-        out_shape=shape_of(parts, 8, rows_y),
-        in_specs=[vmem],
-        out_specs=vmem,
-        compiler_params=params,
-        cost_estimate=pl.CostEstimate(flops=10_000_000_000, bytes_accessed=100_000, transcendentals=0),
-    )(y_before)
-    handed = swap_pairs(handed, handed, "gx")
-    y_after = lax.ppermute(low, "gy", [((i + 1) % size, i) for i in range(size)])
+    def hand_on(columns, ahead, *later_than):
+        handed = pl.pallas_call(
+            functools.partial(hand_on_kernel, groups, ahead),
+            out_shape=shape_of(parts, 8, rows_y),
+            in_specs=[vmem] * (1 + len(later_than)),
+            out_specs=vmem,
+            compiler_params=params,
+            cost_estimate=pl.CostEstimate(flops=10_000_000_000, bytes_accessed=100_000, transcendentals=0),
+        )(columns, *later_than)
+        return swap_pairs(handed, handed, "gx")
+
+    handed = hand_on(y_before, 0)
+    y_after = lax.ppermute(own_columns[0], "gy", [((i + 1) % size, i) for i in range(size)])
     count = lax.axis_size("gx") * size
     field = pltpu.VMEM((19, padded, rows_y), jnp.float32)
     solid_field = pltpu.VMEM((3, padded, rows_y), jnp.float32)
@@ -675,7 +680,7 @@
         out_specs=(vmem,) * 2,
         scratch_shapes=[field, field, solid_field, pltpu.VMEM((9, padded, rows_y), jnp.float32)],
         compiler_params=params,
-        cost_estimate=pl.CostEstimate(flops=1_000_000, bytes_accessed=1_000_000, transcendentals=0),
+        cost_estimate=pl.CostEstimate(flops=20_000_000_000, bytes_accessed=1_000_000, transcendentals=0),
     )(held, flow, tiles, *row_got, low)
     own = pl.pallas_call(
         functools.partial(edge_drag_kernel, groups),
@@ -683,18 +688,19 @@
         in_specs=[vmem] * 5,
         out_specs=vmem,
         compiler_params=params,
-        cost_estimate=pl.CostEstimate(flops=20_000_000_000, bytes_accessed=10_000_000, transcendentals=0),
+        cost_estimate=pl.CostEstimate(flops=1_000_000, bytes_accessed=1_000_000, transcendentals=0),
     )(y_before, *handed, own_blocks, partial)
+    handed_after = hand_on(y_after, 1, own)
     shared = lax.all_to_all(own, ("gx", "gy"), split_axis=0, concat_axis=0, tiled=True)
     result = pl.pallas_call(
         main_kernel,
         out_shape=shape_of(19, rows, rows_y),
-        in_specs=[vmem] * 11,
+        in_specs=[vmem] * 13,
         out_specs=vmem,
         scratch_shapes=[field, field, field, solid_field, pltpu.VMEM((4, 8, rows_y), jnp.float32)],
         compiler_params=params,
-        cost_estimate=pl.CostEstimate(flops=20_000_000_000, bytes_accessed=4_000_000, transcendentals=0),
-    )(held, flow, tiles, *row_got, y_after, y_before, *handed, low, high)
+        cost_estimate=pl.CostEstimate(flops=1_000_000, bytes_accessed=1_000_000, transcendentals=0),
+    )(held, flow, tiles, *row_got, y_before, *handed, y_after, *handed_after, low, high)
     cell_count = rows * rows_y * count
     scale = drag_factor / math.sqrt(cell_count) * 3.0 / 36.0
     total = jnp.sum(shared[:, 0, 0])

time: 27.8 us -> 27.3 us (0.982)
  waiting for transfers between devices: 7.96 us -> 2.79 us
  starting transfers between devices: 10.9 us -> 14.6 us
  Pallas kernels: 5.68 us -> 6.52 us
    all_to_all x1, waiting for transfers between devices: 4.87 us -> 0.9 us  [per_device(): lax.all_to_all(own, ('gx', 'gy'), split_axis=0, concat_axis=0, tiled=True)]
    ppermute x1, waiting for transfers between devices: 3.08 us -> 0.01 us  [per_device(): lax.ppermute(own_columns[1], 'gy', [(i, (i + 1) % size) for i in range(si...]
    ppermute x2 -> x3, starting transfers between devices: 0.01 us -> 2.02 us  [swap_pairs(): return (lax.ppermute(first, axis, inside), second)]
    ppermute x2 -> x3, waiting for transfers between devices: 0.01 us -> 1.88 us  [swap_pairs(): second = lax.ppermute(second, axis, across)]
    ppermute x1, starting transfers between devices: 1.88 us -> 3.1 us  [per_device(): lax.ppermute(own_columns[0], 'gy', [((i + 1) % size, i) for i in range(si...]
    pallas_call x1 -> x2, Pallas kernels: 0.07 us -> 0.9 us  [hand_on(): pl.pallas_call(functools.partial(hand_on_kernel, groups, ahead), out_shap...]
    all_to_all x1, starting transfers between devices: 2.54 us -> 3.22 us  [per_device(): lax.all_to_all(own, ('gx', 'gy'), split_axis=0, concat_axis=0, tiled=True)]
    ppermute x2 -> x3, starting transfers between devices: 3.45 us -> 3.3 us  [swap_pairs(): second = lax.ppermute(second, axis, across)]
  transfers between devices with their start and end apart: 7 -> 9, of which waited for: 2 -> 4; matrix products, arithmetic and copies ran while one was open for 0% -> 0% of each run, Pallas kernels for 15% -> 18%
where the time goes in v15:
time: 27.3 us; the launch traced here: 27 us
  starting transfers between devices  14.6 us (53%)
  Pallas kernels  6.52 us (24%)
  waiting for transfers between devices  2.79 us (10%)
  between operations  2.46 us (9%)
  other arithmetic  0.63 us (2%)
    ppermute x3, starting transfers between devices, swap_pairs(): second = lax.ppermute(second, axis, across)  3.3 us
    all_to_all x1, starting transfers between devices, per_device(): lax.all_to_all(own, ('gx', 'gy'), split_axis=0, concat_axis=0, tiled=True)  3.22 us
    ppermute x1, starting transfers between devices, per_device(): lax.ppermute(own_columns[0], 'gy', [((i + 1) % size, i) for i in range(si...  3.1 us
    ppermute x1, starting transfers between devices, per_device(): lax.ppermute(own_columns[1], 'gy', [(i, (i + 1) % size) for i in range(si...  2.99 us
    pallas_call x1, Pallas kernels, per_device(): pl.pallas_call(main_kernel, out_shape=shape_of(19, rows, rows_y), in_spec...  2.25 us
    ppermute x3, starting transfers between devices, swap_pairs(): return (lax.ppermute(first, axis, inside), second)  2.02 us
    ppermute x3, waiting for transfers between devices, swap_pairs(): second = lax.ppermute(second, axis, across)  1.88 us
    pallas_call x1, Pallas kernels, per_device(): pl.pallas_call(row_message_kernel, out_shape=(pltpu.VMEM((QUANTITIES, lev...  1.24 us
  transfers between devices with their start and end apart: 9, of which 4 were waited for; matrix products, arithmetic and copies ran while one was open for 0% of the time, Pallas kernels for 18%

profile of v15, /device:TPU:0, one launch (start us, length us, event | category | flops | bytes accessed | tf_op | source)
XLA Modules:
  0.0 27.0 jit_solution(14298805570613798013)
XLA Ops:
  0.6 1.2 %shard_map.50 = (f32[31,4,128]{2,1,0:T(4,128)S(1)}, f32[31,4,128]{2,1,0:T(4,128)S(1)}, f32[19,96,128]{2,1,0:T(8,128)S(1)}, bf16[2,3,64,128]{3,2,1,0:T(8,128)(2,1)S(1)}, s32[16,32]{1,0:T(8,128)S(1)}) custom-call(f32[19,64,128]{2,1,0:T(8,128)} %bitcast.6, bf16[2,3,64,128]{3,2,1,0:T(8,128)(2,1)} %bitcast.7, s32[16,32]{1,0:T(8,128)} %bitcast.8), custom_call_target="tpu_custom_call" | custom-call | tf_op jit(solution)/shard_map/pallas_call | solution.py:624
  1.9 0.4 %shard_map.51 = (f32[3,8,128]{2,1,0:T(8,128)S(1)}, f32[3,8,128]{2,1,0:T(8,128)S(1)}) custom-call(f32[19,96,128]{2,1,0:T(8,128)S(1)} %get-tuple-element.13.held.own_held, bf16[2,3,64,128]{3,2,1,0:T(8,128)(2,1)S(1)} %get-tuple-element.14.velocity, s32[16,32]{1,0:T(8,128)S(1)} %get-tuple-element.15.solid), custom_call_target="tpu_custom_call" | custom-call | flops 2000000 | bytes 1000000 | tf_op jit(solution)/shard_map/pallas_call | solution.py:639
  2.3 3.0 %collective-permute-start.2 = (f32[3,8,128]{2,1,0:T(8,128)S(1)}, f32[3,8,128]{2,1,0:T(8,128)S(1)}, u32[]{:S(2)}, u32[]{:S(2)}) collective-permute-start(f32[3,8,128]{2,1,0:T(8,128)S(1)} %get-tuple-element.18.own_high), channel_id=1, source_target_pairs={{0,1},{1,2},{2,3},{3,4},{4,5},{5,6},{6,7},{7,0},{8,9},{9,10},{10,1... | collective-permute-start | bytes 36872 | tf_op jit(solution)/shard_map/ppermute | solution.py:656
  5.3 3.1 %collective-permute-start.5 = (f32[3,8,128]{2,1,0:T(8,128)S(1)}, f32[3,8,128]{2,1,0:T(8,128)S(1)}, u32[]{:S(2)}, u32[]{:S(2)}) collective-permute-start(f32[3,8,128]{2,1,0:T(8,128)S(1)} %get-tuple-element.19.own_low), channel_id=1, source_target_pairs={{1,0},{2,1},{3,2},{4,3},{5,4},{6,5},{7,6},{0,7},{9,8},{10,9},{11,1... | collective-permute-start | bytes 36872 | tf_op jit(solution)/shard_map/ppermute | solution.py:669
  8.4 0.0 collective-permute-start
  8.4 1.8 %collective-permute-start.1 = (f32[31,4,128]{2,1,0:T(4,128)S(1)}, f32[31,4,128]{2,1,0:T(4,128)S(1)}, u32[]{:S(2)}, u32[]{:S(2)}) collective-permute-start(f32[31,4,128]{2,1,0:T(4,128)S(1)} %get-tuple-element.17), channel_id=1, source_target_pairs={{0,24},{8,16},{16,8},{24,0},{1,25},{9,17},{17,9},{25,1},{2,26},{10... | collective-permute-start | bytes 190472 | tf_op jit(solution)/shard_map/ppermute | solution.py:605
  10.1 0.0 collective-permute-done.2.columns
  10.1 0.1 shard_map.52
  10.2 0.0 collective-permute-start.4
  10.2 1.7 %collective-permute-start.3 = (f32[3,8,128]{2,1,0:T(8,128)S(1)}, f32[3,8,128]{2,1,0:T(8,128)S(1)}, u32[]{:S(2)}, u32[]{:S(2)}) collective-permute-start(f32[3,8,128]{2,1,0:T(8,128)S(1)} %shard_map.52), channel_id=1, source_target_pairs={{0,8},{8,0},{16,24},{24,16},{1,9},{9,1},{17,25},{25,17},{2,10},{10... | collective-permute-start | bytes 36872 | tf_op jit(solution)/shard_map/ppermute | solution.py:606
  11.9 0.0 collective-permute-done.row_first
  11.9 0.2 collective-permute-done.1.row_second
  12.1 0.2 shard_map.53
  12.3 0.6 %shard_map.54 = (f32[8,128]{1,0:T(8,128)S(1)}, f32[35,8,128]{2,1,0:T(8,128)S(1)}) custom-call(f32[19,96,128]{2,1,0:T(8,128)S(1)} %get-tuple-element.13.held.own_held, bf16[2,3,64,128]{3,2,1,0:T(8,128)(2,1)S(1)} %get-tuple-element.14.velocity, s32[16,32]{1,0:T(8,128)S(1)} %get-tuple-element.15.solid, f32[31,4,128]{2,1,0:T(4,128)S(1)} %collective-permute-done.row_first, ...), custom_call_target="tpu_custom_call" | custom-call | flops 20000000000 | bytes 1000000 | tf_op jit(solution)/shard_map/pallas_call | solution.py:673
  12.9 0.4 %collective-permute-done.4.handed_second = f32[3,8,128]{2,1,0:T(8,128)S(1)} collective-permute-done((f32[3,8,128]{2,1,0:T(8,128)S(1)}, f32[3,8,128]{2,1,0:T(8,128)S(1)}, u32[]{:S(2)}, u32[]{:S(2)}) %collective-permute-start.4) | collective-permute-done | bytes 12320 | tf_op jit(solution)/shard_map/ppermute | solution.py:605
  13.3 0.0 collective-permute-done.3.handed_first
  13.4 0.9 %shard_map.55.rest_0_ = f32[32,1,128]{2,1,0:T(1,128)} custom-call(f32[3,8,128]{2,1,0:T(8,128)S(1)} %collective-permute-done.2.columns, f32[3,8,128]{2,1,0:T(8,128)S(1)} %collective-permute-done.3.handed_first, f32[3,8,128]{2,1,0:T(8,128)S(1)} %collective-permute-done.4.handed_second, f32[35,8,128]{2,1,0:T(8,128)S(1)} %get-tuple-element.21.own_blocks, ...), custom_call_target="tpu_custom_call" | custom-call | flops 1000000 | bytes 1000000 | tf_op jit(solution)/shard_map/pallas_call | solution.py:685
  14.3 3.2 %all-to-all-start = ((f32[32,1,128]{2,1,0:T(1,128)}), f32[32,1,128]{2,1,0:T(1,128)S(1)}, u32[]{:S(2)}, u32[]{:S(2)}) async-start(f32[32,1,128]{2,1,0:T(1,128)} %shard_map.55.rest_0_), calls=%async_computation | async-start | bytes 32768 | tf_op jit(solution)/shard_map/all_to_all | solution.py:694
  17.5 0.0 collective-permute-done.5.columns.columns_after
  17.5 0.8 %shard_map.56 = f32[3,8,128]{2,1,0:T(8,128)S(1)} custom-call(f32[3,8,128]{2,1,0:T(8,128)S(1)} %collective-permute-done.5.columns.columns_after, f32[32,1,128]{2,1,0:T(1,128)} %shard_map.55.rest_0_), custom_call_target="tpu_custom_call" | custom-call | flops 10000000000 | bytes 100000 | tf_op jit(solution)/shard_map/pallas_call | solution.py:658
  18.4 1.5 %collective-permute-start.7 = (f32[3,8,128]{2,1,0:T(8,128)S(1)}, f32[3,8,128]{2,1,0:T(8,128)S(1)}, u32[]{:S(2)}, u32[]{:S(2)}) collective-permute-start(f32[3,8,128]{2,1,0:T(8,128)S(1)} %shard_map.56), channel_id=1, source_target_pairs={{0,24},{8,16},{16,8},{24,0},{1,25},{9,17},{17,9},{25,1},{2,26},{10... | collective-permute-start | bytes 36872 | tf_op jit(solution)/shard_map/ppermute | solution.py:605
  19.9 0.4 %collective-permute-start.6 = (f32[3,8,128]{2,1,0:T(8,128)S(1)}, f32[3,8,128]{2,1,0:T(8,128)S(1)}, u32[]{:S(2)}, u32[]{:S(2)}) collective-permute-start(f32[3,8,128]{2,1,0:T(8,128)S(1)} %shard_map.56), channel_id=1, source_target_pairs={{0,8},{8,0},{16,24},{24,16},{1,9},{9,1},{17,25},{25,17},{2,10},{10... | collective-permute-start | bytes 36872 | tf_op jit(solution)/shard_map/ppermute | solution.py:606
  20.2 1.2 %collective-permute-done.7.after_second = f32[3,8,128]{2,1,0:T(8,128)S(1)} collective-permute-done((f32[3,8,128]{2,1,0:T(8,128)S(1)}, f32[3,8,128]{2,1,0:T(8,128)S(1)}, u32[]{:S(2)}, u32[]{:S(2)}) %collective-permute-start.7) | collective-permute-done | bytes 12320 | tf_op jit(solution)/shard_map/ppermute | solution.py:605
  21.5 0.0 collective-permute-done.6.after_first
  21.5 2.2 %shard_map.57 = f32[19,64,128]{2,1,0:T(8,128)} custom-call(f32[19,96,128]{2,1,0:T(8,128)S(1)} %get-tuple-element.13.held.own_held, bf16[2,3,64,128]{3,2,1,0:T(8,128)(2,1)S(1)} %get-tuple-element.14.velocity, s32[16,32]{1,0:T(8,128)S(1)} %get-tuple-element.15.solid, f32[31,4,128]{2,1,0:T(4,128)S(1)} %collective-permute-done.row_first, ...), custom_call_target="tpu_custom_call" | custom-call | flops 1000000 | bytes 1000000 | tf_op jit(solution)/shard_map/pallas_call | solution.py:695
  23.7 0.9 %all-to-all-done = f32[32,1,128]{2,1,0:T(1,128)S(1)} async-done(((f32[32,1,128]{2,1,0:T(1,128)}), f32[32,1,128]{2,1,0:T(1,128)S(1)}, u32[]{:S(2)}, u32[]{:S(2)}) %all-to-all-start) | async-done | bytes 16416 | tf_op jit(solution)/shard_map/all_to_all | solution.py:694
  24.6 0.6 %slice_reduce_fusion = f32[]{:T(128)} fusion(f32[32,1,128]{2,1,0:T(1,128)S(1)} %all-to-all-done), kind=kLoop, calls=%fused_computation | loop fusion | flops 31 | bytes 132 | tf_op jit(solution)/shard_map/reduce_sum | solution.py:706
Async XLA Ops:
  2.3 7.9 %collective-permute-start.2 = (f32[3,8,128]{2,1,0:T(8,128)S(1)}, f32[3,8,128]{2,1,0:T(8,128)S(1)}, u32[]{:S(2)}, u32[]{:S(2)}) collective-permute-start(f32[3,8,128]{2,1,0:T(8,128)S(1)} %get-tuple-element.18.own_high), channel_id=1, source_target_pairs={{0,1},{1,2},{2,3},{3,4},{4,5},{5,6},{6,7},{7,0},{8,9},{9,10},{10,1... | collective-permute-start | bytes 36872 | tf_op jit(solution)/shard_map/ppermute | solution.py:656
  5.3 12.2 %collective-permute-start.5 = (f32[3,8,128]{2,1,0:T(8,128)S(1)}, f32[3,8,128]{2,1,0:T(8,128)S(1)}, u32[]{:S(2)}, u32[]{:S(2)}) collective-permute-start(f32[3,8,128]{2,1,0:T(8,128)S(1)} %get-tuple-element.19.own_low), channel_id=1, source_target_pairs={{1,0},{2,1},{3,2},{4,3},{5,4},{6,5},{7,6},{0,7},{9,8},{10,9},{11,1... | collective-permute-start | bytes 36872 | tf_op jit(solution)/shard_map/ppermute | solution.py:669
  8.4 3.5 %collective-permute-start = (f32[31,4,128]{2,1,0:T(4,128)S(1)}, f32[31,4,128]{2,1,0:T(4,128)S(1)}, u32[]{:S(2)}, u32[]{:S(2)}) collective-permute-start(f32[31,4,128]{2,1,0:T(4,128)S(1)} %get-tuple-element.16), channel_id=1, source_target_pairs={{0,8},{8,0},{16,24},{24,16},{1,9},{9,1},{17,25},{25,17},{2,10},{10... | collective-permute-start | bytes 190472 | tf_op jit(solution)/shard_map/ppermute | solution.py:606
  8.4 3.7 %collective-permute-start.1 = (f32[31,4,128]{2,1,0:T(4,128)S(1)}, f32[31,4,128]{2,1,0:T(4,128)S(1)}, u32[]{:S(2)}, u32[]{:S(2)}) collective-permute-start(f32[31,4,128]{2,1,0:T(4,128)S(1)} %get-tuple-element.17), channel_id=1, source_target_pairs={{0,24},{8,16},{16,8},{24,0},{1,25},{9,17},{17,9},{25,1},{2,26},{10... | collective-permute-start | bytes 190472 | tf_op jit(solution)/shard_map/ppermute | solution.py:605
  10.2 3.1 %collective-permute-start.4 = (f32[3,8,128]{2,1,0:T(8,128)S(1)}, f32[3,8,128]{2,1,0:T(8,128)S(1)}, u32[]{:S(2)}, u32[]{:S(2)}) collective-permute-start(f32[3,8,128]{2,1,0:T(8,128)S(1)} %shard_map.52), channel_id=1, source_target_pairs={{0,24},{8,16},{16,8},{24,0},{1,25},{9,17},{17,9},{25,1},{2,26},{10... | collective-permute-start | bytes 36872 | tf_op jit(solution)/shard_map/ppermute | solution.py:605
  10.2 3.1 %collective-permute-start.3 = (f32[3,8,128]{2,1,0:T(8,128)S(1)}, f32[3,8,128]{2,1,0:T(8,128)S(1)}, u32[]{:S(2)}, u32[]{:S(2)}) collective-permute-start(f32[3,8,128]{2,1,0:T(8,128)S(1)} %shard_map.52), channel_id=1, source_target_pairs={{0,8},{8,0},{16,24},{24,16},{1,9},{9,1},{17,25},{25,17},{2,10},{10... | collective-permute-start | bytes 36872 | tf_op jit(solution)/shard_map/ppermute | solution.py:606
  14.3 10.3 %all-to-all-start = ((f32[32,1,128]{2,1,0:T(1,128)}), f32[32,1,128]{2,1,0:T(1,128)S(1)}, u32[]{:S(2)}, u32[]{:S(2)}) async-start(f32[32,1,128]{2,1,0:T(1,128)} %shard_map.55.rest_0_), calls=%async_computation | async-start | bytes 32768 | tf_op jit(solution)/shard_map/all_to_all | solution.py:694
  18.4 3.1 %collective-permute-start.7 = (f32[3,8,128]{2,1,0:T(8,128)S(1)}, f32[3,8,128]{2,1,0:T(8,128)S(1)}, u32[]{:S(2)}, u32[]{:S(2)}) collective-permute-start(f32[3,8,128]{2,1,0:T(8,128)S(1)} %shard_map.56), channel_id=1, source_target_pairs={{0,24},{8,16},{16,8},{24,0},{1,25},{9,17},{17,9},{25,1},{2,26},{10... | collective-permute-start | bytes 36872 | tf_op jit(solution)/shard_map/ppermute | solution.py:605
  19.9 1.6 %collective-permute-start.6 = (f32[3,8,128]{2,1,0:T(8,128)S(1)}, f32[3,8,128]{2,1,0:T(8,128)S(1)}, u32[]{:S(2)}, u32[]{:S(2)}) collective-permute-start(f32[3,8,128]{2,1,0:T(8,128)S(1)} %shard_map.56), channel_id=1, source_target_pairs={{0,8},{8,0},{16,24},{24,16},{1,9},{9,1},{17,25},{25,17},{2,10},{10... | collective-permute-start | bytes 36872 | tf_op jit(solution)/shard_map/ppermute | solution.py:606

commit v16 on v15

--- a/solution.py
+++ b/solution.py
@@ -149,27 +149,23 @@
 
 
 def pack_columns(parts, slot, group, groups, value):
-    low_parts, high_parts = parts
-    part, place = slot_place(slot, group, groups)
-    lane = lane_index()
-    turned = pltpu.roll(value, (place + 1) % LANES, 1)
-    low_parts[part] = jnp.where(lane == place + 1, turned, low_parts[part])
-    high_parts[part] = jnp.where(lane == place, turned, high_parts[part])
-    if slot in y_up:
-        insert_column(low_parts, SECOND + y_up.index(slot), group, groups, value, 1, 1)
-    if slot in y_down:
-        insert_column(high_parts, SECOND + y_down.index(slot), group, groups, value, LANES - 2, 0)
-    if NEXT <= slot < NEXT + 3:
-        insert_column(low_parts, NEXT_SECOND + slot - NEXT, group, groups, value, 1, 1)
-        insert_column(high_parts, NEXT_SECOND + slot - NEXT, group, groups, value, LANES - 2, 0)
-
-
-def own_columns_kernel(held, velocity, solid, low, high):
+    for message, edge, step, ahead, moving in ((parts[0], 0, 1, 1, y_up), (parts[1], LANES - 1, -1, 0, y_down)):
+        if message is None:
+            continue
+        insert_column(message, slot, group, groups, value, edge, ahead)
+        second = second_slot(slot, moving)
+        if second != slot:
+            insert_column(message, second, group, groups, value, edge + step, ahead)
+
+
+def own_columns_kernel(side, held, velocity, solid, *rest):
+    out = rest[-1]
     rows = velocity.shape[2]
     groups = rows // 8 + 2
     solid_parts = spread_solid(solid)
     flow = [flow_blocks(velocity, step, rows) for step in range(2)]
-    parts = [[jnp.zeros((8, LANES), jnp.float32) for _ in range(low.shape[0])] for _ in range(2)]
+    parts = [None, None]
+    parts[side] = [jnp.zeros((8, LANES), jnp.float32) for _ in range(out.shape[0])]
     for group in range(1, groups - 1):
         for slot in range(19):
             pack_columns(parts, slot, group, groups, held[slot, pl.ds(GUARD + 8 * group, 8), :])
@@ -177,13 +173,12 @@
             pack_columns(parts, FLOW + axis, group, groups, flow[0][group - 1][axis])
             pack_columns(parts, NEXT + axis, group, groups, flow[1][group - 1][axis])
         pack_columns(parts, SOLID, group, groups, solid_parts[(group - 1) * 8 // (LEVELS * TILE)])
-    for part in range(low.shape[0]):
-        low[part] = parts[0][part]
-        high[part] = parts[1][part]
+    for part in range(out.shape[0]):
+        out[part] = parts[side][part]
 
 
 def halo_columns_kernel(groups, own_low, own_high, row_first, row_second, low_out, high_out, ends):
-    count = own_low.shape[0]
+    count = own_high.shape[0]
     even = on_even("gx")
     after, before = Chosen(even, row_first, row_second), Chosen(even, row_second, row_first)
     parts = [[own_low[part] for part in range(count)], [own_high[part] for part in range(count)]]
@@ -465,7 +460,7 @@
 def hand_on_kernel(groups, ahead, columns, *rest):
     out = rest[-1]
     above, _ = halo_lanes(groups, ahead)
-    for part in range(columns.shape[0]):
+    for part in range(out.shape[0]):
         value = columns[part]
         last = pltpu.roll(value, LANES - (groups - 2), 1)
         out[part] = jnp.where(above, last, pltpu.roll(value, groups - 2, 1))
@@ -477,7 +472,7 @@
     from_after = Chosen(even, handed_first, handed_second)
     above, below = halo_lanes(groups, ahead)
     whole = []
-    for part in range(columns.shape[0]):
+    for part in range(handed_first.shape[0]):
         value = jnp.where(above, from_before[part], columns[part])
         whole.append(jnp.where(below, from_after[part], value))
     return whole
@@ -636,14 +631,19 @@
         compiler_params=params,
     )(*(pltpu.with_memory_space_constraint(value, pltpu.HBM) for value in (state, flow, solid)))
     row_got = swap_pairs(*row_sent, "gx")
-    own_columns = pl.pallas_call(
-        own_columns_kernel,
-        out_shape=(shape_of(parts, 8, rows_y),) * 2,
-        in_specs=[vmem] * 3,
-        out_specs=(vmem,) * 2,
-        compiler_params=params,
-        cost_estimate=pl.CostEstimate(flops=2_000_000, bytes_accessed=1_000_000, transcendentals=0),
-    )(held, flow, tiles)
+    def pack(side, size, *later_than):
+        return pl.pallas_call(
+            functools.partial(own_columns_kernel, side),
+            out_shape=shape_of(size, 8, rows_y),
+            in_specs=[vmem] * (3 + len(later_than)),
+            out_specs=vmem,
+            compiler_params=params,
+            cost_estimate=pl.CostEstimate(flops=2_000_000, bytes_accessed=1_000_000, transcendentals=0),
+        )(held, flow, tiles, *later_than)
+
+    own_high = pack(1, parts)
+    own_low = pack(0, 16)
+    own_columns = own_low, own_high
     low, high = pl.pallas_call(
         functools.partial(halo_columns_kernel, groups),
         out_shape=(shape_of(parts, 8, rows_y),) * 2,

time: 27.3 us -> 27.2 us (level)
  starting transfers between devices: 14.6 us -> 13.9 us
  waiting for transfers between devices: 2.79 us -> 3.11 us
    all_to_all x1, starting transfers between devices: 3.22 us -> 2.76 us  [per_device(): lax.all_to_all(own, ('gx', 'gy'), split_axis=0, concat_axis=0, tiled=True)]
    ppermute x3, waiting for transfers between devices: 1.88 us -> 2.19 us  [swap_pairs(): second = lax.ppermute(second, axis, across)]
    ppermute x3, starting transfers between devices: 2.02 us -> 1.73 us  [swap_pairs(): return (lax.ppermute(first, axis, inside), second)]
    pallas_call x1 -> x2, Pallas kernels: 0.41 us -> 0.66 us  [pack(): pl.pallas_call(functools.partial(own_columns_kernel, side), out_shape=sha...]
  transfers between devices with their start and end apart: 9 -> 9, of which waited for: 4 -> 3; matrix products, arithmetic and copies ran while one was open for 0% -> 0% of each run, Pallas kernels for 18% -> 19%
where the time goes in v16:
time: 27.2 us; the launch traced here: 26.9 us
  starting transfers between devices  13.9 us (51%)
  Pallas kernels  6.79 us (25%)
  waiting for transfers between devices  3.11 us (11%)
  between operations  2.47 us (9%)
  other arithmetic  0.63 us (2%)
    ppermute x1, starting transfers between devices, per_device(): lax.ppermute(own_columns[0], 'gy', [((i + 1) % size, i) for i in range(si...  3.28 us
    ppermute x3, starting transfers between devices, swap_pairs(): second = lax.ppermute(second, axis, across)  3.17 us
    ppermute x1, starting transfers between devices, per_device(): lax.ppermute(own_columns[1], 'gy', [(i, (i + 1) % size) for i in range(si...  2.99 us
    all_to_all x1, starting transfers between devices, per_device(): lax.all_to_all(own, ('gx', 'gy'), split_axis=0, concat_axis=0, tiled=True)  2.76 us
    pallas_call x1, Pallas kernels, per_device(): pl.pallas_call(main_kernel, out_shape=shape_of(19, rows, rows_y), in_spec...  2.24 us
    ppermute x3, waiting for transfers between devices, swap_pairs(): second = lax.ppermute(second, axis, across)  2.19 us
    ppermute x3, starting transfers between devices, swap_pairs(): return (lax.ppermute(first, axis, inside), second)  1.73 us
    pallas_call x1, Pallas kernels, per_device(): pl.pallas_call(row_message_kernel, out_shape=(pltpu.VMEM((QUANTITIES, lev...  1.24 us
  transfers between devices with their start and end apart: 9, of which 3 were waited for; matrix products, arithmetic and copies ran while one was open for 0% of the time, Pallas kernels for 19%

profile of v16, /device:TPU:0, one launch (start us, length us, event | category | flops | bytes accessed | tf_op | source)
XLA Modules:
  0.0 26.9 jit_solution(14059081625177509364)
XLA Ops:
  0.6 1.2 %shard_map.50 = (f32[31,4,128]{2,1,0:T(4,128)S(1)}, f32[31,4,128]{2,1,0:T(4,128)S(1)}, f32[19,96,128]{2,1,0:T(8,128)S(1)}, bf16[2,3,64,128]{3,2,1,0:T(8,128)(2,1)S(1)}, s32[16,32]{1,0:T(8,128)S(1)}) custom-call(f32[19,64,128]{2,1,0:T(8,128)} %bitcast.5, bf16[2,3,64,128]{3,2,1,0:T(8,128)(2,1)} %bitcast.7, s32[16,32]{1,0:T(8,128)} %bitcast.8), custom_call_target="tpu_custom_call" | custom-call | tf_op jit(solution)/shard_map/pallas_call | solution.py:619
  1.9 0.3 %shard_map.51.own_high = f32[3,8,128]{2,1,0:T(8,128)S(1)} custom-call(f32[19,96,128]{2,1,0:T(8,128)S(1)} %get-tuple-element.11.held.own_held, bf16[2,3,64,128]{3,2,1,0:T(8,128)(2,1)S(1)} %get-tuple-element.12.velocity, s32[16,32]{1,0:T(8,128)S(1)} %get-tuple-element.13.solid), custom_call_target="tpu_custom_call" | custom-call | flops 2000000 | bytes 1000000 | tf_op jit(solution)/shard_map/pallas_call | solution.py:635
  2.2 3.0 %collective-permute-start.2 = (f32[3,8,128]{2,1,0:T(8,128)S(1)}, f32[3,8,128]{2,1,0:T(8,128)S(1)}, u32[]{:S(2)}, u32[]{:S(2)}) collective-permute-start(f32[3,8,128]{2,1,0:T(8,128)S(1)} %shard_map.51.own_high), channel_id=1, source_target_pairs={{0,1},{1,2},{2,3},{3,4},{4,5},{5,6},{6,7},{7,0},{8,9},{9,10},{10,1... | collective-permute-start | bytes 36872 | tf_op jit(solution)/shard_map/ppermute | solution.py:656
  5.2 0.0 collective-permute-start
  5.2 1.6 %collective-permute-start.1 = (f32[31,4,128]{2,1,0:T(4,128)S(1)}, f32[31,4,128]{2,1,0:T(4,128)S(1)}, u32[]{:S(2)}, u32[]{:S(2)}) collective-permute-start(f32[31,4,128]{2,1,0:T(4,128)S(1)} %get-tuple-element.15), channel_id=1, source_target_pairs={{0,24},{8,16},{16,8},{24,0},{1,25},{9,17},{17,9},{25,1},{2,26},{10... | collective-permute-start | bytes 190472 | tf_op jit(solution)/shard_map/ppermute | solution.py:600
  6.8 0.3 %shard_map.53.own_low = f32[16,8,128]{2,1,0:T(8,128)S(1)} custom-call(f32[19,96,128]{2,1,0:T(8,128)S(1)} %get-tuple-element.11.held.own_held, bf16[2,3,64,128]{3,2,1,0:T(8,128)(2,1)S(1)} %get-tuple-element.12.velocity, s32[16,32]{1,0:T(8,128)S(1)} %get-tuple-element.13.solid), custom_call_target="tpu_custom_call" | custom-call | flops 2000000 | bytes 1000000 | tf_op jit(solution)/shard_map/pallas_call | solution.py:635
  7.2 3.3 %collective-permute-start.5 = (f32[16,8,128]{2,1,0:T(8,128)S(1)}, f32[16,8,128]{2,1,0:T(8,128)S(1)}, u32[]{:S(2)}, u32[]{:S(2)}) collective-permute-start(f32[16,8,128]{2,1,0:T(8,128)S(1)} %shard_map.53.own_low), channel_id=1, source_target_pairs={{1,0},{2,1},{3,2},{4,3},{5,4},{6,5},{7,6},{0,7},{9,8},{10,9},{11,1... | collective-permute-start | bytes 196616 | tf_op jit(solution)/shard_map/ppermute | solution.py:669
  10.5 0.0 collective-permute-done.2.columns
  10.5 0.1 shard_map.52
  10.5 0.0 collective-permute-start.4
  10.6 1.4 %collective-permute-start.3 = (f32[3,8,128]{2,1,0:T(8,128)S(1)}, f32[3,8,128]{2,1,0:T(8,128)S(1)}, u32[]{:S(2)}, u32[]{:S(2)}) collective-permute-start(f32[3,8,128]{2,1,0:T(8,128)S(1)} %shard_map.52), channel_id=1, source_target_pairs={{0,8},{8,0},{16,24},{24,16},{1,9},{9,1},{17,25},{25,17},{2,10},{10... | collective-permute-start | bytes 36872 | tf_op jit(solution)/shard_map/ppermute | solution.py:601
  11.9 0.0 collective-permute-done.row_first
  11.9 0.0 collective-permute-done.1.row_second
  11.9 0.2 shard_map.54
  12.1 0.6 %shard_map.55 = (f32[8,128]{1,0:T(8,128)S(1)}, f32[35,8,128]{2,1,0:T(8,128)S(1)}) custom-call(f32[19,96,128]{2,1,0:T(8,128)S(1)} %get-tuple-element.11.held.own_held, bf16[2,3,64,128]{3,2,1,0:T(8,128)(2,1)S(1)} %get-tuple-element.12.velocity, s32[16,32]{1,0:T(8,128)S(1)} %get-tuple-element.13.solid, f32[31,4,128]{2,1,0:T(4,128)S(1)} %collective-permute-done.row_first, ...), custom_call_target="tpu_custom_call" | custom-call | flops 20000000000 | bytes 1000000 | tf_op jit(solution)/shard_map/pallas_call | solution.py:673
  12.7 1.0 %collective-permute-done.4.handed_second = f32[3,8,128]{2,1,0:T(8,128)S(1)} collective-permute-done((f32[3,8,128]{2,1,0:T(8,128)S(1)}, f32[3,8,128]{2,1,0:T(8,128)S(1)}, u32[]{:S(2)}, u32[]{:S(2)}) %collective-permute-start.4) | collective-permute-done | bytes 12320 | tf_op jit(solution)/shard_map/ppermute | solution.py:600
  13.7 0.0 collective-permute-done.3.handed_first
  13.7 0.9 %shard_map.56.rest_0_ = f32[32,1,128]{2,1,0:T(1,128)} custom-call(f32[3,8,128]{2,1,0:T(8,128)S(1)} %collective-permute-done.2.columns, f32[3,8,128]{2,1,0:T(8,128)S(1)} %collective-permute-done.3.handed_first, f32[3,8,128]{2,1,0:T(8,128)S(1)} %collective-permute-done.4.handed_second, f32[35,8,128]{2,1,0:T(8,128)S(1)} %get-tuple-element.17.own_blocks, ...), custom_call_target="tpu_custom_call" | custom-call | flops 1000000 | bytes 1000000 | tf_op jit(solution)/shard_map/pallas_call | solution.py:685
  14.6 2.8 %all-to-all-start = ((f32[32,1,128]{2,1,0:T(1,128)}), f32[32,1,128]{2,1,0:T(1,128)S(1)}, u32[]{:S(2)}, u32[]{:S(2)}) async-start(f32[32,1,128]{2,1,0:T(1,128)} %shard_map.56.rest_0_), calls=%async_computation | async-start | bytes 32768 | tf_op jit(solution)/shard_map/all_to_all | solution.py:694
  17.4 0.0 collective-permute-done.5.columns.columns_after
  17.4 0.8 %shard_map.57 = f32[3,8,128]{2,1,0:T(8,128)S(1)} custom-call(f32[16,8,128]{2,1,0:T(8,128)S(1)} %collective-permute-done.5.columns.columns_after, f32[32,1,128]{2,1,0:T(1,128)} %shard_map.56.rest_0_), custom_call_target="tpu_custom_call" | custom-call | flops 10000000000 | bytes 100000 | tf_op jit(solution)/shard_map/pallas_call | solution.py:658
  18.2 1.5 %collective-permute-start.7 = (f32[3,8,128]{2,1,0:T(8,128)S(1)}, f32[3,8,128]{2,1,0:T(8,128)S(1)}, u32[]{:S(2)}, u32[]{:S(2)}) collective-permute-start(f32[3,8,128]{2,1,0:T(8,128)S(1)} %shard_map.57), channel_id=1, source_target_pairs={{0,24},{8,16},{16,8},{24,0},{1,25},{9,17},{17,9},{25,1},{2,26},{10... | collective-permute-start | bytes 36872 | tf_op jit(solution)/shard_map/ppermute | solution.py:600
  19.8 0.4 %collective-permute-start.6 = (f32[3,8,128]{2,1,0:T(8,128)S(1)}, f32[3,8,128]{2,1,0:T(8,128)S(1)}, u32[]{:S(2)}, u32[]{:S(2)}) collective-permute-start(f32[3,8,128]{2,1,0:T(8,128)S(1)} %shard_map.57), channel_id=1, source_target_pairs={{0,8},{8,0},{16,24},{24,16},{1,9},{9,1},{17,25},{25,17},{2,10},{10... | collective-permute-start | bytes 36872 | tf_op jit(solution)/shard_map/ppermute | solution.py:601
  20.1 1.2 %collective-permute-done.7.after_second = f32[3,8,128]{2,1,0:T(8,128)S(1)} collective-permute-done((f32[3,8,128]{2,1,0:T(8,128)S(1)}, f32[3,8,128]{2,1,0:T(8,128)S(1)}, u32[]{:S(2)}, u32[]{:S(2)}) %collective-permute-start.7) | collective-permute-done | bytes 12320 | tf_op jit(solution)/shard_map/ppermute | solution.py:600
  21.4 0.0 collective-permute-done.6.after_first
  21.4 2.2 %shard_map.58 = f32[19,64,128]{2,1,0:T(8,128)} custom-call(f32[19,96,128]{2,1,0:T(8,128)S(1)} %get-tuple-element.11.held.own_held, bf16[2,3,64,128]{3,2,1,0:T(8,128)(2,1)S(1)} %get-tuple-element.12.velocity, s32[16,32]{1,0:T(8,128)S(1)} %get-tuple-element.13.solid, f32[31,4,128]{2,1,0:T(4,128)S(1)} %collective-permute-done.row_first, ...), custom_call_target="tpu_custom_call" | custom-call | flops 1000000 | bytes 1000000 | tf_op jit(solution)/shard_map/pallas_call | solution.py:695
  23.6 0.9 %all-to-all-done = f32[32,1,128]{2,1,0:T(1,128)S(1)} async-done(((f32[32,1,128]{2,1,0:T(1,128)}), f32[32,1,128]{2,1,0:T(1,128)S(1)}, u32[]{:S(2)}, u32[]{:S(2)}) %all-to-all-start) | async-done | bytes 16416 | tf_op jit(solution)/shard_map/all_to_all | solution.py:694
  24.5 0.6 %slice_reduce_fusion = f32[]{:T(128)} fusion(f32[32,1,128]{2,1,0:T(1,128)S(1)} %all-to-all-done), kind=kLoop, calls=%fused_computation | loop fusion | flops 31 | bytes 132 | tf_op jit(solution)/shard_map/reduce_sum | solution.py:706
Async XLA Ops:
  2.2 8.3 %collective-permute-start.2 = (f32[3,8,128]{2,1,0:T(8,128)S(1)}, f32[3,8,128]{2,1,0:T(8,128)S(1)}, u32[]{:S(2)}, u32[]{:S(2)}) collective-permute-start(f32[3,8,128]{2,1,0:T(8,128)S(1)} %shard_map.51.own_high), channel_id=1, source_target_pairs={{0,1},{1,2},{2,3},{3,4},{4,5},{5,6},{6,7},{7,0},{8,9},{9,10},{10,1... | collective-permute-start | bytes 36872 | tf_op jit(solution)/shard_map/ppermute | solution.py:656
  5.2 6.7 %collective-permute-start = (f32[31,4,128]{2,1,0:T(4,128)S(1)}, f32[31,4,128]{2,1,0:T(4,128)S(1)}, u32[]{:S(2)}, u32[]{:S(2)}) collective-permute-start(f32[31,4,128]{2,1,0:T(4,128)S(1)} %get-tuple-element.14), channel_id=1, source_target_pairs={{0,8},{8,0},{16,24},{24,16},{1,9},{9,1},{17,25},{25,17},{2,10},{10... | collective-permute-start | bytes 190472 | tf_op jit(solution)/shard_map/ppermute | solution.py:601
  5.2 6.7 %collective-permute-start.1 = (f32[31,4,128]{2,1,0:T(4,128)S(1)}, f32[31,4,128]{2,1,0:T(4,128)S(1)}, u32[]{:S(2)}, u32[]{:S(2)}) collective-permute-start(f32[31,4,128]{2,1,0:T(4,128)S(1)} %get-tuple-element.15), channel_id=1, source_target_pairs={{0,24},{8,16},{16,8},{24,0},{1,25},{9,17},{17,9},{25,1},{2,26},{10... | collective-permute-start | bytes 190472 | tf_op jit(solution)/shard_map/ppermute | solution.py:600
  7.2 10.2 %collective-permute-start.5 = (f32[16,8,128]{2,1,0:T(8,128)S(1)}, f32[16,8,128]{2,1,0:T(8,128)S(1)}, u32[]{:S(2)}, u32[]{:S(2)}) collective-permute-start(f32[16,8,128]{2,1,0:T(8,128)S(1)} %shard_map.53.own_low), channel_id=1, source_target_pairs={{1,0},{2,1},{3,2},{4,3},{5,4},{6,5},{7,6},{0,7},{9,8},{10,9},{11,1... | collective-permute-start | bytes 196616 | tf_op jit(solution)/shard_map/ppermute | solution.py:669
  10.5 3.2 %collective-permute-start.4 = (f32[3,8,128]{2,1,0:T(8,128)S(1)}, f32[3,8,128]{2,1,0:T(8,128)S(1)}, u32[]{:S(2)}, u32[]{:S(2)}) collective-permute-start(f32[3,8,128]{2,1,0:T(8,128)S(1)} %shard_map.52), channel_id=1, source_target_pairs={{0,24},{8,16},{16,8},{24,0},{1,25},{9,17},{17,9},{25,1},{2,26},{10... | collective-permute-start | bytes 36872 | tf_op jit(solution)/shard_map/ppermute | solution.py:600
  10.6 3.1 %collective-permute-start.3 = (f32[3,8,128]{2,1,0:T(8,128)S(1)}, f32[3,8,128]{2,1,0:T(8,128)S(1)}, u32[]{:S(2)}, u32[]{:S(2)}) collective-permute-start(f32[3,8,128]{2,1,0:T(8,128)S(1)} %shard_map.52), channel_id=1, source_target_pairs={{0,8},{8,0},{16,24},{24,16},{1,9},{9,1},{17,25},{25,17},{2,10},{10... | collective-permute-start | bytes 36872 | tf_op jit(solution)/shard_map/ppermute | solution.py:601
  14.6 9.9 %all-to-all-start = ((f32[32,1,128]{2,1,0:T(1,128)}), f32[32,1,128]{2,1,0:T(1,128)S(1)}, u32[]{:S(2)}, u32[]{:S(2)}) async-start(f32[32,1,128]{2,1,0:T(1,128)} %shard_map.56.rest_0_), calls=%async_computation | async-start | bytes 32768 | tf_op jit(solution)/shard_map/all_to_all | solution.py:694
  18.2 3.1 %collective-permute-start.7 = (f32[3,8,128]{2,1,0:T(8,128)S(1)}, f32[3,8,128]{2,1,0:T(8,128)S(1)}, u32[]{:S(2)}, u32[]{:S(2)}) collective-permute-start(f32[3,8,128]{2,1,0:T(8,128)S(1)} %shard_map.57), channel_id=1, source_target_pairs={{0,24},{8,16},{16,8},{24,0},{1,25},{9,17},{17,9},{25,1},{2,26},{10... | collective-permute-start | bytes 36872 | tf_op jit(solution)/shard_map/ppermute | solution.py:600
  19.8 1.6 %collective-permute-start.6 = (f32[3,8,128]{2,1,0:T(8,128)S(1)}, f32[3,8,128]{2,1,0:T(8,128)S(1)}, u32[]{:S(2)}, u32[]{:S(2)}) collective-permute-start(f32[3,8,128]{2,1,0:T(8,128)S(1)} %shard_map.57), channel_id=1, source_target_pairs={{0,8},{8,0},{16,24},{24,16},{1,9},{9,1},{17,25},{25,17},{2,10},{10... | collective-permute-start | bytes 36872 | tf_op jit(solution)/shard_map/ppermute | solution.py:601

commit v17 on v16

--- a/solution.py
+++ b/solution.py
@@ -110,20 +110,44 @@
     parts[part] = jnp.where(lane == place + ahead, turned, parts[part])
 
 
-def row_message_kernel(
-    state, velocity, solid, row_first, row_second, held, flow, tiles, arrived
+def first_columns_kernel(
+    state, velocity, solid, high, held, flow, tiles, arrived
 ):
     rows = state.shape[1]
+    groups = rows // 8 + 2
     own = pl.ds(GUARD + 8, rows)
+    chunks = ((0, 5), (5, 5), (10, 5), (15, 4))
     copies = [
-        pltpu.make_async_copy(state, held.at[:, own, :], arrived.at[0]),
-        pltpu.make_async_copy(velocity, flow, arrived.at[1]),
-        pltpu.make_async_copy(solid, tiles, arrived.at[2]),
+        pltpu.make_async_copy(velocity, flow, arrived.at[0]),
+        pltpu.make_async_copy(solid, tiles, arrived.at[1]),
     ]
+    for place, (first, count) in enumerate(chunks):
+        part = pl.ds(first, count)
+        copies.append(pltpu.make_async_copy(state.at[part], held.at[part, own, :], arrived.at[2 + place]))
     for copy in copies:
         copy.start()
-    for copy in copies:
+    parts = [None, [jnp.zeros((8, LANES), jnp.float32) for _ in range(high.shape[0])]]
+    copies[0].wait()
+    blocks = [flow_blocks(flow, step, rows) for step in range(2)]
+    for group in range(1, groups - 1):
+        for axis in range(3):
+            pack_columns(parts, FLOW + axis, group, groups, blocks[0][group - 1][axis])
+            pack_columns(parts, NEXT + axis, group, groups, blocks[1][group - 1][axis])
+    copies[1].wait()
+    solid_parts = spread_solid(tiles)
+    for group in range(1, groups - 1):
+        pack_columns(parts, SOLID, group, groups, solid_parts[(group - 1) * 8 // (LEVELS * TILE)])
+    for copy, (first, count) in zip(copies[2:], chunks):
         copy.wait()
+        for slot in range(first, first + count):
+            for group in range(1, groups - 1):
+                pack_columns(parts, slot, group, groups, held[slot, pl.ds(GUARD + 8 * group, 8), :])
+    for part in range(high.shape[0]):
+        high[part] = parts[1][part]
+
+
+def row_message_kernel(held, flow, tiles, row_first, row_second):
+    rows = flow.shape[2]
     even = on_even("gx")
     low_row, high_row = GUARD + 8, GUARD + 8 + rows - LEVELS
 
@@ -158,14 +182,12 @@
             insert_column(message, second, group, groups, value, edge + step, ahead)
 
 
-def own_columns_kernel(side, held, velocity, solid, *rest):
-    out = rest[-1]
+def own_columns_kernel(held, velocity, solid, row_sent, out):
     rows = velocity.shape[2]
     groups = rows // 8 + 2
     solid_parts = spread_solid(solid)
     flow = [flow_blocks(velocity, step, rows) for step in range(2)]
-    parts = [None, None]
-    parts[side] = [jnp.zeros((8, LANES), jnp.float32) for _ in range(out.shape[0])]
+    parts = [[jnp.zeros((8, LANES), jnp.float32) for _ in range(out.shape[0])], None]
     for group in range(1, groups - 1):
         for slot in range(19):
             pack_columns(parts, slot, group, groups, held[slot, pl.ds(GUARD + 8 * group, 8), :])
@@ -174,7 +196,7 @@
             pack_columns(parts, NEXT + axis, group, groups, flow[1][group - 1][axis])
         pack_columns(parts, SOLID, group, groups, solid_parts[(group - 1) * 8 // (LEVELS * TILE)])
     for part in range(out.shape[0]):
-        out[part] = parts[side][part]
+        out[part] = parts[0][part]
 
 
 def halo_columns_kernel(groups, own_low, own_high, row_first, row_second, low_out, high_out, ends):
@@ -616,33 +638,35 @@
 
     params = pltpu.CompilerParams(vmem_limit_bytes=16 * 1024 * 1024)
     anywhere = pl.BlockSpec(memory_space=pl.ANY)
-    *row_sent, held, flow, tiles = pl.pallas_call(
-        row_message_kernel,
+    own_high, held, flow, tiles = pl.pallas_call(
+        first_columns_kernel,
         out_shape=(
-            pltpu.VMEM((QUANTITIES, levels, rows_y), jnp.float32),
-            pltpu.VMEM((QUANTITIES, levels, rows_y), jnp.float32),
+            pltpu.VMEM((parts, 8, rows_y), jnp.float32),
             pltpu.VMEM((19, padded, rows_y), jnp.float32),
             pltpu.VMEM(flow.shape, flow.dtype),
             pltpu.VMEM(solid.shape, solid.dtype),
         ),
         in_specs=[anywhere] * 3,
-        out_specs=(vmem,) * 5,
-        scratch_shapes=[pltpu.SemaphoreType.DMA((3,))],
+        out_specs=(vmem,) * 4,
+        scratch_shapes=[pltpu.SemaphoreType.DMA((6,))],
         compiler_params=params,
     )(*(pltpu.with_memory_space_constraint(value, pltpu.HBM) for value in (state, flow, solid)))
+    row_sent = pl.pallas_call(
+        row_message_kernel,
+        out_shape=(pltpu.VMEM((QUANTITIES, levels, rows_y), jnp.float32),) * 2,
+        in_specs=[vmem] * 3,
+        out_specs=(vmem,) * 2,
+        compiler_params=params,
+    )(held, flow, tiles)
     row_got = swap_pairs(*row_sent, "gx")
-    def pack(side, size, *later_than):
-        return pl.pallas_call(
-            functools.partial(own_columns_kernel, side),
-            out_shape=shape_of(size, 8, rows_y),
-            in_specs=[vmem] * (3 + len(later_than)),
-            out_specs=vmem,
-            compiler_params=params,
-            cost_estimate=pl.CostEstimate(flops=2_000_000, bytes_accessed=1_000_000, transcendentals=0),
-        )(held, flow, tiles, *later_than)
-
-    own_high = pack(1, parts)
-    own_low = pack(0, 16)
+    own_low = pl.pallas_call(
+        own_columns_kernel,
+        out_shape=shape_of(16, 8, rows_y),
+        in_specs=[vmem] * 4,
+        out_specs=vmem,
+        compiler_params=params,
+        cost_estimate=pl.CostEstimate(flops=2_000_000, bytes_accessed=1_000_000, transcendentals=0),
+    )(held, flow, tiles, row_sent[0])
     own_columns = own_low, own_high
     low, high = pl.pallas_call(
         functools.partial(halo_columns_kernel, groups),

time: 27.2 us -> 27.4 us (level)
  Pallas kernels: 6.79 us -> 7.08 us
    pallas_call x2, Pallas kernels: 0.66 us -> 2.07 us  [the longest x1 1.74 us: per_device(): pl.pallas_call(first_columns_kernel, out_shape=(pltpu.VMEM((parts, 8, row...]
    pallas_call x1, Pallas kernels: 1.24 us -> 0.12 us  [per_device(): pl.pallas_call(row_message_kernel, out_shape=(pltpu.VMEM((QUANTITIES, lev...]
    ppermute x3, starting transfers between devices: 3.17 us -> 2.22 us  [swap_pairs(): second = lax.ppermute(second, axis, across)]
    ppermute x3, starting transfers between devices: 1.73 us -> 2.56 us  [swap_pairs(): return (lax.ppermute(first, axis, inside), second)]
  transfers between devices with their start and end apart: 9 -> 9, of which waited for: 3 -> 3; matrix products, arithmetic and copies ran while one was open for 0% -> 0% of each run, Pallas kernels for 19% -> 20%
where the time goes in v17:
time: 27.4 us; the launch traced here: 27.1 us
  starting transfers between devices  13.7 us (50%)
  Pallas kernels  7.08 us (26%)
  waiting for transfers between devices  3.23 us (12%)
  between operations  2.46 us (9%)
  other arithmetic  0.63 us (2%)
    ppermute x1, starting transfers between devices, per_device(): lax.ppermute(own_columns[0], 'gy', [((i + 1) % size, i) for i in range(si...  3.28 us
    ppermute x1, starting transfers between devices, per_device(): lax.ppermute(own_columns[1], 'gy', [(i, (i + 1) % size) for i in range(si...  2.99 us
    all_to_all x1, starting transfers between devices, per_device(): lax.all_to_all(own, ('gx', 'gy'), split_axis=0, concat_axis=0, tiled=True)  2.63 us
    ppermute x3, starting transfers between devices, swap_pairs(): return (lax.ppermute(first, axis, inside), second)  2.56 us
    ppermute x3, waiting for transfers between devices, swap_pairs(): second = lax.ppermute(second, axis, across)  2.32 us
    pallas_call x1, Pallas kernels, per_device(): pl.pallas_call(main_kernel, out_shape=shape_of(19, rows, rows_y), in_spec...  2.24 us
    ppermute x3, starting transfers between devices, swap_pairs(): second = lax.ppermute(second, axis, across)  2.22 us
    pallas_call x1, Pallas kernels, per_device(): pl.pallas_call(first_columns_kernel, out_shape=(pltpu.VMEM((parts, 8, row...  1.74 us
  transfers between devices with their start and end apart: 9, of which 3 were waited for; matrix products, arithmetic and copies ran while one was open for 0% of the time, Pallas kernels for 20%

profile of v17, /device:TPU:0, one launch (start us, length us, event | category | flops | bytes accessed | tf_op | source)
XLA Modules:
  0.0 27.1 jit_solution(4559642300893633075)
XLA Ops:
  0.6 1.7 %shard_map.50 = (f32[3,8,128]{2,1,0:T(8,128)S(1)}, f32[19,96,128]{2,1,0:T(8,128)S(1)}, bf16[2,3,64,128]{3,2,1,0:T(8,128)(2,1)S(1)}, s32[16,32]{1,0:T(8,128)S(1)}) custom-call(f32[19,64,128]{2,1,0:T(8,128)} %bitcast.5, bf16[2,3,64,128]{3,2,1,0:T(8,128)(2,1)} %bitcast.7, s32[16,32]{1,0:T(8,128)} %bitcast.8), custom_call_target="tpu_custom_call" | custom-call | tf_op jit(solution)/shard_map/pallas_call | solution.py:641
  2.4 3.0 %collective-permute-start.2 = (f32[3,8,128]{2,1,0:T(8,128)S(1)}, f32[3,8,128]{2,1,0:T(8,128)S(1)}, u32[]{:S(2)}, u32[]{:S(2)}) collective-permute-start(f32[3,8,128]{2,1,0:T(8,128)S(1)} %get-tuple-element.17.own_high), channel_id=1, source_target_pairs={{0,1},{1,2},{2,3},{3,4},{4,5},{5,6},{6,7},{7,0},{8,9},{9,10},{10,1... | collective-permute-start | bytes 36872 | tf_op jit(solution)/shard_map/ppermute | solution.py:680
  5.4 0.1 shard_map.51
  5.5 0.7 %collective-permute-start.1 = (f32[31,4,128]{2,1,0:T(4,128)S(1)}, f32[31,4,128]{2,1,0:T(4,128)S(1)}, u32[]{:S(2)}, u32[]{:S(2)}) collective-permute-start(f32[31,4,128]{2,1,0:T(4,128)S(1)} %get-tuple-element.16), channel_id=1, source_target_pairs={{0,24},{8,16},{16,8},{24,0},{1,25},{9,17},{17,9},{25,1},{2,26},{10... | collective-permute-start | bytes 190472 | tf_op jit(solution)/shard_map/ppermute | solution.py:622
  6.2 1.0 %collective-permute-start = (f32[31,4,128]{2,1,0:T(4,128)S(1)}, f32[31,4,128]{2,1,0:T(4,128)S(1)}, u32[]{:S(2)}, u32[]{:S(2)}) collective-permute-start(f32[31,4,128]{2,1,0:T(4,128)S(1)} %get-tuple-element.15.row_sent), channel_id=1, source_target_pairs={{0,8},{8,0},{16,24},{24,16},{1,9},{9,1},{17,25},{25,17},{2,10},{10... | collective-permute-start | bytes 190472 | tf_op jit(solution)/shard_map/ppermute | solution.py:623
  7.1 0.3 %shard_map.53.own_low = f32[16,8,128]{2,1,0:T(8,128)S(1)} custom-call(f32[19,96,128]{2,1,0:T(8,128)S(1)} %get-tuple-element.12.held.own_held, bf16[2,3,64,128]{3,2,1,0:T(8,128)(2,1)S(1)} %get-tuple-element.13.flow.velocity, s32[16,32]{1,0:T(8,128)S(1)} %get-tuple-element.14.tiles.solid, f32[31,4,128]{2,1,0:T(4,128)S(1)} %get-tuple-element.15.row_sent), custom_call_target="tpu_custom_call" | custom-call | flops 2000000 | bytes 1000000 | tf_op jit(solution)/shard_map/pallas_call | solution.py:662
  7.5 3.3 %collective-permute-start.5 = (f32[16,8,128]{2,1,0:T(8,128)S(1)}, f32[16,8,128]{2,1,0:T(8,128)S(1)}, u32[]{:S(2)}, u32[]{:S(2)}) collective-permute-start(f32[16,8,128]{2,1,0:T(8,128)S(1)} %shard_map.53.own_low), channel_id=1, source_target_pairs={{1,0},{2,1},{3,2},{4,3},{5,4},{6,5},{7,6},{0,7},{9,8},{10,9},{11,1... | collective-permute-start | bytes 196616 | tf_op jit(solution)/shard_map/ppermute | solution.py:693
  10.8 0.0 collective-permute-done.2.columns
  10.8 0.1 shard_map.52
  10.8 0.0 collective-permute-start.4
  10.8 1.2 %collective-permute-start.3 = (f32[3,8,128]{2,1,0:T(8,128)S(1)}, f32[3,8,128]{2,1,0:T(8,128)S(1)}, u32[]{:S(2)}, u32[]{:S(2)}) collective-permute-start(f32[3,8,128]{2,1,0:T(8,128)S(1)} %shard_map.52), channel_id=1, source_target_pairs={{0,8},{8,0},{16,24},{24,16},{1,9},{9,1},{17,25},{25,17},{2,10},{10... | collective-permute-start | bytes 36872 | tf_op jit(solution)/shard_map/ppermute | solution.py:623
  12.1 0.0 collective-permute-done.1.row_second
  12.1 0.0 collective-permute-done.row_first
  12.1 0.2 shard_map.54
  12.3 0.6 %shard_map.55 = (f32[8,128]{1,0:T(8,128)S(1)}, f32[35,8,128]{2,1,0:T(8,128)S(1)}) custom-call(f32[19,96,128]{2,1,0:T(8,128)S(1)} %get-tuple-element.12.held.own_held, bf16[2,3,64,128]{3,2,1,0:T(8,128)(2,1)S(1)} %get-tuple-element.13.flow.velocity, s32[16,32]{1,0:T(8,128)S(1)} %get-tuple-element.14.tiles.solid, ...), custom_call_target="tpu_custom_call" | custom-call | flops 20000000000 | bytes 1000000 | tf_op jit(solution)/shard_map/pallas_call | solution.py:697
  12.9 1.1 %collective-permute-done.4.handed_second = f32[3,8,128]{2,1,0:T(8,128)S(1)} collective-permute-done((f32[3,8,128]{2,1,0:T(8,128)S(1)}, f32[3,8,128]{2,1,0:T(8,128)S(1)}, u32[]{:S(2)}, u32[]{:S(2)}) %collective-permute-start.4) | collective-permute-done | bytes 12320 | tf_op jit(solution)/shard_map/ppermute | solution.py:622
  14.0 0.0 collective-permute-done.3.handed_first
  14.0 0.9 %shard_map.56.rest_0_ = f32[32,1,128]{2,1,0:T(1,128)} custom-call(f32[3,8,128]{2,1,0:T(8,128)S(1)} %collective-permute-done.2.columns, f32[3,8,128]{2,1,0:T(8,128)S(1)} %collective-permute-done.3.handed_first, f32[3,8,128]{2,1,0:T(8,128)S(1)} %collective-permute-done.4.handed_second, f32[35,8,128]{2,1,0:T(8,128)S(1)} %get-tuple-element.19.own_blocks, ...), custom_call_target="tpu_custom_call" | custom-call | flops 1000000 | bytes 1000000 | tf_op jit(solution)/shard_map/pallas_call | solution.py:709
  14.9 2.6 %all-to-all-start = ((f32[32,1,128]{2,1,0:T(1,128)}), f32[32,1,128]{2,1,0:T(1,128)S(1)}, u32[]{:S(2)}, u32[]{:S(2)}) async-start(f32[32,1,128]{2,1,0:T(1,128)} %shard_map.56.rest_0_), calls=%async_computation | async-start | bytes 32768 | tf_op jit(solution)/shard_map/all_to_all | solution.py:718
  17.6 0.0 collective-permute-done.5.columns.columns_after
  17.6 0.8 %shard_map.57 = f32[3,8,128]{2,1,0:T(8,128)S(1)} custom-call(f32[16,8,128]{2,1,0:T(8,128)S(1)} %collective-permute-done.5.columns.columns_after, f32[32,1,128]{2,1,0:T(1,128)} %shard_map.56.rest_0_), custom_call_target="tpu_custom_call" | custom-call | flops 10000000000 | bytes 100000 | tf_op jit(solution)/shard_map/pallas_call | solution.py:682
  18.4 1.5 %collective-permute-start.7 = (f32[3,8,128]{2,1,0:T(8,128)S(1)}, f32[3,8,128]{2,1,0:T(8,128)S(1)}, u32[]{:S(2)}, u32[]{:S(2)}) collective-permute-start(f32[3,8,128]{2,1,0:T(8,128)S(1)} %shard_map.57), channel_id=1, source_target_pairs={{0,24},{8,16},{16,8},{24,0},{1,25},{9,17},{17,9},{25,1},{2,26},{10... | collective-permute-start | bytes 36872 | tf_op jit(solution)/shard_map/ppermute | solution.py:622
  19.9 0.4 %collective-permute-start.6 = (f32[3,8,128]{2,1,0:T(8,128)S(1)}, f32[3,8,128]{2,1,0:T(8,128)S(1)}, u32[]{:S(2)}, u32[]{:S(2)}) collective-permute-start(f32[3,8,128]{2,1,0:T(8,128)S(1)} %shard_map.57), channel_id=1, source_target_pairs={{0,8},{8,0},{16,24},{24,16},{1,9},{9,1},{17,25},{25,17},{2,10},{10... | collective-permute-start | bytes 36872 | tf_op jit(solution)/shard_map/ppermute | solution.py:623
  20.3 1.2 %collective-permute-done.7.after_second = f32[3,8,128]{2,1,0:T(8,128)S(1)} collective-permute-done((f32[3,8,128]{2,1,0:T(8,128)S(1)}, f32[3,8,128]{2,1,0:T(8,128)S(1)}, u32[]{:S(2)}, u32[]{:S(2)}) %collective-permute-start.7) | collective-permute-done | bytes 12320 | tf_op jit(solution)/shard_map/ppermute | solution.py:622
  21.5 0.0 collective-permute-done.6.after_first
  21.5 2.2 %shard_map.58 = f32[19,64,128]{2,1,0:T(8,128)} custom-call(f32[19,96,128]{2,1,0:T(8,128)S(1)} %get-tuple-element.12.held.own_held, bf16[2,3,64,128]{3,2,1,0:T(8,128)(2,1)S(1)} %get-tuple-element.13.flow.velocity, s32[16,32]{1,0:T(8,128)S(1)} %get-tuple-element.14.tiles.solid, f32[31,4,128]{2,1,0:T(4,128)S(1)} %collective-permute-done.row_first, ...), custom_call_target="tpu_custom_call" | custom-call | flops 1000000 | bytes 1000000 | tf_op jit(solution)/shard_map/pallas_call | solution.py:719
  23.8 0.9 %all-to-all-done = f32[32,1,128]{2,1,0:T(1,128)S(1)} async-done(((f32[32,1,128]{2,1,0:T(1,128)}), f32[32,1,128]{2,1,0:T(1,128)S(1)}, u32[]{:S(2)}, u32[]{:S(2)}) %all-to-all-start) | async-done | bytes 16416 | tf_op jit(solution)/shard_map/all_to_all | solution.py:718
  24.7 0.6 %slice_reduce_fusion = f32[]{:T(128)} fusion(f32[32,1,128]{2,1,0:T(1,128)S(1)} %all-to-all-done), kind=kLoop, calls=%fused_computation | loop fusion | flops 31 | bytes 132 | tf_op jit(solution)/shard_map/reduce_sum | solution.py:730
Async XLA Ops:
  2.4 8.4 %collective-permute-start.2 = (f32[3,8,128]{2,1,0:T(8,128)S(1)}, f32[3,8,128]{2,1,0:T(8,128)S(1)}, u32[]{:S(2)}, u32[]{:S(2)}) collective-permute-start(f32[3,8,128]{2,1,0:T(8,128)S(1)} %get-tuple-element.17.own_high), channel_id=1, source_target_pairs={{0,1},{1,2},{2,3},{3,4},{4,5},{5,6},{6,7},{7,0},{8,9},{9,10},{10,1... | collective-permute-start | bytes 36872 | tf_op jit(solution)/shard_map/ppermute | solution.py:680
  5.5 6.6 %collective-permute-start.1 = (f32[31,4,128]{2,1,0:T(4,128)S(1)}, f32[31,4,128]{2,1,0:T(4,128)S(1)}, u32[]{:S(2)}, u32[]{:S(2)}) collective-permute-start(f32[31,4,128]{2,1,0:T(4,128)S(1)} %get-tuple-element.16), channel_id=1, source_target_pairs={{0,24},{8,16},{16,8},{24,0},{1,25},{9,17},{17,9},{25,1},{2,26},{10... | collective-permute-start | bytes 190472 | tf_op jit(solution)/shard_map/ppermute | solution.py:622
  6.2 5.9 %collective-permute-start = (f32[31,4,128]{2,1,0:T(4,128)S(1)}, f32[31,4,128]{2,1,0:T(4,128)S(1)}, u32[]{:S(2)}, u32[]{:S(2)}) collective-permute-start(f32[31,4,128]{2,1,0:T(4,128)S(1)} %get-tuple-element.15.row_sent), channel_id=1, source_target_pairs={{0,8},{8,0},{16,24},{24,16},{1,9},{9,1},{17,25},{25,17},{2,10},{10... | collective-permute-start | bytes 190472 | tf_op jit(solution)/shard_map/ppermute | solution.py:623
  7.5 10.1 %collective-permute-start.5 = (f32[16,8,128]{2,1,0:T(8,128)S(1)}, f32[16,8,128]{2,1,0:T(8,128)S(1)}, u32[]{:S(2)}, u32[]{:S(2)}) collective-permute-start(f32[16,8,128]{2,1,0:T(8,128)S(1)} %shard_map.53.own_low), channel_id=1, source_target_pairs={{1,0},{2,1},{3,2},{4,3},{5,4},{6,5},{7,6},{0,7},{9,8},{10,9},{11,1... | collective-permute-start | bytes 196616 | tf_op jit(solution)/shard_map/ppermute | solution.py:693
  10.8 3.2 %collective-permute-start.4 = (f32[3,8,128]{2,1,0:T(8,128)S(1)}, f32[3,8,128]{2,1,0:T(8,128)S(1)}, u32[]{:S(2)}, u32[]{:S(2)}) collective-permute-start(f32[3,8,128]{2,1,0:T(8,128)S(1)} %shard_map.52), channel_id=1, source_target_pairs={{0,24},{8,16},{16,8},{24,0},{1,25},{9,17},{17,9},{25,1},{2,26},{10... | collective-permute-start | bytes 36872 | tf_op jit(solution)/shard_map/ppermute | solution.py:622
  10.8 3.1 %collective-permute-start.3 = (f32[3,8,128]{2,1,0:T(8,128)S(1)}, f32[3,8,128]{2,1,0:T(8,128)S(1)}, u32[]{:S(2)}, u32[]{:S(2)}) collective-permute-start(f32[3,8,128]{2,1,0:T(8,128)S(1)} %shard_map.52), channel_id=1, source_target_pairs={{0,8},{8,0},{16,24},{24,16},{1,9},{9,1},{17,25},{25,17},{2,10},{10... | collective-permute-start | bytes 36872 | tf_op jit(solution)/shard_map/ppermute | solution.py:623
  14.9 9.8 %all-to-all-start = ((f32[32,1,128]{2,1,0:T(1,128)}), f32[32,1,128]{2,1,0:T(1,128)S(1)}, u32[]{:S(2)}, u32[]{:S(2)}) async-start(f32[32,1,128]{2,1,0:T(1,128)} %shard_map.56.rest_0_), calls=%async_computation | async-start | bytes 32768 | tf_op jit(solution)/shard_map/all_to_all | solution.py:718
  18.4 3.1 %collective-permute-start.7 = (f32[3,8,128]{2,1,0:T(8,128)S(1)}, f32[3,8,128]{2,1,0:T(8,128)S(1)}, u32[]{:S(2)}, u32[]{:S(2)}) collective-permute-start(f32[3,8,128]{2,1,0:T(8,128)S(1)} %shard_map.57), channel_id=1, source_target_pairs={{0,24},{8,16},{16,8},{24,0},{1,25},{9,17},{17,9},{25,1},{2,26},{10... | collective-permute-start | bytes 36872 | tf_op jit(solution)/shard_map/ppermute | solution.py:622
  19.9 1.6 %collective-permute-start.6 = (f32[3,8,128]{2,1,0:T(8,128)S(1)}, f32[3,8,128]{2,1,0:T(8,128)S(1)}, u32[]{:S(2)}, u32[]{:S(2)}) collective-permute-start(f32[3,8,128]{2,1,0:T(8,128)S(1)} %shard_map.57), channel_id=1, source_target_pairs={{0,8},{8,0},{16,24},{24,16},{1,9},{9,1},{17,25},{25,17},{2,10},{10... | collective-permute-start | bytes 36872 | tf_op jit(solution)/shard_map/ppermute | solution.py:623

commit v18 on v16

--- a/solution.py
+++ b/solution.py
@@ -478,10 +478,20 @@
     return whole
 
 
-def edge_drag_kernel(groups, columns, handed_first, handed_second, own_blocks, partial, shared):
+def with_diagonals(columns, from_before, from_after, groups):
+    above, below = halo_lanes(groups, 0)
+    whole = []
+    for part in range(columns.shape[0]):
+        last = pltpu.roll(from_before[part], LANES - (groups - 2), 1)
+        first = pltpu.roll(from_after[part], groups - 2, 1)
+        whole.append(jnp.where(above, last, jnp.where(below, first, columns[part])))
+    return whole
+
+
+def edge_drag_kernel(groups, columns, diagonal_before, diagonal_after, own_blocks, partial, shared):
     lane = lane_index()
     column = column_reader(groups)
-    y_before = with_halo_rows(columns, handed_first, handed_second, groups, 0)
+    y_before = with_diagonals(columns, diagonal_before, diagonal_after, groups)
 
     def neighbours(slot, cy):
         if cy == 1:
@@ -511,7 +521,7 @@
 
 
 def main_kernel(
-    own_held, velocity, solid, row_first, row_second, columns, handed_first, handed_second,
+    own_held, velocity, solid, row_first, row_second, columns, diagonal_before, diagonal_after,
     columns_after, after_first, after_second, low, high, out, held, shifted, later, solid_rows, row_flow,
 ):
     rows = velocity.shape[2]
@@ -523,7 +533,7 @@
     lane = lane_index()
     solid_parts = spread_solid(solid)
     column = column_reader(groups)
-    y_before = with_halo_rows(columns, handed_first, handed_second, groups, 0)
+    y_before = with_diagonals(columns, diagonal_before, diagonal_after, groups)
     y_after = with_halo_rows(columns_after, after_first, after_second, groups, 1)
 
     def edge_of(slot, cy, group):
@@ -599,6 +609,14 @@
     across = [(i, (i + 1) % count if i % 2 == 1 else (i - 1) % count) for i in range(count)]
     second = lax.ppermute(second, axis, across)
     return lax.ppermute(first, axis, inside), second
+
+
+def from_diagonal(value, side):
+    nx, ny = lax.axis_size("gx"), lax.axis_size("gy")
+    pairs = [
+        (i * ny + j, (i + side) % nx * ny + (j + 1) % ny) for i in range(nx) for j in range(ny)
+    ]
+    return lax.ppermute(value, ("gx", "gy"), pairs)
 
 
 def per_device(adjoint_in, velocity, solid_tiles, link_blocked):
@@ -665,7 +683,7 @@
         )(columns, *later_than)
         return swap_pairs(handed, handed, "gx")
 
-    handed = hand_on(y_before, 0)
+    diagonals = [from_diagonal(own_columns[1], side) for side in (1, -1)]
     y_after = lax.ppermute(own_columns[0], "gy", [((i + 1) % size, i) for i in range(size)])
     count = lax.axis_size("gx") * size
     field = pltpu.VMEM((19, padded, rows_y), jnp.float32)
@@ -689,7 +707,7 @@
         out_specs=vmem,
         compiler_params=params,
         cost_estimate=pl.CostEstimate(flops=1_000_000, bytes_accessed=1_000_000, transcendentals=0),
-    )(y_before, *handed, own_blocks, partial)
+    )(y_before, *diagonals, own_blocks, partial)
     handed_after = hand_on(y_after, 1, own)
     shared = lax.all_to_all(own, ("gx", "gy"), split_axis=0, concat_axis=0, tiled=True)
     result = pl.pallas_call(
@@ -700,7 +718,7 @@
         scratch_shapes=[field, field, field, solid_field, pltpu.VMEM((4, 8, rows_y), jnp.float32)],
         compiler_params=params,
         cost_estimate=pl.CostEstimate(flops=1_000_000, bytes_accessed=1_000_000, transcendentals=0),
-    )(held, flow, tiles, *row_got, y_before, *handed, y_after, *handed_after, low, high)
+    )(held, flow, tiles, *row_got, y_before, *diagonals, y_after, *handed_after, low, high)
     cell_count = rows * rows_y * count
     scale = drag_factor / math.sqrt(cell_count) * 3.0 / 36.0
     total = jnp.sum(shared[:, 0, 0])

time: 27.2 us -> 28.2 us (1.037)
  starting transfers between devices: 13.9 us -> 15 us
    ppermute x0 -> x2, starting transfers between devices: none -> 2.81 us  [from_diagonal(): return lax.ppermute(value, ('gx', 'gy'), pairs)]
    ppermute x1, starting transfers between devices: 2.99 us -> 1.49 us  [per_device(): lax.ppermute(own_columns[1], 'gy', [(i, (i + 1) % size) for i in range(si...]
    ppermute x3 -> x2, starting transfers between devices: 3.17 us -> 4.06 us  [swap_pairs(): second = lax.ppermute(second, axis, across)]
    ppermute x3 -> x2, starting transfers between devices: 1.73 us -> 0.88 us  [swap_pairs(): return (lax.ppermute(first, axis, inside), second)]
    ppermute x3 -> x2, waiting for transfers between devices: 2.19 us -> 1.35 us  [swap_pairs(): second = lax.ppermute(second, axis, across)]
    ppermute x1, waiting for transfers between devices: 0.01 us -> 0.67 us  [per_device(): lax.ppermute(own_columns[1], 'gy', [(i, (i + 1) % size) for i in range(si...]
    pallas_call x2 -> x1, Pallas kernels: 0.9 us -> 0.83 us  [hand_on(): pl.pallas_call(functools.partial(hand_on_kernel, groups, ahead), out_shap...]
  transfers between devices with their start and end apart: 9 -> 9, of which waited for: 3 -> 3; matrix products, arithmetic and copies ran while one was open for 0% -> 0% of each run, Pallas kernels for 19% -> 20%
where the time goes in v18:
time: 28.2 us; the launch traced here: 27.9 us
  starting transfers between devices  15 us (53%)
  Pallas kernels  6.77 us (24%)
  waiting for transfers between devices  2.94 us (10%)
  between operations  2.48 us (9%)
  other arithmetic  0.63 us (2%)
    ppermute x2, starting transfers between devices, swap_pairs(): second = lax.ppermute(second, axis, across)  4.06 us
    ppermute x1, starting transfers between devices, per_device(): lax.ppermute(own_columns[0], 'gy', [((i + 1) % size, i) for i in range(si...  3.28 us
    ppermute x2, starting transfers between devices, from_diagonal(): return lax.ppermute(value, ('gx', 'gy'), pairs)  2.81 us
    all_to_all x1, starting transfers between devices, per_device(): lax.all_to_all(own, ('gx', 'gy'), split_axis=0, concat_axis=0, tiled=True)  2.51 us
    pallas_call x1, Pallas kernels, per_device(): pl.pallas_call(main_kernel, out_shape=shape_of(19, rows, rows_y), in_spec...  2.24 us
    ppermute x1, starting transfers between devices, per_device(): lax.ppermute(own_columns[1], 'gy', [(i, (i + 1) % size) for i in range(si...  1.49 us
    ppermute x2, waiting for transfers between devices, swap_pairs(): second = lax.ppermute(second, axis, across)  1.35 us
    pallas_call x1, Pallas kernels, per_device(): pl.pallas_call(row_message_kernel, out_shape=(pltpu.VMEM((QUANTITIES, lev...  1.24 us
  transfers between devices with their start and end apart: 9, of which 3 were waited for; matrix products, arithmetic and copies ran while one was open for 0% of the time, Pallas kernels for 20%

profile of v18, /device:TPU:0, one launch (start us, length us, event | category | flops | bytes accessed | tf_op | source)
XLA Modules:
  0.0 27.9 jit_solution(590698914585266230)
XLA Ops:
  0.6 1.2 %shard_map.50 = (f32[31,4,128]{2,1,0:T(4,128)S(1)}, f32[31,4,128]{2,1,0:T(4,128)S(1)}, f32[19,96,128]{2,1,0:T(8,128)S(1)}, bf16[2,3,64,128]{3,2,1,0:T(8,128)(2,1)S(1)}, s32[16,32]{1,0:T(8,128)S(1)}) custom-call(f32[19,64,128]{2,1,0:T(8,128)} %bitcast.5, bf16[2,3,64,128]{3,2,1,0:T(8,128)(2,1)} %bitcast.7, s32[16,32]{1,0:T(8,128)} %bitcast.8), custom_call_target="tpu_custom_call" | custom-call | tf_op jit(solution)/shard_map/pallas_call | solution.py:637
  1.9 0.5 %collective-permute-start = (f32[31,4,128]{2,1,0:T(4,128)S(1)}, f32[31,4,128]{2,1,0:T(4,128)S(1)}, u32[]{:S(2)}, u32[]{:S(2)}) collective-permute-start(f32[31,4,128]{2,1,0:T(4,128)S(1)} %get-tuple-element.14), channel_id=1, source_target_pairs={{0,8},{8,0},{16,24},{24,16},{1,9},{9,1},{17,25},{25,17},{2,10},{10... | collective-permute-start | bytes 190472 | tf_op jit(solution)/shard_map/ppermute | solution.py:611
  2.4 2.6 %collective-permute-start.1 = (f32[31,4,128]{2,1,0:T(4,128)S(1)}, f32[31,4,128]{2,1,0:T(4,128)S(1)}, u32[]{:S(2)}, u32[]{:S(2)}) collective-permute-start(f32[31,4,128]{2,1,0:T(4,128)S(1)} %get-tuple-element.15), channel_id=1, source_target_pairs={{0,24},{8,16},{16,8},{24,0},{1,25},{9,17},{17,9},{25,1},{2,26},{10... | collective-permute-start | bytes 190472 | tf_op jit(solution)/shard_map/ppermute | solution.py:610
  5.0 0.3 %shard_map.51.own_high = f32[3,8,128]{2,1,0:T(8,128)S(1)} custom-call(f32[19,96,128]{2,1,0:T(8,128)S(1)} %get-tuple-element.11.held.own_held, bf16[2,3,64,128]{3,2,1,0:T(8,128)(2,1)S(1)} %get-tuple-element.12.velocity, s32[16,32]{1,0:T(8,128)S(1)} %get-tuple-element.13.solid), custom_call_target="tpu_custom_call" | custom-call | flops 2000000 | bytes 1000000 | tf_op jit(solution)/shard_map/pallas_call | solution.py:653
  5.4 1.2 %collective-permute-start.4 = (f32[3,8,128]{2,1,0:T(8,128)S(1)}, f32[3,8,128]{2,1,0:T(8,128)S(1)}, u32[]{:S(2)}, u32[]{:S(2)}) collective-permute-start(f32[3,8,128]{2,1,0:T(8,128)S(1)} %shard_map.51.own_high), channel_id=1, source_target_pairs={{0,25},{1,26},{2,27},{3,28},{4,29},{5,30},{6,31},{7,24},{8,1},{9,2... | collective-permute-start | bytes 36872 | tf_op jit(solution)/shard_map/ppermute | solution.py:619
  6.5 1.7 %collective-permute-start.3 = (f32[3,8,128]{2,1,0:T(8,128)S(1)}, f32[3,8,128]{2,1,0:T(8,128)S(1)}, u32[]{:S(2)}, u32[]{:S(2)}) collective-permute-start(f32[3,8,128]{2,1,0:T(8,128)S(1)} %shard_map.51.own_high), channel_id=1, source_target_pairs={{0,9},{1,10},{2,11},{3,12},{4,13},{5,14},{6,15},{7,8},{8,17},{9,18... | collective-permute-start | bytes 36872 | tf_op jit(solution)/shard_map/ppermute | solution.py:619
  8.2 1.5 %collective-permute-start.2 = (f32[3,8,128]{2,1,0:T(8,128)S(1)}, f32[3,8,128]{2,1,0:T(8,128)S(1)}, u32[]{:S(2)}, u32[]{:S(2)}) collective-permute-start(f32[3,8,128]{2,1,0:T(8,128)S(1)} %shard_map.51.own_high), channel_id=1, source_target_pairs={{0,1},{1,2},{2,3},{3,4},{4,5},{5,6},{6,7},{7,0},{8,9},{9,10},{10,1... | collective-permute-start | bytes 36872 | tf_op jit(solution)/shard_map/ppermute | solution.py:674
  9.7 0.3 %shard_map.52.own_low = f32[16,8,128]{2,1,0:T(8,128)S(1)} custom-call(f32[19,96,128]{2,1,0:T(8,128)S(1)} %get-tuple-element.11.held.own_held, bf16[2,3,64,128]{3,2,1,0:T(8,128)(2,1)S(1)} %get-tuple-element.12.velocity, s32[16,32]{1,0:T(8,128)S(1)} %get-tuple-element.13.solid), custom_call_target="tpu_custom_call" | custom-call | flops 2000000 | bytes 1000000 | tf_op jit(solution)/shard_map/pallas_call | solution.py:653
  10.0 0.0 collective-permute-done.row_first
  10.0 3.3 %collective-permute-start.5 = (f32[16,8,128]{2,1,0:T(8,128)S(1)}, f32[16,8,128]{2,1,0:T(8,128)S(1)}, u32[]{:S(2)}, u32[]{:S(2)}) collective-permute-start(f32[16,8,128]{2,1,0:T(8,128)S(1)} %shard_map.52.own_low), channel_id=1, source_target_pairs={{1,0},{2,1},{3,2},{4,3},{5,4},{6,5},{7,6},{0,7},{9,8},{10,9},{11,1... | collective-permute-start | bytes 196616 | tf_op jit(solution)/shard_map/ppermute | solution.py:687
  13.3 0.0 collective-permute-done.1.row_second
  13.3 0.2 shard_map.53
  13.5 0.6 %shard_map.54 = (f32[8,128]{1,0:T(8,128)S(1)}, f32[35,8,128]{2,1,0:T(8,128)S(1)}) custom-call(f32[19,96,128]{2,1,0:T(8,128)S(1)} %get-tuple-element.11.held.own_held, bf16[2,3,64,128]{3,2,1,0:T(8,128)(2,1)S(1)} %get-tuple-element.12.velocity, s32[16,32]{1,0:T(8,128)S(1)} %get-tuple-element.13.solid, f32[31,4,128]{2,1,0:T(4,128)S(1)} %collective-permute-done.row_first, ...), custom_call_target="tpu_custom_call" | custom-call | flops 20000000000 | bytes 1000000 | tf_op jit(solution)/shard_map/pallas_call | solution.py:691
  14.1 0.0 collective-permute-done.4.diagonal_after
  14.1 0.0 collective-permute-done.3.diagonal_before
  14.1 0.7 %collective-permute-done.2.columns = f32[3,8,128]{2,1,0:T(8,128)S(1)} collective-permute-done((f32[3,8,128]{2,1,0:T(8,128)S(1)}, f32[3,8,128]{2,1,0:T(8,128)S(1)}, u32[]{:S(2)}, u32[]{:S(2)}) %collective-permute-start.2) | collective-permute-done | bytes 12320 | tf_op jit(solution)/shard_map/ppermute | solution.py:674
  14.8 1.0 %shard_map.55.rest_0_ = f32[32,1,128]{2,1,0:T(1,128)} custom-call(f32[3,8,128]{2,1,0:T(8,128)S(1)} %collective-permute-done.2.columns, f32[3,8,128]{2,1,0:T(8,128)S(1)} %collective-permute-done.3.diagonal_before, f32[3,8,128]{2,1,0:T(8,128)S(1)} %collective-permute-done.4.diagonal_after, f32[35,8,128]{2,1,0:T(8,128)S(1)} %get-tuple-element.17.own_blocks, ...), custom_call_target="tpu_custom_call" | custom-call | flops 1000000 | bytes 1000000 | tf_op jit(solution)/shard_map/pallas_call | solution.py:703
  15.8 2.5 %all-to-all-start = ((f32[32,1,128]{2,1,0:T(1,128)}), f32[32,1,128]{2,1,0:T(1,128)S(1)}, u32[]{:S(2)}, u32[]{:S(2)}) async-start(f32[32,1,128]{2,1,0:T(1,128)} %shard_map.55.rest_0_), calls=%async_computation | async-start | bytes 32768 | tf_op jit(solution)/shard_map/all_to_all | solution.py:712
  18.3 0.0 collective-permute-done.5.columns.columns_after
  18.3 0.8 %shard_map.56 = f32[3,8,128]{2,1,0:T(8,128)S(1)} custom-call(f32[16,8,128]{2,1,0:T(8,128)S(1)} %collective-permute-done.5.columns.columns_after, f32[32,1,128]{2,1,0:T(1,128)} %shard_map.55.rest_0_), custom_call_target="tpu_custom_call" | custom-call | flops 10000000000 | bytes 100000 | tf_op jit(solution)/shard_map/pallas_call | solution.py:676
  19.2 1.4 %collective-permute-start.7 = (f32[3,8,128]{2,1,0:T(8,128)S(1)}, f32[3,8,128]{2,1,0:T(8,128)S(1)}, u32[]{:S(2)}, u32[]{:S(2)}) collective-permute-start(f32[3,8,128]{2,1,0:T(8,128)S(1)} %shard_map.56), channel_id=1, source_target_pairs={{0,24},{8,16},{16,8},{24,0},{1,25},{9,17},{17,9},{25,1},{2,26},{10... | collective-permute-start | bytes 36872 | tf_op jit(solution)/shard_map/ppermute | solution.py:610
  20.6 0.4 %collective-permute-start.6 = (f32[3,8,128]{2,1,0:T(8,128)S(1)}, f32[3,8,128]{2,1,0:T(8,128)S(1)}, u32[]{:S(2)}, u32[]{:S(2)}) collective-permute-start(f32[3,8,128]{2,1,0:T(8,128)S(1)} %shard_map.56), channel_id=1, source_target_pairs={{0,8},{8,0},{16,24},{24,16},{1,9},{9,1},{17,25},{25,17},{2,10},{10... | collective-permute-start | bytes 36872 | tf_op jit(solution)/shard_map/ppermute | solution.py:611
  20.9 1.4 %collective-permute-done.7.after_second = f32[3,8,128]{2,1,0:T(8,128)S(1)} collective-permute-done((f32[3,8,128]{2,1,0:T(8,128)S(1)}, f32[3,8,128]{2,1,0:T(8,128)S(1)}, u32[]{:S(2)}, u32[]{:S(2)}) %collective-permute-start.7) | collective-permute-done | bytes 12320 | tf_op jit(solution)/shard_map/ppermute | solution.py:610
  22.3 0.0 collective-permute-done.6.after_first
  22.3 2.2 %shard_map.57 = f32[19,64,128]{2,1,0:T(8,128)} custom-call(f32[19,96,128]{2,1,0:T(8,128)S(1)} %get-tuple-element.11.held.own_held, bf16[2,3,64,128]{3,2,1,0:T(8,128)(2,1)S(1)} %get-tuple-element.12.velocity, s32[16,32]{1,0:T(8,128)S(1)} %get-tuple-element.13.solid, f32[31,4,128]{2,1,0:T(4,128)S(1)} %collective-permute-done.row_first, ...), custom_call_target="tpu_custom_call" | custom-call | flops 1000000 | bytes 1000000 | tf_op jit(solution)/shard_map/pallas_call | solution.py:713
  24.5 0.9 %all-to-all-done = f32[32,1,128]{2,1,0:T(1,128)S(1)} async-done(((f32[32,1,128]{2,1,0:T(1,128)}), f32[32,1,128]{2,1,0:T(1,128)S(1)}, u32[]{:S(2)}, u32[]{:S(2)}) %all-to-all-start) | async-done | bytes 16416 | tf_op jit(solution)/shard_map/all_to_all | solution.py:712
  25.4 0.6 %slice_reduce_fusion = f32[]{:T(128)} fusion(f32[32,1,128]{2,1,0:T(1,128)S(1)} %all-to-all-done), kind=kLoop, calls=%fused_computation | loop fusion | flops 31 | bytes 132 | tf_op jit(solution)/shard_map/reduce_sum | solution.py:724
Async XLA Ops:
  1.9 8.1 %collective-permute-start = (f32[31,4,128]{2,1,0:T(4,128)S(1)}, f32[31,4,128]{2,1,0:T(4,128)S(1)}, u32[]{:S(2)}, u32[]{:S(2)}) collective-permute-start(f32[31,4,128]{2,1,0:T(4,128)S(1)} %get-tuple-element.14), channel_id=1, source_target_pairs={{0,8},{8,0},{16,24},{24,16},{1,9},{9,1},{17,25},{25,17},{2,10},{10... | collective-permute-start | bytes 190472 | tf_op jit(solution)/shard_map/ppermute | solution.py:611
  2.4 10.9 %collective-permute-start.1 = (f32[31,4,128]{2,1,0:T(4,128)S(1)}, f32[31,4,128]{2,1,0:T(4,128)S(1)}, u32[]{:S(2)}, u32[]{:S(2)}) collective-permute-start(f32[31,4,128]{2,1,0:T(4,128)S(1)} %get-tuple-element.15), channel_id=1, source_target_pairs={{0,24},{8,16},{16,8},{24,0},{1,25},{9,17},{17,9},{25,1},{2,26},{10... | collective-permute-start | bytes 190472 | tf_op jit(solution)/shard_map/ppermute | solution.py:610
  5.4 8.7 %collective-permute-start.4 = (f32[3,8,128]{2,1,0:T(8,128)S(1)}, f32[3,8,128]{2,1,0:T(8,128)S(1)}, u32[]{:S(2)}, u32[]{:S(2)}) collective-permute-start(f32[3,8,128]{2,1,0:T(8,128)S(1)} %shard_map.51.own_high), channel_id=1, source_target_pairs={{0,25},{1,26},{2,27},{3,28},{4,29},{5,30},{6,31},{7,24},{8,1},{9,2... | collective-permute-start | bytes 36872 | tf_op jit(solution)/shard_map/ppermute | solution.py:619
  6.5 7.6 %collective-permute-start.3 = (f32[3,8,128]{2,1,0:T(8,128)S(1)}, f32[3,8,128]{2,1,0:T(8,128)S(1)}, u32[]{:S(2)}, u32[]{:S(2)}) collective-permute-start(f32[3,8,128]{2,1,0:T(8,128)S(1)} %shard_map.51.own_high), channel_id=1, source_target_pairs={{0,9},{1,10},{2,11},{3,12},{4,13},{5,14},{6,15},{7,8},{8,17},{9,18... | collective-permute-start | bytes 36872 | tf_op jit(solution)/shard_map/ppermute | solution.py:619
  8.2 6.6 %collective-permute-start.2 = (f32[3,8,128]{2,1,0:T(8,128)S(1)}, f32[3,8,128]{2,1,0:T(8,128)S(1)}, u32[]{:S(2)}, u32[]{:S(2)}) collective-permute-start(f32[3,8,128]{2,1,0:T(8,128)S(1)} %shard_map.51.own_high), channel_id=1, source_target_pairs={{0,1},{1,2},{2,3},{3,4},{4,5},{5,6},{6,7},{7,0},{8,9},{9,10},{10,1... | collective-permute-start | bytes 36872 | tf_op jit(solution)/shard_map/ppermute | solution.py:674
  10.0 8.3 %collective-permute-start.5 = (f32[16,8,128]{2,1,0:T(8,128)S(1)}, f32[16,8,128]{2,1,0:T(8,128)S(1)}, u32[]{:S(2)}, u32[]{:S(2)}) collective-permute-start(f32[16,8,128]{2,1,0:T(8,128)S(1)} %shard_map.52.own_low), channel_id=1, source_target_pairs={{1,0},{2,1},{3,2},{4,3},{5,4},{6,5},{7,6},{0,7},{9,8},{10,9},{11,1... | collective-permute-start | bytes 196616 | tf_op jit(solution)/shard_map/ppermute | solution.py:687
  15.8 9.6 %all-to-all-start = ((f32[32,1,128]{2,1,0:T(1,128)}), f32[32,1,128]{2,1,0:T(1,128)S(1)}, u32[]{:S(2)}, u32[]{:S(2)}) async-start(f32[32,1,128]{2,1,0:T(1,128)} %shard_map.55.rest_0_), calls=%async_computation | async-start | bytes 32768 | tf_op jit(solution)/shard_map/all_to_all | solution.py:712
  19.2 3.1 %collective-permute-start.7 = (f32[3,8,128]{2,1,0:T(8,128)S(1)}, f32[3,8,128]{2,1,0:T(8,128)S(1)}, u32[]{:S(2)}, u32[]{:S(2)}) collective-permute-start(f32[3,8,128]{2,1,0:T(8,128)S(1)} %shard_map.56), channel_id=1, source_target_pairs={{0,24},{8,16},{16,8},{24,0},{1,25},{9,17},{17,9},{25,1},{2,26},{10... | collective-permute-start | bytes 36872 | tf_op jit(solution)/shard_map/ppermute | solution.py:610
  20.6 1.7 %collective-permute-start.6 = (f32[3,8,128]{2,1,0:T(8,128)S(1)}, f32[3,8,128]{2,1,0:T(8,128)S(1)}, u32[]{:S(2)}, u32[]{:S(2)}) collective-permute-start(f32[3,8,128]{2,1,0:T(8,128)S(1)} %shard_map.56), channel_id=1, source_target_pairs={{0,8},{8,0},{16,24},{24,16},{1,9},{9,1},{17,25},{25,17},{2,10},{10... | collective-permute-start | bytes 36872 | tf_op jit(solution)/shard_map/ppermute | solution.py:611

commit v19 on v16

--- a/solution.py
+++ b/solution.py
@@ -110,11 +110,8 @@
     parts[part] = jnp.where(lane == place + ahead, turned, parts[part])
 
 
-def row_message_kernel(
-    state, velocity, solid, row_first, row_second, held, flow, tiles, arrived
-):
-    rows = state.shape[1]
-    own = pl.ds(GUARD + 8, rows)
+def copy_kernel(state, velocity, solid, held, flow, tiles, arrived):
+    own = pl.ds(GUARD + 8, state.shape[1])
     copies = [
         pltpu.make_async_copy(state, held.at[:, own, :], arrived.at[0]),
         pltpu.make_async_copy(velocity, flow, arrived.at[1]),
@@ -124,6 +121,10 @@
         copy.start()
     for copy in copies:
         copy.wait()
+
+
+def row_message_kernel(held, flow, tiles, row_first, row_second):
+    rows = flow.shape[2]
     even = on_even("gx")
     low_row, high_row = GUARD + 8, GUARD + 8 + rows - LEVELS
 
@@ -478,7 +479,7 @@
     return whole
 
 
-def edge_drag_kernel(groups, columns, handed_first, handed_second, own_blocks, partial, shared):
+def edge_drag_kernel(groups, columns, handed_first, handed_second, own_blocks, partial, shared, summed):
     lane = lane_index()
     column = column_reader(groups)
     y_before = with_halo_rows(columns, handed_first, handed_second, groups, 0)
@@ -507,6 +508,7 @@
     place = jnp.where(lane < AFTER_LANE, lane - BEFORE_LANE, lane - AFTER_LANE)
     inside = jnp.logical_and(place > 0, place < groups - 1)
     total = partial[...] + jnp.where(inside, term, 0.0)
+    summed[...] = total
     shared[...] = jnp.broadcast_to(jnp.sum(total), shared.shape)
 
 
@@ -616,20 +618,25 @@
 
     params = pltpu.CompilerParams(vmem_limit_bytes=16 * 1024 * 1024)
     anywhere = pl.BlockSpec(memory_space=pl.ANY)
-    *row_sent, held, flow, tiles = pl.pallas_call(
-        row_message_kernel,
+    held, flow, tiles = pl.pallas_call(
+        copy_kernel,
         out_shape=(
-            pltpu.VMEM((QUANTITIES, levels, rows_y), jnp.float32),
-            pltpu.VMEM((QUANTITIES, levels, rows_y), jnp.float32),
             pltpu.VMEM((19, padded, rows_y), jnp.float32),
             pltpu.VMEM(flow.shape, flow.dtype),
             pltpu.VMEM(solid.shape, solid.dtype),
         ),
         in_specs=[anywhere] * 3,
-        out_specs=(vmem,) * 5,
+        out_specs=(vmem,) * 3,
         scratch_shapes=[pltpu.SemaphoreType.DMA((3,))],
         compiler_params=params,
     )(*(pltpu.with_memory_space_constraint(value, pltpu.HBM) for value in (state, flow, solid)))
+    row_sent = pl.pallas_call(
+        row_message_kernel,
+        out_shape=(pltpu.VMEM((QUANTITIES, levels, rows_y), jnp.float32),) * 2,
+        in_specs=[vmem] * 3,
+        out_specs=(vmem,) * 2,
+        compiler_params=params,
+    )(held, flow, tiles)
     row_got = swap_pairs(*row_sent, "gx")
     def pack(side, size, *later_than):
         return pl.pallas_call(
@@ -642,7 +649,7 @@
         )(held, flow, tiles, *later_than)
 
     own_high = pack(1, parts)
-    own_low = pack(0, 16)
+    own_low = pack(0, 16, row_sent[0])
     own_columns = own_low, own_high
     low, high = pl.pallas_call(
         functools.partial(halo_columns_kernel, groups),
@@ -682,15 +689,15 @@
         compiler_params=params,
         cost_estimate=pl.CostEstimate(flops=20_000_000_000, bytes_accessed=1_000_000, transcendentals=0),
     )(held, flow, tiles, *row_got, low)
-    own = pl.pallas_call(
+    own, summed = pl.pallas_call(
         functools.partial(edge_drag_kernel, groups),
-        out_shape=pltpu.VMEM((count, 1, rows_y), jnp.float32),
+        out_shape=(shape_of(count, 1, rows_y), pltpu.VMEM((8, rows_y), jnp.float32)),
         in_specs=[vmem] * 5,
-        out_specs=vmem,
+        out_specs=(vmem,) * 2,
         compiler_params=params,
         cost_estimate=pl.CostEstimate(flops=1_000_000, bytes_accessed=1_000_000, transcendentals=0),
     )(y_before, *handed, own_blocks, partial)
-    handed_after = hand_on(y_after, 1, own)
+    handed_after = hand_on(y_after, 1, summed)
     shared = lax.all_to_all(own, ("gx", "gy"), split_axis=0, concat_axis=0, tiled=True)
     result = pl.pallas_call(
         main_kernel,

time: 27.2 us -> 27 us (level)
  waiting for transfers between devices: 3.11 us -> 3.99 us
  Pallas kernels: 6.79 us -> 6.02 us
    pallas_call x1, Pallas kernels: 1.24 us -> 0.12 us  [per_device(): pl.pallas_call(row_message_kernel, out_shape=(pltpu.VMEM((QUANTITIES, lev...]
    pallas_call x1 -> x2, Pallas kernels: 0.95 us -> 2.04 us  [the longest x1 1.11 us: per_device(): pl.pallas_call(copy_kernel, out_shape=(pltpu.VMEM((19, padded, rows_y), j...]
    ppermute x3, starting transfers between devices: 3.17 us -> 2.23 us  [swap_pairs(): second = lax.ppermute(second, axis, across)]
    ppermute x3, starting transfers between devices: 1.73 us -> 2.56 us  [swap_pairs(): return (lax.ppermute(first, axis, inside), second)]
    pallas_call x2, Pallas kernels: 0.9 us -> 0.15 us  [hand_on(): pl.pallas_call(functools.partial(hand_on_kernel, groups, ahead), out_shap...]
    all_to_all x1, waiting for transfers between devices: 0.9 us -> 1.65 us  [per_device(): lax.all_to_all(own, ('gx', 'gy'), split_axis=0, concat_axis=0, tiled=True)]
  transfers between devices with their start and end apart: 9 -> 9, of which waited for: 3 -> 3; matrix products, arithmetic and copies ran while one was open for 0% -> 0% of each run, Pallas kernels for 19% -> 17%
where the time goes in v19:
time: 27 us; the launch traced here: 26.8 us
  starting transfers between devices  13.7 us (51%)
  Pallas kernels  6.02 us (22%)
  waiting for transfers between devices  3.99 us (15%)
  between operations  2.47 us (9%)
  other arithmetic  0.63 us (2%)
    ppermute x1, starting transfers between devices, per_device(): lax.ppermute(own_columns[0], 'gy', [((i + 1) % size, i) for i in range(si...  3.28 us
    ppermute x1, starting transfers between devices, per_device(): lax.ppermute(own_columns[1], 'gy', [(i, (i + 1) % size) for i in range(si...  2.99 us
    all_to_all x1, starting transfers between devices, per_device(): lax.all_to_all(own, ('gx', 'gy'), split_axis=0, concat_axis=0, tiled=True)  2.63 us
    ppermute x3, starting transfers between devices, swap_pairs(): return (lax.ppermute(first, axis, inside), second)  2.56 us
    ppermute x3, waiting for transfers between devices, swap_pairs(): second = lax.ppermute(second, axis, across)  2.32 us
    pallas_call x1, Pallas kernels, per_device(): pl.pallas_call(main_kernel, out_shape=shape_of(19, rows, rows_y), in_spec...  2.24 us
    ppermute x3, starting transfers between devices, swap_pairs(): second = lax.ppermute(second, axis, across)  2.23 us
    all_to_all x1, waiting for transfers between devices, per_device(): lax.all_to_all(own, ('gx', 'gy'), split_axis=0, concat_axis=0, tiled=True)  1.65 us
  transfers between devices with their start and end apart: 9, of which 3 were waited for; matrix products, arithmetic and copies ran while one was open for 0% of the time, Pallas kernels for 17%

profile of v19, /device:TPU:0, one launch (start us, length us, event | category | flops | bytes accessed | tf_op | source)
XLA Modules:
  0.0 26.8 jit_solution(12263646332850669820)
XLA Ops:
  0.6 1.1 %shard_map.50 = (f32[19,96,128]{2,1,0:T(8,128)S(1)}, bf16[2,3,64,128]{3,2,1,0:T(8,128)(2,1)S(1)}, s32[16,32]{1,0:T(8,128)S(1)}) custom-call(f32[19,64,128]{2,1,0:T(8,128)} %bitcast.5, bf16[2,3,64,128]{3,2,1,0:T(8,128)(2,1)} %bitcast.7, s32[16,32]{1,0:T(8,128)} %bitcast.8), custom_call_target="tpu_custom_call" | custom-call | tf_op jit(solution)/shard_map/pallas_call | solution.py:621
  1.7 0.3 %shard_map.52.own_high = f32[3,8,128]{2,1,0:T(8,128)S(1)} custom-call(f32[19,96,128]{2,1,0:T(8,128)S(1)} %get-tuple-element.13.held.own_held, bf16[2,3,64,128]{3,2,1,0:T(8,128)(2,1)S(1)} %get-tuple-element.14.flow.velocity, s32[16,32]{1,0:T(8,128)S(1)} %get-tuple-element.15.tiles.solid), custom_call_target="tpu_custom_call" | custom-call | flops 2000000 | bytes 1000000 | tf_op jit(solution)/shard_map/pallas_call | solution.py:642
  2.1 3.0 %collective-permute-start.2 = (f32[3,8,128]{2,1,0:T(8,128)S(1)}, f32[3,8,128]{2,1,0:T(8,128)S(1)}, u32[]{:S(2)}, u32[]{:S(2)}) collective-permute-start(f32[3,8,128]{2,1,0:T(8,128)S(1)} %shard_map.52.own_high), channel_id=1, source_target_pairs={{0,1},{1,2},{2,3},{3,4},{4,5},{5,6},{6,7},{7,0},{8,9},{9,10},{10,1... | collective-permute-start | bytes 36872 | tf_op jit(solution)/shard_map/ppermute | solution.py:663
  5.1 0.1 shard_map.51
  5.2 0.7 %collective-permute-start.1 = (f32[31,4,128]{2,1,0:T(4,128)S(1)}, f32[31,4,128]{2,1,0:T(4,128)S(1)}, u32[]{:S(2)}, u32[]{:S(2)}) collective-permute-start(f32[31,4,128]{2,1,0:T(4,128)S(1)} %get-tuple-element.17), channel_id=1, source_target_pairs={{0,24},{8,16},{16,8},{24,0},{1,25},{9,17},{17,9},{25,1},{2,26},{10... | collective-permute-start | bytes 190472 | tf_op jit(solution)/shard_map/ppermute | solution.py:602
  5.9 1.0 %collective-permute-start = (f32[31,4,128]{2,1,0:T(4,128)S(1)}, f32[31,4,128]{2,1,0:T(4,128)S(1)}, u32[]{:S(2)}, u32[]{:S(2)}) collective-permute-start(f32[31,4,128]{2,1,0:T(4,128)S(1)} %get-tuple-element.16.rest_0_), channel_id=1, source_target_pairs={{0,8},{8,0},{16,24},{24,16},{1,9},{9,1},{17,25},{25,17},{2,10},{10... | collective-permute-start | bytes 190472 | tf_op jit(solution)/shard_map/ppermute | solution.py:603
  6.8 0.3 %shard_map.54.own_low = f32[16,8,128]{2,1,0:T(8,128)S(1)} custom-call(f32[19,96,128]{2,1,0:T(8,128)S(1)} %get-tuple-element.13.held.own_held, bf16[2,3,64,128]{3,2,1,0:T(8,128)(2,1)S(1)} %get-tuple-element.14.flow.velocity, s32[16,32]{1,0:T(8,128)S(1)} %get-tuple-element.15.tiles.solid, f32[31,4,128]{2,1,0:T(4,128)S(1)} %get-tuple-element.16.rest_0_), custom_call_target="tpu_custom_call" | custom-call | flops 2000000 | bytes 1000000 | tf_op jit(solution)/shard_map/pallas_call | solution.py:642
  7.2 3.3 %collective-permute-start.5 = (f32[16,8,128]{2,1,0:T(8,128)S(1)}, f32[16,8,128]{2,1,0:T(8,128)S(1)}, u32[]{:S(2)}, u32[]{:S(2)}) collective-permute-start(f32[16,8,128]{2,1,0:T(8,128)S(1)} %shard_map.54.own_low), channel_id=1, source_target_pairs={{1,0},{2,1},{3,2},{4,3},{5,4},{6,5},{7,6},{0,7},{9,8},{10,9},{11,1... | collective-permute-start | bytes 196616 | tf_op jit(solution)/shard_map/ppermute | solution.py:676
  10.5 0.0 collective-permute-done.2.columns
  10.5 0.1 shard_map.53
  10.5 0.0 collective-permute-start.4
  10.6 1.2 %collective-permute-start.3 = (f32[3,8,128]{2,1,0:T(8,128)S(1)}, f32[3,8,128]{2,1,0:T(8,128)S(1)}, u32[]{:S(2)}, u32[]{:S(2)}) collective-permute-start(f32[3,8,128]{2,1,0:T(8,128)S(1)} %shard_map.53), channel_id=1, source_target_pairs={{0,8},{8,0},{16,24},{24,16},{1,9},{9,1},{17,25},{25,17},{2,10},{10... | collective-permute-start | bytes 36872 | tf_op jit(solution)/shard_map/ppermute | solution.py:603
  11.8 0.0 collective-permute-done.1.row_second
  11.8 0.0 collective-permute-done.row_first
  11.8 0.2 shard_map.55
  12.0 0.6 %shard_map.56 = (f32[8,128]{1,0:T(8,128)S(1)}, f32[35,8,128]{2,1,0:T(8,128)S(1)}) custom-call(f32[19,96,128]{2,1,0:T(8,128)S(1)} %get-tuple-element.13.held.own_held, bf16[2,3,64,128]{3,2,1,0:T(8,128)(2,1)S(1)} %get-tuple-element.14.flow.velocity, s32[16,32]{1,0:T(8,128)S(1)} %get-tuple-element.15.tiles.solid, ...), custom_call_target="tpu_custom_call" | custom-call | flops 20000000000 | bytes 1000000 | tf_op jit(solution)/shard_map/pallas_call | solution.py:680
  12.6 1.1 %collective-permute-done.4.handed_second = f32[3,8,128]{2,1,0:T(8,128)S(1)} collective-permute-done((f32[3,8,128]{2,1,0:T(8,128)S(1)}, f32[3,8,128]{2,1,0:T(8,128)S(1)}, u32[]{:S(2)}, u32[]{:S(2)}) %collective-permute-start.4) | collective-permute-done | bytes 12320 | tf_op jit(solution)/shard_map/ppermute | solution.py:602
  13.7 0.0 collective-permute-done.3.handed_first
  13.7 0.9 %shard_map.57 = (f32[32,1,128]{2,1,0:T(1,128)}, f32[8,128]{1,0:T(8,128)S(1)}) custom-call(f32[3,8,128]{2,1,0:T(8,128)S(1)} %collective-permute-done.2.columns, f32[3,8,128]{2,1,0:T(8,128)S(1)} %collective-permute-done.3.handed_first, f32[3,8,128]{2,1,0:T(8,128)S(1)} %collective-permute-done.4.handed_second, f32[35,8,128]{2,1,0:T(8,128)S(1)} %get-tuple-element.19.own_blocks, ...), custom_call_target="tpu_custom_call" | custom-call | flops 1000000 | bytes 1000000 | tf_op jit(solution)/shard_map/pallas_call | solution.py:692
  14.6 2.6 %all-to-all-start = ((f32[32,1,128]{2,1,0:T(1,128)}), f32[32,1,128]{2,1,0:T(1,128)S(1)}, u32[]{:S(2)}, u32[]{:S(2)}) async-start(f32[32,1,128]{2,1,0:T(1,128)} %get-tuple-element.23), calls=%async_computation | async-start | bytes 32768 | tf_op jit(solution)/shard_map/all_to_all | solution.py:701
  17.3 0.0 collective-permute-done.5.columns.columns_after
  17.3 0.1 shard_map.58
  17.4 1.5 %collective-permute-start.7 = (f32[3,8,128]{2,1,0:T(8,128)S(1)}, f32[3,8,128]{2,1,0:T(8,128)S(1)}, u32[]{:S(2)}, u32[]{:S(2)}) collective-permute-start(f32[3,8,128]{2,1,0:T(8,128)S(1)} %shard_map.58), channel_id=1, source_target_pairs={{0,24},{8,16},{16,8},{24,0},{1,25},{9,17},{17,9},{25,1},{2,26},{10... | collective-permute-start | bytes 36872 | tf_op jit(solution)/shard_map/ppermute | solution.py:602
  18.9 0.4 %collective-permute-start.6 = (f32[3,8,128]{2,1,0:T(8,128)S(1)}, f32[3,8,128]{2,1,0:T(8,128)S(1)}, u32[]{:S(2)}, u32[]{:S(2)}) collective-permute-start(f32[3,8,128]{2,1,0:T(8,128)S(1)} %shard_map.58), channel_id=1, source_target_pairs={{0,8},{8,0},{16,24},{24,16},{1,9},{9,1},{17,25},{25,17},{2,10},{10... | collective-permute-start | bytes 36872 | tf_op jit(solution)/shard_map/ppermute | solution.py:603
  19.3 1.2 %collective-permute-done.7.after_second = f32[3,8,128]{2,1,0:T(8,128)S(1)} collective-permute-done((f32[3,8,128]{2,1,0:T(8,128)S(1)}, f32[3,8,128]{2,1,0:T(8,128)S(1)}, u32[]{:S(2)}, u32[]{:S(2)}) %collective-permute-start.7) | collective-permute-done | bytes 12320 | tf_op jit(solution)/shard_map/ppermute | solution.py:602
  20.5 0.0 collective-permute-done.6.after_first
  20.5 2.2 %shard_map.59 = f32[19,64,128]{2,1,0:T(8,128)} custom-call(f32[19,96,128]{2,1,0:T(8,128)S(1)} %get-tuple-element.13.held.own_held, bf16[2,3,64,128]{3,2,1,0:T(8,128)(2,1)S(1)} %get-tuple-element.14.flow.velocity, s32[16,32]{1,0:T(8,128)S(1)} %get-tuple-element.15.tiles.solid, f32[31,4,128]{2,1,0:T(4,128)S(1)} %collective-permute-done.row_first, ...), custom_call_target="tpu_custom_call" | custom-call | flops 1000000 | bytes 1000000 | tf_op jit(solution)/shard_map/pallas_call | solution.py:702
  22.7 1.7 %all-to-all-done = f32[32,1,128]{2,1,0:T(1,128)S(1)} async-done(((f32[32,1,128]{2,1,0:T(1,128)}), f32[32,1,128]{2,1,0:T(1,128)S(1)}, u32[]{:S(2)}, u32[]{:S(2)}) %all-to-all-start) | async-done | bytes 16416 | tf_op jit(solution)/shard_map/all_to_all | solution.py:701
  24.4 0.6 %slice_reduce_fusion = f32[]{:T(128)} fusion(f32[32,1,128]{2,1,0:T(1,128)S(1)} %all-to-all-done), kind=kLoop, calls=%fused_computation | loop fusion | flops 31 | bytes 132 | tf_op jit(solution)/shard_map/reduce_sum | solution.py:713
Async XLA Ops:
  2.1 8.4 %collective-permute-start.2 = (f32[3,8,128]{2,1,0:T(8,128)S(1)}, f32[3,8,128]{2,1,0:T(8,128)S(1)}, u32[]{:S(2)}, u32[]{:S(2)}) collective-permute-start(f32[3,8,128]{2,1,0:T(8,128)S(1)} %shard_map.52.own_high), channel_id=1, source_target_pairs={{0,1},{1,2},{2,3},{3,4},{4,5},{5,6},{6,7},{7,0},{8,9},{9,10},{10,1... | collective-permute-start | bytes 36872 | tf_op jit(solution)/shard_map/ppermute | solution.py:663
  5.2 6.6 %collective-permute-start.1 = (f32[31,4,128]{2,1,0:T(4,128)S(1)}, f32[31,4,128]{2,1,0:T(4,128)S(1)}, u32[]{:S(2)}, u32[]{:S(2)}) collective-permute-start(f32[31,4,128]{2,1,0:T(4,128)S(1)} %get-tuple-element.17), channel_id=1, source_target_pairs={{0,24},{8,16},{16,8},{24,0},{1,25},{9,17},{17,9},{25,1},{2,26},{10... | collective-permute-start | bytes 190472 | tf_op jit(solution)/shard_map/ppermute | solution.py:602
  5.9 5.9 %collective-permute-start = (f32[31,4,128]{2,1,0:T(4,128)S(1)}, f32[31,4,128]{2,1,0:T(4,128)S(1)}, u32[]{:S(2)}, u32[]{:S(2)}) collective-permute-start(f32[31,4,128]{2,1,0:T(4,128)S(1)} %get-tuple-element.16.rest_0_), channel_id=1, source_target_pairs={{0,8},{8,0},{16,24},{24,16},{1,9},{9,1},{17,25},{25,17},{2,10},{10... | collective-permute-start | bytes 190472 | tf_op jit(solution)/shard_map/ppermute | solution.py:603
  7.2 10.1 %collective-permute-start.5 = (f32[16,8,128]{2,1,0:T(8,128)S(1)}, f32[16,8,128]{2,1,0:T(8,128)S(1)}, u32[]{:S(2)}, u32[]{:S(2)}) collective-permute-start(f32[16,8,128]{2,1,0:T(8,128)S(1)} %shard_map.54.own_low), channel_id=1, source_target_pairs={{1,0},{2,1},{3,2},{4,3},{5,4},{6,5},{7,6},{0,7},{9,8},{10,9},{11,1... | collective-permute-start | bytes 196616 | tf_op jit(solution)/shard_map/ppermute | solution.py:676
  10.5 3.2 %collective-permute-start.4 = (f32[3,8,128]{2,1,0:T(8,128)S(1)}, f32[3,8,128]{2,1,0:T(8,128)S(1)}, u32[]{:S(2)}, u32[]{:S(2)}) collective-permute-start(f32[3,8,128]{2,1,0:T(8,128)S(1)} %shard_map.53), channel_id=1, source_target_pairs={{0,24},{8,16},{16,8},{24,0},{1,25},{9,17},{17,9},{25,1},{2,26},{10... | collective-permute-start | bytes 36872 | tf_op jit(solution)/shard_map/ppermute | solution.py:602
  10.6 3.1 %collective-permute-start.3 = (f32[3,8,128]{2,1,0:T(8,128)S(1)}, f32[3,8,128]{2,1,0:T(8,128)S(1)}, u32[]{:S(2)}, u32[]{:S(2)}) collective-permute-start(f32[3,8,128]{2,1,0:T(8,128)S(1)} %shard_map.53), channel_id=1, source_target_pairs={{0,8},{8,0},{16,24},{24,16},{1,9},{9,1},{17,25},{25,17},{2,10},{10... | collective-permute-start | bytes 36872 | tf_op jit(solution)/shard_map/ppermute | solution.py:603
  14.6 9.8 %all-to-all-start = ((f32[32,1,128]{2,1,0:T(1,128)}), f32[32,1,128]{2,1,0:T(1,128)S(1)}, u32[]{:S(2)}, u32[]{:S(2)}) async-start(f32[32,1,128]{2,1,0:T(1,128)} %get-tuple-element.23), calls=%async_computation | async-start | bytes 32768 | tf_op jit(solution)/shard_map/all_to_all | solution.py:701
  17.4 3.1 %collective-permute-start.7 = (f32[3,8,128]{2,1,0:T(8,128)S(1)}, f32[3,8,128]{2,1,0:T(8,128)S(1)}, u32[]{:S(2)}, u32[]{:S(2)}) collective-permute-start(f32[3,8,128]{2,1,0:T(8,128)S(1)} %shard_map.58), channel_id=1, source_target_pairs={{0,24},{8,16},{16,8},{24,0},{1,25},{9,17},{17,9},{25,1},{2,26},{10... | collective-permute-start | bytes 36872 | tf_op jit(solution)/shard_map/ppermute | solution.py:602
  18.9 1.6 %collective-permute-start.6 = (f32[3,8,128]{2,1,0:T(8,128)S(1)}, f32[3,8,128]{2,1,0:T(8,128)S(1)}, u32[]{:S(2)}, u32[]{:S(2)}) collective-permute-start(f32[3,8,128]{2,1,0:T(8,128)S(1)} %shard_map.58), channel_id=1, source_target_pairs={{0,8},{8,0},{16,24},{24,16},{1,9},{9,1},{17,25},{25,17},{2,10},{10... | collective-permute-start | bytes 36872 | tf_op jit(solution)/shard_map/ppermute | solution.py:603

commit v20 on v19

--- a/solution.py
+++ b/solution.py
@@ -123,7 +123,7 @@
         copy.wait()
 
 
-def row_message_kernel(held, flow, tiles, row_first, row_second):
+def row_message_kernel(held, flow, tiles, columns_sent, row_first, row_second):
     rows = flow.shape[2]
     even = on_even("gx")
     low_row, high_row = GUARD + 8, GUARD + 8 + rows - LEVELS
@@ -474,8 +474,12 @@
     above, below = halo_lanes(groups, ahead)
     whole = []
     for part in range(handed_first.shape[0]):
-        value = jnp.where(above, from_before[part], columns[part])
-        whole.append(jnp.where(below, from_after[part], value))
+        last, first = from_before[part], from_after[part]
+        if ahead == 0:
+            last = pltpu.roll(last, LANES - (groups - 2), 1)
+            first = pltpu.roll(first, groups - 2, 1)
+        value = jnp.where(above, last, columns[part])
+        whole.append(jnp.where(below, first, value))
     return whole
 
 
@@ -630,14 +634,6 @@
         scratch_shapes=[pltpu.SemaphoreType.DMA((3,))],
         compiler_params=params,
     )(*(pltpu.with_memory_space_constraint(value, pltpu.HBM) for value in (state, flow, solid)))
-    row_sent = pl.pallas_call(
-        row_message_kernel,
-        out_shape=(pltpu.VMEM((QUANTITIES, levels, rows_y), jnp.float32),) * 2,
-        in_specs=[vmem] * 3,
-        out_specs=(vmem,) * 2,
-        compiler_params=params,
-    )(held, flow, tiles)
-    row_got = swap_pairs(*row_sent, "gx")
     def pack(side, size, *later_than):
         return pl.pallas_call(
             functools.partial(own_columns_kernel, side),
@@ -649,6 +645,14 @@
         )(held, flow, tiles, *later_than)
 
     own_high = pack(1, parts)
+    row_sent = pl.pallas_call(
+        row_message_kernel,
+        out_shape=(pltpu.VMEM((QUANTITIES, levels, rows_y), jnp.float32),) * 2,
+        in_specs=[vmem] * 4,
+        out_specs=(vmem,) * 2,
+        compiler_params=params,
+    )(held, flow, tiles, own_high)
+    row_got = swap_pairs(*row_sent, "gx")
     own_low = pack(0, 16, row_sent[0])
     own_columns = own_low, own_high
     low, high = pl.pallas_call(
@@ -672,7 +676,7 @@
         )(columns, *later_than)
         return swap_pairs(handed, handed, "gx")
 
-    handed = hand_on(y_before, 0)
+    handed = swap_pairs(y_before, y_before, "gx")
     y_after = lax.ppermute(own_columns[0], "gy", [((i + 1) % size, i) for i in range(size)])
     count = lax.axis_size("gx") * size
     field = pltpu.VMEM((19, padded, rows_y), jnp.float32)

time: 27 us -> 28 us (1.037)
  waiting for transfers between devices: 3.99 us -> 6.06 us
  starting transfers between devices: 13.7 us -> 12.7 us
    ppermute x3, starting transfers between devices: 2.23 us -> 3.83 us  [swap_pairs(): second = lax.ppermute(second, axis, across)]
    ppermute x1, starting transfers between devices: 2.99 us -> 1.49 us  [per_device(): lax.ppermute(own_columns[1], 'gy', [(i, (i + 1) % size) for i in range(si...]
    ppermute x1, waiting for transfers between devices: 0.01 us -> 1.28 us  [per_device(): lax.ppermute(own_columns[1], 'gy', [(i, (i + 1) % size) for i in range(si...]
    ppermute x3, starting transfers between devices: 2.56 us -> 1.57 us  [swap_pairs(): return (lax.ppermute(first, axis, inside), second)]
    ppermute x3, waiting for transfers between devices: 2.32 us -> 3.13 us  [swap_pairs(): second = lax.ppermute(second, axis, across)]
  transfers between devices with their start and end apart: 9 -> 9, of which waited for: 3 -> 4; matrix products, arithmetic and copies ran while one was open for 0% -> 0% of each run, Pallas kernels for 17% -> 16%
where the time goes in v20:
time: 28 us; the launch traced here: 27.9 us
  starting transfers between devices  12.7 us (45%)
  waiting for transfers between devices  6.06 us (22%)
  Pallas kernels  6.02 us (22%)
  between operations  2.46 us (9%)
  other arithmetic  0.63 us (2%)
    ppermute x3, starting transfers between devices, swap_pairs(): second = lax.ppermute(second, axis, across)  3.83 us
    ppermute x1, starting transfers between devices, per_device(): lax.ppermute(own_columns[0], 'gy', [((i + 1) % size, i) for i in range(si...  3.28 us
    ppermute x3, waiting for transfers between devices, swap_pairs(): second = lax.ppermute(second, axis, across)  3.13 us
    all_to_all x1, starting transfers between devices, per_device(): lax.all_to_all(own, ('gx', 'gy'), split_axis=0, concat_axis=0, tiled=True)  2.5 us
    pallas_call x1, Pallas kernels, per_device(): pl.pallas_call(main_kernel, out_shape=shape_of(19, rows, rows_y), in_spec...  2.24 us
    all_to_all x1, waiting for transfers between devices, per_device(): lax.all_to_all(own, ('gx', 'gy'), split_axis=0, concat_axis=0, tiled=True)  1.65 us
    ppermute x3, starting transfers between devices, swap_pairs(): return (lax.ppermute(first, axis, inside), second)  1.57 us
    ppermute x1, starting transfers between devices, per_device(): lax.ppermute(own_columns[1], 'gy', [(i, (i + 1) % size) for i in range(si...  1.49 us
  transfers between devices with their start and end apart: 9, of which 4 were waited for; matrix products, arithmetic and copies ran while one was open for 0% of the time, Pallas kernels for 16%

profile of v20, /device:TPU:0, one launch (start us, length us, event | category | flops | bytes accessed | tf_op | source)
XLA Modules:
  0.0 27.9 jit_solution(9946354765369679547)
XLA Ops:
  0.6 1.1 %shard_map.50 = (f32[19,96,128]{2,1,0:T(8,128)S(1)}, bf16[2,3,64,128]{3,2,1,0:T(8,128)(2,1)S(1)}, s32[16,32]{1,0:T(8,128)S(1)}) custom-call(f32[19,64,128]{2,1,0:T(8,128)} %bitcast.5, bf16[2,3,64,128]{3,2,1,0:T(8,128)(2,1)} %bitcast.7, s32[16,32]{1,0:T(8,128)} %bitcast.8), custom_call_target="tpu_custom_call" | custom-call | tf_op jit(solution)/shard_map/pallas_call | solution.py:625
  1.7 0.3 %shard_map.51.columns_sent.own_high = f32[3,8,128]{2,1,0:T(8,128)S(1)} custom-call(f32[19,96,128]{2,1,0:T(8,128)S(1)} %get-tuple-element.13.held.own_held, bf16[2,3,64,128]{3,2,1,0:T(8,128)(2,1)S(1)} %get-tuple-element.14.velocity.flow, s32[16,32]{1,0:T(8,128)S(1)} %get-tuple-element.15.solid.tiles), custom_call_target="tpu_custom_call" | custom-call | flops 2000000 | bytes 1000000 | tf_op jit(solution)/shard_map/pallas_call | solution.py:638
  2.1 0.1 shard_map.52
  2.2 2.4 %collective-permute-start.1 = (f32[31,4,128]{2,1,0:T(4,128)S(1)}, f32[31,4,128]{2,1,0:T(4,128)S(1)}, u32[]{:S(2)}, u32[]{:S(2)}) collective-permute-start(f32[31,4,128]{2,1,0:T(4,128)S(1)} %get-tuple-element.17), channel_id=1, source_target_pairs={{0,24},{8,16},{16,8},{24,0},{1,25},{9,17},{17,9},{25,1},{2,26},{10... | collective-permute-start | bytes 190472 | tf_op jit(solution)/shard_map/ppermute | solution.py:606
  4.6 0.7 %collective-permute-start = (f32[31,4,128]{2,1,0:T(4,128)S(1)}, f32[31,4,128]{2,1,0:T(4,128)S(1)}, u32[]{:S(2)}, u32[]{:S(2)}) collective-permute-start(f32[31,4,128]{2,1,0:T(4,128)S(1)} %get-tuple-element.16.rest_0_), channel_id=1, source_target_pairs={{0,8},{8,0},{16,24},{24,16},{1,9},{9,1},{17,25},{25,17},{2,10},{10... | collective-permute-start | bytes 190472 | tf_op jit(solution)/shard_map/ppermute | solution.py:607
  5.3 1.5 %collective-permute-start.2 = (f32[3,8,128]{2,1,0:T(8,128)S(1)}, f32[3,8,128]{2,1,0:T(8,128)S(1)}, u32[]{:S(2)}, u32[]{:S(2)}) collective-permute-start(f32[3,8,128]{2,1,0:T(8,128)S(1)} %shard_map.51.columns_sent.own_high), channel_id=1, source_target_pairs={{0,1},{1,2},{2,3},{3,4},{4,5},{5,6},{6,7},{7,0},{8,9},{9,10},{10,1... | collective-permute-start | bytes 36872 | tf_op jit(solution)/shard_map/ppermute | solution.py:667
  6.8 0.3 %shard_map.53.own_low = f32[16,8,128]{2,1,0:T(8,128)S(1)} custom-call(f32[19,96,128]{2,1,0:T(8,128)S(1)} %get-tuple-element.13.held.own_held, bf16[2,3,64,128]{3,2,1,0:T(8,128)(2,1)S(1)} %get-tuple-element.14.velocity.flow, s32[16,32]{1,0:T(8,128)S(1)} %get-tuple-element.15.solid.tiles, f32[31,4,128]{2,1,0:T(4,128)S(1)} %get-tuple-element.16.rest_0_), custom_call_target="tpu_custom_call" | custom-call | flops 2000000 | bytes 1000000 | tf_op jit(solution)/shard_map/pallas_call | solution.py:638
  7.1 3.3 %collective-permute-start.5 = (f32[16,8,128]{2,1,0:T(8,128)S(1)}, f32[16,8,128]{2,1,0:T(8,128)S(1)}, u32[]{:S(2)}, u32[]{:S(2)}) collective-permute-start(f32[16,8,128]{2,1,0:T(8,128)S(1)} %shard_map.53.own_low), channel_id=1, source_target_pairs={{1,0},{2,1},{3,2},{4,3},{5,4},{6,5},{7,6},{0,7},{9,8},{10,9},{11,1... | collective-permute-start | bytes 196616 | tf_op jit(solution)/shard_map/ppermute | solution.py:680
  10.4 1.3 %collective-permute-done.2.columns = f32[3,8,128]{2,1,0:T(8,128)S(1)} collective-permute-done((f32[3,8,128]{2,1,0:T(8,128)S(1)}, f32[3,8,128]{2,1,0:T(8,128)S(1)}, u32[]{:S(2)}, u32[]{:S(2)}) %collective-permute-start.2) | collective-permute-done | bytes 12320 | tf_op jit(solution)/shard_map/ppermute | solution.py:667
  11.7 0.0 collective-permute-start.4
  11.7 0.5 %collective-permute-start.3 = (f32[3,8,128]{2,1,0:T(8,128)S(1)}, f32[3,8,128]{2,1,0:T(8,128)S(1)}, u32[]{:S(2)}, u32[]{:S(2)}) collective-permute-start(f32[3,8,128]{2,1,0:T(8,128)S(1)} %collective-permute-done.2.columns), channel_id=1, source_target_pairs={{0,8},{8,0},{16,24},{24,16},{1,9},{9,1},{17,25},{25,17},{2,10},{10... | collective-permute-start | bytes 36872 | tf_op jit(solution)/shard_map/ppermute | solution.py:607
  12.2 0.0 collective-permute-done.1.row_second
  12.2 0.0 collective-permute-done.row_first
  12.2 0.2 shard_map.54
  12.4 0.6 %shard_map.55 = (f32[8,128]{1,0:T(8,128)S(1)}, f32[35,8,128]{2,1,0:T(8,128)S(1)}) custom-call(f32[19,96,128]{2,1,0:T(8,128)S(1)} %get-tuple-element.13.held.own_held, bf16[2,3,64,128]{3,2,1,0:T(8,128)(2,1)S(1)} %get-tuple-element.14.velocity.flow, s32[16,32]{1,0:T(8,128)S(1)} %get-tuple-element.15.solid.tiles, ...), custom_call_target="tpu_custom_call" | custom-call | flops 20000000000 | bytes 1000000 | tf_op jit(solution)/shard_map/pallas_call | solution.py:684
  13.0 1.8 %collective-permute-done.4.handed_second = f32[3,8,128]{2,1,0:T(8,128)S(1)} collective-permute-done((f32[3,8,128]{2,1,0:T(8,128)S(1)}, f32[3,8,128]{2,1,0:T(8,128)S(1)}, u32[]{:S(2)}, u32[]{:S(2)}) %collective-permute-start.4) | collective-permute-done | bytes 12320 | tf_op jit(solution)/shard_map/ppermute | solution.py:606
  14.8 0.0 collective-permute-done.3.handed_first
  14.8 1.0 %shard_map.56 = (f32[32,1,128]{2,1,0:T(1,128)}, f32[8,128]{1,0:T(8,128)S(1)}) custom-call(f32[3,8,128]{2,1,0:T(8,128)S(1)} %collective-permute-done.2.columns, f32[3,8,128]{2,1,0:T(8,128)S(1)} %collective-permute-done.3.handed_first, f32[3,8,128]{2,1,0:T(8,128)S(1)} %collective-permute-done.4.handed_second, f32[35,8,128]{2,1,0:T(8,128)S(1)} %get-tuple-element.19.own_blocks, ...), custom_call_target="tpu_custom_call" | custom-call | flops 1000000 | bytes 1000000 | tf_op jit(solution)/shard_map/pallas_call | solution.py:696
  15.8 2.5 %all-to-all-start = ((f32[32,1,128]{2,1,0:T(1,128)}), f32[32,1,128]{2,1,0:T(1,128)S(1)}, u32[]{:S(2)}, u32[]{:S(2)}) async-start(f32[32,1,128]{2,1,0:T(1,128)} %get-tuple-element.23), calls=%async_computation | async-start | bytes 32768 | tf_op jit(solution)/shard_map/all_to_all | solution.py:705
  18.3 0.0 collective-permute-done.5.columns.columns_after
  18.3 0.1 shard_map.57
  18.4 1.4 %collective-permute-start.7 = (f32[3,8,128]{2,1,0:T(8,128)S(1)}, f32[3,8,128]{2,1,0:T(8,128)S(1)}, u32[]{:S(2)}, u32[]{:S(2)}) collective-permute-start(f32[3,8,128]{2,1,0:T(8,128)S(1)} %shard_map.57), channel_id=1, source_target_pairs={{0,24},{8,16},{16,8},{24,0},{1,25},{9,17},{17,9},{25,1},{2,26},{10... | collective-permute-start | bytes 36872 | tf_op jit(solution)/shard_map/ppermute | solution.py:606
  19.8 0.4 %collective-permute-start.6 = (f32[3,8,128]{2,1,0:T(8,128)S(1)}, f32[3,8,128]{2,1,0:T(8,128)S(1)}, u32[]{:S(2)}, u32[]{:S(2)}) collective-permute-start(f32[3,8,128]{2,1,0:T(8,128)S(1)} %shard_map.57), channel_id=1, source_target_pairs={{0,8},{8,0},{16,24},{24,16},{1,9},{9,1},{17,25},{25,17},{2,10},{10... | collective-permute-start | bytes 36872 | tf_op jit(solution)/shard_map/ppermute | solution.py:607
  20.2 1.4 %collective-permute-done.7.after_second = f32[3,8,128]{2,1,0:T(8,128)S(1)} collective-permute-done((f32[3,8,128]{2,1,0:T(8,128)S(1)}, f32[3,8,128]{2,1,0:T(8,128)S(1)}, u32[]{:S(2)}, u32[]{:S(2)}) %collective-permute-start.7) | collective-permute-done | bytes 12320 | tf_op jit(solution)/shard_map/ppermute | solution.py:606
  21.6 0.0 collective-permute-done.6.after_first
  21.6 2.2 %shard_map.58 = f32[19,64,128]{2,1,0:T(8,128)} custom-call(f32[19,96,128]{2,1,0:T(8,128)S(1)} %get-tuple-element.13.held.own_held, bf16[2,3,64,128]{3,2,1,0:T(8,128)(2,1)S(1)} %get-tuple-element.14.velocity.flow, s32[16,32]{1,0:T(8,128)S(1)} %get-tuple-element.15.solid.tiles, f32[31,4,128]{2,1,0:T(4,128)S(1)} %collective-permute-done.row_first, ...), custom_call_target="tpu_custom_call" | custom-call | flops 1000000 | bytes 1000000 | tf_op jit(solution)/shard_map/pallas_call | solution.py:706
  23.8 1.7 %all-to-all-done = f32[32,1,128]{2,1,0:T(1,128)S(1)} async-done(((f32[32,1,128]{2,1,0:T(1,128)}), f32[32,1,128]{2,1,0:T(1,128)S(1)}, u32[]{:S(2)}, u32[]{:S(2)}) %all-to-all-start) | async-done | bytes 16416 | tf_op jit(solution)/shard_map/all_to_all | solution.py:705
  25.4 0.6 %slice_reduce_fusion = f32[]{:T(128)} fusion(f32[32,1,128]{2,1,0:T(1,128)S(1)} %all-to-all-done), kind=kLoop, calls=%fused_computation | loop fusion | flops 31 | bytes 132 | tf_op jit(solution)/shard_map/reduce_sum | solution.py:717
Async XLA Ops:
  2.2 10.0 %collective-permute-start.1 = (f32[31,4,128]{2,1,0:T(4,128)S(1)}, f32[31,4,128]{2,1,0:T(4,128)S(1)}, u32[]{:S(2)}, u32[]{:S(2)}) collective-permute-start(f32[31,4,128]{2,1,0:T(4,128)S(1)} %get-tuple-element.17), channel_id=1, source_target_pairs={{0,24},{8,16},{16,8},{24,0},{1,25},{9,17},{17,9},{25,1},{2,26},{10... | collective-permute-start | bytes 190472 | tf_op jit(solution)/shard_map/ppermute | solution.py:606
  4.6 7.6 %collective-permute-start = (f32[31,4,128]{2,1,0:T(4,128)S(1)}, f32[31,4,128]{2,1,0:T(4,128)S(1)}, u32[]{:S(2)}, u32[]{:S(2)}) collective-permute-start(f32[31,4,128]{2,1,0:T(4,128)S(1)} %get-tuple-element.16.rest_0_), channel_id=1, source_target_pairs={{0,8},{8,0},{16,24},{24,16},{1,9},{9,1},{17,25},{25,17},{2,10},{10... | collective-permute-start | bytes 190472 | tf_op jit(solution)/shard_map/ppermute | solution.py:607
  5.3 6.4 %collective-permute-start.2 = (f32[3,8,128]{2,1,0:T(8,128)S(1)}, f32[3,8,128]{2,1,0:T(8,128)S(1)}, u32[]{:S(2)}, u32[]{:S(2)}) collective-permute-start(f32[3,8,128]{2,1,0:T(8,128)S(1)} %shard_map.51.columns_sent.own_high), channel_id=1, source_target_pairs={{0,1},{1,2},{2,3},{3,4},{4,5},{5,6},{6,7},{7,0},{8,9},{9,10},{10,1... | collective-permute-start | bytes 36872 | tf_op jit(solution)/shard_map/ppermute | solution.py:667
  7.1 11.2 %collective-permute-start.5 = (f32[16,8,128]{2,1,0:T(8,128)S(1)}, f32[16,8,128]{2,1,0:T(8,128)S(1)}, u32[]{:S(2)}, u32[]{:S(2)}) collective-permute-start(f32[16,8,128]{2,1,0:T(8,128)S(1)} %shard_map.53.own_low), channel_id=1, source_target_pairs={{1,0},{2,1},{3,2},{4,3},{5,4},{6,5},{7,6},{0,7},{9,8},{10,9},{11,1... | collective-permute-start | bytes 196616 | tf_op jit(solution)/shard_map/ppermute | solution.py:680
  11.7 3.1 %collective-permute-start.4 = (f32[3,8,128]{2,1,0:T(8,128)S(1)}, f32[3,8,128]{2,1,0:T(8,128)S(1)}, u32[]{:S(2)}, u32[]{:S(2)}) collective-permute-start(f32[3,8,128]{2,1,0:T(8,128)S(1)} %collective-permute-done.2.columns), channel_id=1, source_target_pairs={{0,24},{8,16},{16,8},{24,0},{1,25},{9,17},{17,9},{25,1},{2,26},{10... | collective-permute-start | bytes 36872 | tf_op jit(solution)/shard_map/ppermute | solution.py:606
  11.7 3.1 %collective-permute-start.3 = (f32[3,8,128]{2,1,0:T(8,128)S(1)}, f32[3,8,128]{2,1,0:T(8,128)S(1)}, u32[]{:S(2)}, u32[]{:S(2)}) collective-permute-start(f32[3,8,128]{2,1,0:T(8,128)S(1)} %collective-permute-done.2.columns), channel_id=1, source_target_pairs={{0,8},{8,0},{16,24},{24,16},{1,9},{9,1},{17,25},{25,17},{2,10},{10... | collective-permute-start | bytes 36872 | tf_op jit(solution)/shard_map/ppermute | solution.py:607
  15.8 9.6 %all-to-all-start = ((f32[32,1,128]{2,1,0:T(1,128)}), f32[32,1,128]{2,1,0:T(1,128)S(1)}, u32[]{:S(2)}, u32[]{:S(2)}) async-start(f32[32,1,128]{2,1,0:T(1,128)} %get-tuple-element.23), calls=%async_computation | async-start | bytes 32768 | tf_op jit(solution)/shard_map/all_to_all | solution.py:705
  18.4 3.1 %collective-permute-start.7 = (f32[3,8,128]{2,1,0:T(8,128)S(1)}, f32[3,8,128]{2,1,0:T(8,128)S(1)}, u32[]{:S(2)}, u32[]{:S(2)}) collective-permute-start(f32[3,8,128]{2,1,0:T(8,128)S(1)} %shard_map.57), channel_id=1, source_target_pairs={{0,24},{8,16},{16,8},{24,0},{1,25},{9,17},{17,9},{25,1},{2,26},{10... | collective-permute-start | bytes 36872 | tf_op jit(solution)/shard_map/ppermute | solution.py:606
  19.8 1.7 %collective-permute-start.6 = (f32[3,8,128]{2,1,0:T(8,128)S(1)}, f32[3,8,128]{2,1,0:T(8,128)S(1)}, u32[]{:S(2)}, u32[]{:S(2)}) collective-permute-start(f32[3,8,128]{2,1,0:T(8,128)S(1)} %shard_map.57), channel_id=1, source_target_pairs={{0,8},{8,0},{16,24},{24,16},{1,9},{9,1},{17,25},{25,17},{2,10},{10... | collective-permute-start | bytes 36872 | tf_op jit(solution)/shard_map/ppermute | solution.py:607
